TPU v7x, 512 devices: a whole 4x8x8 slice. The times are simulated.
512 devices in a mesh: row: 32 (over y, z_hi), col: 16 (over x, z_lo, core).
Axes of the slice: x: 4, y: 8, z: 8 (z_hi: 4, z_lo: 2; z = z_hi * 2 + z_lo), core: 2. Of those that a mesh axis runs over, the one named last changes fastest.
Arguments:
- activations: bfloat16 [1024, 8192], P('row', 'col'), may hold values from -6 to 6
- out_grad: bfloat16 [1024, 8192], P('row', 'col'), may hold values from -6 to 6
- gate_pre: bfloat16 [1024, 8192], P('row', 'col'), may hold values from -8 to 8
- up_pre: bfloat16 [1024, 8192], P('row', 'col'), may hold values from -6 to 6
- gate_weight: bfloat16 [8192, 8192], P('row', 'col'), may hold values from -0.0625 to 0.0625
- up_weight: bfloat16 [8192, 8192], P('row', 'col'), may hold values from -0.0625 to 0.0625
- down_weight: bfloat16 [8192, 8192], P('col', 'row'), may hold values from -0.0625 to 0.0625
Outputs:
- input_grad: bfloat16 [1024, 8192], P('row', 'col')
- gate_weight_grad: bfloat16 [8192, 8192], P('row', 'col')
- up_weight_grad: bfloat16 [8192, 8192], P('row', 'col')
- down_weight_grad: bfloat16 [8192, 8192], P('col', 'row')
All inputs are finite; a program needn't handle non-finite values.
Results may differ from a plain program's by a relative error of at most 0.005.
Values may be sent and summed in bfloat16 or wider, within the bound.
No kernel may reach another device: no remote copies, remote signals or barrier semaphores. Data moves between devices by JAX's collectives and lax.ppermute only.
A program may use at most 64 MiB of HBM per device.

v0:
```python
import jax
import jax.numpy as jnp
from jax import lax
from jax.sharding import PartitionSpec as P


def broadcast(value, axis, source):
    kept = jnp.where(lax.axis_index(axis) == source, value, 0).astype(value.dtype)
    return lax.psum(kept, axis)


def contract_rows(left, right):
    return lax.dot_general(
        left, right, (((0,), (0,)), ((), ())), preferred_element_type=jnp.float32
    )


def contract_cols(left, right):
    return lax.dot_general(
        left, right, (((1,), (1,)), ((), ())), preferred_element_type=jnp.float32
    )


def swiglu_back(hidden_grad, gate_pre, up_pre):
    gate_float = gate_pre.astype(jnp.float32)
    up_float = up_pre.astype(jnp.float32)
    sigmoid_gate = jax.nn.sigmoid(gate_float)
    activated = gate_float * sigmoid_gate
    hidden = (activated * up_float).astype(jnp.bfloat16)
    gate_grad = (
        hidden_grad * up_float * sigmoid_gate * (1.0 + gate_float * (1.0 - sigmoid_gate))
    ).astype(jnp.bfloat16)
    up_grad = (hidden_grad * activated).astype(jnp.bfloat16)
    return (gate_grad, up_grad, hidden)


def local(activations, out_grad, gate_pre, up_pre, gate_weight, up_weight, down_weight):
    block_width = gate_weight.shape[0]
    tokens_all, grads_all = (
        lax.all_gather(activations, "row", axis=0, tiled=True),
        lax.all_gather(out_grad, "row", axis=0, tiled=True),
    )
    factor = lax.axis_size("row") // lax.axis_size("col")
    row_index = lax.axis_index("row")
    offset = row_index % factor * block_width
    token_piece = lax.dynamic_slice_in_dim(tokens_all, offset, block_width, 1)
    grad_piece = lax.dynamic_slice_in_dim(grads_all, offset, block_width, 1)
    token_cols, grad_cols = (
        broadcast(token_piece, "col", row_index // factor),
        broadcast(grad_piece, "col", row_index // factor),
    )
    hidden_grad = lax.psum_scatter(
        contract_cols(grad_cols, down_weight), "row", scatter_dimension=0, tiled=True
    )
    gate_grad, up_grad, hidden = swiglu_back(hidden_grad, gate_pre, up_pre)
    gate_all, up_all, hidden_all = (
        lax.all_gather(gate_grad, "row", axis=0, tiled=True),
        lax.all_gather(up_grad, "row", axis=0, tiled=True),
        lax.all_gather(hidden, "row", axis=0, tiled=True),
    )
    partial_input = contract_cols(gate_all, gate_weight) + contract_cols(up_all, up_weight)
    exchanged = lax.all_to_all(partial_input, "row", split_axis=0, concat_axis=1, tiled=True)
    input_grad = lax.psum_scatter(exchanged, "col", scatter_dimension=1, tiled=True).astype(
        jnp.bfloat16
    )
    gate_weight_grad = contract_rows(token_cols, gate_all).astype(jnp.bfloat16)
    up_weight_grad = contract_rows(token_cols, up_all).astype(jnp.bfloat16)
    down_weight_grad = contract_rows(hidden_all, grad_cols).astype(jnp.bfloat16)
    return (input_grad, gate_weight_grad, up_weight_grad, down_weight_grad)


def solution(mesh):
    return jax.shard_map(
        local,
        mesh=mesh,
        in_specs=(
            P("row", "col"),
            P("row", "col"),
            P("row", "col"),
            P("row", "col"),
            P("row", "col"),
            P("row", "col"),
            P("col", "row"),
        ),
        out_specs=(P("row", "col"), P("row", "col"), P("row", "col"), P("col", "row")),
        check_vma=False,
    )
```

profile of v0, /device:TPU:8, one launch (start us, length us, event | category | flops | bytes accessed | tf_op | source)
XLA Modules:
  0.0 891.3 jit_solution(12098875758942119454)
XLA Ops:
  7.2 0.0 copy-start
  7.2 0.0 all-gather.12.cloned.1.call-start
  7.2 0.7 all-gather.12.cloned.1.call-update
  7.9 0.0 all-gather.6.cloned.1.call-start
  8.0 0.7 all-gather.6.cloned.1.call-update
  8.7 0.0 all-reduce.3.cloned.1.call-start
  8.7 90.0 %all-gather.12.cloned.1.call-done = bf16[1024,512]{1,0:T(8,128)(2,1)} async-done(((bf16[32,512]{1,0:T(8,128)(2,1)}), bf16[1024,512]{1,0:T(8,128)(2,1)}) %all-gather.12.cloned.1.call-update) | async-done | bytes 1048592 | tf_op jit(solution)/shard_map/all_gather | solution.py:40
  98.8 1.9 dynamic-slice_select_fusion
  100.7 81.9 %all-gather.6.cloned.1.call-done = bf16[1024,512]{1,0:T(8,128)(2,1)} async-done(((bf16[32,512]{1,0:T(8,128)(2,1)}), bf16[1024,512]{1,0:T(8,128)(2,1)}) %all-gather.6.cloned.1.call-update) | async-done | bytes 1048592 | tf_op jit(solution)/shard_map/all_gather | solution.py:41
  182.6 1.9 dynamic-slice_select_fusion.1
  184.5 0.0 all-reduce.3.cloned.1.call-update
  184.6 0.0 reduce-scatter.3.cloned.1.call-start
  184.6 129.3 %all-reduce.3.cloned.1.call-done = (bf16[1024,256]{1,0:T(8,128)(2,1)}, bf16[1024,256]{1,0:T(8,128)(2,1)}) async-done(((bf16[1024,256]{1,0:T(8,128)(2,1)}, bf16[1024,256]{1,0:T(8,128)(2,1)}), (bf16[1024,256]{1,0:T(8,128)(2,1)}, bf16[1024,256]{1,0:T(8,128)(2,1)})) %all-reduce.3.cloned.1.call-update) | async-done | bytes 1048592 | tf_op jit(solution)/shard_map/psum | solution.py:9
  313.9 0.0 copy-done
  313.9 2.9 fusion.8
  316.8 0.0 reduce-scatter.3.cloned.1.call-update
  316.8 0.0 all-gather.8.cloned.1.call-start
  316.9 230.9 %reduce-scatter.3.cloned.1.call-done = f32[32,512]{1,0:T(8,128)} async-done(((f32[1024,512]{1,0:T(8,128)}), f32[32,512]{1,0:T(8,128)}) %reduce-scatter.3.cloned.1.call-update) | async-done | bytes 65552 | tf_op jit(solution)/shard_map/reduce_scatter | solution.py:52
  547.8 0.0 copy-done.6
  547.8 0.0 copy-done.7
  547.8 1.5 multiply_convert_fusion
  549.3 0.0 all-gather.8.cloned.1.call-update
  549.3 0.0 all-gather.10.cloned.1.call-start
  549.3 0.5 all-gather.10.cloned.1.call-update
  549.9 81.9 %all-gather.8.cloned.1.call-done = bf16[1024,512]{1,0:T(8,128)(2,1)} async-done(((bf16[32,512]{1,0:T(8,128)(2,1)}), bf16[1024,512]{1,0:T(8,128)(2,1)}) %all-gather.8.cloned.1.call-update) | async-done | bytes 1048592 | tf_op jit(solution)/shard_map/all_gather | solution.py:57
  631.8 0.0 copy-done.4
  631.8 1.7 fusion.9
  633.5 82.6 %all-gather.10.cloned.1.call-done = bf16[1024,512]{1,0:T(8,128)(2,1)} async-done(((bf16[32,512]{1,0:T(8,128)(2,1)}), bf16[1024,512]{1,0:T(8,128)(2,1)}) %all-gather.10.cloned.1.call-update) | async-done | bytes 1048592 | tf_op jit(solution)/shard_map/all_gather | solution.py:58
  716.1 0.0 copy-done.5
  716.1 2.6 convolution_add_fusion
  718.7 9.3 %all-to-all-start = ((f32[32,32,256]{2,1,0:T(8,128)}), f32[32,32,256]{2,1,0:T(8,128)S(1)}, u32[]{:S(2)}, u32[]{:S(2)}) async-start(f32[32,32,256]{2,1,0:T(8,128)} %bitcast), calls=%async_computation.1 | async-start | bytes 2097152 | tf_op jit(solution)/shard_map/all_to_all | solution.py:62
  728.1 0.0 copy-start.1
  728.1 0.0 all-gather.14.cloned.1.call-start
  728.1 0.7 all-gather.14.cloned.1.call-update
  728.8 0.0 reduce-scatter.5.cloned.1.call-start
  728.9 24.7 %all-to-all-done = f32[32,32,256]{2,1,0:T(8,128)S(1)} async-done(((f32[32,32,256]{2,1,0:T(8,128)}), f32[32,32,256]{2,1,0:T(8,128)S(1)}, u32[]{:S(2)}, u32[]{:S(2)}) %all-to-all-start) | async-done | bytes 1048608 | tf_op jit(solution)/shard_map/all_to_all | solution.py:62
  753.6 1.1 copy.12
  754.6 0.0 reduce-scatter.5.cloned.1.call-update
  754.7 0.0 copy-start.3
  754.7 0.0 copy-done.1
  754.7 2.3 convolution_convert_fusion.2
  757.0 0.0 copy-done.2
  757.0 0.0 copy-done.8
  757.0 1.2 convolution_convert_fusion.1
  758.1 57.5 %all-gather.14.cloned.1.call-done = bf16[1024,512]{1,0:T(8,128)(2,1)} async-done(((bf16[32,512]{1,0:T(8,128)(2,1)}), bf16[1024,512]{1,0:T(8,128)(2,1)}) %all-gather.14.cloned.1.call-update) | async-done | bytes 1048592 | tf_op jit(solution)/shard_map/all_gather | solution.py:59
  815.6 2.4 convolution_convert_fusion
  818.1 64.9 %reduce-scatter.5.cloned.1.call-done = f32[32,512]{1,0:T(8,128)} async-done(((f32[32,8192]{1,0:T(8,128)}), f32[32,512]{1,0:T(8,128)}) %reduce-scatter.5.cloned.1.call-update) | async-done | bytes 65552 | tf_op jit(solution)/shard_map/reduce_scatter | solution.py:63
  883.0 1.5 convert_element_type.34
  (7 shorter events, 0.0 us)
Async XLA Ops:
  7.2 306.7 %copy-start = (bf16[512,256]{1,0:T(8,128)(2,1)S(1)}, bf16[512,256]{1,0:T(8,128)(2,1)}, u32[]{:S(2)}) copy-start(bf16[512,256]{1,0:T(8,128)(2,1)} %param.13) | copy-start | bytes 786436
  7.2 91.6 %all-gather.12.cloned.1.call-start = ((), (), s32[]{:S(2)}) async-start(), calls=%async_computation.8 | async-start | bytes 1081344 | tf_op jit(solution)/shard_map/all_gather | solution.py:40
  7.9 174.7 %all-gather.6.cloned.1.call-start = ((), (), s32[]{:S(2)}) async-start(), calls=%async_computation.3 | async-start | bytes 1081344 | tf_op jit(solution)/shard_map/all_gather | solution.py:41
  8.7 305.2 %all-reduce.3.cloned.1.call-start = ((), (), s32[]{:S(2)}) async-start(), calls=%async_computation.10 | async-start | bytes 2097152 | tf_op jit(solution)/shard_map/psum | solution.py:9
  184.6 363.2 %reduce-scatter.3.cloned.1.call-start = ((), (), s32[]{:S(2)}) async-start(), calls=%async_computation.4 | async-start | bytes 2162688 | tf_op jit(solution)/shard_map/reduce_scatter | solution.py:52
  313.9 233.8 %copy-start.6 = (bf16[32,512]{1,0:T(8,128)(2,1)S(1)}, bf16[32,512]{1,0:T(8,128)(2,1)}, u32[]{:S(2)}) copy-start(bf16[32,512]{1,0:T(8,128)(2,1)} %param.9) | copy-start | bytes 98308
  313.9 233.8 %copy-start.7 = (bf16[32,512]{1,0:T(8,128)(2,1)S(1)}, bf16[32,512]{1,0:T(8,128)(2,1)}, u32[]{:S(2)}) copy-start(bf16[32,512]{1,0:T(8,128)(2,1)} %param.10) | copy-start | bytes 98308
  313.9 317.9 %copy-start.4 = (bf16[256,512]{1,0:T(8,128)(2,1)S(1)}, bf16[256,512]{1,0:T(8,128)(2,1)}, u32[]{:S(2)}) copy-start(bf16[256,512]{1,0:T(8,128)(2,1)} %param.11) | copy-start | bytes 786436
  316.8 399.3 %copy-start.5 = (bf16[256,512]{1,0:T(8,128)(2,1)S(1)}, bf16[256,512]{1,0:T(8,128)(2,1)}, u32[]{:S(2)}) copy-start(bf16[256,512]{1,0:T(8,128)(2,1)} %param.12) | copy-start | bytes 786436
  316.8 315.0 %all-gather.8.cloned.1.call-start = ((), (), s32[]{:S(2)}) async-start(), calls=%async_computation.5 | async-start | bytes 1081344 | tf_op jit(solution)/shard_map/all_gather | solution.py:57
  549.3 166.8 %all-gather.10.cloned.1.call-start = ((), (), s32[]{:S(2)}) async-start(), calls=%async_computation.6 | async-start | bytes 1081344 | tf_op jit(solution)/shard_map/all_gather | solution.py:58
  718.7 34.8 %all-to-all-start = ((f32[32,32,256]{2,1,0:T(8,128)}), f32[32,32,256]{2,1,0:T(8,128)S(1)}, u32[]{:S(2)}, u32[]{:S(2)}) async-start(f32[32,32,256]{2,1,0:T(8,128)} %bitcast), calls=%async_computation.1 | async-start | bytes 2097152 | tf_op jit(solution)/shard_map/all_to_all | solution.py:62
  728.1 26.6 %copy-start.1 = (bf16[1024,512]{1,0:T(8,128)(2,1)S(1)}, bf16[1024,512]{1,0:T(8,128)(2,1)}, u32[]{:S(2)}) copy-start(bf16[1024,512]{1,0:T(8,128)(2,1)} %all-gather.8.cloned.1.call-done) | copy-start | bytes 3145732
  728.1 87.5 %all-gather.14.cloned.1.call-start = ((), (), s32[]{:S(2)}) async-start(), calls=%async_computation.9 | async-start | bytes 1081344 | tf_op jit(solution)/shard_map/all_gather | solution.py:59
  728.8 154.1 %reduce-scatter.5.cloned.1.call-start = ((), (), s32[]{:S(2)}) async-start(), calls=%async_computation.7 | async-start | bytes 1114112 | tf_op jit(solution)/shard_map/reduce_scatter | solution.py:63
  753.6 3.4 copy-start.2
  754.6 2.3 copy-start.8
  754.7 61.0 %copy-start.3 = (bf16[1024,256]{1,0:T(8,128)(2,1)S(1)}, bf16[1024,256]{1,0:T(8,128)(2,1)}, u32[]{:S(2)}) copy-start(bf16[1024,256]{1,0:T(8,128)(2,1)} %get-tuple-element.4) | copy-start | bytes 1572868
Sparse Core Ops, SparseCore 0:
  11.2 87.5 all-gather.11
  101.9 80.6 all-gather.5
  185.6 128.2 all-reduce.2
  318.9 228.8 reduce-scatter.2
  551.3 80.4 all-gather.7
  635.4 80.6 all-gather.9
  732.1 83.4 all-gather.13
  818.4 64.4 reduce-scatter.4
where the time goes:
time: 892 us; the launch traced here: 891 us
  waiting for transfers between devices  846 us (95%)
  between operations  14.2 us (2%)
  matrix products  13.1 us (1%)
  starting transfers between devices  9.65 us (1%)
    reduce_scatter x1, waiting for transfers between devices, local(): lax.psum_scatter(contract_cols(grad_cols, down_weight), 'row', scatter_di...  231 us
    psum x1, waiting for transfers between devices, broadcast(): return lax.psum(kept, axis)  129 us
    all_gather x1, waiting for transfers between devices, local(): lax.all_gather(activations, 'row', axis=0, tiled=True)  90 us
    all_gather x1, waiting for transfers between devices, local(): lax.all_gather(up_grad, 'row', axis=0, tiled=True)  82.6 us
    all_gather x1, waiting for transfers between devices, local(): lax.all_gather(gate_grad, 'row', axis=0, tiled=True)  81.9 us
    all_gather x1, waiting for transfers between devices, local(): lax.all_gather(out_grad, 'row', axis=0, tiled=True)  81.9 us
    reduce_scatter x1, waiting for transfers between devices, local(): lax.psum_scatter(exchanged, 'col', scatter_dimension=1, tiled=True)  64.9 us
    all_gather x1, waiting for transfers between devices, local(): lax.all_gather(hidden, 'row', axis=0, tiled=True)  57.5 us
  transfers between devices with their start and end apart: 9, of which 9 were waited for; matrix products, arithmetic and copies ran while one was open for 1% of the time, Pallas kernels for 0%

commit v1 on v0

v1 whole, which is shorter than its diff:
```python
import jax
import jax.numpy as jnp
from jax import lax
from jax.sharding import Mesh
from jax.sharding import PartitionSpec as P

ROW = ("y", "zh")
COL = ("x", "zl", "core")
ALL = ROW + COL
R, C = 32, 16

SAME = [(t * C + f, (2 * f + t % 2) * C + t // 2) for t in range(R) for f in range(C)]
OTHER = [(t * C + f, (2 * f + 1 - t % 2) * C + t // 2) for t in range(R) for f in range(C)]


def inverse(pairs):
    return [(b, a) for a, b in pairs]


def contract_rows(left, right):
    return lax.dot_general(
        left, right, (((0,), (0,)), ((), ())), preferred_element_type=jnp.float32
    )


def contract_cols(left, right):
    return lax.dot_general(
        left, right, (((1,), (1,)), ((), ())), preferred_element_type=jnp.float32
    )


def to_features(tile, parity):
    low, high = tile[..., :256], tile[..., 256:]
    mine = jnp.where(parity == 0, low, high)
    rest = jnp.where(parity == 0, high, low)
    mine = lax.ppermute(mine, ALL, SAME)
    rest = lax.ppermute(rest, ALL, OTHER)
    first = jnp.where(parity == 0, mine, rest)
    second = jnp.where(parity == 0, rest, mine)
    return jnp.concatenate([first, second], axis=-2)


def to_tokens(piece, parity):
    first, second = piece[:32], piece[32:]
    mine = jnp.where(parity == 0, first, second)
    rest = jnp.where(parity == 0, second, first)
    mine = lax.ppermute(mine, ALL, inverse(SAME))
    rest = lax.ppermute(rest, ALL, inverse(OTHER))
    low = jnp.where(parity == 0, mine, rest)
    high = jnp.where(parity == 0, rest, mine)
    return jnp.concatenate([low, high], axis=1)


def gather_copies(block, axes, size):
    copies = jnp.broadcast_to(block[None], (size,) + block.shape)
    got = lax.all_to_all(copies, axes, 0, 0, tiled=True)
    return got.reshape((size * block.shape[0],) + block.shape[1:])


def scatter_sum(partial, axes, size):
    pieces = partial.astype(jnp.bfloat16).reshape((size, partial.shape[0] // size, partial.shape[1]))
    got = lax.all_to_all(pieces, axes, 0, 0, tiled=True)
    return jnp.sum(got.astype(jnp.float32), axis=0).astype(jnp.bfloat16)


def swiglu_back(hidden_grad, gate_pre, up_pre):
    grad_float = hidden_grad.astype(jnp.float32)
    gate_float = gate_pre.astype(jnp.float32)
    up_float = up_pre.astype(jnp.float32)
    sigmoid_gate = jax.nn.sigmoid(gate_float)
    activated = gate_float * sigmoid_gate
    gate_grad = (
        grad_float * up_float * sigmoid_gate * (1.0 + gate_float * (1.0 - sigmoid_gate))
    ).astype(jnp.bfloat16)
    up_grad = (grad_float * activated).astype(jnp.bfloat16)
    hidden = (activated * up_float).astype(jnp.bfloat16)
    return gate_grad, up_grad, hidden


def local(activations, out_grad, gate_pre, up_pre, gate_weight, up_weight, down_weight):
    parity = lax.axis_index("zh") % 2
    pre = lax.all_gather(jnp.concatenate([gate_pre, up_pre], axis=1), ROW, axis=0, tiled=True)
    pieces = to_features(jnp.stack([out_grad, activations]), parity)
    grad_cols = gather_copies(pieces[0], COL, C)
    token_cols = gather_copies(pieces[1], COL, C)
    hidden_grad = scatter_sum(contract_cols(grad_cols, down_weight), ROW, R)
    hidden_grad = gather_copies(hidden_grad, ROW, R)
    gate_all, up_all, hidden_all = swiglu_back(hidden_grad, pre[:, :512], pre[:, 512:])
    partial_input = contract_cols(gate_all, gate_weight) + contract_cols(up_all, up_weight)
    input_grad = to_tokens(scatter_sum(partial_input, COL, C), parity)
    gate_weight_grad = contract_rows(token_cols, gate_all).astype(jnp.bfloat16)
    up_weight_grad = contract_rows(token_cols, up_all).astype(jnp.bfloat16)
    down_weight_grad = contract_rows(hidden_all, grad_cols).astype(jnp.bfloat16)
    return (input_grad, gate_weight_grad, up_weight_grad, down_weight_grad)


def solution(mesh):
    fine = Mesh(mesh.devices.reshape(8, 4, 4, 2, 2), ALL)
    return jax.shard_map(
        local,
        mesh=fine,
        in_specs=(P(ROW, COL),) * 6 + (P(COL, ROW),),
        out_specs=(P(ROW, COL),) * 3 + (P(COL, ROW),),
        check_vma=False,
    )
```

time: 892 us -> 218 us (0.24)
  the two profiles are of different devices: /device:TPU:8 before, /device:TPU:5 now
where the time goes in v1:
time: 218 us; the launch traced here: 217 us
  waiting for transfers between devices  82.2 us (38%)
  starting transfers between devices  56.3 us (26%)
  blocking collectives  46 us (21%)
  between operations  14.2 us (7%)
  matrix products  10.8 us (5%)
  other arithmetic  5.14 us (2%)
  local copies, waits for them, and re-layouts  2.27 us (1%)
    all_to_all x2, blocking collectives, gather_copies(): got = lax.all_to_all(copies, axes, 0, 0, tiled=True)  46 us
    all_gather x1, waiting for transfers between devices, local(): lax.all_gather(jnp.concatenate([gate_pre, up_pre], axis=1), ROW, axis=0,...  33.6 us
    all_to_all x2, waiting for transfers between devices, scatter_sum(): got = lax.all_to_all(pieces, axes, 0, 0, tiled=True)  29.1 us
    ppermute x1, starting transfers between devices, to_features(): rest = lax.ppermute(rest, ALL, OTHER)  16.4 us
    ppermute x1, waiting for transfers between devices, to_features(): mine = lax.ppermute(mine, ALL, SAME)  14.3 us
    all_to_all x2, starting transfers between devices, scatter_sum(): got = lax.all_to_all(pieces, axes, 0, 0, tiled=True)  12.1 us
    all_to_all x1, starting transfers between devices, gather_copies(): got = lax.all_to_all(copies, axes, 0, 0, tiled=True)  11.6 us
    dot_general x3, matrix products, contract_rows(): lax.dot_general(left, right, (((0,), (0,)), ((), ())), preferred_element_...  7.59 us
  transfers between devices with their start and end apart: 8, of which 5 were waited for; matrix products, arithmetic and copies ran while one was open for 6% of the time, Pallas kernels for 0%

profile of v1, /device:TPU:5, one launch (start us, length us, event | category | flops | bytes accessed | tf_op | source)
XLA Modules:
  0.0 216.8 jit_solution(17905003749446685553)
XLA Ops:
  7.2 0.0 copy-start
  7.2 0.9 broadcast_select_fusion.2
  8.1 16.4 %collective-permute-start.1 = (bf16[2,32,256]{2,1,0:T(8,128)(2,1)S(1)}, bf16[2,32,256]{2,1,0:T(8,128)(2,1)S(1)}, u32[]{:S(2)}, u32[]{:S(2)}) collective-permute-start(bf16[2,32,256]{2,1,0:T(8,128)(2,1)S(1)} %get-tuple-element.10), channel_id=1, source_target_pairs={{0,16},{1,48},{2,80},{3,112},{4,144},{5,176},{6,208},{7,240},{8,27... | collective-permute-start | bytes 98312 | tf_op jit(solution)/shard_map/ppermute | solution.py:37
  24.5 2.1 collective-permute-start
  26.6 0.0 collective-permute-done.1
  26.6 14.3 %collective-permute-done = bf16[2,32,256]{2,1,0:T(8,128)(2,1)S(1)} collective-permute-done((bf16[2,32,256]{2,1,0:T(8,128)(2,1)S(1)}, bf16[2,32,256]{2,1,0:T(8,128)(2,1)S(1)}, u32[]{:S(2)}, u32[]{:S(2)}) %collective-permute-start) | collective-permute-done | bytes 32800 | tf_op jit(solution)/shard_map/ppermute | solution.py:36
  40.9 12.3 %all_to_all.25 = bf16[16,64,256]{2,1,0:T(8,128)(2,1)S(1)} all-to-all(bf16[16,64,256]{2,1,0:T(8,128)(2,1)S(1)} %broadcast_in_dim.21), channel_id=1, replica_groups=mesh['y'=8,'zh'=4,'x'=4,'zl'=2,'core'=2] {'x','zl','core'}, dimensions={0} | all-to-all | bytes 1048576 | tf_op jit(solution)/shard_map/all_to_all | solution.py:56
  53.2 0.0 copy-start.1
  53.2 0.0 copy-start.5
  53.2 0.0 copy-start.6
  53.2 0.8 copy-done.1
  54.0 0.0 copy-done
  54.0 1.5 convolution_convert_fusion
  55.5 4.2 %all-to-all-start.1 = ((bf16[32,32,512]{2,1,0:T(8,128)(2,1)}), bf16[32,32,512]{2,1,0:T(8,128)(2,1)S(1)}, u32[]{:S(2)}, u32[]{:S(2)}) async-start(bf16[32,32,512]{2,1,0:T(8,128)(2,1)} %bitcast.4), calls=%async_computation.1 | async-start | bytes 2097152 | tf_op jit(solution)/shard_map/all_to_all | solution.py:62
  59.7 0.0 all-gather.2.cloned.1.call-start
  59.7 0.0 copy-done.5
  59.7 0.0 copy-done.6
  59.7 0.6 pad_maximum_fusion
  60.4 0.0 all-gather.2.cloned.1.call-update
  60.4 26.5 %all-to-all-done.1 = bf16[32,32,512]{2,1,0:T(8,128)(2,1)S(1)} async-done(((bf16[32,32,512]{2,1,0:T(8,128)(2,1)}), bf16[32,32,512]{2,1,0:T(8,128)(2,1)S(1)}, u32[]{:S(2)}, u32[]{:S(2)}) %all-to-all-start.1) | async-done | bytes 1048608 | tf_op jit(solution)/shard_map/all_to_all | solution.py:62
  86.9 0.2 reduce_sum.24
  87.1 0.1 broadcast_in_dim.22
  87.2 33.6 %all_to_all.26 = bf16[32,32,512]{2,1,0:T(8,128)(2,1)S(1)} all-to-all(bf16[32,32,512]{2,1,0:T(8,128)(2,1)S(1)} %broadcast_in_dim.22), channel_id=1, replica_groups=mesh['y'=8,'zh'=4,'x'=4,'zl'=2,'core'=2] {'y','zh'}, dimensions={0} | all-to-all | bytes 2097152 | tf_op jit(solution)/shard_map/all_to_all | solution.py:56
  120.8 0.8 broadcast_in_dim.24
  121.7 11.6 %all-to-all-start.4 = ((bf16[16,64,256]{2,1,0:T(8,128)(2,1)}), bf16[16,64,256]{2,1,0:T(8,128)(2,1)}, u32[]{:S(2)}, u32[]{:S(2)}) async-start(bf16[16,64,256]{2,1,0:T(8,128)(2,1)} %broadcast_in_dim.24), calls=%async_computation.4 | async-start | bytes 1048576 | tf_op jit(solution)/shard_map/all_to_all | solution.py:56
  133.3 33.6 %all-gather.2.cloned.1.call-done = bf16[1024,1024]{1,0:T(8,128)(2,1)} async-done(((bf16[32,1024]{1,0:T(8,128)(2,1)}), bf16[1024,1024]{1,0:T(8,128)(2,1)}) %all-gather.2.cloned.1.call-update) | async-done | bytes 2097168 | tf_op jit(solution)/shard_map/all_gather | solution.py:82
  166.9 0.0 copy-start.3
  166.9 2.8 %fusion.4 = (bf16[1024,512]{1,0:T(8,128)(2,1)S(1)}, bf16[1024,512]{1,0:T(8,128)(2,1)S(1)}) fusion(bf16[32,32,512]{2,1,0:T(8,128)(2,1)S(1)} %all_to_all.26, bf16[1024,1024]{1,0:T(8,128)(2,1)} %all-gather.2.cloned.1.call-done), kind=kLoop, calls=%fused_computation.10 | loop fusion | flops 8388608 | bytes 5242880 | tf_op jit(solution)/shard_map/convert_element_type | solution.py:75
  169.6 0.0 copy-start.4
  169.6 0.0 copy-done.3
  169.6 0.5 fusion.17
  170.1 0.0 copy-start.2
  170.1 0.5 copy-done.4
  170.6 1.3 fusion.9
  171.8 0.0 all-to-all-done.4
  171.8 7.9 %all-to-all-start.3 = ((bf16[16,64,256]{2,1,0:T(8,128)(2,1)}), bf16[16,64,256]{2,1,0:T(8,128)(2,1)S(1)}, u32[]{:S(2)}, u32[]{:S(2)}) async-start(bf16[16,64,256]{2,1,0:T(8,128)(2,1)} %bitcast.27), calls=%async_computation.3 | async-start | bytes 1048576 | tf_op jit(solution)/shard_map/all_to_all | solution.py:62
  179.7 0.0 copy-done.2
  179.7 3.2 %convolution_convert_fusion.1 = bf16[512,256]{1,0:T(8,128)(2,1)} fusion(bf16[1024,256]{1,0:T(8,128)(2,1)S(1)} %bitcast.26, bf16[1024,1024]{1,0:T(8,128)(2,1)} %all-gather.2.cloned.1.call-done), kind=kOutput, calls=%fused_computation.18 | convolution fusion | flops 272760832 | bytes 2883584 | tf_op jit(solution)/shard_map/dot_general | solution.py:21
  182.9 2.2 %convolution_convert_fusion.2 = bf16[256,512]{1,0:T(8,128)(2,1)} fusion(bf16[1024,256]{1,0:T(8,128)(2,1)} %bitcast.9, bf16[1024,512]{1,0:T(8,128)(2,1)S(1)} %get-tuple-element.4), kind=kOutput, calls=%fused_computation.19 | convolution fusion | flops 268566528 | bytes 1835008 | tf_op jit(solution)/shard_map/dot_general | solution.py:21
  185.1 2.6 %all-to-all-done.3 = bf16[16,64,256]{2,1,0:T(8,128)(2,1)S(1)} async-done(((bf16[16,64,256]{2,1,0:T(8,128)(2,1)}), bf16[16,64,256]{2,1,0:T(8,128)(2,1)S(1)}, u32[]{:S(2)}, u32[]{:S(2)}) %all-to-all-start.3) | async-done | bytes 524320 | tf_op jit(solution)/shard_map/all_to_all | solution.py:62
  187.7 0.1 reduce_sum.25
  187.8 7.2 %collective-permute-start.2 = (bf16[32,256]{1,0:T(8,128)(2,1)S(1)}, bf16[32,256]{1,0:T(8,128)(2,1)S(1)}, u32[]{:S(2)}, u32[]{:S(2)}) collective-permute-start(bf16[32,256]{1,0:T(8,128)(2,1)S(1)} %get-tuple-element.14), channel_id=1, source_target_pairs={{0,0},{32,1},{64,2},{96,3},{128,4},{160,5},{192,6},{224,7},{256,8}... | collective-permute-start | bytes 49160 | tf_op jit(solution)/shard_map/ppermute | solution.py:47
  195.0 6.9 %collective-permute-start.3 = (bf16[32,256]{1,0:T(8,128)(2,1)S(1)}, bf16[32,256]{1,0:T(8,128)(2,1)S(1)}, u32[]{:S(2)}, u32[]{:S(2)}) collective-permute-start(bf16[32,256]{1,0:T(8,128)(2,1)S(1)} %get-tuple-element.15), channel_id=1, source_target_pairs={{16,0},{48,1},{80,2},{112,3},{144,4},{176,5},{208,6},{240,7},{272,... | collective-permute-start | bytes 49160 | tf_op jit(solution)/shard_map/ppermute | solution.py:48
  201.9 2.2 %convolution_convert_fusion.3 = bf16[256,512]{1,0:T(8,128)(2,1)} fusion(bf16[1024,256]{1,0:T(8,128)(2,1)} %bitcast.9, bf16[1024,512]{1,0:T(8,128)(2,1)S(1)} %get-tuple-element.5), kind=kOutput, calls=%fused_computation.20 | convolution fusion | flops 268566528 | bytes 1835008 | tf_op jit(solution)/shard_map/dot_general | solution.py:21
  204.1 0.0 collective-permute-done.2
  204.1 5.2 %collective-permute-done.3 = bf16[32,256]{1,0:T(8,128)(2,1)S(1)} collective-permute-done((bf16[32,256]{1,0:T(8,128)(2,1)S(1)}, bf16[32,256]{1,0:T(8,128)(2,1)S(1)}, u32[]{:S(2)}, u32[]{:S(2)}) %collective-permute-start.3) | collective-permute-done | bytes 16416 | tf_op jit(solution)/shard_map/ppermute | solution.py:48
  209.3 0.6 pad_maximum_fusion.3
  (5 shorter events, 0.1 us)
Async XLA Ops:
  7.2 46.9 %copy-start = (bf16[512,256]{1,0:T(8,128)(2,1)S(1)}, bf16[512,256]{1,0:T(8,128)(2,1)}, u32[]{:S(2)}) copy-start(bf16[512,256]{1,0:T(8,128)(2,1)} %param.13) | copy-start | bytes 786436
  8.1 18.5 %collective-permute-start.1 = (bf16[2,32,256]{2,1,0:T(8,128)(2,1)S(1)}, bf16[2,32,256]{2,1,0:T(8,128)(2,1)S(1)}, u32[]{:S(2)}, u32[]{:S(2)}) collective-permute-start(bf16[2,32,256]{2,1,0:T(8,128)(2,1)S(1)} %get-tuple-element.10), channel_id=1, source_target_pairs={{0,16},{1,48},{2,80},{3,112},{4,144},{5,176},{6,208},{7,240},{8,27... | collective-permute-start | bytes 98312 | tf_op jit(solution)/shard_map/ppermute | solution.py:37
  24.5 16.4 %collective-permute-start = (bf16[2,32,256]{2,1,0:T(8,128)(2,1)S(1)}, bf16[2,32,256]{2,1,0:T(8,128)(2,1)S(1)}, u32[]{:S(2)}, u32[]{:S(2)}) collective-permute-start(bf16[2,32,256]{2,1,0:T(8,128)(2,1)S(1)} %get-tuple-element.11), channel_id=1, source_target_pairs={{0,0},{1,32},{2,64},{3,96},{4,128},{5,160},{6,192},{7,224},{8,256}... | collective-permute-start | bytes 98312 | tf_op jit(solution)/shard_map/ppermute | solution.py:36
  53.2 0.8 copy-start.1
  53.2 6.5 %copy-start.5 = (bf16[32,512]{1,0:T(8,128)(2,1)S(1)}, bf16[32,512]{1,0:T(8,128)(2,1)}, u32[]{:S(2)}) copy-start(bf16[32,512]{1,0:T(8,128)(2,1)} %param.10) | copy-start | bytes 98308
  53.2 6.5 %copy-start.6 = (bf16[32,512]{1,0:T(8,128)(2,1)S(1)}, bf16[32,512]{1,0:T(8,128)(2,1)}, u32[]{:S(2)}) copy-start(bf16[32,512]{1,0:T(8,128)(2,1)} %param.9) | copy-start | bytes 98308
  55.5 31.4 %all-to-all-start.1 = ((bf16[32,32,512]{2,1,0:T(8,128)(2,1)}), bf16[32,32,512]{2,1,0:T(8,128)(2,1)S(1)}, u32[]{:S(2)}, u32[]{:S(2)}) async-start(bf16[32,32,512]{2,1,0:T(8,128)(2,1)} %bitcast.4), calls=%async_computation.1 | async-start | bytes 2097152 | tf_op jit(solution)/shard_map/all_to_all | solution.py:62
  59.7 107.2 %all-gather.2.cloned.1.call-start = ((), (), s32[]{:S(2)}) async-start(), calls=%async_computation.5 | async-start | bytes 2162688 | tf_op jit(solution)/shard_map/all_gather | solution.py:82
  121.7 50.2 %all-to-all-start.4 = ((bf16[16,64,256]{2,1,0:T(8,128)(2,1)}), bf16[16,64,256]{2,1,0:T(8,128)(2,1)}, u32[]{:S(2)}, u32[]{:S(2)}) async-start(bf16[16,64,256]{2,1,0:T(8,128)(2,1)} %broadcast_in_dim.24), calls=%async_computation.4 | async-start | bytes 1048576 | tf_op jit(solution)/shard_map/all_to_all | solution.py:56
  166.9 2.8 %copy-start.3 = (bf16[256,512]{1,0:T(8,128)(2,1)S(1)}, bf16[256,512]{1,0:T(8,128)(2,1)}, u32[]{:S(2)}) copy-start(bf16[256,512]{1,0:T(8,128)(2,1)} %param.11) | copy-start | bytes 786436
  169.6 1.0 copy-start.4
  170.1 9.6 %copy-start.2 = (bf16[16,64,256]{2,1,0:T(8,128)(2,1)S(1)}, bf16[16,64,256]{2,1,0:T(8,128)(2,1)}, u32[]{:S(2)}) copy-start(bf16[16,64,256]{2,1,0:T(8,128)(2,1)} %copy-done.1) | copy-start | bytes 1572868
  171.8 15.9 %all-to-all-start.3 = ((bf16[16,64,256]{2,1,0:T(8,128)(2,1)}), bf16[16,64,256]{2,1,0:T(8,128)(2,1)S(1)}, u32[]{:S(2)}, u32[]{:S(2)}) async-start(bf16[16,64,256]{2,1,0:T(8,128)(2,1)} %bitcast.27), calls=%async_computation.3 | async-start | bytes 1048576 | tf_op jit(solution)/shard_map/all_to_all | solution.py:62
  187.8 16.3 %collective-permute-start.2 = (bf16[32,256]{1,0:T(8,128)(2,1)S(1)}, bf16[32,256]{1,0:T(8,128)(2,1)S(1)}, u32[]{:S(2)}, u32[]{:S(2)}) collective-permute-start(bf16[32,256]{1,0:T(8,128)(2,1)S(1)} %get-tuple-element.14), channel_id=1, source_target_pairs={{0,0},{32,1},{64,2},{96,3},{128,4},{160,5},{192,6},{224,7},{256,8}... | collective-permute-start | bytes 49160 | tf_op jit(solution)/shard_map/ppermute | solution.py:47
  195.0 14.4 %collective-permute-start.3 = (bf16[32,256]{1,0:T(8,128)(2,1)S(1)}, bf16[32,256]{1,0:T(8,128)(2,1)S(1)}, u32[]{:S(2)}, u32[]{:S(2)}) collective-permute-start(bf16[32,256]{1,0:T(8,128)(2,1)S(1)} %get-tuple-element.15), channel_id=1, source_target_pairs={{16,0},{48,1},{80,2},{112,3},{144,4},{176,5},{208,6},{240,7},{272,... | collective-permute-start | bytes 49160 | tf_op jit(solution)/shard_map/ppermute | solution.py:48
Sparse Core Ops, SparseCore 0:
  64.2 102.5 all-gather.1

commit v2 on v1

v2 whole, which is shorter than its diff:
```python
import jax
import jax.numpy as jnp
from jax import lax
from jax.sharding import Mesh
from jax.sharding import PartitionSpec as P

AXES = ("yh", "yl", "zh", "x", "zl", "core")
ROW = ("yh", "yl", "zh")
HALF = ("yh", "zh")
COL = ("x", "zl", "core")
R, C = 32, 16


def turn_pairs(half_of):
    pairs = []
    for t in range(R):
        yh, yl, zh = t // 8, t // 4 % 2, t % 4
        for f in range(C):
            h = half_of(f // 2 % 2)
            row = (f // 4) * 8 + yl * 4 + (f % 2) * 2 + h
            pairs.append((t * C + f, row * C + yh * 4 + zh))
    return pairs


FIRST = turn_pairs(lambda b: b)
SECOND = turn_pairs(lambda b: 1 - b)


def inverse(pairs):
    return [(b, a) for a, b in pairs]


def contract_rows(left, right):
    return lax.dot_general(
        left, right, (((0,), (0,)), ((), ())), preferred_element_type=jnp.float32
    )


def contract_cols(left, right):
    return lax.dot_general(
        left, right, (((1,), (1,)), ((), ())), preferred_element_type=jnp.float32
    )


def swap(value):
    return lax.ppermute(value, "yl", [(0, 1), (1, 0)])


def choose(flag, one, other):
    return jnp.where(flag, one, other), jnp.where(flag, other, one)


def to_features(tile, upper, mine):
    one, two = choose(upper, tile[..., 256:], tile[..., :256])
    one = lax.ppermute(one, AXES, FIRST)
    two = lax.ppermute(two, AXES, SECOND)
    return choose(mine, one, two)


def to_tokens(own, other, upper, mine):
    one, two = choose(mine, own, other)
    one = lax.ppermute(one, AXES, inverse(FIRST))
    two = lax.ppermute(two, AXES, inverse(SECOND))
    high, low = choose(upper, one, two)
    return jnp.concatenate([low, high], axis=-1)


def gather_copies(block, axes, size):
    copies = jnp.broadcast_to(block[None], (size,) + block.shape)
    got = lax.all_to_all(copies, axes, 0, 0, tiled=True)
    return got.reshape((size * block.shape[0],) + block.shape[1:])


def scatter_sum(partial, axes, size):
    pieces = partial.astype(jnp.bfloat16).reshape((size, partial.shape[0] // size, partial.shape[1]))
    got = lax.all_to_all(pieces, axes, 0, 0, tiled=True)
    return jnp.sum(got.astype(jnp.float32), axis=0).astype(jnp.bfloat16)


def swiglu_back(hidden_grad, gate_pre, up_pre):
    grad_float = hidden_grad.astype(jnp.float32)
    gate_float = gate_pre.astype(jnp.float32)
    up_float = up_pre.astype(jnp.float32)
    sigmoid_gate = jax.nn.sigmoid(gate_float)
    activated = gate_float * sigmoid_gate
    gate_grad = (
        grad_float * up_float * sigmoid_gate * (1.0 + gate_float * (1.0 - sigmoid_gate))
    ).astype(jnp.bfloat16)
    up_grad = (grad_float * activated).astype(jnp.bfloat16)
    hidden = (activated * up_float).astype(jnp.bfloat16)
    return gate_grad, up_grad, hidden


def local(activations, out_grad, gate_pre, up_pre, gate_weight, up_weight, down_weight):
    upper = lax.axis_index("zl") == 1
    mine = lax.axis_index("zh") % 2 == lax.axis_index("yl")
    own, other = to_features(jnp.stack([out_grad, activations]), upper, mine)
    pre = jnp.concatenate([gate_pre, up_pre], axis=1)
    pre = jnp.concatenate([pre, swap(pre)], axis=1)
    pre = lax.all_gather(pre, HALF, axis=0, tiled=True)
    grads = gather_copies(jnp.concatenate([own[0], other[0]], axis=1), COL, C)
    swapped = swap(other)
    cols = jnp.concatenate([own[1], swapped[1], own[0], swapped[0]], axis=1)
    cols = lax.all_gather(cols, COL, axis=0, tiled=True)
    down_other = swap(down_weight)
    gate_other, up_other = swap(gate_weight), swap(up_weight)

    partial = contract_cols(grads[:, :256], down_weight) + contract_cols(grads[:, 256:], down_other)
    hidden_grad = scatter_sum(partial, HALF, C)
    hidden_grad, pre = lax.optimization_barrier((hidden_grad, pre))
    hidden_grad = gather_copies(hidden_grad, HALF, C)
    gate_a, up_a, hidden_a = swiglu_back(hidden_grad, pre[:, :512], pre[:, 512:1024])
    swapped_grad, pre, cols = lax.optimization_barrier((swap(hidden_grad), pre, cols))
    gate_b, up_b, hidden_b = swiglu_back(swapped_grad, pre[:, 1024:1536], pre[:, 1536:])
    partial = jnp.concatenate(
        [
            contract_cols(gate_a, gate_weight) + contract_cols(up_a, up_weight),
            contract_cols(gate_a, gate_other) + contract_cols(up_a, up_other),
        ],
        axis=1,
    )
    summed = scatter_sum(partial, COL, C)
    input_grad = to_tokens(summed[:, :256], summed[:, 256:], upper, mine)
    tokens_a, tokens_b = cols[:, :256], cols[:, 256:512]
    grads_a, grads_b = cols[:, 512:768], cols[:, 768:]
    gate_weight_grad = contract_rows(tokens_a, gate_a) + contract_rows(tokens_b, gate_b)
    up_weight_grad = contract_rows(tokens_a, up_a) + contract_rows(tokens_b, up_b)
    down_weight_grad = contract_rows(hidden_a, grads_a) + contract_rows(hidden_b, grads_b)
    return (
        input_grad,
        gate_weight_grad.astype(jnp.bfloat16),
        up_weight_grad.astype(jnp.bfloat16),
        down_weight_grad.astype(jnp.bfloat16),
    )


def solution(mesh):
    fine = Mesh(mesh.devices.reshape(4, 2, 4, 4, 2, 2), AXES)
    return jax.shard_map(
        local,
        mesh=fine,
        in_specs=(P(ROW, COL),) * 6 + (P(COL, ROW),),
        out_specs=(P(ROW, COL),) * 3 + (P(COL, ROW),),
        check_vma=False,
    )
```

time: 218 us -> 205 us (0.940)
  waiting for transfers between devices: 82.2 us -> 60.7 us
  starting transfers between devices: 56.3 us -> 74.4 us
  blocking collectives: 46 us -> 35.1 us
    all_to_all x2 -> x1, waiting for transfers between devices: 29.1 us -> 0.01 us  [scatter_sum(): got = lax.all_to_all(pieces, axes, 0, 0, tiled=True)]
    ppermute x4 -> x10, starting transfers between devices: 32.6 us -> 50.5 us  [the longest x1 17.6 us: to_features(): one = lax.ppermute(one, AXES, FIRST)]
    ppermute x4 -> x10, waiting for transfers between devices: 19.5 us -> 37.1 us  [the longest x1 13.1 us: to_tokens(): one = lax.ppermute(one, AXES, inverse(FIRST))]
    all_gather x1 -> x2, waiting for transfers between devices: 33.6 us -> 17.8 us  [the longest x1 17.8 us: local(): cols = lax.all_gather(cols, COL, axis=0, tiled=True)]
    all_to_all x2 -> x1, blocking collectives: 46 us -> 35.1 us  [scatter_sum(): got = lax.all_to_all(pieces, axes, 0, 0, tiled=True)]
    all_to_all x1 -> x2, waiting for transfers between devices: 0.01 us -> 5.77 us  [gather_copies(): got = lax.all_to_all(copies, axes, 0, 0, tiled=True)]
    concatenate x2 -> x6, other arithmetic: 1.26 us -> 4.36 us  [the longest x1 1.44 us: local(): pre = jnp.concatenate([pre, swap(pre)], axis=1)]
    dot_general x3 -> x6, matrix products: 7.59 us -> 7.73 us  [contract_rows(): lax.dot_general(left, right, (((0,), (0,)), ((), ())), preferred_element_...]
  transfers between devices with their start and end apart: 8 -> 15, of which waited for: 5 -> 9; matrix products, arithmetic and copies ran while one was open for 6% -> 7% of each run, Pallas kernels for 0% -> 0%
where the time goes in v2:
time: 205 us
  starting transfers between devices  74.4 us (36%)
  waiting for transfers between devices  60.7 us (30%)
  blocking collectives  35.1 us (17%)
  between operations  15.8 us (8%)
  matrix products  9.71 us (5%)
  other arithmetic  7.14 us (3%)
    all_to_all x1, blocking collectives, scatter_sum(): got = lax.all_to_all(pieces, axes, 0, 0, tiled=True)  35.1 us
    all_gather x1, waiting for transfers between devices, local(): cols = lax.all_gather(cols, COL, axis=0, tiled=True)  17.8 us
    ppermute x1, starting transfers between devices, to_features(): one = lax.ppermute(one, AXES, FIRST)  17.6 us
    ppermute x6, starting transfers between devices, swap(): return lax.ppermute(value, 'yl', [(0, 1), (1, 0)])  17.2 us
    ppermute x1, waiting for transfers between devices, to_tokens(): one = lax.ppermute(one, AXES, inverse(FIRST))  13.1 us
    ppermute x1, waiting for transfers between devices, to_features(): two = lax.ppermute(two, AXES, SECOND)  12.5 us
    all_to_all x1, starting transfers between devices, scatter_sum(): got = lax.all_to_all(pieces, axes, 0, 0, tiled=True)  12 us
    ppermute x1, starting transfers between devices, to_tokens(): two = lax.ppermute(two, AXES, inverse(SECOND))  11.8 us
  transfers between devices with their start and end apart: 15, of which 9 were waited for; matrix products, arithmetic and copies ran while one was open for 7% of the time, Pallas kernels for 0%

profile of v2, /device:TPU:5, one launch (start us, length us, event | category | flops | bytes accessed | tf_op | source)
XLA Modules:
  0.0 204.6 jit_solution(2156370642396185539)
XLA Ops:
  8.0 0.0 all-gather.3.cloned.1.call-start
  8.1 0.8 pad_maximum_fusion.2
  8.9 3.2 %collective-permute-start.3 = (bf16[32,1024]{1,0:T(8,128)(2,1)S(1)}, bf16[32,1024]{1,0:T(8,128)(2,1)S(1)}, u32[]{:S(2)}, u32[]{:S(2)}) collective-permute-start(bf16[32,1024]{1,0:T(8,128)(2,1)S(1)} %pad_maximum_fusion.2), channel_id=1, source_target_pairs={{0,64},{64,0},{1,65},{65,1},{2,66},{66,2},{3,67},{67,3},{4,68},{68... | collective-permute-start | bytes 196616 | tf_op jit(solution)/shard_map/ppermute | solution.py:46
  12.1 1.8 collective-permute-done.3
  13.9 1.4 pad_maximum_fusion.1
  15.3 0.8 broadcast_select_fusion.1
  16.2 17.6 %collective-permute-start = (bf16[2,32,256]{2,1,0:T(8,128)(2,1)S(1)}, bf16[2,32,256]{2,1,0:T(8,128)(2,1)S(1)}, u32[]{:S(2)}, u32[]{:S(2)}) collective-permute-start(bf16[2,32,256]{2,1,0:T(8,128)(2,1)S(1)} %get-tuple-element.18), channel_id=1, source_target_pairs={{0,0},{1,32},{2,16},{3,48},{4,128},{5,160},{6,144},{7,176},{8,256}... | collective-permute-start | bytes 98312 | tf_op jit(solution)/shard_map/ppermute | solution.py:55
  33.7 1.9 collective-permute-start.1
  35.7 12.5 %collective-permute-done.1 = bf16[2,32,256]{2,1,0:T(8,128)(2,1)S(1)} collective-permute-done((bf16[2,32,256]{2,1,0:T(8,128)(2,1)S(1)}, bf16[2,32,256]{2,1,0:T(8,128)(2,1)S(1)}, u32[]{:S(2)}, u32[]{:S(2)}) %collective-permute-start.1) | collective-permute-done | bytes 32800 | tf_op jit(solution)/shard_map/ppermute | solution.py:56
  48.3 0.9 broadcast_in_dim.4
  49.1 5.6 %all-to-all-start = ((bf16[16,32,512]{2,1,0:T(8,128)(2,1)}), bf16[16,32,512]{2,1,0:T(8,128)(2,1)S(1)}, u32[]{:S(2)}, u32[]{:S(2)}) async-start(bf16[16,32,512]{2,1,0:T(8,128)(2,1)} %broadcast_in_dim.4), calls=%async_computation | async-start | bytes 1048576 | tf_op jit(solution)/shard_map/all_to_all | solution.py:70
  54.8 2.3 %collective-permute-start.2 = (bf16[512,256]{1,0:T(8,128)(2,1)S(1)}, bf16[512,256]{1,0:T(8,128)(2,1)S(1)}, u32[]{:S(2)}, u32[]{:S(2)}) collective-permute-start(bf16[512,256]{1,0:T(8,128)(2,1)S(1)} %copy-done.3), channel_id=1, source_target_pairs={{0,64},{64,0},{1,65},{65,1},{2,66},{66,2},{3,67},{67,3},{4,68},{68... | collective-permute-start | bytes 786440 | tf_op jit(solution)/shard_map/ppermute | solution.py:46
  57.1 5.6 %all-to-all-done = bf16[16,32,512]{2,1,0:T(8,128)(2,1)S(1)} async-done(((bf16[16,32,512]{2,1,0:T(8,128)(2,1)}), bf16[16,32,512]{2,1,0:T(8,128)(2,1)S(1)}, u32[]{:S(2)}, u32[]{:S(2)}) %all-to-all-start) | async-done | bytes 524320 | tf_op jit(solution)/shard_map/all_to_all | solution.py:70
  62.7 0.3 fusion.36
  63.0 1.1 collective-permute-done.2
  64.2 0.3 fusion
  64.5 35.1 %all_to_all.20 = bf16[16,32,512]{2,1,0:T(8,128)(2,1)S(1)} all-to-all(bf16[16,32,512]{2,1,0:T(8,128)(2,1)S(1)} %bitcast.32), channel_id=1, replica_groups=mesh['yh'=4,'yl'=2,'zh'=4,'x'=4,'zl'=2,'core'=2] {'yh','zh'}, dimensions={0} | all-to-all | bytes 1048576 | tf_op jit(solution)/shard_map/all_to_all | solution.py:76
  99.7 0.1 reduce_sum.24
  99.8 0.9 broadcast_in_dim.5
  100.7 6.1 %all-to-all-start.2 = ((bf16[16,32,512]{2,1,0:T(8,128)(2,1)}), bf16[16,32,512]{2,1,0:T(8,128)(2,1)S(1)}, u32[]{:S(2)}, u32[]{:S(2)}) async-start(bf16[16,32,512]{2,1,0:T(8,128)(2,1)} %broadcast_in_dim.5), calls=%async_computation.2 | async-start | bytes 1048576 | tf_op jit(solution)/shard_map/all_to_all | solution.py:70
  106.8 0.0 all-gather.5.cloned.1.call-start
  106.8 2.7 %collective-permute-start.9 = (bf16[2,32,256]{2,1,0:T(8,128)(2,1)S(1)}, bf16[2,32,256]{2,1,0:T(8,128)(2,1)S(1)}, u32[]{:S(2)}, u32[]{:S(2)}) collective-permute-start(bf16[2,32,256]{2,1,0:T(8,128)(2,1)S(1)} %get-tuple-element.17), channel_id=1, source_target_pairs={{0,64},{64,0},{1,65},{65,1},{2,66},{66,2},{3,67},{67,3},{4,68},{68... | collective-permute-start | bytes 98312 | tf_op jit(solution)/shard_map/ppermute | solution.py:46
  109.5 8.3 %collective-permute-done.9 = bf16[2,32,256]{2,1,0:T(8,128)(2,1)S(1)} collective-permute-done((bf16[2,32,256]{2,1,0:T(8,128)(2,1)S(1)}, bf16[2,32,256]{2,1,0:T(8,128)(2,1)S(1)}, u32[]{:S(2)}, u32[]{:S(2)}) %collective-permute-start.9) | collective-permute-done | bytes 32800 | tf_op jit(solution)/shard_map/ppermute | solution.py:46
  117.8 0.6 pad_maximum_fusion.3
  118.4 1.9 collective-permute-start.5
  120.4 3.4 %collective-permute-start.4 = (bf16[256,512]{1,0:T(8,128)(2,1)S(1)}, bf16[256,512]{1,0:T(8,128)(2,1)S(1)}, u32[]{:S(2)}, u32[]{:S(2)}) collective-permute-start(bf16[256,512]{1,0:T(8,128)(2,1)S(1)} %copy-done.1), channel_id=1, source_target_pairs={{0,64},{64,0},{1,65},{65,1},{2,66},{66,2},{3,67},{67,3},{4,68},{68... | collective-permute-start | bytes 786440 | tf_op jit(solution)/shard_map/ppermute | solution.py:46
  123.7 0.1 all-to-all-done.2
  123.9 3.7 %collective-permute-start.8 = (bf16[512,512]{1,0:T(8,128)(2,1)S(1)}, bf16[512,512]{1,0:T(8,128)(2,1)}, u32[]{:S(2)}, u32[]{:S(2)}) collective-permute-start(bf16[512,512]{1,0:T(8,128)(2,1)S(1)} %bitcast.31), channel_id=1, source_target_pairs={{0,64},{64,0},{1,65},{65,1},{2,66},{66,2},{3,67},{67,3},{4,68},{68... | collective-permute-start | bytes 1572872 | tf_op jit(solution)/shard_map/ppermute | solution.py:46
  127.6 1.8 fusion.9
  129.4 0.3 fusion.49
  129.7 0.3 fusion.1
  130.1 0.3 fusion.50
  130.4 0.3 collective-permute-done.4
  130.7 0.3 fusion.2
  131.0 0.8 pad_maximum_fusion
  131.9 12.0 %all-to-all-start.3 = ((bf16[16,32,512]{2,1,0:T(8,128)(2,1)}), bf16[16,32,512]{2,1,0:T(8,128)(2,1)S(1)}, u32[]{:S(2)}, u32[]{:S(2)}) async-start(bf16[16,32,512]{2,1,0:T(8,128)(2,1)} %pad_maximum_fusion), calls=%async_computation.3 | async-start | bytes 1048576 | tf_op jit(solution)/shard_map/all_to_all | solution.py:76
  143.9 17.8 %all-gather.5.cloned.1.call-done = bf16[512,1024]{1,0:T(8,128)(2,1)} async-done(((bf16[32,1024]{1,0:T(8,128)(2,1)}), bf16[512,1024]{1,0:T(8,128)(2,1)}) %all-gather.5.cloned.1.call-update) | async-done | bytes 1048592 | tf_op jit(solution)/shard_map/all_gather | solution.py:104
  161.7 2.3 %fusion.29 = f32[256,512]{1,0:T(8,128)S(1)} fusion(bf16[512,512]{1,0:T(8,128)(2,1)} %collective-permute-done.8, bf16[512,2048]{1,0:T(8,128)(2,1)} %all-gather.3.cloned.1.call-done, bf16[512,1024]{1,0:T(8,128)(2,1)} %all-gather.5.cloned.1.call-done), kind=kOutput, calls=%fused_computation.45 | convolution fusion | flops 137625600 | bytes 2359296 | tf_op jit(solution)/shard_map/dot_general | solution.py:34
  164.0 1.0 fusion.3
  165.0 0.5 fusion.24
  165.5 1.6 fusion.26
  167.1 1.3 fusion.5
  168.4 0.1 reduce_sum.25
  168.5 11.8 %collective-permute-start.6 = (bf16[32,256]{1,0:T(8,128)(2,1)S(1)}, bf16[32,256]{1,0:T(8,128)(2,1)S(1)}, u32[]{:S(2)}, u32[]{:S(2)}) collective-permute-start(bf16[32,256]{1,0:T(8,128)(2,1)S(1)} %get-tuple-element.26), channel_id=1, source_target_pairs={{16,0},{48,1},{0,2},{32,3},{144,4},{176,5},{128,6},{160,7},{272,8}... | collective-permute-start | bytes 49160 | tf_op jit(solution)/shard_map/ppermute | solution.py:63
  180.3 2.0 collective-permute-start.7
  182.3 1.0 fusion.4
  183.4 13.1 %collective-permute-done.7 = bf16[32,256]{1,0:T(8,128)(2,1)S(1)} collective-permute-done((bf16[32,256]{1,0:T(8,128)(2,1)S(1)}, bf16[32,256]{1,0:T(8,128)(2,1)S(1)}, u32[]{:S(2)}, u32[]{:S(2)}) %collective-permute-start.7) | collective-permute-done | bytes 16416 | tf_op jit(solution)/shard_map/ppermute | solution.py:62
  196.5 0.6 pad_maximum_fusion.6
  (24 shorter events, 0.1 us)
Async XLA Ops:
  8.0 46.8 %copy-start.3 = (bf16[512,256]{1,0:T(8,128)(2,1)S(1)}, bf16[512,256]{1,0:T(8,128)(2,1)}, u32[]{:S(2)}) copy-start(bf16[512,256]{1,0:T(8,128)(2,1)} %param.13) | copy-start | bytes 786436
  8.0 91.8 %all-gather.3.cloned.1.call-start = ((), (), s32[]{:S(2)}) async-start(), calls=%async_computation.4 | async-start | bytes 2228224 | tf_op jit(solution)/shard_map/all_gather | solution.py:100
  8.9 5.0 %collective-permute-start.3 = (bf16[32,1024]{1,0:T(8,128)(2,1)S(1)}, bf16[32,1024]{1,0:T(8,128)(2,1)S(1)}, u32[]{:S(2)}, u32[]{:S(2)}) collective-permute-start(bf16[32,1024]{1,0:T(8,128)(2,1)S(1)} %pad_maximum_fusion.2), channel_id=1, source_target_pairs={{0,64},{64,0},{1,65},{65,1},{2,66},{66,2},{3,67},{67,3},{4,68},{68... | collective-permute-start | bytes 196616 | tf_op jit(solution)/shard_map/ppermute | solution.py:46
  16.2 19.5 %collective-permute-start = (bf16[2,32,256]{2,1,0:T(8,128)(2,1)S(1)}, bf16[2,32,256]{2,1,0:T(8,128)(2,1)S(1)}, u32[]{:S(2)}, u32[]{:S(2)}) collective-permute-start(bf16[2,32,256]{2,1,0:T(8,128)(2,1)S(1)} %get-tuple-element.18), channel_id=1, source_target_pairs={{0,0},{1,32},{2,16},{3,48},{4,128},{5,160},{6,144},{7,176},{8,256}... | collective-permute-start | bytes 98312 | tf_op jit(solution)/shard_map/ppermute | solution.py:55
  33.7 14.5 %collective-permute-start.1 = (bf16[2,32,256]{2,1,0:T(8,128)(2,1)S(1)}, bf16[2,32,256]{2,1,0:T(8,128)(2,1)S(1)}, u32[]{:S(2)}, u32[]{:S(2)}) collective-permute-start(bf16[2,32,256]{2,1,0:T(8,128)(2,1)S(1)} %get-tuple-element.19), channel_id=1, source_target_pairs={{0,16},{1,48},{2,0},{3,32},{4,144},{5,176},{6,128},{7,160},{8,272}... | collective-permute-start | bytes 98312 | tf_op jit(solution)/shard_map/ppermute | solution.py:56
  49.1 13.6 %all-to-all-start = ((bf16[16,32,512]{2,1,0:T(8,128)(2,1)}), bf16[16,32,512]{2,1,0:T(8,128)(2,1)S(1)}, u32[]{:S(2)}, u32[]{:S(2)}) async-start(bf16[16,32,512]{2,1,0:T(8,128)(2,1)} %broadcast_in_dim.4), calls=%async_computation | async-start | bytes 1048576 | tf_op jit(solution)/shard_map/all_to_all | solution.py:70
  54.8 9.4 %collective-permute-start.2 = (bf16[512,256]{1,0:T(8,128)(2,1)S(1)}, bf16[512,256]{1,0:T(8,128)(2,1)S(1)}, u32[]{:S(2)}, u32[]{:S(2)}) collective-permute-start(bf16[512,256]{1,0:T(8,128)(2,1)S(1)} %copy-done.3), channel_id=1, source_target_pairs={{0,64},{64,0},{1,65},{65,1},{2,66},{66,2},{3,67},{67,3},{4,68},{68... | collective-permute-start | bytes 786440 | tf_op jit(solution)/shard_map/ppermute | solution.py:46
  64.5 53.9 %copy-start.4 = (bf16[256,512]{1,0:T(8,128)(2,1)S(1)}, bf16[256,512]{1,0:T(8,128)(2,1)}, u32[]{:S(2)}) copy-start(bf16[256,512]{1,0:T(8,128)(2,1)} %param.12) | copy-start | bytes 786436
  64.5 55.8 %copy-start.1 = (bf16[256,512]{1,0:T(8,128)(2,1)S(1)}, bf16[256,512]{1,0:T(8,128)(2,1)}, u32[]{:S(2)}) copy-start(bf16[256,512]{1,0:T(8,128)(2,1)} %param.11) | copy-start | bytes 786436
  100.7 23.2 %all-to-all-start.2 = ((bf16[16,32,512]{2,1,0:T(8,128)(2,1)}), bf16[16,32,512]{2,1,0:T(8,128)(2,1)S(1)}, u32[]{:S(2)}, u32[]{:S(2)}) async-start(bf16[16,32,512]{2,1,0:T(8,128)(2,1)} %broadcast_in_dim.5), calls=%async_computation.2 | async-start | bytes 1048576 | tf_op jit(solution)/shard_map/all_to_all | solution.py:70
  106.8 54.9 %all-gather.5.cloned.1.call-start = ((), (), s32[]{:S(2)}) async-start(), calls=%async_computation.5 | async-start | bytes 1114112 | tf_op jit(solution)/shard_map/all_gather | solution.py:104
  106.8 10.9 %collective-permute-start.9 = (bf16[2,32,256]{2,1,0:T(8,128)(2,1)S(1)}, bf16[2,32,256]{2,1,0:T(8,128)(2,1)S(1)}, u32[]{:S(2)}, u32[]{:S(2)}) collective-permute-start(bf16[2,32,256]{2,1,0:T(8,128)(2,1)S(1)} %get-tuple-element.17), channel_id=1, source_target_pairs={{0,64},{64,0},{1,65},{65,1},{2,66},{66,2},{3,67},{67,3},{4,68},{68... | collective-permute-start | bytes 98312 | tf_op jit(solution)/shard_map/ppermute | solution.py:46
  118.4 11.6 %collective-permute-start.5 = (bf16[256,512]{1,0:T(8,128)(2,1)S(1)}, bf16[256,512]{1,0:T(8,128)(2,1)S(1)}, u32[]{:S(2)}, u32[]{:S(2)}) collective-permute-start(bf16[256,512]{1,0:T(8,128)(2,1)S(1)} %copy-done.4), channel_id=1, source_target_pairs={{0,64},{64,0},{1,65},{65,1},{2,66},{66,2},{3,67},{67,3},{4,68},{68... | collective-permute-start | bytes 786440 | tf_op jit(solution)/shard_map/ppermute | solution.py:46
  120.4 10.3 %collective-permute-start.4 = (bf16[256,512]{1,0:T(8,128)(2,1)S(1)}, bf16[256,512]{1,0:T(8,128)(2,1)S(1)}, u32[]{:S(2)}, u32[]{:S(2)}) collective-permute-start(bf16[256,512]{1,0:T(8,128)(2,1)S(1)} %copy-done.1), channel_id=1, source_target_pairs={{0,64},{64,0},{1,65},{65,1},{2,66},{66,2},{3,67},{67,3},{4,68},{68... | collective-permute-start | bytes 786440 | tf_op jit(solution)/shard_map/ppermute | solution.py:46
  123.9 37.8 %collective-permute-start.8 = (bf16[512,512]{1,0:T(8,128)(2,1)S(1)}, bf16[512,512]{1,0:T(8,128)(2,1)}, u32[]{:S(2)}, u32[]{:S(2)}) collective-permute-start(bf16[512,512]{1,0:T(8,128)(2,1)S(1)} %bitcast.31), channel_id=1, source_target_pairs={{0,64},{64,0},{1,65},{65,1},{2,66},{66,2},{3,67},{67,3},{4,68},{68... | collective-permute-start | bytes 1572872 | tf_op jit(solution)/shard_map/ppermute | solution.py:46
  131.9 36.5 %all-to-all-start.3 = ((bf16[16,32,512]{2,1,0:T(8,128)(2,1)}), bf16[16,32,512]{2,1,0:T(8,128)(2,1)S(1)}, u32[]{:S(2)}, u32[]{:S(2)}) async-start(bf16[16,32,512]{2,1,0:T(8,128)(2,1)} %pad_maximum_fusion), calls=%async_computation.3 | async-start | bytes 1048576 | tf_op jit(solution)/shard_map/all_to_all | solution.py:76
  161.7 2.3 %copy-start.2 = (bf16[512,1024]{1,0:T(8,128)(2,1)S(1)}, bf16[512,1024]{1,0:T(8,128)(2,1)}, u32[]{:S(2)}) copy-start(bf16[512,1024]{1,0:T(8,128)(2,1)} %all-gather.5.cloned.1.call-done) | copy-start | bytes 3145732
  161.7 3.3 %copy-start = (bf16[512,2048]{1,0:T(8,128)(2,1)S(1)}, bf16[512,2048]{1,0:T(8,128)(2,1)}, u32[]{:S(2)}) copy-start(bf16[512,2048]{1,0:T(8,128)(2,1)} %all-gather.3.cloned.1.call-done) | copy-start | bytes 6291460
  168.5 14.9 %collective-permute-start.6 = (bf16[32,256]{1,0:T(8,128)(2,1)S(1)}, bf16[32,256]{1,0:T(8,128)(2,1)S(1)}, u32[]{:S(2)}, u32[]{:S(2)}) collective-permute-start(bf16[32,256]{1,0:T(8,128)(2,1)S(1)} %get-tuple-element.26), channel_id=1, source_target_pairs={{16,0},{48,1},{0,2},{32,3},{144,4},{176,5},{128,6},{160,7},{272,8}... | collective-permute-start | bytes 49160 | tf_op jit(solution)/shard_map/ppermute | solution.py:63
  180.3 16.2 %collective-permute-start.7 = (bf16[32,256]{1,0:T(8,128)(2,1)S(1)}, bf16[32,256]{1,0:T(8,128)(2,1)S(1)}, u32[]{:S(2)}, u32[]{:S(2)}) collective-permute-start(bf16[32,256]{1,0:T(8,128)(2,1)S(1)} %get-tuple-element.27), channel_id=1, source_target_pairs={{0,0},{32,1},{16,2},{48,3},{128,4},{160,5},{144,6},{176,7},{256,8}... | collective-permute-start | bytes 49160 | tf_op jit(solution)/shard_map/ppermute | solution.py:62
Sparse Core Ops, SparseCore 0:
  15.4 79.8 all-gather.2
Sparse Core Ops, SparseCore 1:
  118.5 43.1 all-gather.4

commit v3 on v2

--- a/solution.py
+++ b/solution.py
@@ -50,6 +50,15 @@
     return jnp.where(flag, one, other), jnp.where(flag, other, one)
 
 
+def halves(value):
+    parts = value.reshape((4, 2, value.shape[0] // 8, value.shape[1]))
+    yl = lax.axis_index("yl")
+    return tuple(
+        lax.dynamic_index_in_dim(parts, at, 1, keepdims=False).reshape((-1, value.shape[1]))
+        for at in (yl, 1 - yl)
+    )
+
+
 def to_features(tile, upper, mine):
     one, two = choose(upper, tile[..., 256:], tile[..., :256])
     one = lax.ppermute(one, AXES, FIRST)
@@ -94,10 +103,10 @@
 def local(activations, out_grad, gate_pre, up_pre, gate_weight, up_weight, down_weight):
     upper = lax.axis_index("zl") == 1
     mine = lax.axis_index("zh") % 2 == lax.axis_index("yl")
-    own, other = to_features(jnp.stack([out_grad, activations]), upper, mine)
-    pre = jnp.concatenate([gate_pre, up_pre], axis=1)
-    pre = jnp.concatenate([pre, swap(pre)], axis=1)
-    pre = lax.all_gather(pre, HALF, axis=0, tiled=True)
+    pre = gather_copies(jnp.concatenate([gate_pre, up_pre], axis=1), "zh", 4)
+    tiles = to_features(jnp.stack([out_grad, activations]), upper, mine)
+    (own, other), pre = lax.optimization_barrier((tiles, pre))
+    pre = lax.all_gather(pre, ("yh", "yl"), axis=0, tiled=True)
     grads = gather_copies(jnp.concatenate([own[0], other[0]], axis=1), COL, C)
     swapped = swap(other)
     cols = jnp.concatenate([own[1], swapped[1], own[0], swapped[0]], axis=1)
@@ -106,12 +115,16 @@
     gate_other, up_other = swap(gate_weight), swap(up_weight)
 
     partial = contract_cols(grads[:, :256], down_weight) + contract_cols(grads[:, 256:], down_other)
+    partial, gate_other, up_other = lax.optimization_barrier(
+        (partial.astype(jnp.bfloat16), gate_other, up_other)
+    )
     hidden_grad = scatter_sum(partial, HALF, C)
-    hidden_grad, pre = lax.optimization_barrier((hidden_grad, pre))
+    hidden_grad, pre, cols = lax.optimization_barrier((hidden_grad, pre, cols))
     hidden_grad = gather_copies(hidden_grad, HALF, C)
-    gate_a, up_a, hidden_a = swiglu_back(hidden_grad, pre[:, :512], pre[:, 512:1024])
-    swapped_grad, pre, cols = lax.optimization_barrier((swap(hidden_grad), pre, cols))
-    gate_b, up_b, hidden_b = swiglu_back(swapped_grad, pre[:, 1024:1536], pre[:, 1536:])
+    pre_a, pre_b = halves(pre)
+    gate_a, up_a, hidden_a = swiglu_back(hidden_grad, pre_a[:, :512], pre_a[:, 512:])
+    swapped_grad, pre_b, cols = lax.optimization_barrier((swap(hidden_grad), pre_b, cols))
+    gate_b, up_b, hidden_b = swiglu_back(swapped_grad, pre_b[:, :512], pre_b[:, 512:])
     partial = jnp.concatenate(
         [
             contract_cols(gate_a, gate_weight) + contract_cols(up_a, up_weight),

time: 205 us -> 211 us (1.029)
  blocking collectives: 35.1 us -> 21.3 us
  waiting for transfers between devices: 60.7 us -> 70.2 us
  starting transfers between devices: 74.4 us -> 83.8 us
  local copies, waits for them, and re-layouts: 1.75 us -> 5.25 us
  other arithmetic: 7.14 us -> 4.54 us
    all_gather x1, waiting for transfers between devices: 0.02 us -> 26 us  [local(): pre = lax.all_gather(pre, ('yh', 'yl'), axis=0, tiled=True)]
    all_gather x1, waiting for transfers between devices: 17.8 us -> 0.02 us  [local(): cols = lax.all_gather(cols, COL, axis=0, tiled=True)]
    all_to_all x2 -> x3, starting transfers between devices: 11.7 us -> 28 us  [gather_copies(): got = lax.all_to_all(copies, axes, 0, 0, tiled=True)]
    all_to_all x1, blocking collectives: 35.1 us -> 21.3 us  [scatter_sum(): got = lax.all_to_all(pieces, axes, 0, 0, tiled=True)]
    ppermute x1, waiting for transfers between devices: 12.5 us -> 0.01 us  [to_features(): two = lax.ppermute(two, AXES, SECOND)]
    ppermute x1, starting transfers between devices: 17.6 us -> 6.28 us  [to_features(): one = lax.ppermute(one, AXES, FIRST)]
    ppermute x1, starting transfers between devices: 1.94 us -> 11.8 us  [to_features(): two = lax.ppermute(two, AXES, SECOND)]
    all_to_all x2 -> x3, waiting for transfers between devices: 5.77 us -> 14.9 us  [gather_copies(): got = lax.all_to_all(copies, axes, 0, 0, tiled=True)]
where the time goes in v3:
time: 211 us; the launch traced here: 210 us
  starting transfers between devices  83.8 us (40%)
  waiting for transfers between devices  70.2 us (33%)
  blocking collectives  21.3 us (10%)
  between operations  14.4 us (7%)
  matrix products  10.7 us (5%)
  local copies, waits for them, and re-layouts  5.25 us (2%)
  other arithmetic  4.54 us (2%)
    all_to_all x3, starting transfers between devices, gather_copies(): got = lax.all_to_all(copies, axes, 0, 0, tiled=True)  28 us
    all_gather x1, waiting for transfers between devices, local(): pre = lax.all_gather(pre, ('yh', 'yl'), axis=0, tiled=True)  26 us
    all_to_all x1, blocking collectives, scatter_sum(): got = lax.all_to_all(pieces, axes, 0, 0, tiled=True)  21.3 us
    all_to_all x3, waiting for transfers between devices, gather_copies(): got = lax.all_to_all(copies, axes, 0, 0, tiled=True)  14.9 us
    ppermute x5, waiting for transfers between devices, swap(): return lax.ppermute(value, 'yl', [(0, 1), (1, 0)])  13.2 us
    ppermute x5, starting transfers between devices, swap(): return lax.ppermute(value, 'yl', [(0, 1), (1, 0)])  11.8 us
    ppermute x1, starting transfers between devices, to_features(): two = lax.ppermute(two, AXES, SECOND)  11.8 us
    all_to_all x1, starting transfers between devices, scatter_sum(): got = lax.all_to_all(pieces, axes, 0, 0, tiled=True)  11.6 us
  transfers between devices with their start and end apart: 15, of which 9 were waited for; matrix products, arithmetic and copies ran while one was open for 7% of the time, Pallas kernels for 0%

profile of v3, /device:TPU:5, one launch (start us, length us, event | category | flops | bytes accessed | tf_op | source)
XLA Modules:
  0.0 210.0 jit_solution(14152511958212875017)
XLA Ops:
  7.2 0.8 pad_maximum_fusion.1
  8.0 0.7 broadcast_in_dim.6
  8.8 10.0 %all-to-all-start = ((bf16[4,32,1024]{2,1,0:T(8,128)(2,1)}), bf16[4,32,1024]{2,1,0:T(8,128)(2,1)S(1)}, u32[]{:S(2)}, u32[]{:S(2)}) async-start(bf16[4,32,1024]{2,1,0:T(8,128)(2,1)} %broadcast_in_dim.6), calls=%async_computation | async-start | bytes 524288 | tf_op jit(solution)/shard_map/all_to_all | solution.py:79
  18.8 0.8 broadcast_select_fusion
  19.6 11.8 %collective-permute-start.1 = (bf16[2,32,256]{2,1,0:T(8,128)(2,1)S(1)}, bf16[2,32,256]{2,1,0:T(8,128)(2,1)S(1)}, u32[]{:S(2)}, u32[]{:S(2)}) collective-permute-start(bf16[2,32,256]{2,1,0:T(8,128)(2,1)S(1)} %get-tuple-element.34), channel_id=1, source_target_pairs={{0,16},{1,48},{2,0},{3,32},{4,144},{5,176},{6,128},{7,160},{8,272}... | collective-permute-start | bytes 98312 | tf_op jit(solution)/shard_map/ppermute | solution.py:65
  31.4 6.3 %collective-permute-start = (bf16[2,32,256]{2,1,0:T(8,128)(2,1)S(1)}, bf16[2,32,256]{2,1,0:T(8,128)(2,1)S(1)}, u32[]{:S(2)}, u32[]{:S(2)}) collective-permute-start(bf16[2,32,256]{2,1,0:T(8,128)(2,1)S(1)} %get-tuple-element.35), channel_id=1, source_target_pairs={{0,0},{1,32},{2,16},{3,48},{4,128},{5,160},{6,144},{7,176},{8,256}... | collective-permute-start | bytes 98312 | tf_op jit(solution)/shard_map/ppermute | solution.py:64
  37.8 7.2 %collective-permute-done = bf16[2,32,256]{2,1,0:T(8,128)(2,1)S(1)} collective-permute-done((bf16[2,32,256]{2,1,0:T(8,128)(2,1)S(1)}, bf16[2,32,256]{2,1,0:T(8,128)(2,1)S(1)}, u32[]{:S(2)}, u32[]{:S(2)}) %collective-permute-start) | collective-permute-done | bytes 32800 | tf_op jit(solution)/shard_map/ppermute | solution.py:64
  45.0 2.3 %collective-permute-start.5 = (bf16[2,32,256]{2,1,0:T(8,128)(2,1)S(1)}, bf16[2,32,256]{2,1,0:T(8,128)(2,1)S(1)}, u32[]{:S(2)}, u32[]{:S(2)}) collective-permute-start(bf16[2,32,256]{2,1,0:T(8,128)(2,1)S(1)} %get-tuple-element.17), channel_id=1, source_target_pairs={{0,64},{64,0},{1,65},{65,1},{2,66},{66,2},{3,67},{67,3},{4,68},{68... | collective-permute-start | bytes 98312 | tf_op jit(solution)/shard_map/ppermute | solution.py:46
  47.3 2.3 %collective-permute-done.5 = bf16[2,32,256]{2,1,0:T(8,128)(2,1)S(1)} collective-permute-done((bf16[2,32,256]{2,1,0:T(8,128)(2,1)S(1)}, bf16[2,32,256]{2,1,0:T(8,128)(2,1)S(1)}, u32[]{:S(2)}, u32[]{:S(2)}) %collective-permute-start.5) | collective-permute-done | bytes 32800 | tf_op jit(solution)/shard_map/ppermute | solution.py:46
  49.7 0.6 pad_maximum_fusion.2
  50.4 0.7 all-gather.3.cloned.1.call-update
  51.1 0.9 broadcast_in_dim.7
  52.0 8.3 %all-to-all-start.1 = ((bf16[16,32,512]{2,1,0:T(8,128)(2,1)}), bf16[16,32,512]{2,1,0:T(8,128)(2,1)S(1)}, u32[]{:S(2)}, u32[]{:S(2)}) async-start(bf16[16,32,512]{2,1,0:T(8,128)(2,1)} %broadcast_in_dim.7), calls=%async_computation.1 | async-start | bytes 1048576 | tf_op jit(solution)/shard_map/all_to_all | solution.py:79
  60.2 2.3 %collective-permute-start.2 = (bf16[512,256]{1,0:T(8,128)(2,1)S(1)}, bf16[512,256]{1,0:T(8,128)(2,1)S(1)}, u32[]{:S(2)}, u32[]{:S(2)}) collective-permute-start(bf16[512,256]{1,0:T(8,128)(2,1)S(1)} %copy-done.4), channel_id=1, source_target_pairs={{0,64},{64,0},{1,65},{65,1},{2,66},{66,2},{3,67},{67,3},{4,68},{68... | collective-permute-start | bytes 786440 | tf_op jit(solution)/shard_map/ppermute | solution.py:46
  62.6 3.0 %collective-permute-start.3 = (bf16[256,512]{1,0:T(8,128)(2,1)S(1)}, bf16[256,512]{1,0:T(8,128)(2,1)S(1)}, u32[]{:S(2)}, u32[]{:S(2)}) collective-permute-start(bf16[256,512]{1,0:T(8,128)(2,1)S(1)} %copy-done.2), channel_id=1, source_target_pairs={{0,64},{64,0},{1,65},{65,1},{2,66},{66,2},{3,67},{67,3},{4,68},{68... | collective-permute-start | bytes 786440 | tf_op jit(solution)/shard_map/ppermute | solution.py:46
  65.6 2.3 %collective-permute-start.4 = (bf16[256,512]{1,0:T(8,128)(2,1)S(1)}, bf16[256,512]{1,0:T(8,128)(2,1)S(1)}, u32[]{:S(2)}, u32[]{:S(2)}) collective-permute-start(bf16[256,512]{1,0:T(8,128)(2,1)S(1)} %copy-done.5), channel_id=1, source_target_pairs={{0,64},{64,0},{1,65},{65,1},{2,66},{66,2},{3,67},{67,3},{4,68},{68... | collective-permute-start | bytes 786440 | tf_op jit(solution)/shard_map/ppermute | solution.py:46
  67.9 1.5 all-to-all-done.1
  69.4 0.3 fusion.36
  69.8 0.3 fusion
  70.1 5.2 %collective-permute-done.3 = bf16[256,512]{1,0:T(8,128)(2,1)S(1)} collective-permute-done((bf16[256,512]{1,0:T(8,128)(2,1)S(1)}, bf16[256,512]{1,0:T(8,128)(2,1)S(1)}, u32[]{:S(2)}, u32[]{:S(2)}) %collective-permute-start.3) | collective-permute-done | bytes 262176 | tf_op jit(solution)/shard_map/ppermute | solution.py:46
  75.3 5.7 %collective-permute-done.4 = bf16[256,512]{1,0:T(8,128)(2,1)S(1)} collective-permute-done((bf16[256,512]{1,0:T(8,128)(2,1)S(1)}, bf16[256,512]{1,0:T(8,128)(2,1)S(1)}, u32[]{:S(2)}, u32[]{:S(2)}) %collective-permute-start.4) | collective-permute-done | bytes 262176 | tf_op jit(solution)/shard_map/ppermute | solution.py:46
  81.0 21.3 %all_to_all.25 = bf16[16,32,512]{2,1,0:T(8,128)(2,1)S(1)} all-to-all(bf16[16,32,512]{2,1,0:T(8,128)(2,1)S(1)} %bitcast.39), channel_id=1, replica_groups=mesh['yh'=4,'yl'=2,'zh'=4,'x'=4,'zl'=2,'core'=2] {'yh','zh'}, dimensions={0} | all-to-all | bytes 1048576 | tf_op jit(solution)/shard_map/all_to_all | solution.py:85
  102.3 0.1 reduce_sum.24
  102.4 26.0 %all-gather.3.cloned.1.call-done = bf16[1024,1024]{1,0:T(8,128)(2,1)} async-done(((bf16[128,1024]{1,0:T(8,128)(2,1)}), bf16[1024,1024]{1,0:T(8,128)(2,1)}) %all-gather.3.cloned.1.call-update) | async-done | bytes 2097168 | tf_op jit(solution)/shard_map/all_gather | solution.py:109
  128.4 0.9 broadcast_in_dim.8
  129.3 9.7 %all-to-all-start.3 = ((bf16[16,32,512]{2,1,0:T(8,128)(2,1)}), bf16[16,32,512]{2,1,0:T(8,128)(2,1)S(1)}, u32[]{:S(2)}, u32[]{:S(2)}) async-start(bf16[16,32,512]{2,1,0:T(8,128)(2,1)} %broadcast_in_dim.8), calls=%async_computation.3 | async-start | bytes 1048576 | tf_op jit(solution)/shard_map/all_to_all | solution.py:79
  139.0 2.8 %constant_dynamic-slice_fusion = (bf16[4,1,128,1024]{3,2,1,0:T(8,128)(2,1)}, bf16[4,1,128,1024]{3,2,1,0:T(8,128)(2,1)S(1)}) fusion(bf16[4,2,128,1024]{3,2,1,0:T(8,128)(2,1)} %bitcast.37, s32[]{:T(128)S(6)} %select_n.72, s32[]{:T(128)S(6)} %select_n.67), kind=kLoop, calls=%fused_computation.80 | loop fusion | bytes 4194312 | tf_op jit(solution)/shard_map/jit(dynamic_index_in_dim)/dynamic_slice | solution.py:57
  141.8 13.4 %all-to-all-done.3 = bf16[16,32,512]{2,1,0:T(8,128)(2,1)S(1)} async-done(((bf16[16,32,512]{2,1,0:T(8,128)(2,1)}), bf16[16,32,512]{2,1,0:T(8,128)(2,1)S(1)}, u32[]{:S(2)}, u32[]{:S(2)}) %all-to-all-start.3) | async-done | bytes 524320 | tf_op jit(solution)/shard_map/all_to_all | solution.py:79
  155.1 0.6 fusion.9
  155.7 0.3 fusion.49
  156.1 1.9 collective-permute-start.8
  158.0 0.3 fusion.1
  158.3 0.3 fusion.50
  158.7 0.3 fusion.2
  159.0 0.8 pad_maximum_fusion
  159.8 11.6 %all-to-all-start.4 = ((bf16[16,32,512]{2,1,0:T(8,128)(2,1)}), bf16[16,32,512]{2,1,0:T(8,128)(2,1)S(1)}, u32[]{:S(2)}, u32[]{:S(2)}) async-start(bf16[16,32,512]{2,1,0:T(8,128)(2,1)} %pad_maximum_fusion), calls=%async_computation.4 | async-start | bytes 1048576 | tf_op jit(solution)/shard_map/all_to_all | solution.py:85
  171.4 2.3 %fusion.29 = f32[256,512]{1,0:T(8,128)S(1)} fusion(bf16[512,512]{1,0:T(8,128)(2,1)} %collective-permute-done.8, bf16[512,1024]{1,0:T(8,128)(2,1)} %bitcast.42, bf16[512,1024]{1,0:T(8,128)(2,1)} %all-gather.5.cloned.1.call-done), kind=kOutput, calls=%fused_computation.45 | convolution fusion | flops 137625600 | bytes 2359296 | tf_op jit(solution)/shard_map/dot_general | solution.py:34
  173.7 1.0 fusion.3
  174.8 0.5 fusion.24
  175.3 1.6 fusion.26
  176.9 1.3 fusion.5
  178.2 1.2 all-to-all-done.4
  179.4 0.1 reduce_sum.25
  179.5 6.9 %collective-permute-start.6 = (bf16[32,256]{1,0:T(8,128)(2,1)S(1)}, bf16[32,256]{1,0:T(8,128)(2,1)S(1)}, u32[]{:S(2)}, u32[]{:S(2)}) collective-permute-start(bf16[32,256]{1,0:T(8,128)(2,1)S(1)} %get-tuple-element.38), channel_id=1, source_target_pairs={{16,0},{48,1},{0,2},{32,3},{144,4},{176,5},{128,6},{160,7},{272,8}... | collective-permute-start | bytes 49160 | tf_op jit(solution)/shard_map/ppermute | solution.py:72
  186.4 7.3 %collective-permute-start.7 = (bf16[32,256]{1,0:T(8,128)(2,1)S(1)}, bf16[32,256]{1,0:T(8,128)(2,1)S(1)}, u32[]{:S(2)}, u32[]{:S(2)}) collective-permute-start(bf16[32,256]{1,0:T(8,128)(2,1)S(1)} %get-tuple-element.39), channel_id=1, source_target_pairs={{0,0},{32,1},{16,2},{48,3},{128,4},{160,5},{144,6},{176,7},{256,8}... | collective-permute-start | bytes 49160 | tf_op jit(solution)/shard_map/ppermute | solution.py:71
  193.7 2.0 fusion.4
  195.7 6.8 %collective-permute-done.7 = bf16[32,256]{1,0:T(8,128)(2,1)S(1)} collective-permute-done((bf16[32,256]{1,0:T(8,128)(2,1)S(1)}, bf16[32,256]{1,0:T(8,128)(2,1)S(1)}, u32[]{:S(2)}, u32[]{:S(2)}) %collective-permute-start.7) | collective-permute-done | bytes 16416 | tf_op jit(solution)/shard_map/ppermute | solution.py:71
  202.6 0.6 pad_maximum_fusion.5
  (31 shorter events, 0.2 us)
Async XLA Ops:
  7.2 53.1 %copy-start.4 = (bf16[512,256]{1,0:T(8,128)(2,1)S(1)}, bf16[512,256]{1,0:T(8,128)(2,1)}, u32[]{:S(2)}) copy-start(bf16[512,256]{1,0:T(8,128)(2,1)} %param.13) | copy-start | bytes 786436
  7.2 55.4 %copy-start.2 = (bf16[256,512]{1,0:T(8,128)(2,1)S(1)}, bf16[256,512]{1,0:T(8,128)(2,1)}, u32[]{:S(2)}) copy-start(bf16[256,512]{1,0:T(8,128)(2,1)} %param.11) | copy-start | bytes 786436
  7.2 58.4 %copy-start.5 = (bf16[256,512]{1,0:T(8,128)(2,1)S(1)}, bf16[256,512]{1,0:T(8,128)(2,1)}, u32[]{:S(2)}) copy-start(bf16[256,512]{1,0:T(8,128)(2,1)} %param.12) | copy-start | bytes 786436
  8.8 36.2 %all-to-all-start = ((bf16[4,32,1024]{2,1,0:T(8,128)(2,1)}), bf16[4,32,1024]{2,1,0:T(8,128)(2,1)S(1)}, u32[]{:S(2)}, u32[]{:S(2)}) async-start(bf16[4,32,1024]{2,1,0:T(8,128)(2,1)} %broadcast_in_dim.6), calls=%async_computation | async-start | bytes 524288 | tf_op jit(solution)/shard_map/all_to_all | solution.py:79
  18.8 83.6 %all-gather.5.cloned.1.call-start = ((), (), s32[]{:S(2)}) async-start(), calls=%async_computation.6 | async-start | bytes 1114112 | tf_op jit(solution)/shard_map/all_gather | solution.py:113
  19.6 18.1 %collective-permute-start.1 = (bf16[2,32,256]{2,1,0:T(8,128)(2,1)S(1)}, bf16[2,32,256]{2,1,0:T(8,128)(2,1)S(1)}, u32[]{:S(2)}, u32[]{:S(2)}) collective-permute-start(bf16[2,32,256]{2,1,0:T(8,128)(2,1)S(1)} %get-tuple-element.34), channel_id=1, source_target_pairs={{0,16},{1,48},{2,0},{3,32},{4,144},{5,176},{6,128},{7,160},{8,272}... | collective-permute-start | bytes 98312 | tf_op jit(solution)/shard_map/ppermute | solution.py:65
  31.4 13.5 %collective-permute-start = (bf16[2,32,256]{2,1,0:T(8,128)(2,1)S(1)}, bf16[2,32,256]{2,1,0:T(8,128)(2,1)S(1)}, u32[]{:S(2)}, u32[]{:S(2)}) collective-permute-start(bf16[2,32,256]{2,1,0:T(8,128)(2,1)S(1)} %get-tuple-element.35), channel_id=1, source_target_pairs={{0,0},{1,32},{2,16},{3,48},{4,128},{5,160},{6,144},{7,176},{8,256}... | collective-permute-start | bytes 98312 | tf_op jit(solution)/shard_map/ppermute | solution.py:64
  45.0 5.4 %copy-start.1 = (bf16[4,32,1024]{2,1,0:T(8,128)(2,1)}, bf16[4,32,1024]{2,1,0:T(8,128)(2,1)S(1)}, u32[]{:S(2)}) copy-start(bf16[4,32,1024]{2,1,0:T(8,128)(2,1)S(1)} %all-to-all-done) | copy-start | bytes 786436
  45.0 4.7 %collective-permute-start.5 = (bf16[2,32,256]{2,1,0:T(8,128)(2,1)S(1)}, bf16[2,32,256]{2,1,0:T(8,128)(2,1)S(1)}, u32[]{:S(2)}, u32[]{:S(2)}) collective-permute-start(bf16[2,32,256]{2,1,0:T(8,128)(2,1)S(1)} %get-tuple-element.17), channel_id=1, source_target_pairs={{0,64},{64,0},{1,65},{65,1},{2,66},{66,2},{3,67},{67,3},{4,68},{68... | collective-permute-start | bytes 98312 | tf_op jit(solution)/shard_map/ppermute | solution.py:46
  50.3 78.1 %all-gather.3.cloned.1.call-start = ((), (), s32[]{:S(2)}) async-start(), calls=%async_computation.5 | async-start | bytes 2359296 | tf_op jit(solution)/shard_map/all_gather | solution.py:109
  52.0 17.5 %all-to-all-start.1 = ((bf16[16,32,512]{2,1,0:T(8,128)(2,1)}), bf16[16,32,512]{2,1,0:T(8,128)(2,1)S(1)}, u32[]{:S(2)}, u32[]{:S(2)}) async-start(bf16[16,32,512]{2,1,0:T(8,128)(2,1)} %broadcast_in_dim.7), calls=%async_computation.1 | async-start | bytes 1048576 | tf_op jit(solution)/shard_map/all_to_all | solution.py:79
  60.2 9.5 %collective-permute-start.2 = (bf16[512,256]{1,0:T(8,128)(2,1)S(1)}, bf16[512,256]{1,0:T(8,128)(2,1)S(1)}, u32[]{:S(2)}, u32[]{:S(2)}) collective-permute-start(bf16[512,256]{1,0:T(8,128)(2,1)S(1)} %copy-done.4), channel_id=1, source_target_pairs={{0,64},{64,0},{1,65},{65,1},{2,66},{66,2},{3,67},{67,3},{4,68},{68... | collective-permute-start | bytes 786440 | tf_op jit(solution)/shard_map/ppermute | solution.py:46
  62.6 12.7 %collective-permute-start.3 = (bf16[256,512]{1,0:T(8,128)(2,1)S(1)}, bf16[256,512]{1,0:T(8,128)(2,1)S(1)}, u32[]{:S(2)}, u32[]{:S(2)}) collective-permute-start(bf16[256,512]{1,0:T(8,128)(2,1)S(1)} %copy-done.2), channel_id=1, source_target_pairs={{0,64},{64,0},{1,65},{65,1},{2,66},{66,2},{3,67},{67,3},{4,68},{68... | collective-permute-start | bytes 786440 | tf_op jit(solution)/shard_map/ppermute | solution.py:46
  65.6 15.4 %collective-permute-start.4 = (bf16[256,512]{1,0:T(8,128)(2,1)S(1)}, bf16[256,512]{1,0:T(8,128)(2,1)S(1)}, u32[]{:S(2)}, u32[]{:S(2)}) collective-permute-start(bf16[256,512]{1,0:T(8,128)(2,1)S(1)} %copy-done.5), channel_id=1, source_target_pairs={{0,64},{64,0},{1,65},{65,1},{2,66},{66,2},{3,67},{67,3},{4,68},{68... | collective-permute-start | bytes 786440 | tf_op jit(solution)/shard_map/ppermute | solution.py:46
  75.3 54.0 %copy-start.6 = (bf16[256,512]{1,0:T(8,128)(2,1)}, bf16[256,512]{1,0:T(8,128)(2,1)S(1)}, u32[]{:S(2)}) copy-start(bf16[256,512]{1,0:T(8,128)(2,1)S(1)} %collective-permute-done.3) | copy-start | bytes 786436
  129.3 25.8 %all-to-all-start.3 = ((bf16[16,32,512]{2,1,0:T(8,128)(2,1)}), bf16[16,32,512]{2,1,0:T(8,128)(2,1)S(1)}, u32[]{:S(2)}, u32[]{:S(2)}) async-start(bf16[16,32,512]{2,1,0:T(8,128)(2,1)} %broadcast_in_dim.8), calls=%async_computation.3 | async-start | bytes 1048576 | tf_op jit(solution)/shard_map/all_to_all | solution.py:79
  155.7 2.9 %copy-start.7 = (bf16[256,512]{1,0:T(8,128)(2,1)S(1)}, bf16[256,512]{1,0:T(8,128)(2,1)}, u32[]{:S(2)}) copy-start(bf16[256,512]{1,0:T(8,128)(2,1)} %copy-done.6) | copy-start | bytes 786436
  156.1 15.4 %collective-permute-start.8 = (bf16[512,512]{1,0:T(8,128)(2,1)S(1)}, bf16[512,512]{1,0:T(8,128)(2,1)}, u32[]{:S(2)}, u32[]{:S(2)}) collective-permute-start(bf16[512,512]{1,0:T(8,128)(2,1)S(1)} %bitcast.38), channel_id=1, source_target_pairs={{0,64},{64,0},{1,65},{65,1},{2,66},{66,2},{3,67},{67,3},{4,68},{68... | collective-permute-start | bytes 1572872 | tf_op jit(solution)/shard_map/ppermute | solution.py:46
  159.8 19.5 %all-to-all-start.4 = ((bf16[16,32,512]{2,1,0:T(8,128)(2,1)}), bf16[16,32,512]{2,1,0:T(8,128)(2,1)S(1)}, u32[]{:S(2)}, u32[]{:S(2)}) async-start(bf16[16,32,512]{2,1,0:T(8,128)(2,1)} %pad_maximum_fusion), calls=%async_computation.4 | async-start | bytes 1048576 | tf_op jit(solution)/shard_map/all_to_all | solution.py:85
  171.4 2.3 %copy-start.3 = (bf16[512,1024]{1,0:T(8,128)(2,1)S(1)}, bf16[512,1024]{1,0:T(8,128)(2,1)}, u32[]{:S(2)}) copy-start(bf16[512,1024]{1,0:T(8,128)(2,1)} %all-gather.5.cloned.1.call-done) | copy-start | bytes 3145732
  171.4 3.3 %copy-start = (bf16[4,1,128,1024]{3,2,1,0:T(8,128)(2,1)S(1)}, bf16[4,1,128,1024]{3,2,1,0:T(8,128)(2,1)}, u32[]{:S(2)}) copy-start(bf16[4,1,128,1024]{3,2,1,0:T(8,128)(2,1)} %get-tuple-element.28) | copy-start | bytes 3145732
  179.5 16.2 %collective-permute-start.6 = (bf16[32,256]{1,0:T(8,128)(2,1)S(1)}, bf16[32,256]{1,0:T(8,128)(2,1)S(1)}, u32[]{:S(2)}, u32[]{:S(2)}) collective-permute-start(bf16[32,256]{1,0:T(8,128)(2,1)S(1)} %get-tuple-element.38), channel_id=1, source_target_pairs={{16,0},{48,1},{0,2},{32,3},{144,4},{176,5},{128,6},{160,7},{272,8}... | collective-permute-start | bytes 49160 | tf_op jit(solution)/shard_map/ppermute | solution.py:72
  186.4 16.2 %collective-permute-start.7 = (bf16[32,256]{1,0:T(8,128)(2,1)S(1)}, bf16[32,256]{1,0:T(8,128)(2,1)S(1)}, u32[]{:S(2)}, u32[]{:S(2)}) collective-permute-start(bf16[32,256]{1,0:T(8,128)(2,1)S(1)} %get-tuple-element.39), channel_id=1, source_target_pairs={{0,0},{32,1},{16,2},{48,3},{128,4},{160,5},{144,6},{176,7},{256,8}... | collective-permute-start | bytes 49160 | tf_op jit(solution)/shard_map/ppermute | solution.py:71
Sparse Core Ops, SparseCore 0:
  50.5 37.5 all-gather.4
  90.7 37.7 all-gather.2

commit v4 on v3

--- a/solution.py
+++ b/solution.py
@@ -110,17 +110,16 @@
     grads = gather_copies(jnp.concatenate([own[0], other[0]], axis=1), COL, C)
     swapped = swap(other)
     cols = jnp.concatenate([own[1], swapped[1], own[0], swapped[0]], axis=1)
-    cols = lax.all_gather(cols, COL, axis=0, tiled=True)
     down_other = swap(down_weight)
     gate_other, up_other = swap(gate_weight), swap(up_weight)
 
     partial = contract_cols(grads[:, :256], down_weight) + contract_cols(grads[:, 256:], down_other)
-    partial, gate_other, up_other = lax.optimization_barrier(
-        (partial.astype(jnp.bfloat16), gate_other, up_other)
-    )
+    partial, cols = lax.optimization_barrier((partial.astype(jnp.bfloat16), cols))
+    cols = lax.all_gather(cols, COL, axis=0, tiled=True)
     hidden_grad = scatter_sum(partial, HALF, C)
-    hidden_grad, pre, cols = lax.optimization_barrier((hidden_grad, pre, cols))
+    hidden_grad, pre = lax.optimization_barrier((hidden_grad, pre))
     hidden_grad = gather_copies(hidden_grad, HALF, C)
+    hidden_grad, cols = lax.optimization_barrier((hidden_grad, cols))
     pre_a, pre_b = halves(pre)
     gate_a, up_a, hidden_a = swiglu_back(hidden_grad, pre_a[:, :512], pre_a[:, 512:])
     swapped_grad, pre_b, cols = lax.optimization_barrier((swap(hidden_grad), pre_b, cols))

time: 211 us -> 200 us (0.948)
  the two profiles are of different devices: /device:TPU:5 before, /device:TPU:13 now
where the time goes in v4:
time: 200 us; the launch traced here: 199 us
  starting transfers between devices  81.6 us (41%)
  waiting for transfers between devices  79.9 us (40%)
  between operations  14.3 us (7%)
  matrix products  12.4 us (6%)
  local copies, waits for them, and re-layouts  5.93 us (3%)
  other arithmetic  4.52 us (2%)
    all_gather x1, waiting for transfers between devices, local(): cols = lax.all_gather(cols, COL, axis=0, tiled=True)  27 us
    all_to_all x3, starting transfers between devices, gather_copies(): got = lax.all_to_all(copies, axes, 0, 0, tiled=True)  26.8 us
    all_to_all x2, waiting for transfers between devices, scatter_sum(): got = lax.all_to_all(pieces, axes, 0, 0, tiled=True)  19.4 us
    ppermute x5, waiting for transfers between devices, swap(): return lax.ppermute(value, 'yl', [(0, 1), (1, 0)])  13.6 us
    ppermute x5, starting transfers between devices, swap(): return lax.ppermute(value, 'yl', [(0, 1), (1, 0)])  12.5 us
    ppermute x1, starting transfers between devices, to_tokens(): two = lax.ppermute(two, AXES, inverse(SECOND))  11.5 us
    ppermute x1, waiting for transfers between devices, to_tokens(): one = lax.ppermute(one, AXES, inverse(FIRST))  11.1 us
    ppermute x1, starting transfers between devices, to_features(): two = lax.ppermute(two, AXES, SECOND)  10.9 us
  transfers between devices with their start and end apart: 16, of which 8 were waited for; matrix products, arithmetic and copies ran while one was open for 10% of the time, Pallas kernels for 0%

profile of v4, /device:TPU:13, one launch (start us, length us, event | category | flops | bytes accessed | tf_op | source)
XLA Modules:
  0.0 198.7 jit_solution(1108899373487862372)
XLA Ops:
  7.2 0.8 pad_maximum_fusion.1
  8.0 0.7 broadcast_in_dim.6
  8.7 10.0 %all-to-all-start = ((bf16[4,32,1024]{2,1,0:T(8,128)(2,1)}), bf16[4,32,1024]{2,1,0:T(8,128)(2,1)S(1)}, u32[]{:S(2)}, u32[]{:S(2)}) async-start(bf16[4,32,1024]{2,1,0:T(8,128)(2,1)} %broadcast_in_dim.6), calls=%async_computation | async-start | bytes 524288 | tf_op jit(solution)/shard_map/all_to_all | solution.py:79
  18.7 0.8 broadcast_select_fusion
  19.6 10.9 %collective-permute-start.1 = (bf16[2,32,256]{2,1,0:T(8,128)(2,1)S(1)}, bf16[2,32,256]{2,1,0:T(8,128)(2,1)S(1)}, u32[]{:S(2)}, u32[]{:S(2)}) collective-permute-start(bf16[2,32,256]{2,1,0:T(8,128)(2,1)S(1)} %get-tuple-element.34), channel_id=1, source_target_pairs={{0,16},{1,48},{2,0},{3,32},{4,144},{5,176},{6,128},{7,160},{8,272}... | collective-permute-start | bytes 98312 | tf_op jit(solution)/shard_map/ppermute | solution.py:65
  30.5 7.2 %collective-permute-start = (bf16[2,32,256]{2,1,0:T(8,128)(2,1)S(1)}, bf16[2,32,256]{2,1,0:T(8,128)(2,1)S(1)}, u32[]{:S(2)}, u32[]{:S(2)}) collective-permute-start(bf16[2,32,256]{2,1,0:T(8,128)(2,1)S(1)} %get-tuple-element.35), channel_id=1, source_target_pairs={{0,0},{1,32},{2,16},{3,48},{4,128},{5,160},{6,144},{7,176},{8,256}... | collective-permute-start | bytes 98312 | tf_op jit(solution)/shard_map/ppermute | solution.py:64
  37.7 6.3 %collective-permute-done = bf16[2,32,256]{2,1,0:T(8,128)(2,1)S(1)} collective-permute-done((bf16[2,32,256]{2,1,0:T(8,128)(2,1)S(1)}, bf16[2,32,256]{2,1,0:T(8,128)(2,1)S(1)}, u32[]{:S(2)}, u32[]{:S(2)}) %collective-permute-start) | collective-permute-done | bytes 32800 | tf_op jit(solution)/shard_map/ppermute | solution.py:64
  44.1 0.7 copy-done.1
  44.8 0.9 broadcast_in_dim.7
  45.7 8.3 %all-to-all-start.1 = ((bf16[16,32,512]{2,1,0:T(8,128)(2,1)}), bf16[16,32,512]{2,1,0:T(8,128)(2,1)S(1)}, u32[]{:S(2)}, u32[]{:S(2)}) async-start(bf16[16,32,512]{2,1,0:T(8,128)(2,1)} %broadcast_in_dim.7), calls=%async_computation.1 | async-start | bytes 1048576 | tf_op jit(solution)/shard_map/all_to_all | solution.py:79
  53.9 3.0 %collective-permute-start.3 = (bf16[2,32,256]{2,1,0:T(8,128)(2,1)S(1)}, bf16[2,32,256]{2,1,0:T(8,128)(2,1)S(1)}, u32[]{:S(2)}, u32[]{:S(2)}) collective-permute-start(bf16[2,32,256]{2,1,0:T(8,128)(2,1)S(1)} %get-tuple-element.17), channel_id=1, source_target_pairs={{0,64},{64,0},{1,65},{65,1},{2,66},{66,2},{3,67},{67,3},{4,68},{68... | collective-permute-start | bytes 98312 | tf_op jit(solution)/shard_map/ppermute | solution.py:46
  56.9 2.3 %collective-permute-start.2 = (bf16[512,256]{1,0:T(8,128)(2,1)S(1)}, bf16[512,256]{1,0:T(8,128)(2,1)S(1)}, u32[]{:S(2)}, u32[]{:S(2)}) collective-permute-start(bf16[512,256]{1,0:T(8,128)(2,1)S(1)} %copy-done.4), channel_id=1, source_target_pairs={{0,64},{64,0},{1,65},{65,1},{2,66},{66,2},{3,67},{67,3},{4,68},{68... | collective-permute-start | bytes 786440 | tf_op jit(solution)/shard_map/ppermute | solution.py:46
  59.2 0.2 collective-permute-done.3
  59.4 0.6 pad_maximum_fusion.2
  60.1 1.8 all-to-all-done.1
  61.9 0.3 fusion.36
  62.2 8.7 %collective-permute-done.2 = bf16[512,256]{1,0:T(8,128)(2,1)S(1)} collective-permute-done((bf16[512,256]{1,0:T(8,128)(2,1)S(1)}, bf16[512,256]{1,0:T(8,128)(2,1)S(1)}, u32[]{:S(2)}, u32[]{:S(2)}) %collective-permute-start.2) | collective-permute-done | bytes 262176 | tf_op jit(solution)/shard_map/ppermute | solution.py:46
  70.9 1.1 fusion
  72.0 4.8 %all-to-all-start.2 = ((bf16[16,32,512]{2,1,0:T(8,128)(2,1)}), bf16[16,32,512]{2,1,0:T(8,128)(2,1)S(1)}, u32[]{:S(2)}, u32[]{:S(2)}) async-start(bf16[16,32,512]{2,1,0:T(8,128)(2,1)} %bitcast.9), calls=%async_computation.2 | async-start | bytes 1048576 | tf_op jit(solution)/shard_map/all_to_all | solution.py:85
  76.9 0.7 all-gather.5.cloned.1.call-update
  77.6 19.4 %all-to-all-done.2 = bf16[16,32,512]{2,1,0:T(8,128)(2,1)S(1)} async-done(((bf16[16,32,512]{2,1,0:T(8,128)(2,1)}), bf16[16,32,512]{2,1,0:T(8,128)(2,1)S(1)}, u32[]{:S(2)}, u32[]{:S(2)}) %all-to-all-start.2) | async-done | bytes 524320 | tf_op jit(solution)/shard_map/all_to_all | solution.py:85
  96.9 0.1 reduce_sum.24
  97.0 0.9 broadcast_in_dim.8
  97.9 8.5 %all-to-all-start.3 = ((bf16[16,32,512]{2,1,0:T(8,128)(2,1)}), bf16[16,32,512]{2,1,0:T(8,128)(2,1)S(1)}, u32[]{:S(2)}, u32[]{:S(2)}) async-start(bf16[16,32,512]{2,1,0:T(8,128)(2,1)} %broadcast_in_dim.8), calls=%async_computation.3 | async-start | bytes 1048576 | tf_op jit(solution)/shard_map/all_to_all | solution.py:79
  106.4 1.9 collective-permute-start.5
  108.3 3.4 %collective-permute-start.4 = (bf16[256,512]{1,0:T(8,128)(2,1)S(1)}, bf16[256,512]{1,0:T(8,128)(2,1)}, u32[]{:S(2)}, u32[]{:S(2)}) collective-permute-start(bf16[256,512]{1,0:T(8,128)(2,1)S(1)} %copy-done.2), channel_id=1, source_target_pairs={{0,64},{64,0},{1,65},{65,1},{2,66},{66,2},{3,67},{67,3},{4,68},{68... | collective-permute-start | bytes 786440 | tf_op jit(solution)/shard_map/ppermute | solution.py:46
  111.7 2.8 %constant_dynamic-slice_fusion = (bf16[4,1,128,1024]{3,2,1,0:T(8,128)(2,1)}, bf16[4,1,128,1024]{3,2,1,0:T(8,128)(2,1)S(1)}) fusion(bf16[4,2,128,1024]{3,2,1,0:T(8,128)(2,1)} %bitcast.35, s32[]{:T(128)S(6)} %select_n.72, s32[]{:T(128)S(6)} %select_n.67), kind=kLoop, calls=%fused_computation.80 | loop fusion | bytes 4194312 | tf_op jit(solution)/shard_map/jit(dynamic_index_in_dim)/dynamic_slice | solution.py:57
  114.5 27.0 %all-gather.5.cloned.1.call-done = bf16[512,1024]{1,0:T(8,128)(2,1)} async-done(((bf16[32,1024]{1,0:T(8,128)(2,1)}), bf16[512,1024]{1,0:T(8,128)(2,1)}) %all-gather.5.cloned.1.call-update) | async-done | bytes 1048592 | tf_op jit(solution)/shard_map/all_gather | solution.py:118
  141.4 1.9 collective-permute-start.8
  143.3 0.6 fusion.9
  143.9 0.3 fusion.49
  144.3 0.3 fusion.1
  144.6 0.3 fusion.50
  145.0 1.3 fusion.2
  146.3 0.8 pad_maximum_fusion
  147.1 4.8 %all-to-all-start.4 = ((bf16[16,32,512]{2,1,0:T(8,128)(2,1)}), bf16[16,32,512]{2,1,0:T(8,128)(2,1)S(1)}, u32[]{:S(2)}, u32[]{:S(2)}) async-start(bf16[16,32,512]{2,1,0:T(8,128)(2,1)} %pad_maximum_fusion), calls=%async_computation.4 | async-start | bytes 1048576 | tf_op jit(solution)/shard_map/all_to_all | solution.py:85
  151.9 4.7 %collective-permute-done.8 = bf16[512,512]{1,0:T(8,128)(2,1)} collective-permute-done((bf16[512,512]{1,0:T(8,128)(2,1)S(1)}, bf16[512,512]{1,0:T(8,128)(2,1)}, u32[]{:S(2)}, u32[]{:S(2)}) %collective-permute-start.8) | collective-permute-done | bytes 524320 | tf_op jit(solution)/shard_map/ppermute | solution.py:46
  156.7 2.3 %fusion.29 = f32[256,512]{1,0:T(8,128)S(1)} fusion(bf16[512,512]{1,0:T(8,128)(2,1)} %collective-permute-done.8, bf16[512,1024]{1,0:T(8,128)(2,1)} %bitcast.40, bf16[512,1024]{1,0:T(8,128)(2,1)} %all-gather.5.cloned.1.call-done), kind=kOutput, calls=%fused_computation.45 | convolution fusion | flops 137625600 | bytes 2359296 | tf_op jit(solution)/shard_map/dot_general | solution.py:34
  159.0 1.0 fusion.3
  160.0 0.5 fusion.24
  160.5 1.6 fusion.26
  162.1 1.3 fusion.5
  163.4 0.1 reduce_sum.25
  163.5 11.5 %collective-permute-start.6 = (bf16[32,256]{1,0:T(8,128)(2,1)S(1)}, bf16[32,256]{1,0:T(8,128)(2,1)S(1)}, u32[]{:S(2)}, u32[]{:S(2)}) collective-permute-start(bf16[32,256]{1,0:T(8,128)(2,1)S(1)} %get-tuple-element.38), channel_id=1, source_target_pairs={{16,0},{48,1},{0,2},{32,3},{144,4},{176,5},{128,6},{160,7},{272,8}... | collective-permute-start | bytes 49160 | tf_op jit(solution)/shard_map/ppermute | solution.py:72
  175.1 3.1 %collective-permute-start.7 = (bf16[32,256]{1,0:T(8,128)(2,1)S(1)}, bf16[32,256]{1,0:T(8,128)(2,1)S(1)}, u32[]{:S(2)}, u32[]{:S(2)}) collective-permute-start(bf16[32,256]{1,0:T(8,128)(2,1)S(1)} %get-tuple-element.39), channel_id=1, source_target_pairs={{0,0},{32,1},{16,2},{48,3},{128,4},{160,5},{144,6},{176,7},{256,8}... | collective-permute-start | bytes 49160 | tf_op jit(solution)/shard_map/ppermute | solution.py:71
  178.2 2.0 fusion.4
  180.2 11.1 %collective-permute-done.7 = bf16[32,256]{1,0:T(8,128)(2,1)S(1)} collective-permute-done((bf16[32,256]{1,0:T(8,128)(2,1)S(1)}, bf16[32,256]{1,0:T(8,128)(2,1)S(1)}, u32[]{:S(2)}, u32[]{:S(2)}) %collective-permute-start.7) | collective-permute-done | bytes 16416 | tf_op jit(solution)/shard_map/ppermute | solution.py:71
  191.3 0.6 pad_maximum_fusion.5
  (28 shorter events, 0.2 us)
Async XLA Ops:
  7.2 49.8 %copy-start.4 = (bf16[512,256]{1,0:T(8,128)(2,1)S(1)}, bf16[512,256]{1,0:T(8,128)(2,1)}, u32[]{:S(2)}) copy-start(bf16[512,256]{1,0:T(8,128)(2,1)} %param.13) | copy-start | bytes 786436
  8.7 35.3 %all-to-all-start = ((bf16[4,32,1024]{2,1,0:T(8,128)(2,1)}), bf16[4,32,1024]{2,1,0:T(8,128)(2,1)S(1)}, u32[]{:S(2)}, u32[]{:S(2)}) async-start(bf16[4,32,1024]{2,1,0:T(8,128)(2,1)} %broadcast_in_dim.6), calls=%async_computation | async-start | bytes 524288 | tf_op jit(solution)/shard_map/all_to_all | solution.py:79
  18.7 78.3 %all-gather.3.cloned.1.call-start = ((), (), s32[]{:S(2)}) async-start(), calls=%async_computation.5 | async-start | bytes 2359296 | tf_op jit(solution)/shard_map/all_gather | solution.py:109
  19.6 18.1 %collective-permute-start.1 = (bf16[2,32,256]{2,1,0:T(8,128)(2,1)S(1)}, bf16[2,32,256]{2,1,0:T(8,128)(2,1)S(1)}, u32[]{:S(2)}, u32[]{:S(2)}) collective-permute-start(bf16[2,32,256]{2,1,0:T(8,128)(2,1)S(1)} %get-tuple-element.34), channel_id=1, source_target_pairs={{0,16},{1,48},{2,0},{3,32},{4,144},{5,176},{6,128},{7,160},{8,272}... | collective-permute-start | bytes 98312 | tf_op jit(solution)/shard_map/ppermute | solution.py:65
  30.5 13.5 %collective-permute-start = (bf16[2,32,256]{2,1,0:T(8,128)(2,1)S(1)}, bf16[2,32,256]{2,1,0:T(8,128)(2,1)S(1)}, u32[]{:S(2)}, u32[]{:S(2)}) collective-permute-start(bf16[2,32,256]{2,1,0:T(8,128)(2,1)S(1)} %get-tuple-element.35), channel_id=1, source_target_pairs={{0,0},{1,32},{2,16},{3,48},{4,128},{5,160},{6,144},{7,176},{8,256}... | collective-permute-start | bytes 98312 | tf_op jit(solution)/shard_map/ppermute | solution.py:64
  44.1 0.7 copy-start.1
  45.7 16.2 %all-to-all-start.1 = ((bf16[16,32,512]{2,1,0:T(8,128)(2,1)}), bf16[16,32,512]{2,1,0:T(8,128)(2,1)S(1)}, u32[]{:S(2)}, u32[]{:S(2)}) async-start(bf16[16,32,512]{2,1,0:T(8,128)(2,1)} %broadcast_in_dim.7), calls=%async_computation.1 | async-start | bytes 1048576 | tf_op jit(solution)/shard_map/all_to_all | solution.py:79
  53.9 5.5 %collective-permute-start.3 = (bf16[2,32,256]{2,1,0:T(8,128)(2,1)S(1)}, bf16[2,32,256]{2,1,0:T(8,128)(2,1)S(1)}, u32[]{:S(2)}, u32[]{:S(2)}) collective-permute-start(bf16[2,32,256]{2,1,0:T(8,128)(2,1)S(1)} %get-tuple-element.17), channel_id=1, source_target_pairs={{0,64},{64,0},{1,65},{65,1},{2,66},{66,2},{3,67},{67,3},{4,68},{68... | collective-permute-start | bytes 98312 | tf_op jit(solution)/shard_map/ppermute | solution.py:46
  56.9 14.0 %collective-permute-start.2 = (bf16[512,256]{1,0:T(8,128)(2,1)S(1)}, bf16[512,256]{1,0:T(8,128)(2,1)S(1)}, u32[]{:S(2)}, u32[]{:S(2)}) collective-permute-start(bf16[512,256]{1,0:T(8,128)(2,1)S(1)} %copy-done.4), channel_id=1, source_target_pairs={{0,64},{64,0},{1,65},{65,1},{2,66},{66,2},{3,67},{67,3},{4,68},{68... | collective-permute-start | bytes 786440 | tf_op jit(solution)/shard_map/ppermute | solution.py:46
  72.0 34.4 %copy-start.5 = (bf16[256,512]{1,0:T(8,128)(2,1)S(1)}, bf16[256,512]{1,0:T(8,128)(2,1)}, u32[]{:S(2)}) copy-start(bf16[256,512]{1,0:T(8,128)(2,1)} %param.12) | copy-start | bytes 786436
  72.0 36.3 %copy-start.2 = (bf16[256,512]{1,0:T(8,128)(2,1)S(1)}, bf16[256,512]{1,0:T(8,128)(2,1)}, u32[]{:S(2)}) copy-start(bf16[256,512]{1,0:T(8,128)(2,1)} %param.11) | copy-start | bytes 786436
  72.0 24.9 %all-to-all-start.2 = ((bf16[16,32,512]{2,1,0:T(8,128)(2,1)}), bf16[16,32,512]{2,1,0:T(8,128)(2,1)S(1)}, u32[]{:S(2)}, u32[]{:S(2)}) async-start(bf16[16,32,512]{2,1,0:T(8,128)(2,1)} %bitcast.9), calls=%async_computation.2 | async-start | bytes 1048576 | tf_op jit(solution)/shard_map/all_to_all | solution.py:85
  76.8 64.6 %all-gather.5.cloned.1.call-start = ((), (), s32[]{:S(2)}) async-start(), calls=%async_computation.6 | async-start | bytes 1114112 | tf_op jit(solution)/shard_map/all_gather | solution.py:118
  97.9 43.5 %all-to-all-start.3 = ((bf16[16,32,512]{2,1,0:T(8,128)(2,1)}), bf16[16,32,512]{2,1,0:T(8,128)(2,1)S(1)}, u32[]{:S(2)}, u32[]{:S(2)}) async-start(bf16[16,32,512]{2,1,0:T(8,128)(2,1)} %broadcast_in_dim.8), calls=%async_computation.3 | async-start | bytes 1048576 | tf_op jit(solution)/shard_map/all_to_all | solution.py:79
  106.4 38.2 %collective-permute-start.5 = (bf16[256,512]{1,0:T(8,128)(2,1)S(1)}, bf16[256,512]{1,0:T(8,128)(2,1)S(1)}, u32[]{:S(2)}, u32[]{:S(2)}) collective-permute-start(bf16[256,512]{1,0:T(8,128)(2,1)S(1)} %copy-done.5), channel_id=1, source_target_pairs={{0,64},{64,0},{1,65},{65,1},{2,66},{66,2},{3,67},{67,3},{4,68},{68... | collective-permute-start | bytes 786440 | tf_op jit(solution)/shard_map/ppermute | solution.py:46
  108.3 36.6 %collective-permute-start.4 = (bf16[256,512]{1,0:T(8,128)(2,1)S(1)}, bf16[256,512]{1,0:T(8,128)(2,1)}, u32[]{:S(2)}, u32[]{:S(2)}) collective-permute-start(bf16[256,512]{1,0:T(8,128)(2,1)S(1)} %copy-done.2), channel_id=1, source_target_pairs={{0,64},{64,0},{1,65},{65,1},{2,66},{66,2},{3,67},{67,3},{4,68},{68... | collective-permute-start | bytes 786440 | tf_op jit(solution)/shard_map/ppermute | solution.py:46
  141.4 15.2 %collective-permute-start.8 = (bf16[512,512]{1,0:T(8,128)(2,1)S(1)}, bf16[512,512]{1,0:T(8,128)(2,1)}, u32[]{:S(2)}, u32[]{:S(2)}) collective-permute-start(bf16[512,512]{1,0:T(8,128)(2,1)S(1)} %bitcast.36), channel_id=1, source_target_pairs={{0,64},{64,0},{1,65},{65,1},{2,66},{66,2},{3,67},{67,3},{4,68},{68... | collective-permute-start | bytes 1572872 | tf_op jit(solution)/shard_map/ppermute | solution.py:46
  147.1 16.3 %all-to-all-start.4 = ((bf16[16,32,512]{2,1,0:T(8,128)(2,1)}), bf16[16,32,512]{2,1,0:T(8,128)(2,1)S(1)}, u32[]{:S(2)}, u32[]{:S(2)}) async-start(bf16[16,32,512]{2,1,0:T(8,128)(2,1)} %pad_maximum_fusion), calls=%async_computation.4 | async-start | bytes 1048576 | tf_op jit(solution)/shard_map/all_to_all | solution.py:85
  156.7 2.3 %copy-start.3 = (bf16[512,1024]{1,0:T(8,128)(2,1)S(1)}, bf16[512,1024]{1,0:T(8,128)(2,1)}, u32[]{:S(2)}) copy-start(bf16[512,1024]{1,0:T(8,128)(2,1)} %all-gather.5.cloned.1.call-done) | copy-start | bytes 3145732
  156.7 3.3 %copy-start = (bf16[4,1,128,1024]{3,2,1,0:T(8,128)(2,1)S(1)}, bf16[4,1,128,1024]{3,2,1,0:T(8,128)(2,1)}, u32[]{:S(2)}) copy-start(bf16[4,1,128,1024]{3,2,1,0:T(8,128)(2,1)} %get-tuple-element.28) | copy-start | bytes 3145732
  163.5 16.6 %collective-permute-start.6 = (bf16[32,256]{1,0:T(8,128)(2,1)S(1)}, bf16[32,256]{1,0:T(8,128)(2,1)S(1)}, u32[]{:S(2)}, u32[]{:S(2)}) collective-permute-start(bf16[32,256]{1,0:T(8,128)(2,1)S(1)} %get-tuple-element.38), channel_id=1, source_target_pairs={{16,0},{48,1},{0,2},{32,3},{144,4},{176,5},{128,6},{160,7},{272,8}... | collective-permute-start | bytes 49160 | tf_op jit(solution)/shard_map/ppermute | solution.py:72
  175.1 16.2 %collective-permute-start.7 = (bf16[32,256]{1,0:T(8,128)(2,1)S(1)}, bf16[32,256]{1,0:T(8,128)(2,1)S(1)}, u32[]{:S(2)}, u32[]{:S(2)}) collective-permute-start(bf16[32,256]{1,0:T(8,128)(2,1)S(1)} %get-tuple-element.39), channel_id=1, source_target_pairs={{0,0},{32,1},{16,2},{48,3},{128,4},{160,5},{144,6},{176,7},{256,8}... | collective-permute-start | bytes 49160 | tf_op jit(solution)/shard_map/ppermute | solution.py:71
Sparse Core Ops, SparseCore 0:
  44.9 50.6 all-gather.2
  98.3 43.0 all-gather.4

commit v5 on v4

--- a/solution.py
+++ b/solution.py
@@ -105,24 +105,22 @@
     mine = lax.axis_index("zh") % 2 == lax.axis_index("yl")
     pre = gather_copies(jnp.concatenate([gate_pre, up_pre], axis=1), "zh", 4)
     tiles = to_features(jnp.stack([out_grad, activations]), upper, mine)
-    (own, other), pre = lax.optimization_barrier((tiles, pre))
+    (own, other), pre, down_other = lax.optimization_barrier((tiles, pre, swap(down_weight)))
     pre = lax.all_gather(pre, ("yh", "yl"), axis=0, tiled=True)
-    grads = gather_copies(jnp.concatenate([own[0], other[0]], axis=1), COL, C)
-    swapped = swap(other)
-    cols = jnp.concatenate([own[1], swapped[1], own[0], swapped[0]], axis=1)
-    down_other = swap(down_weight)
+    cols = jnp.concatenate([own[0], other[0], other[1], own[1]], axis=1)
+    cols = gather_copies(cols, COL, C)
+    grads_a, grads_other, tokens_a = cols[:, :256], cols[:, 256:512], cols[:, 768:]
     gate_other, up_other = swap(gate_weight), swap(up_weight)
 
-    partial = contract_cols(grads[:, :256], down_weight) + contract_cols(grads[:, 256:], down_other)
-    partial, cols = lax.optimization_barrier((partial.astype(jnp.bfloat16), cols))
-    cols = lax.all_gather(cols, COL, axis=0, tiled=True)
+    partial = contract_cols(grads_a, down_weight) + contract_cols(grads_other, down_other)
     hidden_grad = scatter_sum(partial, HALF, C)
-    hidden_grad, pre = lax.optimization_barrier((hidden_grad, pre))
+    hidden_grad, pre, gate_other, up_other = lax.optimization_barrier(
+        (hidden_grad, pre, gate_other, up_other)
+    )
     hidden_grad = gather_copies(hidden_grad, HALF, C)
-    hidden_grad, cols = lax.optimization_barrier((hidden_grad, cols))
     pre_a, pre_b = halves(pre)
     gate_a, up_a, hidden_a = swiglu_back(hidden_grad, pre_a[:, :512], pre_a[:, 512:])
-    swapped_grad, pre_b, cols = lax.optimization_barrier((swap(hidden_grad), pre_b, cols))
+    swapped_grad, pre_b = lax.optimization_barrier((swap(hidden_grad), pre_b))
     gate_b, up_b, hidden_b = swiglu_back(swapped_grad, pre_b[:, :512], pre_b[:, 512:])
     partial = jnp.concatenate(
         [
@@ -133,8 +131,8 @@
     )
     summed = scatter_sum(partial, COL, C)
     input_grad = to_tokens(summed[:, :256], summed[:, 256:], upper, mine)
-    tokens_a, tokens_b = cols[:, :256], cols[:, 256:512]
-    grads_a, grads_b = cols[:, 512:768], cols[:, 768:]
+    swapped_cols = swap(cols[:, 256:768])
+    grads_b, tokens_b = swapped_cols[:, :256], swapped_cols[:, 256:]
     gate_weight_grad = contract_rows(tokens_a, gate_a) + contract_rows(tokens_b, gate_b)
     up_weight_grad = contract_rows(tokens_a, up_a) + contract_rows(tokens_b, up_b)
     down_weight_grad = contract_rows(hidden_a, grads_a) + contract_rows(hidden_b, grads_b)

time: 200 us -> 194 us (0.970)
  the two profiles are of different devices: /device:TPU:13 before, /device:TPU:41 now
where the time goes in v5:
time: 194 us; the launch traced here: 193 us
  starting transfers between devices  83.6 us (43%)
  waiting for transfers between devices  51.4 us (26%)
  blocking collectives  20.8 us (11%)
  between operations  14.3 us (7%)
  matrix products  11.6 us (6%)
  local copies, waits for them, and re-layouts  6.11 us (3%)
  other arithmetic  4.92 us (3%)
    all_to_all x2, starting transfers between devices, gather_copies(): got = lax.all_to_all(copies, axes, 0, 0, tiled=True)  22.2 us
    all_to_all x1, blocking collectives, gather_copies(): got = lax.all_to_all(copies, axes, 0, 0, tiled=True)  20.8 us
    all_to_all x2, starting transfers between devices, scatter_sum(): got = lax.all_to_all(pieces, axes, 0, 0, tiled=True)  14.9 us
    all_to_all x2, waiting for transfers between devices, scatter_sum(): got = lax.all_to_all(pieces, axes, 0, 0, tiled=True)  13.9 us
    ppermute x5, waiting for transfers between devices, swap(): return lax.ppermute(value, 'yl', [(0, 1), (1, 0)])  13.8 us
    ppermute x5, starting transfers between devices, swap(): return lax.ppermute(value, 'yl', [(0, 1), (1, 0)])  12.5 us
    all_to_all x2, waiting for transfers between devices, gather_copies(): got = lax.all_to_all(copies, axes, 0, 0, tiled=True)  11.4 us
    ppermute x1, starting transfers between devices, to_tokens(): two = lax.ppermute(two, AXES, inverse(SECOND))  9.87 us
  transfers between devices with their start and end apart: 14, of which 7 were waited for; matrix products, arithmetic and copies ran while one was open for 10% of the time, Pallas kernels for 0%

profile of v5, /device:TPU:41, one launch (start us, length us, event | category | flops | bytes accessed | tf_op | source)
XLA Modules:
  0.0 192.8 jit_solution(1564935506476992623)
XLA Ops:
  7.2 0.8 pad_maximum_fusion.1
  7.9 0.7 broadcast_in_dim.6
  8.7 10.0 %all-to-all-start = ((bf16[4,32,1024]{2,1,0:T(8,128)(2,1)}), bf16[4,32,1024]{2,1,0:T(8,128)(2,1)S(1)}, u32[]{:S(2)}, u32[]{:S(2)}) async-start(bf16[4,32,1024]{2,1,0:T(8,128)(2,1)} %broadcast_in_dim.6), calls=%async_computation | async-start | bytes 524288 | tf_op jit(solution)/shard_map/all_to_all | solution.py:79
  18.7 3.1 %collective-permute-start.2 = (bf16[512,256]{1,0:T(8,128)(2,1)}, bf16[512,256]{1,0:T(8,128)(2,1)S(1)}, u32[]{:S(2)}, u32[]{:S(2)}) collective-permute-start(bf16[512,256]{1,0:T(8,128)(2,1)} %param.13), channel_id=1, source_target_pairs={{0,64},{64,0},{1,65},{65,1},{2,66},{66,2},{3,67},{67,3},{4,68},{68... | collective-permute-start | bytes 786440 | tf_op jit(solution)/shard_map/ppermute | solution.py:46
  21.8 0.8 broadcast_select_fusion
  22.6 8.9 %collective-permute-start.1 = (bf16[2,32,256]{2,1,0:T(8,128)(2,1)S(1)}, bf16[2,32,256]{2,1,0:T(8,128)(2,1)S(1)}, u32[]{:S(2)}, u32[]{:S(2)}) collective-permute-start(bf16[2,32,256]{2,1,0:T(8,128)(2,1)S(1)} %get-tuple-element.30), channel_id=1, source_target_pairs={{0,16},{1,48},{2,0},{3,32},{4,144},{5,176},{6,128},{7,160},{8,272}... | collective-permute-start | bytes 98312 | tf_op jit(solution)/shard_map/ppermute | solution.py:65
  31.5 9.5 %collective-permute-start = (bf16[2,32,256]{2,1,0:T(8,128)(2,1)S(1)}, bf16[2,32,256]{2,1,0:T(8,128)(2,1)S(1)}, u32[]{:S(2)}, u32[]{:S(2)}) collective-permute-start(bf16[2,32,256]{2,1,0:T(8,128)(2,1)S(1)} %get-tuple-element.31), channel_id=1, source_target_pairs={{0,0},{1,32},{2,16},{3,48},{4,128},{5,160},{6,144},{7,176},{8,256}... | collective-permute-start | bytes 98312 | tf_op jit(solution)/shard_map/ppermute | solution.py:64
  41.0 4.1 %collective-permute-done = bf16[2,32,256]{2,1,0:T(8,128)(2,1)S(1)} collective-permute-done((bf16[2,32,256]{2,1,0:T(8,128)(2,1)S(1)}, bf16[2,32,256]{2,1,0:T(8,128)(2,1)S(1)}, u32[]{:S(2)}, u32[]{:S(2)}) %collective-permute-start) | collective-permute-done | bytes 32800 | tf_op jit(solution)/shard_map/ppermute | solution.py:64
  45.2 0.0 copy-start.2
  45.2 0.7 copy-done.2
  45.9 0.0 all-gather.2.cloned.1.call-update
  45.9 0.1 broadcast_in_dim.7
  46.0 20.8 %all_to_all.25 = bf16[16,32,1024]{2,1,0:T(8,128)(2,1)S(1)} all-to-all(bf16[16,32,1024]{2,1,0:T(8,128)(2,1)S(1)} %broadcast_in_dim.7), channel_id=1, replica_groups=mesh['yh'=4,'yl'=2,'zh'=4,'x'=4,'zl'=2,'core'=2] {'x','zl','core'}, dimensions={0} | all-to-all | bytes 2097152 | tf_op jit(solution)/shard_map/all_to_all | solution.py:79
  66.9 0.3 fusion.42
  67.2 1.1 fusion
  68.4 9.4 %all-to-all-start.2 = ((bf16[16,32,512]{2,1,0:T(8,128)(2,1)}), bf16[16,32,512]{2,1,0:T(8,128)(2,1)S(1)}, u32[]{:S(2)}, u32[]{:S(2)}) async-start(bf16[16,32,512]{2,1,0:T(8,128)(2,1)} %bitcast.8), calls=%async_computation.2 | async-start | bytes 1048576 | tf_op jit(solution)/shard_map/all_to_all | solution.py:85
  77.8 2.7 %collective-permute-start.3 = (bf16[256,512]{1,0:T(8,128)(2,1)S(1)}, bf16[256,512]{1,0:T(8,128)(2,1)S(1)}, u32[]{:S(2)}, u32[]{:S(2)}) collective-permute-start(bf16[256,512]{1,0:T(8,128)(2,1)S(1)} %copy-done.3), channel_id=1, source_target_pairs={{0,64},{64,0},{1,65},{65,1},{2,66},{66,2},{3,67},{67,3},{4,68},{68... | collective-permute-start | bytes 786440 | tf_op jit(solution)/shard_map/ppermute | solution.py:46
  80.4 2.6 %collective-permute-start.4 = (bf16[256,512]{1,0:T(8,128)(2,1)S(1)}, bf16[256,512]{1,0:T(8,128)(2,1)S(1)}, u32[]{:S(2)}, u32[]{:S(2)}) collective-permute-start(bf16[256,512]{1,0:T(8,128)(2,1)S(1)} %copy-done.7), channel_id=1, source_target_pairs={{0,64},{64,0},{1,65},{65,1},{2,66},{66,2},{3,67},{67,3},{4,68},{68... | collective-permute-start | bytes 786440 | tf_op jit(solution)/shard_map/ppermute | solution.py:46
  83.1 13.9 %all-to-all-done.2 = bf16[16,32,512]{2,1,0:T(8,128)(2,1)S(1)} async-done(((bf16[16,32,512]{2,1,0:T(8,128)(2,1)}), bf16[16,32,512]{2,1,0:T(8,128)(2,1)S(1)}, u32[]{:S(2)}, u32[]{:S(2)}) %all-to-all-start.2) | async-done | bytes 524320 | tf_op jit(solution)/shard_map/all_to_all | solution.py:85
  97.0 0.1 reduce_sum.24
  97.1 3.1 %collective-permute-done.3 = bf16[256,512]{1,0:T(8,128)(2,1)S(1)} collective-permute-done((bf16[256,512]{1,0:T(8,128)(2,1)S(1)}, bf16[256,512]{1,0:T(8,128)(2,1)S(1)}, u32[]{:S(2)}, u32[]{:S(2)}) %collective-permute-start.3) | collective-permute-done | bytes 262176 | tf_op jit(solution)/shard_map/ppermute | solution.py:46
  100.1 5.6 %collective-permute-done.4 = bf16[256,512]{1,0:T(8,128)(2,1)S(1)} collective-permute-done((bf16[256,512]{1,0:T(8,128)(2,1)S(1)}, bf16[256,512]{1,0:T(8,128)(2,1)S(1)}, u32[]{:S(2)}, u32[]{:S(2)}) %collective-permute-start.4) | collective-permute-done | bytes 262176 | tf_op jit(solution)/shard_map/ppermute | solution.py:46
  105.7 0.9 broadcast_in_dim.8
  106.6 12.2 %all-to-all-start.3 = ((bf16[16,32,512]{2,1,0:T(8,128)(2,1)}), bf16[16,32,512]{2,1,0:T(8,128)(2,1)}, u32[]{:S(2)}, u32[]{:S(2)}) async-start(bf16[16,32,512]{2,1,0:T(8,128)(2,1)} %broadcast_in_dim.8), calls=%async_computation.3 | async-start | bytes 1048576 | tf_op jit(solution)/shard_map/all_to_all | solution.py:79
  118.8 0.8 slice.81
  119.7 2.2 %collective-permute-start.7 = (bf16[512,512]{1,0:T(8,128)(2,1)}, bf16[512,512]{1,0:T(8,128)(2,1)}, u32[]{:S(2)}, u32[]{:S(2)}) collective-permute-start(bf16[512,512]{1,0:T(8,128)(2,1)} %slice.81), channel_id=1, source_target_pairs={{0,64},{64,0},{1,65},{65,1},{2,66},{66,2},{3,67},{67,3},{4,68},{68... | collective-permute-start | bytes 1572872 | tf_op jit(solution)/shard_map/ppermute | solution.py:46
  121.9 2.8 %constant_dynamic-slice_fusion = (bf16[4,1,128,1024]{3,2,1,0:T(8,128)(2,1)}, bf16[4,1,128,1024]{3,2,1,0:T(8,128)(2,1)S(1)}) fusion(bf16[4,2,128,1024]{3,2,1,0:T(8,128)(2,1)} %bitcast.41, s32[]{:T(128)S(6)} %select_n.72, s32[]{:T(128)S(6)} %select_n.67), kind=kLoop, calls=%fused_computation.78 | loop fusion | bytes 4194312 | tf_op jit(solution)/shard_map/jit(dynamic_index_in_dim)/dynamic_slice | solution.py:57
  124.7 1.3 fusion.26
  126.0 11.4 %all-to-all-done.3 = bf16[16,32,512]{2,1,0:T(8,128)(2,1)} async-done(((bf16[16,32,512]{2,1,0:T(8,128)(2,1)}), bf16[16,32,512]{2,1,0:T(8,128)(2,1)}, u32[]{:S(2)}, u32[]{:S(2)}) %all-to-all-start.3) | async-done | bytes 524320 | tf_op jit(solution)/shard_map/all_to_all | solution.py:79
  137.4 1.7 fusion.9
  139.1 0.3 fusion.49
  139.4 0.3 fusion.50
  139.8 0.3 fusion.1
  140.1 1.9 collective-permute-start.8
  142.1 0.3 fusion.2
  142.4 0.8 pad_maximum_fusion
  143.2 5.5 %all-to-all-start.4 = ((bf16[16,32,512]{2,1,0:T(8,128)(2,1)}), bf16[16,32,512]{2,1,0:T(8,128)(2,1)S(1)}, u32[]{:S(2)}, u32[]{:S(2)}) async-start(bf16[16,32,512]{2,1,0:T(8,128)(2,1)} %pad_maximum_fusion), calls=%async_computation.4 | async-start | bytes 1048576 | tf_op jit(solution)/shard_map/all_to_all | solution.py:85
  148.8 0.3 fusion.39
  149.1 0.3 fusion.37
  149.4 5.1 %collective-permute-done.8 = bf16[512,512]{1,0:T(8,128)(2,1)S(1)} collective-permute-done((bf16[512,512]{1,0:T(8,128)(2,1)}, bf16[512,512]{1,0:T(8,128)(2,1)S(1)}, u32[]{:S(2)}, u32[]{:S(2)}) %collective-permute-start.8) | collective-permute-done | bytes 524320 | tf_op jit(solution)/shard_map/ppermute | solution.py:46
  154.6 2.2 %fusion.4 = bf16[256,512]{1,0:T(8,128)(2,1)} fusion(f32[256,512]{1,0:T(8,128)S(1)} %fusion.37, bf16[512,512]{1,0:T(8,128)(2,1)S(1)} %collective-permute-done.8, bf16[512,1024]{1,0:T(8,128)(2,1)S(1)} %bitcast.42, bf16[512,512]{1,0:T(8,128)(2,1)} %collective-permute-done.7), kind=kOutput, calls=%fused_computation.22 | convolution fusion | flops 136577024 | bytes 2097152 | tf_op jit(solution)/shard_map/dot_general | solution.py:34
  156.8 2.5 %fusion.3 = bf16[256,512]{1,0:T(8,128)(2,1)} fusion(f32[256,512]{1,0:T(8,128)S(1)} %fusion.39, bf16[512,512]{1,0:T(8,128)(2,1)S(1)} %collective-permute-done.8, bf16[512,1024]{1,0:T(8,128)(2,1)S(1)} %bitcast.43, bf16[512,512]{1,0:T(8,128)(2,1)} %collective-permute-done.7), kind=kOutput, calls=%fused_computation.21 | convolution fusion | flops 137887744 | bytes 2621440 | tf_op jit(solution)/shard_map/dot_general | solution.py:34
  159.2 0.1 reduce_sum.25
  159.3 9.9 %collective-permute-start.5 = (bf16[32,256]{1,0:T(8,128)(2,1)S(1)}, bf16[32,256]{1,0:T(8,128)(2,1)S(1)}, u32[]{:S(2)}, u32[]{:S(2)}) collective-permute-start(bf16[32,256]{1,0:T(8,128)(2,1)S(1)} %get-tuple-element.34), channel_id=1, source_target_pairs={{16,0},{48,1},{0,2},{32,3},{144,4},{176,5},{128,6},{160,7},{272,8}... | collective-permute-start | bytes 49160 | tf_op jit(solution)/shard_map/ppermute | solution.py:72
  169.2 5.7 %collective-permute-start.6 = (bf16[32,256]{1,0:T(8,128)(2,1)S(1)}, bf16[32,256]{1,0:T(8,128)(2,1)S(1)}, u32[]{:S(2)}, u32[]{:S(2)}) collective-permute-start(bf16[32,256]{1,0:T(8,128)(2,1)S(1)} %get-tuple-element.35), channel_id=1, source_target_pairs={{0,0},{32,1},{16,2},{48,3},{128,4},{160,5},{144,6},{176,7},{256,8}... | collective-permute-start | bytes 49160 | tf_op jit(solution)/shard_map/ppermute | solution.py:71
  174.9 2.2 %fusion.5 = bf16[512,256]{1,0:T(8,128)(2,1)} fusion(f32[512,256]{1,0:T(8,128)S(1)} %copy-done.11, bf16[512,1024]{1,0:T(8,128)(2,1)S(1)} %bitcast.44, bf16[512,512]{1,0:T(8,128)(2,1)} %collective-permute-done.7), kind=kOutput, calls=%fused_computation.23 | convolution fusion | flops 136577024 | bytes 2097152 | tf_op jit(solution)/shard_map/dot_general | solution.py:34
  177.2 8.2 %collective-permute-done.6 = bf16[32,256]{1,0:T(8,128)(2,1)S(1)} collective-permute-done((bf16[32,256]{1,0:T(8,128)(2,1)S(1)}, bf16[32,256]{1,0:T(8,128)(2,1)S(1)}, u32[]{:S(2)}, u32[]{:S(2)}) %collective-permute-start.6) | collective-permute-done | bytes 16416 | tf_op jit(solution)/shard_map/ppermute | solution.py:71
  185.4 0.6 pad_maximum_fusion.4
  (35 shorter events, 0.1 us)
Async XLA Ops:
  8.7 36.5 %all-to-all-start = ((bf16[4,32,1024]{2,1,0:T(8,128)(2,1)}), bf16[4,32,1024]{2,1,0:T(8,128)(2,1)S(1)}, u32[]{:S(2)}, u32[]{:S(2)}) async-start(bf16[4,32,1024]{2,1,0:T(8,128)(2,1)} %broadcast_in_dim.6), calls=%async_computation | async-start | bytes 524288 | tf_op jit(solution)/shard_map/all_to_all | solution.py:79
  18.7 48.2 %copy-start.6 = (bf16[512,256]{1,0:T(8,128)(2,1)S(1)}, bf16[512,256]{1,0:T(8,128)(2,1)}, u32[]{:S(2)}) copy-start(bf16[512,256]{1,0:T(8,128)(2,1)} %param.13) | copy-start | bytes 786436
  18.7 87.0 %all-gather.2.cloned.1.call-start = ((), (), s32[]{:S(2)}) async-start(), calls=%async_computation.5 | async-start | bytes 2359296 | tf_op jit(solution)/shard_map/all_gather | solution.py:109
  18.7 26.4 %collective-permute-start.2 = (bf16[512,256]{1,0:T(8,128)(2,1)}, bf16[512,256]{1,0:T(8,128)(2,1)S(1)}, u32[]{:S(2)}, u32[]{:S(2)}) collective-permute-start(bf16[512,256]{1,0:T(8,128)(2,1)} %param.13), channel_id=1, source_target_pairs={{0,64},{64,0},{1,65},{65,1},{2,66},{66,2},{3,67},{67,3},{4,68},{68... | collective-permute-start | bytes 786440 | tf_op jit(solution)/shard_map/ppermute | solution.py:46
  22.6 18.4 %collective-permute-start.1 = (bf16[2,32,256]{2,1,0:T(8,128)(2,1)S(1)}, bf16[2,32,256]{2,1,0:T(8,128)(2,1)S(1)}, u32[]{:S(2)}, u32[]{:S(2)}) collective-permute-start(bf16[2,32,256]{2,1,0:T(8,128)(2,1)S(1)} %get-tuple-element.30), channel_id=1, source_target_pairs={{0,16},{1,48},{2,0},{3,32},{4,144},{5,176},{6,128},{7,160},{8,272}... | collective-permute-start | bytes 98312 | tf_op jit(solution)/shard_map/ppermute | solution.py:65
  31.5 13.6 %collective-permute-start = (bf16[2,32,256]{2,1,0:T(8,128)(2,1)S(1)}, bf16[2,32,256]{2,1,0:T(8,128)(2,1)S(1)}, u32[]{:S(2)}, u32[]{:S(2)}) collective-permute-start(bf16[2,32,256]{2,1,0:T(8,128)(2,1)S(1)} %get-tuple-element.31), channel_id=1, source_target_pairs={{0,0},{1,32},{2,16},{3,48},{4,128},{5,160},{6,144},{7,176},{8,256}... | collective-permute-start | bytes 98312 | tf_op jit(solution)/shard_map/ppermute | solution.py:64
  45.2 0.7 copy-start.2
  66.9 10.9 %copy-start.3 = (bf16[256,512]{1,0:T(8,128)(2,1)S(1)}, bf16[256,512]{1,0:T(8,128)(2,1)}, u32[]{:S(2)}) copy-start(bf16[256,512]{1,0:T(8,128)(2,1)} %param.11) | copy-start | bytes 786436
  66.9 13.6 %copy-start.7 = (bf16[256,512]{1,0:T(8,128)(2,1)S(1)}, bf16[256,512]{1,0:T(8,128)(2,1)}, u32[]{:S(2)}) copy-start(bf16[256,512]{1,0:T(8,128)(2,1)} %param.12) | copy-start | bytes 786436
  68.4 28.6 %all-to-all-start.2 = ((bf16[16,32,512]{2,1,0:T(8,128)(2,1)}), bf16[16,32,512]{2,1,0:T(8,128)(2,1)S(1)}, u32[]{:S(2)}, u32[]{:S(2)}) async-start(bf16[16,32,512]{2,1,0:T(8,128)(2,1)} %bitcast.8), calls=%async_computation.2 | async-start | bytes 1048576 | tf_op jit(solution)/shard_map/all_to_all | solution.py:85
  77.8 22.3 %collective-permute-start.3 = (bf16[256,512]{1,0:T(8,128)(2,1)S(1)}, bf16[256,512]{1,0:T(8,128)(2,1)S(1)}, u32[]{:S(2)}, u32[]{:S(2)}) collective-permute-start(bf16[256,512]{1,0:T(8,128)(2,1)S(1)} %copy-done.3), channel_id=1, source_target_pairs={{0,64},{64,0},{1,65},{65,1},{2,66},{66,2},{3,67},{67,3},{4,68},{68... | collective-permute-start | bytes 786440 | tf_op jit(solution)/shard_map/ppermute | solution.py:46
  80.4 25.3 %collective-permute-start.4 = (bf16[256,512]{1,0:T(8,128)(2,1)S(1)}, bf16[256,512]{1,0:T(8,128)(2,1)S(1)}, u32[]{:S(2)}, u32[]{:S(2)}) collective-permute-start(bf16[256,512]{1,0:T(8,128)(2,1)S(1)} %copy-done.7), channel_id=1, source_target_pairs={{0,64},{64,0},{1,65},{65,1},{2,66},{66,2},{3,67},{67,3},{4,68},{68... | collective-permute-start | bytes 786440 | tf_op jit(solution)/shard_map/ppermute | solution.py:46
  100.1 21.8 %copy-start.9 = (bf16[256,512]{1,0:T(8,128)(2,1)}, bf16[256,512]{1,0:T(8,128)(2,1)S(1)}, u32[]{:S(2)}) copy-start(bf16[256,512]{1,0:T(8,128)(2,1)S(1)} %collective-permute-done.3) | copy-start | bytes 786436
  105.7 19.0 %copy-start.4 = (bf16[256,512]{1,0:T(8,128)(2,1)}, bf16[256,512]{1,0:T(8,128)(2,1)S(1)}, u32[]{:S(2)}) copy-start(bf16[256,512]{1,0:T(8,128)(2,1)S(1)} %collective-permute-done.4) | copy-start | bytes 786436
  106.6 30.8 %all-to-all-start.3 = ((bf16[16,32,512]{2,1,0:T(8,128)(2,1)}), bf16[16,32,512]{2,1,0:T(8,128)(2,1)}, u32[]{:S(2)}, u32[]{:S(2)}) async-start(bf16[16,32,512]{2,1,0:T(8,128)(2,1)} %broadcast_in_dim.8), calls=%async_computation.3 | async-start | bytes 1048576 | tf_op jit(solution)/shard_map/all_to_all | solution.py:79
  119.7 34.9 %collective-permute-start.7 = (bf16[512,512]{1,0:T(8,128)(2,1)}, bf16[512,512]{1,0:T(8,128)(2,1)}, u32[]{:S(2)}, u32[]{:S(2)}) collective-permute-start(bf16[512,512]{1,0:T(8,128)(2,1)} %slice.81), channel_id=1, source_target_pairs={{0,64},{64,0},{1,65},{65,1},{2,66},{66,2},{3,67},{67,3},{4,68},{68... | collective-permute-start | bytes 1572872 | tf_op jit(solution)/shard_map/ppermute | solution.py:46
  137.4 2.0 %copy-start.5 = (bf16[256,512]{1,0:T(8,128)(2,1)S(1)}, bf16[256,512]{1,0:T(8,128)(2,1)}, u32[]{:S(2)}) copy-start(bf16[256,512]{1,0:T(8,128)(2,1)} %copy-done.4) | copy-start | bytes 786436
  137.4 2.4 %copy-start.8 = (bf16[256,512]{1,0:T(8,128)(2,1)S(1)}, bf16[256,512]{1,0:T(8,128)(2,1)}, u32[]{:S(2)}) copy-start(bf16[256,512]{1,0:T(8,128)(2,1)} %param.12) | copy-start | bytes 786436
  139.1 3.0 %copy-start.10 = (bf16[256,512]{1,0:T(8,128)(2,1)S(1)}, bf16[256,512]{1,0:T(8,128)(2,1)}, u32[]{:S(2)}) copy-start(bf16[256,512]{1,0:T(8,128)(2,1)} %copy-done.9) | copy-start | bytes 786436
  140.1 14.4 %collective-permute-start.8 = (bf16[512,512]{1,0:T(8,128)(2,1)}, bf16[512,512]{1,0:T(8,128)(2,1)S(1)}, u32[]{:S(2)}, u32[]{:S(2)}) collective-permute-start(bf16[512,512]{1,0:T(8,128)(2,1)} %bitcast.9), channel_id=1, source_target_pairs={{0,64},{64,0},{1,65},{65,1},{2,66},{66,2},{3,67},{67,3},{4,68},{68... | collective-permute-start | bytes 1572872 | tf_op jit(solution)/shard_map/ppermute | solution.py:46
  143.2 16.0 %all-to-all-start.4 = ((bf16[16,32,512]{2,1,0:T(8,128)(2,1)}), bf16[16,32,512]{2,1,0:T(8,128)(2,1)S(1)}, u32[]{:S(2)}, u32[]{:S(2)}) async-start(bf16[16,32,512]{2,1,0:T(8,128)(2,1)} %pad_maximum_fusion), calls=%async_computation.4 | async-start | bytes 1048576 | tf_op jit(solution)/shard_map/all_to_all | solution.py:85
  148.8 5.8 %copy-start = (bf16[4,1,128,1024]{3,2,1,0:T(8,128)(2,1)S(1)}, bf16[4,1,128,1024]{3,2,1,0:T(8,128)(2,1)}, u32[]{:S(2)}) copy-start(bf16[4,1,128,1024]{3,2,1,0:T(8,128)(2,1)} %get-tuple-element.24) | copy-start | bytes 3145732
  156.8 18.1 %copy-start.1 = (bf16[4,1,128,1024]{3,2,1,0:T(8,128)(2,1)S(1)}, bf16[4,1,128,1024]{3,2,1,0:T(8,128)(2,1)}, u32[]{:S(2)}) copy-start(bf16[4,1,128,1024]{3,2,1,0:T(8,128)(2,1)} %get-tuple-element.24) | copy-start | bytes 3145732
  156.8 18.2 %copy-start.11 = (f32[512,256]{1,0:T(8,128)S(1)}, f32[512,256]{1,0:T(8,128)}, u32[]{:S(2)}) copy-start(f32[512,256]{1,0:T(8,128)} %fusion.26) | copy-start | bytes 1572868
  159.3 17.8 %collective-permute-start.5 = (bf16[32,256]{1,0:T(8,128)(2,1)S(1)}, bf16[32,256]{1,0:T(8,128)(2,1)S(1)}, u32[]{:S(2)}, u32[]{:S(2)}) collective-permute-start(bf16[32,256]{1,0:T(8,128)(2,1)S(1)} %get-tuple-element.34), channel_id=1, source_target_pairs={{16,0},{48,1},{0,2},{32,3},{144,4},{176,5},{128,6},{160,7},{272,8}... | collective-permute-start | bytes 49160 | tf_op jit(solution)/shard_map/ppermute | solution.py:72
  169.2 16.2 %collective-permute-start.6 = (bf16[32,256]{1,0:T(8,128)(2,1)S(1)}, bf16[32,256]{1,0:T(8,128)(2,1)S(1)}, u32[]{:S(2)}, u32[]{:S(2)}) collective-permute-start(bf16[32,256]{1,0:T(8,128)(2,1)S(1)} %get-tuple-element.35), channel_id=1, source_target_pairs={{0,0},{32,1},{16,2},{48,3},{128,4},{160,5},{144,6},{176,7},{256,8}... | collective-permute-start | bytes 49160 | tf_op jit(solution)/shard_map/ppermute | solution.py:71
Sparse Core Ops, SparseCore 0:
  46.0 43.6 all-gather.1

commit v6 on v5

--- a/solution.py
+++ b/solution.py
@@ -113,10 +113,11 @@
     gate_other, up_other = swap(gate_weight), swap(up_weight)
 
     partial = contract_cols(grads_a, down_weight) + contract_cols(grads_other, down_other)
+    partial, gate_other, up_other = lax.optimization_barrier(
+        (partial.astype(jnp.bfloat16), gate_other, up_other)
+    )
     hidden_grad = scatter_sum(partial, HALF, C)
-    hidden_grad, pre, gate_other, up_other = lax.optimization_barrier(
-        (hidden_grad, pre, gate_other, up_other)
-    )
+    hidden_grad, pre = lax.optimization_barrier((hidden_grad, pre))
     hidden_grad = gather_copies(hidden_grad, HALF, C)
     pre_a, pre_b = halves(pre)
     gate_a, up_a, hidden_a = swiglu_back(hidden_grad, pre_a[:, :512], pre_a[:, 512:])
@@ -131,7 +132,8 @@
     )
     summed = scatter_sum(partial, COL, C)
     input_grad = to_tokens(summed[:, :256], summed[:, 256:], upper, mine)
-    swapped_cols = swap(cols[:, 256:768])
+    (cols_other, _) = lax.optimization_barrier((cols[:, 256:768], gate_a))
+    swapped_cols = swap(cols_other)
     grads_b, tokens_b = swapped_cols[:, :256], swapped_cols[:, 256:]
     gate_weight_grad = contract_rows(tokens_a, gate_a) + contract_rows(tokens_b, gate_b)
     up_weight_grad = contract_rows(tokens_a, up_a) + contract_rows(tokens_b, up_b)

time: 194 us -> 201 us (1.036)
  blocking collectives: 20.8 us -> 28.3 us
  waiting for transfers between devices: 51.4 us -> 48 us
    all_to_all x2 -> x1, waiting for transfers between devices: 13.9 us -> 0.01 us  [scatter_sum(): got = lax.all_to_all(pieces, axes, 0, 0, tiled=True)]
    all_to_all x1, blocking collectives: 20.8 us -> 28.3 us  [scatter_sum(): got = lax.all_to_all(pieces, axes, 0, 0, tiled=True)]
    all_to_all x2 -> x3, waiting for transfers between devices: 11.4 us -> 17.6 us  [gather_copies(): got = lax.all_to_all(copies, axes, 0, 0, tiled=True)]
    all_to_all x2 -> x1, starting transfers between devices: 14.9 us -> 8.92 us  [scatter_sum(): got = lax.all_to_all(pieces, axes, 0, 0, tiled=True)]
    ppermute x5, starting transfers between devices: 12.5 us -> 17.5 us  [swap(): return lax.ppermute(value, 'yl', [(0, 1), (1, 0)])]
    ppermute x1, starting transfers between devices: 9.87 us -> 12.8 us  [to_tokens(): two = lax.ppermute(two, AXES, inverse(SECOND))]
    all_to_all x2 -> x3, starting transfers between devices: 22.2 us -> 25.1 us  [gather_copies(): got = lax.all_to_all(copies, axes, 0, 0, tiled=True)]
    ppermute x1, starting transfers between devices: 5.7 us -> 2.83 us  [to_tokens(): one = lax.ppermute(one, AXES, inverse(FIRST))]
  transfers between devices with their start and end apart: 14 -> 14, of which waited for: 7 -> 6; matrix products, arithmetic and copies ran while one was open for 10% -> 8% of each run, Pallas kernels for 0% -> 0%
where the time goes in v6:
time: 201 us; the launch traced here: 200 us
  starting transfers between devices  85.6 us (43%)
  waiting for transfers between devices  48 us (24%)
  blocking collectives  28.3 us (14%)
  between operations  14.4 us (7%)
  matrix products  11.1 us (6%)
  local copies, waits for them, and re-layouts  7.79 us (4%)
  other arithmetic  4.92 us (2%)
    all_to_all x1, blocking collectives, scatter_sum(): got = lax.all_to_all(pieces, axes, 0, 0, tiled=True)  28.3 us
    all_to_all x3, starting transfers between devices, gather_copies(): got = lax.all_to_all(copies, axes, 0, 0, tiled=True)  25.1 us
    all_to_all x3, waiting for transfers between devices, gather_copies(): got = lax.all_to_all(copies, axes, 0, 0, tiled=True)  17.6 us
    ppermute x5, starting transfers between devices, swap(): return lax.ppermute(value, 'yl', [(0, 1), (1, 0)])  17.5 us
    ppermute x5, waiting for transfers between devices, swap(): return lax.ppermute(value, 'yl', [(0, 1), (1, 0)])  15.2 us
    ppermute x1, starting transfers between devices, to_tokens(): two = lax.ppermute(two, AXES, inverse(SECOND))  12.8 us
    ppermute x1, waiting for transfers between devices, to_tokens(): one = lax.ppermute(one, AXES, inverse(FIRST))  11.1 us
    ppermute x1, starting transfers between devices, to_features(): one = lax.ppermute(one, AXES, FIRST)  9.48 us
  transfers between devices with their start and end apart: 14, of which 6 were waited for; matrix products, arithmetic and copies ran while one was open for 8% of the time, Pallas kernels for 0%

profile of v6, /device:TPU:41, one launch (start us, length us, event | category | flops | bytes accessed | tf_op | source)
XLA Modules:
  0.0 200.2 jit_solution(8527747877065449373)
XLA Ops:
  7.2 0.8 pad_maximum_fusion.1
  7.9 0.7 broadcast_in_dim.6
  8.7 10.0 %all-to-all-start = ((bf16[4,32,1024]{2,1,0:T(8,128)(2,1)}), bf16[4,32,1024]{2,1,0:T(8,128)(2,1)S(1)}, u32[]{:S(2)}, u32[]{:S(2)}) async-start(bf16[4,32,1024]{2,1,0:T(8,128)(2,1)} %broadcast_in_dim.6), calls=%async_computation | async-start | bytes 524288 | tf_op jit(solution)/shard_map/all_to_all | solution.py:79
  18.7 0.0 all-gather.2.cloned.1.call-start
  18.8 3.1 %collective-permute-start.2 = (bf16[512,256]{1,0:T(8,128)(2,1)}, bf16[512,256]{1,0:T(8,128)(2,1)S(1)}, u32[]{:S(2)}, u32[]{:S(2)}) collective-permute-start(bf16[512,256]{1,0:T(8,128)(2,1)} %param.13), channel_id=1, source_target_pairs={{0,64},{64,0},{1,65},{65,1},{2,66},{66,2},{3,67},{67,3},{4,68},{68... | collective-permute-start | bytes 786440 | tf_op jit(solution)/shard_map/ppermute | solution.py:46
  21.9 0.8 broadcast_select_fusion
  22.7 8.9 %collective-permute-start.1 = (bf16[2,32,256]{2,1,0:T(8,128)(2,1)S(1)}, bf16[2,32,256]{2,1,0:T(8,128)(2,1)S(1)}, u32[]{:S(2)}, u32[]{:S(2)}) collective-permute-start(bf16[2,32,256]{2,1,0:T(8,128)(2,1)S(1)} %get-tuple-element.34), channel_id=1, source_target_pairs={{0,16},{1,48},{2,0},{3,32},{4,144},{5,176},{6,128},{7,160},{8,272}... | collective-permute-start | bytes 98312 | tf_op jit(solution)/shard_map/ppermute | solution.py:65
  31.6 9.5 %collective-permute-start = (bf16[2,32,256]{2,1,0:T(8,128)(2,1)S(1)}, bf16[2,32,256]{2,1,0:T(8,128)(2,1)S(1)}, u32[]{:S(2)}, u32[]{:S(2)}) collective-permute-start(bf16[2,32,256]{2,1,0:T(8,128)(2,1)S(1)} %get-tuple-element.35), channel_id=1, source_target_pairs={{0,0},{1,32},{2,16},{3,48},{4,128},{5,160},{6,144},{7,176},{8,256}... | collective-permute-start | bytes 98312 | tf_op jit(solution)/shard_map/ppermute | solution.py:64
  41.1 4.1 %collective-permute-done = bf16[2,32,256]{2,1,0:T(8,128)(2,1)S(1)} collective-permute-done((bf16[2,32,256]{2,1,0:T(8,128)(2,1)S(1)}, bf16[2,32,256]{2,1,0:T(8,128)(2,1)S(1)}, u32[]{:S(2)}, u32[]{:S(2)}) %collective-permute-start) | collective-permute-done | bytes 32800 | tf_op jit(solution)/shard_map/ppermute | solution.py:64
  45.2 0.7 copy-done.2
  46.0 1.1 broadcast_in_dim.7
  47.1 5.6 %all-to-all-start.1 = ((bf16[16,32,1024]{2,1,0:T(8,128)(2,1)}), bf16[16,32,1024]{2,1,0:T(8,128)(2,1)S(1)}, u32[]{:S(2)}, u32[]{:S(2)}) async-start(bf16[16,32,1024]{2,1,0:T(8,128)(2,1)} %broadcast_in_dim.7), calls=%async_computation.1 | async-start | bytes 2097152 | tf_op jit(solution)/shard_map/all_to_all | solution.py:79
  52.7 3.2 %collective-permute-start.3 = (bf16[256,512]{1,0:T(8,128)(2,1)S(1)}, bf16[256,512]{1,0:T(8,128)(2,1)S(1)}, u32[]{:S(2)}, u32[]{:S(2)}) collective-permute-start(bf16[256,512]{1,0:T(8,128)(2,1)S(1)} %copy-done.4), channel_id=1, source_target_pairs={{0,64},{64,0},{1,65},{65,1},{2,66},{66,2},{3,67},{67,3},{4,68},{68... | collective-permute-start | bytes 786440 | tf_op jit(solution)/shard_map/ppermute | solution.py:46
  56.0 2.1 %collective-permute-start.4 = (bf16[256,512]{1,0:T(8,128)(2,1)S(1)}, bf16[256,512]{1,0:T(8,128)(2,1)S(1)}, u32[]{:S(2)}, u32[]{:S(2)}) collective-permute-start(bf16[256,512]{1,0:T(8,128)(2,1)S(1)} %copy-done.8), channel_id=1, source_target_pairs={{0,64},{64,0},{1,65},{65,1},{2,66},{66,2},{3,67},{67,3},{4,68},{68... | collective-permute-start | bytes 786440 | tf_op jit(solution)/shard_map/ppermute | solution.py:46
  58.1 10.5 %all-to-all-done.1 = bf16[16,32,1024]{2,1,0:T(8,128)(2,1)S(1)} async-done(((bf16[16,32,1024]{2,1,0:T(8,128)(2,1)}), bf16[16,32,1024]{2,1,0:T(8,128)(2,1)S(1)}, u32[]{:S(2)}, u32[]{:S(2)}) %all-to-all-start.1) | async-done | bytes 1048608 | tf_op jit(solution)/shard_map/all_to_all | solution.py:79
  68.6 0.3 fusion.42
  68.9 0.3 fusion
  69.3 5.6 %collective-permute-done.4 = bf16[256,512]{1,0:T(8,128)(2,1)S(1)} collective-permute-done((bf16[256,512]{1,0:T(8,128)(2,1)S(1)}, bf16[256,512]{1,0:T(8,128)(2,1)S(1)}, u32[]{:S(2)}, u32[]{:S(2)}) %collective-permute-start.4) | collective-permute-done | bytes 262176 | tf_op jit(solution)/shard_map/ppermute | solution.py:46
  74.9 0.7 copy-done.5
  75.6 28.3 %all_to_all.25 = bf16[16,32,512]{2,1,0:T(8,128)(2,1)S(1)} all-to-all(bf16[16,32,512]{2,1,0:T(8,128)(2,1)S(1)} %bitcast.42), channel_id=1, replica_groups=mesh['yh'=4,'yl'=2,'zh'=4,'x'=4,'zl'=2,'core'=2] {'yh','zh'}, dimensions={0} | all-to-all | bytes 1048576 | tf_op jit(solution)/shard_map/all_to_all | solution.py:85
  103.9 0.1 reduce_sum.24
  104.0 0.0 all-gather.2.cloned.1.call-done
  104.0 0.8 broadcast_in_dim.8
  104.9 9.4 %all-to-all-start.3 = ((bf16[16,32,512]{2,1,0:T(8,128)(2,1)}), bf16[16,32,512]{2,1,0:T(8,128)(2,1)}, u32[]{:S(2)}, u32[]{:S(2)}) async-start(bf16[16,32,512]{2,1,0:T(8,128)(2,1)} %broadcast_in_dim.8), calls=%async_computation.3 | async-start | bytes 1048576 | tf_op jit(solution)/shard_map/all_to_all | solution.py:79
  114.3 0.9 slice.81
  115.2 2.8 %constant_dynamic-slice_fusion = (bf16[4,1,128,1024]{3,2,1,0:T(8,128)(2,1)}, bf16[4,1,128,1024]{3,2,1,0:T(8,128)(2,1)S(1)}) fusion(bf16[4,2,128,1024]{3,2,1,0:T(8,128)(2,1)} %bitcast.41, s32[]{:T(128)S(6)} %select_n.72, s32[]{:T(128)S(6)} %select_n.67), kind=kLoop, calls=%fused_computation.78 | loop fusion | bytes 4194312 | tf_op jit(solution)/shard_map/jit(dynamic_index_in_dim)/dynamic_slice | solution.py:57
  117.9 1.3 fusion.26
  119.2 7.1 %all-to-all-done.3 = bf16[16,32,512]{2,1,0:T(8,128)(2,1)} async-done(((bf16[16,32,512]{2,1,0:T(8,128)(2,1)}), bf16[16,32,512]{2,1,0:T(8,128)(2,1)}, u32[]{:S(2)}, u32[]{:S(2)}) %all-to-all-start.3) | async-done | bytes 524320 | tf_op jit(solution)/shard_map/all_to_all | solution.py:79
  126.4 1.7 fusion.9
  128.1 0.3 fusion.49
  128.4 0.3 fusion.50
  128.8 0.3 fusion.1
  129.1 7.2 %collective-permute-start.8 = (bf16[512,512]{1,0:T(8,128)(2,1)}, bf16[512,512]{1,0:T(8,128)(2,1)}, u32[]{:S(2)}, u32[]{:S(2)}) collective-permute-start(bf16[512,512]{1,0:T(8,128)(2,1)} %bitcast.9), channel_id=1, source_target_pairs={{0,64},{64,0},{1,65},{65,1},{2,66},{66,2},{3,67},{67,3},{4,68},{68... | collective-permute-start | bytes 1572872 | tf_op jit(solution)/shard_map/ppermute | solution.py:46
  136.3 1.9 collective-permute-start.7
  138.2 0.3 fusion.2
  138.6 0.8 pad_maximum_fusion
  139.4 8.9 %all-to-all-start.4 = ((bf16[16,32,512]{2,1,0:T(8,128)(2,1)}), bf16[16,32,512]{2,1,0:T(8,128)(2,1)S(1)}, u32[]{:S(2)}, u32[]{:S(2)}) async-start(bf16[16,32,512]{2,1,0:T(8,128)(2,1)} %pad_maximum_fusion), calls=%async_computation.4 | async-start | bytes 1048576 | tf_op jit(solution)/shard_map/all_to_all | solution.py:85
  148.3 0.3 fusion.39
  148.7 0.3 fusion.37
  149.0 9.6 %collective-permute-done.7 = bf16[512,512]{1,0:T(8,128)(2,1)} collective-permute-done((bf16[512,512]{1,0:T(8,128)(2,1)S(1)}, bf16[512,512]{1,0:T(8,128)(2,1)}, u32[]{:S(2)}, u32[]{:S(2)}) %collective-permute-start.7) | collective-permute-done | bytes 524320 | tf_op jit(solution)/shard_map/ppermute | solution.py:46
  158.6 2.4 %fusion.4 = bf16[256,512]{1,0:T(8,128)(2,1)} fusion(f32[256,512]{1,0:T(8,128)S(1)} %fusion.37, bf16[512,512]{1,0:T(8,128)(2,1)} %collective-permute-done.8, bf16[512,1024]{1,0:T(8,128)(2,1)S(1)} %bitcast.43, bf16[512,512]{1,0:T(8,128)(2,1)} %collective-permute-done.7), kind=kOutput, calls=%fused_computation.22 | convolution fusion | flops 136577024 | bytes 2097152 | tf_op jit(solution)/shard_map/dot_general | solution.py:34
  161.0 2.6 %fusion.3 = bf16[256,512]{1,0:T(8,128)(2,1)} fusion(f32[256,512]{1,0:T(8,128)S(1)} %fusion.39, bf16[512,512]{1,0:T(8,128)(2,1)} %collective-permute-done.8, bf16[512,1024]{1,0:T(8,128)(2,1)S(1)} %bitcast.44, bf16[512,512]{1,0:T(8,128)(2,1)} %collective-permute-done.7), kind=kOutput, calls=%fused_computation.21 | convolution fusion | flops 137887744 | bytes 2621440 | tf_op jit(solution)/shard_map/dot_general | solution.py:34
  163.6 0.1 reduce_sum.25
  163.7 12.8 %collective-permute-start.5 = (bf16[32,256]{1,0:T(8,128)(2,1)S(1)}, bf16[32,256]{1,0:T(8,128)(2,1)S(1)}, u32[]{:S(2)}, u32[]{:S(2)}) collective-permute-start(bf16[32,256]{1,0:T(8,128)(2,1)S(1)} %get-tuple-element.38), channel_id=1, source_target_pairs={{16,0},{48,1},{0,2},{32,3},{144,4},{176,5},{128,6},{160,7},{272,8}... | collective-permute-start | bytes 49160 | tf_op jit(solution)/shard_map/ppermute | solution.py:72
  176.5 2.8 %collective-permute-start.6 = (bf16[32,256]{1,0:T(8,128)(2,1)S(1)}, bf16[32,256]{1,0:T(8,128)(2,1)S(1)}, u32[]{:S(2)}, u32[]{:S(2)}) collective-permute-start(bf16[32,256]{1,0:T(8,128)(2,1)S(1)} %get-tuple-element.39), channel_id=1, source_target_pairs={{0,0},{32,1},{16,2},{48,3},{128,4},{160,5},{144,6},{176,7},{256,8}... | collective-permute-start | bytes 49160 | tf_op jit(solution)/shard_map/ppermute | solution.py:71
  179.4 2.2 %fusion.5 = bf16[512,256]{1,0:T(8,128)(2,1)} fusion(f32[512,256]{1,0:T(8,128)S(1)} %copy-done.12, bf16[512,1024]{1,0:T(8,128)(2,1)S(1)} %bitcast.45, bf16[512,512]{1,0:T(8,128)(2,1)} %collective-permute-done.7), kind=kOutput, calls=%fused_computation.23 | convolution fusion | flops 136577024 | bytes 2097152 | tf_op jit(solution)/shard_map/dot_general | solution.py:34
  181.6 11.1 %collective-permute-done.6 = bf16[32,256]{1,0:T(8,128)(2,1)S(1)} collective-permute-done((bf16[32,256]{1,0:T(8,128)(2,1)S(1)}, bf16[32,256]{1,0:T(8,128)(2,1)S(1)}, u32[]{:S(2)}, u32[]{:S(2)}) %collective-permute-start.6) | collective-permute-done | bytes 16416 | tf_op jit(solution)/shard_map/ppermute | solution.py:71
  192.7 0.6 pad_maximum_fusion.4
  (37 shorter events, 0.1 us)
Async XLA Ops:
  8.7 36.5 %all-to-all-start = ((bf16[4,32,1024]{2,1,0:T(8,128)(2,1)}), bf16[4,32,1024]{2,1,0:T(8,128)(2,1)S(1)}, u32[]{:S(2)}, u32[]{:S(2)}) async-start(bf16[4,32,1024]{2,1,0:T(8,128)(2,1)} %broadcast_in_dim.6), calls=%async_computation | async-start | bytes 524288 | tf_op jit(solution)/shard_map/all_to_all | solution.py:79
  18.7 34.0 %copy-start.4 = (bf16[256,512]{1,0:T(8,128)(2,1)S(1)}, bf16[256,512]{1,0:T(8,128)(2,1)}, u32[]{:S(2)}) copy-start(bf16[256,512]{1,0:T(8,128)(2,1)} %param.11) | copy-start | bytes 786436
  18.7 37.3 %copy-start.8 = (bf16[256,512]{1,0:T(8,128)(2,1)S(1)}, bf16[256,512]{1,0:T(8,128)(2,1)}, u32[]{:S(2)}) copy-start(bf16[256,512]{1,0:T(8,128)(2,1)} %param.12) | copy-start | bytes 786436
  18.7 49.9 %copy-start.7 = (bf16[512,256]{1,0:T(8,128)(2,1)S(1)}, bf16[512,256]{1,0:T(8,128)(2,1)}, u32[]{:S(2)}) copy-start(bf16[512,256]{1,0:T(8,128)(2,1)} %param.13) | copy-start | bytes 786436
  18.7 85.3 %all-gather.2.cloned.1.call-start = ((), (), s32[]{:S(2)}) async-start(), calls=%async_computation.5 | async-start | bytes 2359296 | tf_op jit(solution)/shard_map/all_gather | solution.py:109
  18.8 26.5 %collective-permute-start.2 = (bf16[512,256]{1,0:T(8,128)(2,1)}, bf16[512,256]{1,0:T(8,128)(2,1)S(1)}, u32[]{:S(2)}, u32[]{:S(2)}) collective-permute-start(bf16[512,256]{1,0:T(8,128)(2,1)} %param.13), channel_id=1, source_target_pairs={{0,64},{64,0},{1,65},{65,1},{2,66},{66,2},{3,67},{67,3},{4,68},{68... | collective-permute-start | bytes 786440 | tf_op jit(solution)/shard_map/ppermute | solution.py:46
  22.7 18.4 %collective-permute-start.1 = (bf16[2,32,256]{2,1,0:T(8,128)(2,1)S(1)}, bf16[2,32,256]{2,1,0:T(8,128)(2,1)S(1)}, u32[]{:S(2)}, u32[]{:S(2)}) collective-permute-start(bf16[2,32,256]{2,1,0:T(8,128)(2,1)S(1)} %get-tuple-element.34), channel_id=1, source_target_pairs={{0,16},{1,48},{2,0},{3,32},{4,144},{5,176},{6,128},{7,160},{8,272}... | collective-permute-start | bytes 98312 | tf_op jit(solution)/shard_map/ppermute | solution.py:65
  31.6 13.6 %collective-permute-start = (bf16[2,32,256]{2,1,0:T(8,128)(2,1)S(1)}, bf16[2,32,256]{2,1,0:T(8,128)(2,1)S(1)}, u32[]{:S(2)}, u32[]{:S(2)}) collective-permute-start(bf16[2,32,256]{2,1,0:T(8,128)(2,1)S(1)} %get-tuple-element.35), channel_id=1, source_target_pairs={{0,0},{1,32},{2,16},{3,48},{4,128},{5,160},{6,144},{7,176},{8,256}... | collective-permute-start | bytes 98312 | tf_op jit(solution)/shard_map/ppermute | solution.py:64
  45.2 0.7 copy-start.2
  47.1 21.4 %all-to-all-start.1 = ((bf16[16,32,1024]{2,1,0:T(8,128)(2,1)}), bf16[16,32,1024]{2,1,0:T(8,128)(2,1)S(1)}, u32[]{:S(2)}, u32[]{:S(2)}) async-start(bf16[16,32,1024]{2,1,0:T(8,128)(2,1)} %broadcast_in_dim.7), calls=%async_computation.1 | async-start | bytes 2097152 | tf_op jit(solution)/shard_map/all_to_all | solution.py:79
  52.7 16.5 %collective-permute-start.3 = (bf16[256,512]{1,0:T(8,128)(2,1)S(1)}, bf16[256,512]{1,0:T(8,128)(2,1)S(1)}, u32[]{:S(2)}, u32[]{:S(2)}) collective-permute-start(bf16[256,512]{1,0:T(8,128)(2,1)S(1)} %copy-done.4), channel_id=1, source_target_pairs={{0,64},{64,0},{1,65},{65,1},{2,66},{66,2},{3,67},{67,3},{4,68},{68... | collective-permute-start | bytes 786440 | tf_op jit(solution)/shard_map/ppermute | solution.py:46
  56.0 18.9 %collective-permute-start.4 = (bf16[256,512]{1,0:T(8,128)(2,1)S(1)}, bf16[256,512]{1,0:T(8,128)(2,1)S(1)}, u32[]{:S(2)}, u32[]{:S(2)}) collective-permute-start(bf16[256,512]{1,0:T(8,128)(2,1)S(1)} %copy-done.8), channel_id=1, source_target_pairs={{0,64},{64,0},{1,65},{65,1},{2,66},{66,2},{3,67},{67,3},{4,68},{68... | collective-permute-start | bytes 786440 | tf_op jit(solution)/shard_map/ppermute | solution.py:46
  69.2 50.0 %copy-start.10 = (bf16[256,512]{1,0:T(8,128)(2,1)}, bf16[256,512]{1,0:T(8,128)(2,1)S(1)}, u32[]{:S(2)}) copy-start(bf16[256,512]{1,0:T(8,128)(2,1)S(1)} %collective-permute-done.3) | copy-start | bytes 786436
  74.9 0.7 copy-start.5
  104.9 21.5 %all-to-all-start.3 = ((bf16[16,32,512]{2,1,0:T(8,128)(2,1)}), bf16[16,32,512]{2,1,0:T(8,128)(2,1)}, u32[]{:S(2)}, u32[]{:S(2)}) async-start(bf16[16,32,512]{2,1,0:T(8,128)(2,1)} %broadcast_in_dim.8), calls=%async_computation.3 | async-start | bytes 1048576 | tf_op jit(solution)/shard_map/all_to_all | solution.py:79
  126.4 2.0 %copy-start.6 = (bf16[256,512]{1,0:T(8,128)(2,1)S(1)}, bf16[256,512]{1,0:T(8,128)(2,1)}, u32[]{:S(2)}) copy-start(bf16[256,512]{1,0:T(8,128)(2,1)} %copy-done.5) | copy-start | bytes 786436
  126.4 2.4 %copy-start.9 = (bf16[256,512]{1,0:T(8,128)(2,1)S(1)}, bf16[256,512]{1,0:T(8,128)(2,1)}, u32[]{:S(2)}) copy-start(bf16[256,512]{1,0:T(8,128)(2,1)} %param.12) | copy-start | bytes 786436
  128.0 8.2 %copy-start.3 = (bf16[512,512]{1,0:T(8,128)(2,1)S(1)}, bf16[512,512]{1,0:T(8,128)(2,1)}, u32[]{:S(2)}) copy-start(bf16[512,512]{1,0:T(8,128)(2,1)} %slice.81) | copy-start | bytes 1572868
  128.1 10.2 %copy-start.11 = (bf16[256,512]{1,0:T(8,128)(2,1)S(1)}, bf16[256,512]{1,0:T(8,128)(2,1)}, u32[]{:S(2)}) copy-start(bf16[256,512]{1,0:T(8,128)(2,1)} %copy-done.10) | copy-start | bytes 786436
  129.1 19.9 %collective-permute-start.8 = (bf16[512,512]{1,0:T(8,128)(2,1)}, bf16[512,512]{1,0:T(8,128)(2,1)}, u32[]{:S(2)}, u32[]{:S(2)}) collective-permute-start(bf16[512,512]{1,0:T(8,128)(2,1)} %bitcast.9), channel_id=1, source_target_pairs={{0,64},{64,0},{1,65},{65,1},{2,66},{66,2},{3,67},{67,3},{4,68},{68... | collective-permute-start | bytes 1572872 | tf_op jit(solution)/shard_map/ppermute | solution.py:46
  136.3 22.3 %collective-permute-start.7 = (bf16[512,512]{1,0:T(8,128)(2,1)S(1)}, bf16[512,512]{1,0:T(8,128)(2,1)}, u32[]{:S(2)}, u32[]{:S(2)}) collective-permute-start(bf16[512,512]{1,0:T(8,128)(2,1)S(1)} %copy-done.3), channel_id=1, source_target_pairs={{0,64},{64,0},{1,65},{65,1},{2,66},{66,2},{3,67},{67,3},{4,68},{68... | collective-permute-start | bytes 1572872 | tf_op jit(solution)/shard_map/ppermute | solution.py:46
  139.4 24.2 %all-to-all-start.4 = ((bf16[16,32,512]{2,1,0:T(8,128)(2,1)}), bf16[16,32,512]{2,1,0:T(8,128)(2,1)S(1)}, u32[]{:S(2)}, u32[]{:S(2)}) async-start(bf16[16,32,512]{2,1,0:T(8,128)(2,1)} %pad_maximum_fusion), calls=%async_computation.4 | async-start | bytes 1048576 | tf_op jit(solution)/shard_map/all_to_all | solution.py:85
  148.3 10.3 %copy-start = (bf16[4,1,128,1024]{3,2,1,0:T(8,128)(2,1)S(1)}, bf16[4,1,128,1024]{3,2,1,0:T(8,128)(2,1)}, u32[]{:S(2)}) copy-start(bf16[4,1,128,1024]{3,2,1,0:T(8,128)(2,1)} %get-tuple-element.28) | copy-start | bytes 3145732
  161.0 18.4 %copy-start.1 = (bf16[4,1,128,1024]{3,2,1,0:T(8,128)(2,1)S(1)}, bf16[4,1,128,1024]{3,2,1,0:T(8,128)(2,1)}, u32[]{:S(2)}) copy-start(bf16[4,1,128,1024]{3,2,1,0:T(8,128)(2,1)} %get-tuple-element.28) | copy-start | bytes 3145732
  161.0 18.4 %copy-start.12 = (f32[512,256]{1,0:T(8,128)S(1)}, f32[512,256]{1,0:T(8,128)}, u32[]{:S(2)}) copy-start(f32[512,256]{1,0:T(8,128)} %fusion.26) | copy-start | bytes 1572868
  163.7 17.9 %collective-permute-start.5 = (bf16[32,256]{1,0:T(8,128)(2,1)S(1)}, bf16[32,256]{1,0:T(8,128)(2,1)S(1)}, u32[]{:S(2)}, u32[]{:S(2)}) collective-permute-start(bf16[32,256]{1,0:T(8,128)(2,1)S(1)} %get-tuple-element.38), channel_id=1, source_target_pairs={{16,0},{48,1},{0,2},{32,3},{144,4},{176,5},{128,6},{160,7},{272,8}... | collective-permute-start | bytes 49160 | tf_op jit(solution)/shard_map/ppermute | solution.py:72
  176.5 16.2 %collective-permute-start.6 = (bf16[32,256]{1,0:T(8,128)(2,1)S(1)}, bf16[32,256]{1,0:T(8,128)(2,1)S(1)}, u32[]{:S(2)}, u32[]{:S(2)}) collective-permute-start(bf16[32,256]{1,0:T(8,128)(2,1)S(1)} %get-tuple-element.39), channel_id=1, source_target_pairs={{0,0},{32,1},{16,2},{48,3},{128,4},{160,5},{144,6},{176,7},{256,8}... | collective-permute-start | bytes 49160 | tf_op jit(solution)/shard_map/ppermute | solution.py:71
Sparse Core Ops, SparseCore 0:
  46.1 48.8 all-gather.1

commit v7 on v1

v7 whole, which is shorter than its diff:
```python
import jax
import jax.numpy as jnp
from jax import lax
from jax.sharding import Mesh
from jax.sharding import PartitionSpec as P

AXES = ("y", "zh", "x", "zl", "core")
ROW = ("y", "zh")
COL = ("x", "zl", "core")
PLANE = ("x", "zl")
R, C = 32, 16

SAME = [(t * C + f, (2 * f + t % 2) * C + t // 2) for t in range(R) for f in range(C)]
OTHER = [(t * C + f, (2 * f + 1 - t % 2) * C + t // 2) for t in range(R) for f in range(C)]


def inverse(pairs):
    return [(b, a) for a, b in pairs]


def contract_rows(left, right):
    return lax.dot_general(
        left, right, (((0,), (0,)), ((), ())), preferred_element_type=jnp.float32
    )


def contract_cols(left, right):
    return lax.dot_general(
        left, right, (((1,), (1,)), ((), ())), preferred_element_type=jnp.float32
    )


def swap(value):
    return lax.ppermute(value, "core", [(0, 1), (1, 0)])


def choose(flag, one, other):
    return jnp.where(flag, one, other), jnp.where(flag, other, one)


def to_features(tile, odd):
    one, two = choose(odd, tile[..., 256:], tile[..., :256])
    one = lax.ppermute(one, AXES, SAME)
    two = lax.ppermute(two, AXES, OTHER)
    second, first = choose(odd, one, two)
    return jnp.concatenate([first, second], axis=-2)


def to_tokens(piece, odd):
    one, two = choose(odd, piece[32:], piece[:32])
    one = lax.ppermute(one, AXES, inverse(SAME))
    two = lax.ppermute(two, AXES, inverse(OTHER))
    high, low = choose(odd, one, two)
    return jnp.concatenate([low, high], axis=1)


def gather_copies(block, axes, size):
    copies = jnp.broadcast_to(block[None], (size,) + block.shape)
    got = lax.all_to_all(copies, axes, 0, 0, tiled=True)
    return got.reshape((size * block.shape[0],) + block.shape[1:])


def scatter_sum(partial, axes, size):
    pieces = partial.astype(jnp.bfloat16).reshape((size, partial.shape[0] // size, partial.shape[1]))
    got = lax.all_to_all(pieces, axes, 0, 0, tiled=True)
    return jnp.sum(got.astype(jnp.float32), axis=0).astype(jnp.bfloat16)


def swiglu_back(hidden_grad, gate_pre, up_pre):
    grad_float = hidden_grad.astype(jnp.float32)
    gate_float = gate_pre.astype(jnp.float32)
    up_float = up_pre.astype(jnp.float32)
    sigmoid_gate = jax.nn.sigmoid(gate_float)
    activated = gate_float * sigmoid_gate
    gate_grad = (
        grad_float * up_float * sigmoid_gate * (1.0 + gate_float * (1.0 - sigmoid_gate))
    ).astype(jnp.bfloat16)
    up_grad = (grad_float * activated).astype(jnp.bfloat16)
    hidden = (activated * up_float).astype(jnp.bfloat16)
    return gate_grad, up_grad, hidden


def local(activations, out_grad, gate_pre, up_pre, gate_weight, up_weight, down_weight):
    odd = lax.axis_index("zh") % 2 == 1
    upper = lax.axis_index("core") == 1
    pre = gather_copies(jnp.concatenate([gate_pre, up_pre], axis=1), "zh", 4)
    tiles = to_features(jnp.stack([out_grad, activations]), odd)
    tiles, pre = lax.optimization_barrier((tiles, pre))
    mine, theirs = choose(upper, pre[64:], pre[:64])
    theirs = swap(theirs)
    pre = jnp.concatenate([mine[:, :512], theirs[:, :512], mine[:, 512:], theirs[:, 512:]], axis=1)
    pre = lax.all_gather(pre, "y", axis=0, tiled=True)
    cols = gather_copies(jnp.concatenate([tiles[0], tiles[1]], axis=1), PLANE, 8)
    grads, tokens = cols[:, :256], cols[:, 256:]
    down_both = jnp.concatenate([down_weight, swap(down_weight)], axis=0)
    gate_both = jnp.concatenate([gate_weight, swap(gate_weight)], axis=1)
    up_both = jnp.concatenate([up_weight, swap(up_weight)], axis=1)

    hidden_grad = scatter_sum(contract_cols(grads, down_both), ROW, R)
    hidden_grad, pre = lax.optimization_barrier((hidden_grad, pre))
    hidden_grad = gather_copies(hidden_grad, ROW, R)
    gate, up, hidden = swiglu_back(hidden_grad, pre[:, :1024], pre[:, 1024:])
    partial = contract_cols(gate, gate_both) + contract_cols(up, up_both)
    summed = scatter_sum(partial, PLANE, 8)
    cols_x = swap(cols)
    grads_x, tokens_x = cols_x[:, :256], cols_x[:, 256:]
    swapped = swap(jnp.concatenate([gate[:, 512:], up[:, 512:], hidden[:, 512:]], axis=1))
    summed, swapped = lax.optimization_barrier((summed, swapped))
    gate_x, up_x, hidden_x = swapped[:, :512], swapped[:, 512:1024], swapped[:, 1024:]
    input_grad = to_tokens(summed, odd)
    gate_weight_grad = contract_rows(tokens, gate[:, :512]) + contract_rows(tokens_x, gate_x)
    up_weight_grad = contract_rows(tokens, up[:, :512]) + contract_rows(tokens_x, up_x)
    down_weight_grad = contract_rows(hidden[:, :512], grads) + contract_rows(hidden_x, grads_x)
    return (
        input_grad,
        gate_weight_grad.astype(jnp.bfloat16),
        up_weight_grad.astype(jnp.bfloat16),
        down_weight_grad.astype(jnp.bfloat16),
    )


def solution(mesh):
    fine = Mesh(mesh.devices.reshape(8, 4, 4, 2, 2), AXES)
    return jax.shard_map(
        local,
        mesh=fine,
        in_specs=(P(ROW, COL),) * 6 + (P(COL, ROW),),
        out_specs=(P(ROW, COL),) * 3 + (P(COL, ROW),),
        check_vma=False,
    )
```

time: 218 us -> 204 us (0.936)
  waiting for transfers between devices: 82.2 us -> 23 us
  blocking collectives: 46 us -> 77.6 us
  starting transfers between devices: 56.3 us -> 68.4 us
    all_to_all x0 -> x1, blocking collectives: none -> 43.1 us  [scatter_sum(): got = lax.all_to_all(pieces, axes, 0, 0, tiled=True)]
    all_gather x1, waiting for transfers between devices: 33.6 us -> 0.01 us  [local(): pre = lax.all_gather(pre, 'y', axis=0, tiled=True)]
    all_to_all x2 -> x1, waiting for transfers between devices: 29.1 us -> 1.47 us  [scatter_sum(): got = lax.all_to_all(pieces, axes, 0, 0, tiled=True)]
    ppermute x4 -> x10, starting transfers between devices: 32.6 us -> 49.3 us  [the longest x6 16.6 us: swap(): return lax.ppermute(value, 'core', [(0, 1), (1, 0)])]
    all_to_all x2 -> x1, blocking collectives: 46 us -> 34.5 us  [gather_copies(): got = lax.all_to_all(copies, axes, 0, 0, tiled=True)]
    all_to_all x2 -> x1, starting transfers between devices: 12.1 us -> 4.87 us  [scatter_sum(): got = lax.all_to_all(pieces, axes, 0, 0, tiled=True)]
    all_to_all x1 -> x2, waiting for transfers between devices: 0.01 us -> 3.7 us  [gather_copies(): got = lax.all_to_all(copies, axes, 0, 0, tiled=True)]
    all_to_all x1 -> x2, starting transfers between devices: 11.6 us -> 14.3 us  [gather_copies(): got = lax.all_to_all(copies, axes, 0, 0, tiled=True)]
  transfers between devices with their start and end apart: 8 -> 14, of which waited for: 5 -> 6; matrix products, arithmetic and copies ran while one was open for 6% -> 7% of each run, Pallas kernels for 0% -> 0%
where the time goes in v7:
time: 204 us; the launch traced here: 203 us
  blocking collectives  77.6 us (38%)
  starting transfers between devices  68.4 us (34%)
  waiting for transfers between devices  23 us (11%)
  between operations  14.3 us (7%)
  matrix products  11.6 us (6%)
  other arithmetic  5.96 us (3%)
    all_to_all x1, blocking collectives, scatter_sum(): got = lax.all_to_all(pieces, axes, 0, 0, tiled=True)  43.1 us
    all_to_all x1, blocking collectives, gather_copies(): got = lax.all_to_all(copies, axes, 0, 0, tiled=True)  34.5 us
    ppermute x6, starting transfers between devices, swap(): return lax.ppermute(value, 'core', [(0, 1), (1, 0)])  16.6 us
    all_to_all x2, starting transfers between devices, gather_copies(): got = lax.all_to_all(copies, axes, 0, 0, tiled=True)  14.3 us
    ppermute x1, starting transfers between devices, to_features(): two = lax.ppermute(two, AXES, OTHER)  11.8 us
    ppermute x1, waiting for transfers between devices, to_features(): one = lax.ppermute(one, AXES, SAME)  11.5 us
    ppermute x1, starting transfers between devices, to_tokens(): two = lax.ppermute(two, AXES, inverse(OTHER))  10 us
    dot_general x6, matrix products, contract_rows(): lax.dot_general(left, right, (((0,), (0,)), ((), ())), preferred_element_...  9.44 us
  transfers between devices with their start and end apart: 14, of which 6 were waited for; matrix products, arithmetic and copies ran while one was open for 7% of the time, Pallas kernels for 0%

profile of v7, /device:TPU:5, one launch (start us, length us, event | category | flops | bytes accessed | tf_op | source)
XLA Modules:
  0.0 202.7 jit_solution(15228605928960679831)
XLA Ops:
  7.2 0.8 pad_maximum_fusion.3
  7.9 0.7 broadcast_in_dim.6
  8.7 10.0 %all-to-all-start = ((bf16[4,32,1024]{2,1,0:T(8,128)(2,1)}), bf16[4,32,1024]{2,1,0:T(8,128)(2,1)S(1)}, u32[]{:S(2)}, u32[]{:S(2)}) async-start(bf16[4,32,1024]{2,1,0:T(8,128)(2,1)} %broadcast_in_dim.6), calls=%async_computation | async-start | bytes 524288 | tf_op jit(solution)/shard_map/all_to_all | solution.py:59
  18.7 0.9 broadcast_select_fusion.5
  19.6 11.8 %collective-permute-start = (bf16[2,32,256]{2,1,0:T(8,128)(2,1)S(1)}, bf16[2,32,256]{2,1,0:T(8,128)(2,1)S(1)}, u32[]{:S(2)}, u32[]{:S(2)}) collective-permute-start(bf16[2,32,256]{2,1,0:T(8,128)(2,1)S(1)} %get-tuple-element.29), channel_id=1, source_target_pairs={{0,16},{1,48},{2,80},{3,112},{4,144},{5,176},{6,208},{7,240},{8,27... | collective-permute-start | bytes 98312 | tf_op jit(solution)/shard_map/ppermute | solution.py:44
  31.4 5.2 %collective-permute-start.1 = (bf16[2,32,256]{2,1,0:T(8,128)(2,1)S(1)}, bf16[2,32,256]{2,1,0:T(8,128)(2,1)S(1)}, u32[]{:S(2)}, u32[]{:S(2)}) collective-permute-start(bf16[2,32,256]{2,1,0:T(8,128)(2,1)S(1)} %get-tuple-element.30), channel_id=1, source_target_pairs={{0,0},{1,32},{2,64},{3,96},{4,128},{5,160},{6,192},{7,224},{8,256}... | collective-permute-start | bytes 98312 | tf_op jit(solution)/shard_map/ppermute | solution.py:43
  36.5 11.5 %collective-permute-done.1 = bf16[2,32,256]{2,1,0:T(8,128)(2,1)S(1)} collective-permute-done((bf16[2,32,256]{2,1,0:T(8,128)(2,1)S(1)}, bf16[2,32,256]{2,1,0:T(8,128)(2,1)S(1)}, u32[]{:S(2)}, u32[]{:S(2)}) %collective-permute-start.1) | collective-permute-done | bytes 32800 | tf_op jit(solution)/shard_map/ppermute | solution.py:43
  48.1 0.0 all-to-all-done
  48.2 1.9 collective-permute-start.3
  50.1 1.3 collective-permute-done.3
  51.4 0.7 pad_maximum_fusion.1
  52.1 0.0 all-gather.2.cloned.1.call-update
  52.2 0.8 broadcast_in_dim.7
  53.0 4.2 %all-to-all-start.1 = ((bf16[8,64,512]{2,1,0:T(8,128)(2,1)}), bf16[8,64,512]{2,1,0:T(8,128)(2,1)S(1)}, u32[]{:S(2)}, u32[]{:S(2)}) async-start(bf16[8,64,512]{2,1,0:T(8,128)(2,1)} %broadcast_in_dim.7), calls=%async_computation.1 | async-start | bytes 1048576 | tf_op jit(solution)/shard_map/all_to_all | solution.py:59
  57.3 2.6 %collective-permute-start.2 = (bf16[512,256]{1,0:T(8,128)(2,1)S(1)}, bf16[512,256]{1,0:T(8,128)(2,1)S(1)}, u32[]{:S(2)}, u32[]{:S(2)}) collective-permute-start(bf16[512,256]{1,0:T(8,128)(2,1)S(1)} %copy-done.2), channel_id=1, source_target_pairs={{0,1},{1,0},{2,3},{3,2},{4,5},{5,4},{6,7},{7,6},{8,9},{9,8},{10,11... | collective-permute-start | bytes 786440 | tf_op jit(solution)/shard_map/ppermute | solution.py:34
  59.9 1.1 collective-permute-done.2
  61.0 3.7 %all-to-all-done.1 = bf16[8,64,512]{2,1,0:T(8,128)(2,1)S(1)} async-done(((bf16[8,64,512]{2,1,0:T(8,128)(2,1)}), bf16[8,64,512]{2,1,0:T(8,128)(2,1)S(1)}, u32[]{:S(2)}, u32[]{:S(2)}) %all-to-all-start.1) | async-done | bytes 524320 | tf_op jit(solution)/shard_map/all_to_all | solution.py:59
  64.7 0.5 convolution_convert_fusion
  65.2 43.1 %all_to_all.25 = bf16[32,16,1024]{2,1,0:T(8,128)(2,1)S(1)} all-to-all(bf16[32,16,1024]{2,1,0:T(8,128)(2,1)S(1)} %bitcast.16), channel_id=1, replica_groups=mesh['y'=8,'zh'=4,'x'=4,'zl'=2,'core'=2] {'y','zh'}, dimensions={0} | all-to-all | bytes 2097152 | tf_op jit(solution)/shard_map/all_to_all | solution.py:65
  108.3 0.2 reduce_sum.24
  108.4 0.0 all-gather.2.cloned.1.call-done
  108.5 0.1 broadcast_in_dim.8
  108.6 34.5 %all_to_all.26 = bf16[32,16,1024]{2,1,0:T(8,128)(2,1)S(1)} all-to-all(bf16[32,16,1024]{2,1,0:T(8,128)(2,1)S(1)} %broadcast_in_dim.8), channel_id=1, replica_groups=mesh['y'=8,'zh'=4,'x'=4,'zl'=2,'core'=2] {'y','zh'}, dimensions={0} | all-to-all | bytes 2097152 | tf_op jit(solution)/shard_map/all_to_all | solution.py:59
  143.1 1.5 fusion.3
  144.7 0.0 copy-start.3
  144.7 0.0 copy-start.4
  144.7 1.3 pad_maximum_fusion
  146.0 0.1 copy-done
  146.0 5.8 %collective-permute-start.6 = (bf16[512,1536]{1,0:T(8,128)(2,1)}, bf16[512,1536]{1,0:T(8,128)(2,1)}, u32[]{:S(2)}, u32[]{:S(2)}) collective-permute-start(bf16[512,1536]{1,0:T(8,128)(2,1)} %pad_maximum_fusion), channel_id=1, source_target_pairs={{0,1},{1,0},{2,3},{3,2},{4,5},{5,4},{6,7},{7,6},{8,9},{9,8},{10,11... | collective-permute-start | bytes 4718600 | tf_op jit(solution)/shard_map/ppermute | solution.py:34
  151.8 1.9 collective-permute-start.5
  153.8 2.4 %collective-permute-start.4 = (bf16[256,512]{1,0:T(8,128)(2,1)S(1)}, bf16[256,512]{1,0:T(8,128)(2,1)S(1)}, u32[]{:S(2)}, u32[]{:S(2)}) collective-permute-start(bf16[256,512]{1,0:T(8,128)(2,1)S(1)} %copy-done.4), channel_id=1, source_target_pairs={{0,1},{1,0},{2,3},{3,2},{4,5},{5,4},{6,7},{7,6},{8,9},{9,8},{10,11... | collective-permute-start | bytes 786440 | tf_op jit(solution)/shard_map/ppermute | solution.py:34
  156.2 1.9 collective-permute-start.9
  158.1 0.0 collective-permute-done.5
  158.1 0.5 fusion.25
  158.6 0.0 collective-permute-done.4
  158.6 1.2 fusion.9
  159.8 4.9 %all-to-all-start.4 = ((bf16[8,64,256]{2,1,0:T(8,128)(2,1)}), bf16[8,64,256]{2,1,0:T(8,128)(2,1)S(1)}, u32[]{:S(2)}, u32[]{:S(2)}) async-start(bf16[8,64,256]{2,1,0:T(8,128)(2,1)} %bitcast.9), calls=%async_computation.4 | async-start | bytes 524288 | tf_op jit(solution)/shard_map/all_to_all | solution.py:65
  164.7 2.2 %fusion.13 = f32[512,256]{1,0:T(8,128)} fusion(bf16[512,1024]{1,0:T(8,128)(2,1)} %copy-done, bf16[512,512]{1,0:T(8,128)(2,1)S(1)} %bitcast.19), kind=kOutput, calls=%fused_computation.25 | convolution fusion | flops 134217728 | bytes 1310720 | tf_op jit(solution)/shard_map/dot_general | solution.py:22
  166.9 0.3 fusion.15
  167.2 0.3 fusion.17
  167.5 1.5 all-to-all-done.4
  169.0 10.0 %collective-permute-start.7 = (bf16[32,256]{1,0:T(8,128)(2,1)S(1)}, bf16[32,256]{1,0:T(8,128)(2,1)S(1)}, u32[]{:S(2)}, u32[]{:S(2)}) collective-permute-start(bf16[32,256]{1,0:T(8,128)(2,1)S(1)} %get-tuple-element.33), channel_id=1, source_target_pairs={{16,0},{48,1},{80,2},{112,3},{144,4},{176,5},{208,6},{240,7},{272,... | collective-permute-start | bytes 49160 | tf_op jit(solution)/shard_map/ppermute | solution.py:52
  179.1 5.7 %collective-permute-start.8 = (bf16[32,256]{1,0:T(8,128)(2,1)S(1)}, bf16[32,256]{1,0:T(8,128)(2,1)S(1)}, u32[]{:S(2)}, u32[]{:S(2)}) collective-permute-start(bf16[32,256]{1,0:T(8,128)(2,1)S(1)} %get-tuple-element.34), channel_id=1, source_target_pairs={{0,0},{32,1},{64,2},{96,3},{128,4},{160,5},{192,6},{224,7},{256,8}... | collective-permute-start | bytes 49160 | tf_op jit(solution)/shard_map/ppermute | solution.py:51
  184.8 2.3 %fusion.12 = bf16[512,256]{1,0:T(8,128)(2,1)} fusion(f32[512,256]{1,0:T(8,128)} %fusion.13, bf16[512,1536]{1,0:T(8,128)(2,1)} %collective-permute-done.6, bf16[512,512]{1,0:T(8,128)(2,1)} %collective-permute-done.9), kind=kOutput, calls=%fused_computation.24 | convolution fusion | flops 134479872 | bytes 1572864 | tf_op jit(solution)/shard_map/dot_general | solution.py:22
  187.1 2.1 %fusion.11 = bf16[256,512]{1,0:T(8,128)(2,1)} fusion(f32[256,512]{1,0:T(8,128)S(1)} %fusion.15, bf16[512,1536]{1,0:T(8,128)(2,1)} %collective-permute-done.6, bf16[512,512]{1,0:T(8,128)(2,1)} %collective-permute-done.9), kind=kOutput, calls=%fused_computation.23 | convolution fusion | flops 134479872 | bytes 1572864 | tf_op jit(solution)/shard_map/dot_general | solution.py:22
  189.3 2.1 %fusion.10 = bf16[256,512]{1,0:T(8,128)(2,1)} fusion(f32[256,512]{1,0:T(8,128)S(1)} %fusion.17, bf16[512,1536]{1,0:T(8,128)(2,1)} %collective-permute-done.6, bf16[512,512]{1,0:T(8,128)(2,1)} %collective-permute-done.9), kind=kOutput, calls=%fused_computation.22 | convolution fusion | flops 134479872 | bytes 1572864 | tf_op jit(solution)/shard_map/dot_general | solution.py:22
  191.4 3.8 %collective-permute-done.8 = bf16[32,256]{1,0:T(8,128)(2,1)S(1)} collective-permute-done((bf16[32,256]{1,0:T(8,128)(2,1)S(1)}, bf16[32,256]{1,0:T(8,128)(2,1)S(1)}, u32[]{:S(2)}, u32[]{:S(2)}) %collective-permute-start.8) | collective-permute-done | bytes 16416 | tf_op jit(solution)/shard_map/ppermute | solution.py:51
  195.3 0.6 pad_maximum_fusion.6
  (25 shorter events, 0.3 us)
Async XLA Ops:
  8.7 39.4 %all-to-all-start = ((bf16[4,32,1024]{2,1,0:T(8,128)(2,1)}), bf16[4,32,1024]{2,1,0:T(8,128)(2,1)S(1)}, u32[]{:S(2)}, u32[]{:S(2)}) async-start(bf16[4,32,1024]{2,1,0:T(8,128)(2,1)} %broadcast_in_dim.6), calls=%async_computation | async-start | bytes 524288 | tf_op jit(solution)/shard_map/all_to_all | solution.py:59
  18.7 89.8 %all-gather.2.cloned.1.call-start = ((), (), s32[]{:S(2)}) async-start(), calls=%async_computation.5 | async-start | bytes 2359296 | tf_op jit(solution)/shard_map/all_gather | solution.py:92
  18.7 38.6 %copy-start.2 = (bf16[512,256]{1,0:T(8,128)(2,1)S(1)}, bf16[512,256]{1,0:T(8,128)(2,1)}, u32[]{:S(2)}) copy-start(bf16[512,256]{1,0:T(8,128)(2,1)} %param.13) | copy-start | bytes 786436
  19.6 17.0 %collective-permute-start = (bf16[2,32,256]{2,1,0:T(8,128)(2,1)S(1)}, bf16[2,32,256]{2,1,0:T(8,128)(2,1)S(1)}, u32[]{:S(2)}, u32[]{:S(2)}) collective-permute-start(bf16[2,32,256]{2,1,0:T(8,128)(2,1)S(1)} %get-tuple-element.29), channel_id=1, source_target_pairs={{0,16},{1,48},{2,80},{3,112},{4,144},{5,176},{6,208},{7,240},{8,27... | collective-permute-start | bytes 98312 | tf_op jit(solution)/shard_map/ppermute | solution.py:44
  31.4 16.7 %collective-permute-start.1 = (bf16[2,32,256]{2,1,0:T(8,128)(2,1)S(1)}, bf16[2,32,256]{2,1,0:T(8,128)(2,1)S(1)}, u32[]{:S(2)}, u32[]{:S(2)}) collective-permute-start(bf16[2,32,256]{2,1,0:T(8,128)(2,1)S(1)} %get-tuple-element.30), channel_id=1, source_target_pairs={{0,0},{1,32},{2,64},{3,96},{4,128},{5,160},{6,192},{7,224},{8,256}... | collective-permute-start | bytes 98312 | tf_op jit(solution)/shard_map/ppermute | solution.py:43
  48.2 3.2 %collective-permute-start.3 = (bf16[64,1024]{1,0:T(8,128)(2,1)S(1)}, bf16[64,1024]{1,0:T(8,128)(2,1)S(1)}, u32[]{:S(2)}, u32[]{:S(2)}) collective-permute-start(bf16[64,1024]{1,0:T(8,128)(2,1)S(1)} %get-tuple-element.20), channel_id=1, source_target_pairs={{0,1},{1,0},{2,3},{3,2},{4,5},{5,4},{6,7},{7,6},{8,9},{9,8},{10,11... | collective-permute-start | bytes 393224 | tf_op jit(solution)/shard_map/ppermute | solution.py:34
  53.0 11.7 %all-to-all-start.1 = ((bf16[8,64,512]{2,1,0:T(8,128)(2,1)}), bf16[8,64,512]{2,1,0:T(8,128)(2,1)S(1)}, u32[]{:S(2)}, u32[]{:S(2)}) async-start(bf16[8,64,512]{2,1,0:T(8,128)(2,1)} %broadcast_in_dim.7), calls=%async_computation.1 | async-start | bytes 1048576 | tf_op jit(solution)/shard_map/all_to_all | solution.py:59
  57.3 3.8 %collective-permute-start.2 = (bf16[512,256]{1,0:T(8,128)(2,1)S(1)}, bf16[512,256]{1,0:T(8,128)(2,1)S(1)}, u32[]{:S(2)}, u32[]{:S(2)}) collective-permute-start(bf16[512,256]{1,0:T(8,128)(2,1)S(1)} %copy-done.2), channel_id=1, source_target_pairs={{0,1},{1,0},{2,3},{3,2},{4,5},{5,4},{6,7},{7,6},{8,9},{9,8},{10,11... | collective-permute-start | bytes 786440 | tf_op jit(solution)/shard_map/ppermute | solution.py:34
  108.5 34.6 %copy-start.1 = (bf16[512,2048]{1,0:T(8,128)(2,1)S(1)}, bf16[512,2048]{1,0:T(8,128)(2,1)}, u32[]{:S(2)}) copy-start(bf16[512,2048]{1,0:T(8,128)(2,1)} %all-gather.2.cloned.1.call-done) | copy-start | bytes 6291460
  144.6 1.5 copy-start
  144.7 7.2 %copy-start.3 = (bf16[256,512]{1,0:T(8,128)(2,1)S(1)}, bf16[256,512]{1,0:T(8,128)(2,1)}, u32[]{:S(2)}) copy-start(bf16[256,512]{1,0:T(8,128)(2,1)} %param.12) | copy-start | bytes 786436
  144.7 9.1 %copy-start.4 = (bf16[256,512]{1,0:T(8,128)(2,1)S(1)}, bf16[256,512]{1,0:T(8,128)(2,1)}, u32[]{:S(2)}) copy-start(bf16[256,512]{1,0:T(8,128)(2,1)} %param.11) | copy-start | bytes 786436
  146.0 23.0 %collective-permute-start.6 = (bf16[512,1536]{1,0:T(8,128)(2,1)}, bf16[512,1536]{1,0:T(8,128)(2,1)}, u32[]{:S(2)}, u32[]{:S(2)}) collective-permute-start(bf16[512,1536]{1,0:T(8,128)(2,1)} %pad_maximum_fusion), channel_id=1, source_target_pairs={{0,1},{1,0},{2,3},{3,2},{4,5},{5,4},{6,7},{7,6},{8,9},{9,8},{10,11... | collective-permute-start | bytes 4718600 | tf_op jit(solution)/shard_map/ppermute | solution.py:34
  151.8 6.3 %collective-permute-start.5 = (bf16[256,512]{1,0:T(8,128)(2,1)S(1)}, bf16[256,512]{1,0:T(8,128)(2,1)S(1)}, u32[]{:S(2)}, u32[]{:S(2)}) collective-permute-start(bf16[256,512]{1,0:T(8,128)(2,1)S(1)} %copy-done.3), channel_id=1, source_target_pairs={{0,1},{1,0},{2,3},{3,2},{4,5},{5,4},{6,7},{7,6},{8,9},{9,8},{10,11... | collective-permute-start | bytes 786440 | tf_op jit(solution)/shard_map/ppermute | solution.py:34
  153.8 4.8 %collective-permute-start.4 = (bf16[256,512]{1,0:T(8,128)(2,1)S(1)}, bf16[256,512]{1,0:T(8,128)(2,1)S(1)}, u32[]{:S(2)}, u32[]{:S(2)}) collective-permute-start(bf16[256,512]{1,0:T(8,128)(2,1)S(1)} %copy-done.4), channel_id=1, source_target_pairs={{0,1},{1,0},{2,3},{3,2},{4,5},{5,4},{6,7},{7,6},{8,9},{9,8},{10,11... | collective-permute-start | bytes 786440 | tf_op jit(solution)/shard_map/ppermute | solution.py:34
  156.2 28.6 %collective-permute-start.9 = (bf16[512,512]{1,0:T(8,128)(2,1)S(1)}, bf16[512,512]{1,0:T(8,128)(2,1)}, u32[]{:S(2)}, u32[]{:S(2)}) collective-permute-start(bf16[512,512]{1,0:T(8,128)(2,1)S(1)} %bitcast.18), channel_id=1, source_target_pairs={{0,1},{1,0},{2,3},{3,2},{4,5},{5,4},{6,7},{7,6},{8,9},{9,8},{10,11... | collective-permute-start | bytes 1572872 | tf_op jit(solution)/shard_map/ppermute | solution.py:34
  159.8 9.2 %all-to-all-start.4 = ((bf16[8,64,256]{2,1,0:T(8,128)(2,1)}), bf16[8,64,256]{2,1,0:T(8,128)(2,1)S(1)}, u32[]{:S(2)}, u32[]{:S(2)}) async-start(bf16[8,64,256]{2,1,0:T(8,128)(2,1)} %bitcast.9), calls=%async_computation.4 | async-start | bytes 524288 | tf_op jit(solution)/shard_map/all_to_all | solution.py:65
  169.0 22.4 %collective-permute-start.7 = (bf16[32,256]{1,0:T(8,128)(2,1)S(1)}, bf16[32,256]{1,0:T(8,128)(2,1)S(1)}, u32[]{:S(2)}, u32[]{:S(2)}) collective-permute-start(bf16[32,256]{1,0:T(8,128)(2,1)S(1)} %get-tuple-element.33), channel_id=1, source_target_pairs={{16,0},{48,1},{80,2},{112,3},{144,4},{176,5},{208,6},{240,7},{272,... | collective-permute-start | bytes 49160 | tf_op jit(solution)/shard_map/ppermute | solution.py:52
  179.1 16.2 %collective-permute-start.8 = (bf16[32,256]{1,0:T(8,128)(2,1)S(1)}, bf16[32,256]{1,0:T(8,128)(2,1)S(1)}, u32[]{:S(2)}, u32[]{:S(2)}) collective-permute-start(bf16[32,256]{1,0:T(8,128)(2,1)S(1)} %get-tuple-element.34), channel_id=1, source_target_pairs={{0,0},{32,1},{64,2},{96,3},{128,4},{160,5},{192,6},{224,7},{256,8}... | collective-permute-start | bytes 49160 | tf_op jit(solution)/shard_map/ppermute | solution.py:51
Sparse Core Ops, SparseCore 0:
  52.3 52.3 all-gather.1

commit v8 on v7

v8 whole, which is shorter than its diff:
```python
import jax
import jax.numpy as jnp
from jax import lax
from jax.sharding import Mesh
from jax.sharding import PartitionSpec as P

AXES = ("yh", "yl", "zh", "x", "zl", "core")
ROW = ("yh", "yl", "zh")
ORDER = ("yl", "yh", "zh")
HALF = ("yh", "zh")
COL = ("x", "zl", "core")
PLANE = ("x", "zl")
R, C = 32, 16
TILES = [(t, t // 8, t // 4 % 2, t % 4) for t in range(R)]


def turn_in(half_of):
    return [
        (
            t * C + f,
            (f // 4 * 8 + yl * 4 + f % 2 * 2 + half_of(f // 2 % 2)) * C + yh * 4 + zh % 2 * 2 + zh // 2,
        )
        for t, yh, yl, zh in TILES
        for f in range(C)
    ]


def turn_out(half_of):
    return [
        ((2 * f + half_of(zh % 2)) * C + (yl * 2 + yh // 2) * 4 + yh % 2 * 2 + zh // 2, t * C + f)
        for t, yh, yl, zh in TILES
        for f in range(C)
    ]


IN_ONE, IN_TWO = turn_in(lambda b: b), turn_in(lambda b: 1 - b)
OUT_ONE, OUT_TWO = turn_out(lambda b: b), turn_out(lambda b: 1 - b)


def contract_rows(left, right):
    return lax.dot_general(
        left, right, (((0,), (0,)), ((), ())), preferred_element_type=jnp.float32
    )


def contract_cols(left, right):
    return lax.dot_general(
        left, right, (((1,), (1,)), ((), ())), preferred_element_type=jnp.float32
    )


def swap(value, axis="core"):
    return lax.ppermute(value, axis, [(0, 1), (1, 0)])


def choose(flag, one, other):
    return jnp.where(flag, one, other), jnp.where(flag, other, one)


def to_features(tile, upper, mine):
    one, two = choose(upper, tile[..., 256:], tile[..., :256])
    return choose(mine, lax.ppermute(one, AXES, IN_ONE), lax.ppermute(two, AXES, IN_TWO))


def to_tokens(piece, odd):
    one, two = choose(odd, piece[32:], piece[:32])
    high, low = choose(odd, lax.ppermute(one, AXES, OUT_ONE), lax.ppermute(two, AXES, OUT_TWO))
    return jnp.concatenate([low, high], axis=1)


def gather_copies(block, axes, size):
    copies = jnp.broadcast_to(block[None], (size,) + block.shape)
    got = lax.all_to_all(copies, axes, 0, 0, tiled=True)
    return got.reshape((size * block.shape[0],) + block.shape[1:])


def scatter_sum(partial, axes, size):
    pieces = partial.astype(jnp.bfloat16).reshape((size, partial.shape[0] // size, partial.shape[1]))
    got = lax.all_to_all(pieces, axes, 0, 0, tiled=True)
    return jnp.sum(got.astype(jnp.float32), axis=0).astype(jnp.bfloat16)


def swiglu_back(hidden_grad, gate_pre, up_pre):
    grad_float = hidden_grad.astype(jnp.float32)
    gate_float = gate_pre.astype(jnp.float32)
    up_float = up_pre.astype(jnp.float32)
    sigmoid_gate = jax.nn.sigmoid(gate_float)
    activated = gate_float * sigmoid_gate
    gate_grad = (
        grad_float * up_float * sigmoid_gate * (1.0 + gate_float * (1.0 - sigmoid_gate))
    ).astype(jnp.bfloat16)
    up_grad = (grad_float * activated).astype(jnp.bfloat16)
    hidden = (activated * up_float).astype(jnp.bfloat16)
    return gate_grad, up_grad, hidden


def local(activations, out_grad, gate_pre, up_pre, gate_weight, up_weight, down_weight):
    yl, zh, core = lax.axis_index("yl"), lax.axis_index("zh"), lax.axis_index("core")
    upper, mine, odd = lax.axis_index("zl") == 1, zh % 2 == yl, zh % 2 == 1
    pre = gather_copies(jnp.concatenate([gate_pre, up_pre], axis=1), "zh", 4)
    tiles = to_features(jnp.stack([out_grad, activations]), upper, mine)
    (own, other), pre, down_y = lax.optimization_barrier((tiles, pre, swap(down_weight, "yl")))
    pre = lax.all_gather(pre, ("yl", "yh"), axis=0, tiled=True)
    cols = gather_copies(jnp.concatenate([own[0], other[0], other[1], own[1]], axis=1), PLANE, 8)
    down = jnp.concatenate([down_weight, down_y], axis=1)
    down = jnp.concatenate([down, swap(down)], axis=0)
    partial = contract_cols(cols[:, :512], down).astype(jnp.bfloat16)
    hidden_grad = scatter_sum(partial, HALF, C)
    hidden_grad, pre, cols = lax.optimization_barrier((hidden_grad, pre, cols))

    hidden_grad = gather_copies(hidden_grad, ORDER, R)
    pre_mine, pre_theirs = choose(core == 1, *(pre.reshape(8, 2, 64, 1024)[:, at] for at in (1, 0)))
    pre_mine, pre_theirs = pre_mine.reshape(512, 1024), swap(pre_theirs.reshape(512, 1024))
    cols_y = swap(cols[:, 256:768], "yl")
    cols_own = jnp.concatenate([cols[:, :256], cols[:, 768:]], axis=1)
    cols = jnp.where(
        yl == 0,
        jnp.concatenate([cols_own, cols_y], axis=0),
        jnp.concatenate([cols_y, cols_own], axis=0),
    )
    hidden_grad, pre_mine, pre_theirs, gate_other, up_other, cols, cols_x = lax.optimization_barrier(
        (hidden_grad, pre_mine, pre_theirs, swap(gate_weight), swap(up_weight), cols, swap(cols))
    )
    gate, up, hidden = swiglu_back(hidden_grad[:, :512], pre_mine[:, :512], pre_mine[:, 512:])
    gate_y, up_y, hidden_y = swiglu_back(hidden_grad[:, 512:], pre_theirs[:, :512], pre_theirs[:, 512:])
    partial = contract_cols(gate, gate_weight) + contract_cols(up, up_weight)
    partial = partial + contract_cols(gate_y, gate_other) + contract_cols(up_y, up_other)
    summed = scatter_sum(partial, PLANE, 8)

    grads, tokens = cols[:, :256], cols[:, 256:]
    grads_x, tokens_x = cols_x[:, :256], cols_x[:, 256:]
    swapped = swap(jnp.concatenate([gate_y, up_y, hidden_y], axis=1))
    summed, swapped = lax.optimization_barrier((summed, swapped))
    gate_x, up_x, hidden_x = swapped[:, :512], swapped[:, 512:1024], swapped[:, 1024:]
    input_grad = to_tokens(summed, odd)
    gate_weight_grad = contract_rows(tokens, gate) + contract_rows(tokens_x, gate_x)
    up_weight_grad = contract_rows(tokens, up) + contract_rows(tokens_x, up_x)
    down_weight_grad = contract_rows(hidden, grads) + contract_rows(hidden_x, grads_x)
    return (
        input_grad,
        gate_weight_grad.astype(jnp.bfloat16),
        up_weight_grad.astype(jnp.bfloat16),
        down_weight_grad.astype(jnp.bfloat16),
    )


def solution(mesh):
    fine = Mesh(mesh.devices.reshape(4, 2, 4, 4, 2, 2), AXES)
    return jax.shard_map(
        local,
        mesh=fine,
        in_specs=(P(ROW, COL),) * 6 + (P(COL, ROW),),
        out_specs=(P(ROW, COL),) * 3 + (P(COL, ROW),),
        check_vma=False,
    )
```

time: 204 us -> 223 us (1.093)
  the two profiles are of different devices: /device:TPU:5 before, /device:TPU:7 now
where the time goes in v8:
time: 223 us; the launch traced here: 222 us
  starting transfers between devices  88.1 us (40%)
  waiting for transfers between devices  58.9 us (26%)
  blocking collectives  36.3 us (16%)
  between operations  14.4 us (6%)
  matrix products  10.5 us (5%)
  other arithmetic  8.81 us (4%)
  local copies, waits for them, and re-layouts  4.82 us (2%)
    all_to_all x1, blocking collectives, scatter_sum(): got = lax.all_to_all(pieces, axes, 0, 0, tiled=True)  36.3 us
    all_to_all x3, starting transfers between devices, gather_copies(): got = lax.all_to_all(copies, axes, 0, 0, tiled=True)  29.3 us
    ppermute x8, starting transfers between devices, swap(): return lax.ppermute(value, axis, [(0, 1), (1, 0)])  23.7 us
    ppermute x8, waiting for transfers between devices, swap(): return lax.ppermute(value, axis, [(0, 1), (1, 0)])  21.4 us
    all_gather x1, waiting for transfers between devices, local(): pre = lax.all_gather(pre, ('yl', 'yh'), axis=0, tiled=True)  14.7 us
    ppermute x1, starting transfers between devices, to_tokens(): lax.ppermute(two, AXES, OUT_TWO)  12.1 us
    ppermute x1, starting transfers between devices, to_features(): lax.ppermute(two, AXES, IN_TWO)  9.59 us
    ppermute x1, waiting for transfers between devices, to_features(): lax.ppermute(one, AXES, IN_ONE)  9.39 us
  transfers between devices with their start and end apart: 17, of which 8 were waited for; matrix products, arithmetic and copies ran while one was open for 5% of the time, Pallas kernels for 0%

profile of v8, /device:TPU:7, one launch (start us, length us, event | category | flops | bytes accessed | tf_op | source)
XLA Modules:
  0.0 221.9 jit_solution(872712445100684147)
XLA Ops:
  7.2 0.8 pad_maximum_fusion.1
  7.9 0.7 broadcast_in_dim.6
  8.7 10.1 %all-to-all-start = ((bf16[4,32,1024]{2,1,0:T(8,128)(2,1)}), bf16[4,32,1024]{2,1,0:T(8,128)(2,1)S(1)}, u32[]{:S(2)}, u32[]{:S(2)}) async-start(bf16[4,32,1024]{2,1,0:T(8,128)(2,1)} %broadcast_in_dim.6), calls=%async_computation | async-start | bytes 524288 | tf_op jit(solution)/shard_map/all_to_all | solution.py:73
  18.8 3.2 %collective-permute-start.2 = (bf16[512,256]{1,0:T(8,128)(2,1)}, bf16[512,256]{1,0:T(8,128)(2,1)S(1)}, u32[]{:S(2)}, u32[]{:S(2)}) collective-permute-start(bf16[512,256]{1,0:T(8,128)(2,1)} %param.13), channel_id=1, source_target_pairs={{0,64},{64,0},{1,65},{65,1},{2,66},{66,2},{3,67},{67,3},{4,68},{68... | collective-permute-start | bytes 786440 | tf_op jit(solution)/shard_map/ppermute | solution.py:53
  22.0 0.8 broadcast_select_fusion.2
  22.9 9.6 %collective-permute-start.1 = (bf16[2,32,256]{2,1,0:T(8,128)(2,1)S(1)}, bf16[2,32,256]{2,1,0:T(8,128)(2,1)S(1)}, u32[]{:S(2)}, u32[]{:S(2)}) collective-permute-start(bf16[2,32,256]{2,1,0:T(8,128)(2,1)S(1)} %get-tuple-element.46), channel_id=1, source_target_pairs={{0,16},{1,48},{2,0},{3,32},{4,144},{5,176},{6,128},{7,160},{8,272}... | collective-permute-start | bytes 98312 | tf_op jit(solution)/shard_map/ppermute | solution.py:62
  32.5 5.3 %collective-permute-start = (bf16[2,32,256]{2,1,0:T(8,128)(2,1)S(1)}, bf16[2,32,256]{2,1,0:T(8,128)(2,1)S(1)}, u32[]{:S(2)}, u32[]{:S(2)}) collective-permute-start(bf16[2,32,256]{2,1,0:T(8,128)(2,1)S(1)} %get-tuple-element.47), channel_id=1, source_target_pairs={{0,0},{1,32},{2,16},{3,48},{4,128},{5,160},{6,144},{7,176},{8,256}... | collective-permute-start | bytes 98312 | tf_op jit(solution)/shard_map/ppermute | solution.py:62
  37.8 9.4 %collective-permute-done = bf16[2,32,256]{2,1,0:T(8,128)(2,1)S(1)} collective-permute-done((bf16[2,32,256]{2,1,0:T(8,128)(2,1)S(1)}, bf16[2,32,256]{2,1,0:T(8,128)(2,1)S(1)}, u32[]{:S(2)}, u32[]{:S(2)}) %collective-permute-start) | collective-permute-done | bytes 32800 | tf_op jit(solution)/shard_map/ppermute | solution.py:62
  47.2 0.7 copy-done
  48.0 0.9 broadcast_in_dim.7
  48.8 8.7 %all-to-all-start.1 = ((bf16[8,32,1024]{2,1,0:T(8,128)(2,1)}), bf16[8,32,1024]{2,1,0:T(8,128)(2,1)S(1)}, u32[]{:S(2)}, u32[]{:S(2)}) async-start(bf16[8,32,1024]{2,1,0:T(8,128)(2,1)} %broadcast_in_dim.7), calls=%async_computation.1 | async-start | bytes 1048576 | tf_op jit(solution)/shard_map/all_to_all | solution.py:73
  57.6 1.9 collective-permute-start.3
  59.5 1.9 collective-permute-done.3
  61.4 1.6 all-to-all-done.1
  63.0 0.5 convolution_convert_fusion
  63.4 36.3 %all_to_all.25 = bf16[16,16,1024]{2,1,0:T(8,128)(2,1)S(1)} all-to-all(bf16[16,16,1024]{2,1,0:T(8,128)(2,1)S(1)} %bitcast.39), channel_id=1, replica_groups=mesh['yh'=4,'yl'=2,'zh'=4,'x'=4,'zl'=2,'core'=2] {'yh','zh'}, dimensions={0} | all-to-all | bytes 1048576 | tf_op jit(solution)/shard_map/all_to_all | solution.py:79
  99.8 14.7 %all-gather.2.cloned.1.call-done = bf16[1024,1024]{1,0:T(8,128)(2,1)} async-done(((bf16[128,1024]{1,0:T(8,128)(2,1)}), bf16[1024,1024]{1,0:T(8,128)(2,1)}) %all-gather.2.cloned.1.call-update) | async-done | bytes 2097168 | tf_op jit(solution)/shard_map/all_gather | solution.py:103
  114.5 1.1 broadcast_in_dim.8
  115.6 10.5 %all-to-all-start.3 = ((bf16[32,16,1024]{2,1,0:T(8,128)(2,1)}), bf16[32,16,1024]{2,1,0:T(8,128)(2,1)S(1)}, u32[]{:S(2)}, u32[]{:S(2)}) async-start(bf16[32,16,1024]{2,1,0:T(8,128)(2,1)} %broadcast_in_dim.8), calls=%async_computation.3 | async-start | bytes 2097152 | tf_op jit(solution)/shard_map/all_to_all | solution.py:73
  126.1 2.7 %broadcast_select_fusion = (bf16[8,1,64,1024]{3,2,1,0:T(8,128)(2,1)}, bf16[8,1,64,1024]{3,2,1,0:T(8,128)(2,1)S(1)}) fusion(pred[]{:T(512)S(6)} %eq.21, bf16[8,2,64,1024]{3,2,1,0:T(8,128)(2,1)} %bitcast.33), kind=kLoop, calls=%fused_computation.45 | loop fusion | flops 1048576 | bytes 4194305 | tf_op jit(solution)/shard_map/jit(_where)/select_n | solution.py:57
  128.8 4.4 %collective-permute-start.4 = (bf16[512,1024]{1,0:T(8,128)(2,1)}, bf16[512,1024]{1,0:T(8,128)(2,1)}, u32[]{:S(2)}, u32[]{:S(2)}) collective-permute-start(bf16[512,1024]{1,0:T(8,128)(2,1)} %bitcast.12), channel_id=1, source_target_pairs={{0,1},{1,0},{2,3},{3,2},{4,5},{5,4},{6,7},{7,6},{8,9},{9,8},{10,11... | collective-permute-start | bytes 3145736 | tf_op jit(solution)/shard_map/ppermute | solution.py:53
  133.1 3.4 %collective-permute-start.7 = (bf16[256,512]{1,0:T(8,128)(2,1)S(1)}, bf16[256,512]{1,0:T(8,128)(2,1)S(1)}, u32[]{:S(2)}, u32[]{:S(2)}) collective-permute-start(bf16[256,512]{1,0:T(8,128)(2,1)S(1)} %slice.92), channel_id=1, source_target_pairs={{0,64},{64,0},{1,65},{65,1},{2,66},{66,2},{3,67},{67,3},{4,68},{68... | collective-permute-start | bytes 786440 | tf_op jit(solution)/shard_map/ppermute | solution.py:53
  136.6 18.4 %collective-permute-done.7 = bf16[256,512]{1,0:T(8,128)(2,1)S(1)} collective-permute-done((bf16[256,512]{1,0:T(8,128)(2,1)S(1)}, bf16[256,512]{1,0:T(8,128)(2,1)S(1)}, u32[]{:S(2)}, u32[]{:S(2)}) %collective-permute-start.7) | collective-permute-done | bytes 262176 | tf_op jit(solution)/shard_map/ppermute | solution.py:53
  155.2 4.0 %collective-permute-start.8 = (bf16[512,512]{1,0:T(8,128)(2,1)S(1)}, bf16[512,512]{1,0:T(8,128)(2,1)S(1)}, u32[]{:S(2)}, u32[]{:S(2)}) collective-permute-start(bf16[512,512]{1,0:T(8,128)(2,1)S(1)} %maximum_select_fusion), channel_id=1, source_target_pairs={{0,1},{1,0},{2,3},{3,2},{4,5},{5,4},{6,7},{7,6},{8,9},{9,8},{10,11... | collective-permute-start | bytes 1572872 | tf_op jit(solution)/shard_map/ppermute | solution.py:53
  159.3 1.9 collective-permute-start.5
  161.2 2.4 %collective-permute-start.6 = (bf16[256,512]{1,0:T(8,128)(2,1)S(1)}, bf16[256,512]{1,0:T(8,128)(2,1)S(1)}, u32[]{:S(2)}, u32[]{:S(2)}) collective-permute-start(bf16[256,512]{1,0:T(8,128)(2,1)S(1)} %copy-done.9), channel_id=1, source_target_pairs={{0,1},{1,0},{2,3},{3,2},{4,5},{5,4},{6,7},{7,6},{8,9},{9,8},{10,11... | collective-permute-start | bytes 786440 | tf_op jit(solution)/shard_map/ppermute | solution.py:53
  163.7 1.1 collective-permute-done.6
  164.8 0.8 copy-done.1
  165.6 2.3 %fusion.13 = (bf16[512,512]{1,0:T(8,128)(2,1)S(1)}, bf16[512,512]{1,0:T(8,128)(2,1)S(1)}, bf16[512,512]{1,0:T(8,128)(2,1)S(1)}, bf16[512,512]{1,0:T(8,128)(2,1)S(1)}) fusion(bf16[512,1024]{1,0:T(8,128)(2,1)} %collective-permute-done.4, bf16[512,1024]{1,0:T(8,128)(2,1)S(1)} %bitcast.30, bf16[512,1024]{1,0:T(8,128)(2,1)S(1)} %bitcast.26), kind=kLoop, calls=%fused_computation.32 | loop fusion | flops 8126464 | bytes 5242880 | tf_op jit(solution)/shard_map/convert_element_type | solution.py:91
  168.0 1.2 pad_maximum_fusion
  169.2 2.4 %collective-permute-start.9 = (bf16[512,1536]{1,0:T(8,128)(2,1)}, bf16[512,1536]{1,0:T(8,128)(2,1)}, u32[]{:S(2)}, u32[]{:S(2)}) collective-permute-start(bf16[512,1536]{1,0:T(8,128)(2,1)} %pad_maximum_fusion), channel_id=1, source_target_pairs={{0,1},{1,0},{2,3},{3,2},{4,5},{5,4},{6,7},{7,6},{8,9},{9,8},{10,11... | collective-permute-start | bytes 4718600 | tf_op jit(solution)/shard_map/ppermute | solution.py:53
  171.6 0.3 fusion.48
  172.0 0.3 fusion.47
  172.3 0.5 convolution_add_fusion.4
  172.8 0.4 copy-done.8
  173.3 1.0 fusion.1
  174.3 4.5 %all-to-all-start.4 = ((bf16[8,64,256]{2,1,0:T(8,128)(2,1)}), bf16[8,64,256]{2,1,0:T(8,128)(2,1)S(1)}, u32[]{:S(2)}, u32[]{:S(2)}) async-start(bf16[8,64,256]{2,1,0:T(8,128)(2,1)} %bitcast.38), calls=%async_computation.4 | async-start | bytes 524288 | tf_op jit(solution)/shard_map/all_to_all | solution.py:79
  178.8 4.9 %all-to-all-done.4 = bf16[8,64,256]{2,1,0:T(8,128)(2,1)S(1)} async-done(((bf16[8,64,256]{2,1,0:T(8,128)(2,1)}), bf16[8,64,256]{2,1,0:T(8,128)(2,1)S(1)}, u32[]{:S(2)}, u32[]{:S(2)}) %all-to-all-start.4) | async-done | bytes 262176 | tf_op jit(solution)/shard_map/all_to_all | solution.py:79
  183.7 1.5 fusion.31
  185.2 1.4 fusion.29
  186.7 1.4 fusion.27
  188.1 12.1 %collective-permute-start.10 = (bf16[32,256]{1,0:T(8,128)(2,1)S(1)}, bf16[32,256]{1,0:T(8,128)(2,1)S(1)}, u32[]{:S(2)}, u32[]{:S(2)}) collective-permute-start(bf16[32,256]{1,0:T(8,128)(2,1)S(1)} %get-tuple-element.50), channel_id=1, source_target_pairs={{16,0},{48,1},{80,2},{112,3},{144,4},{176,5},{208,6},{240,7},{272,... | collective-permute-start | bytes 49160 | tf_op jit(solution)/shard_map/ppermute | solution.py:67
  200.2 3.7 %collective-permute-start.11 = (bf16[32,256]{1,0:T(8,128)(2,1)S(1)}, bf16[32,256]{1,0:T(8,128)(2,1)S(1)}, u32[]{:S(2)}, u32[]{:S(2)}) collective-permute-start(bf16[32,256]{1,0:T(8,128)(2,1)S(1)} %get-tuple-element.51), channel_id=1, source_target_pairs={{0,0},{32,1},{64,2},{96,3},{128,4},{160,5},{192,6},{224,7},{256,8}... | collective-permute-start | bytes 49160 | tf_op jit(solution)/shard_map/ppermute | solution.py:67
  203.9 1.2 fusion.3
  205.1 1.3 fusion.4
  206.4 1.0 fusion.2
  207.4 7.0 %collective-permute-done.11 = bf16[32,256]{1,0:T(8,128)(2,1)S(1)} collective-permute-done((bf16[32,256]{1,0:T(8,128)(2,1)S(1)}, bf16[32,256]{1,0:T(8,128)(2,1)S(1)}, u32[]{:S(2)}, u32[]{:S(2)}) %collective-permute-start.11) | collective-permute-done | bytes 16416 | tf_op jit(solution)/shard_map/ppermute | solution.py:67
  214.4 0.6 pad_maximum_fusion.4
  (42 shorter events, 0.6 us)
Async XLA Ops:
  8.7 48.9 %copy-start.6 = (bf16[512,256]{1,0:T(8,128)(2,1)S(1)}, bf16[512,256]{1,0:T(8,128)(2,1)}, u32[]{:S(2)}) copy-start(bf16[512,256]{1,0:T(8,128)(2,1)} %param.13) | copy-start | bytes 786436
  8.7 38.5 %all-to-all-start = ((bf16[4,32,1024]{2,1,0:T(8,128)(2,1)}), bf16[4,32,1024]{2,1,0:T(8,128)(2,1)S(1)}, u32[]{:S(2)}, u32[]{:S(2)}) async-start(bf16[4,32,1024]{2,1,0:T(8,128)(2,1)} %broadcast_in_dim.6), calls=%async_computation | async-start | bytes 524288 | tf_op jit(solution)/shard_map/all_to_all | solution.py:73
  18.8 95.7 %all-gather.2.cloned.1.call-start = ((), (), s32[]{:S(2)}) async-start(), calls=%async_computation.5 | async-start | bytes 2359296 | tf_op jit(solution)/shard_map/all_gather | solution.py:103
  18.8 28.3 %collective-permute-start.2 = (bf16[512,256]{1,0:T(8,128)(2,1)}, bf16[512,256]{1,0:T(8,128)(2,1)S(1)}, u32[]{:S(2)}, u32[]{:S(2)}) collective-permute-start(bf16[512,256]{1,0:T(8,128)(2,1)} %param.13), channel_id=1, source_target_pairs={{0,64},{64,0},{1,65},{65,1},{2,66},{66,2},{3,67},{67,3},{4,68},{68... | collective-permute-start | bytes 786440 | tf_op jit(solution)/shard_map/ppermute | solution.py:53
  22.9 14.9 %collective-permute-start.1 = (bf16[2,32,256]{2,1,0:T(8,128)(2,1)S(1)}, bf16[2,32,256]{2,1,0:T(8,128)(2,1)S(1)}, u32[]{:S(2)}, u32[]{:S(2)}) collective-permute-start(bf16[2,32,256]{2,1,0:T(8,128)(2,1)S(1)} %get-tuple-element.46), channel_id=1, source_target_pairs={{0,16},{1,48},{2,0},{3,32},{4,144},{5,176},{6,128},{7,160},{8,272}... | collective-permute-start | bytes 98312 | tf_op jit(solution)/shard_map/ppermute | solution.py:62
  32.5 14.7 %collective-permute-start = (bf16[2,32,256]{2,1,0:T(8,128)(2,1)S(1)}, bf16[2,32,256]{2,1,0:T(8,128)(2,1)S(1)}, u32[]{:S(2)}, u32[]{:S(2)}) collective-permute-start(bf16[2,32,256]{2,1,0:T(8,128)(2,1)S(1)} %get-tuple-element.47), channel_id=1, source_target_pairs={{0,0},{1,32},{2,16},{3,48},{4,128},{5,160},{6,144},{7,176},{8,256}... | collective-permute-start | bytes 98312 | tf_op jit(solution)/shard_map/ppermute | solution.py:62
  47.2 0.7 copy-start
  48.8 14.2 %all-to-all-start.1 = ((bf16[8,32,1024]{2,1,0:T(8,128)(2,1)}), bf16[8,32,1024]{2,1,0:T(8,128)(2,1)S(1)}, u32[]{:S(2)}, u32[]{:S(2)}) async-start(bf16[8,32,1024]{2,1,0:T(8,128)(2,1)} %broadcast_in_dim.7), calls=%async_computation.1 | async-start | bytes 1048576 | tf_op jit(solution)/shard_map/all_to_all | solution.py:73
  57.6 3.8 %collective-permute-start.3 = (bf16[512,512]{1,0:T(8,128)(2,1)S(1)}, bf16[512,512]{1,0:T(8,128)(2,1)S(1)}, u32[]{:S(2)}, u32[]{:S(2)}) collective-permute-start(bf16[512,512]{1,0:T(8,128)(2,1)S(1)} %constant_dynamic-update-slice_fusion), channel_id=1, source_target_pairs={{0,1},{1,0},{2,3},{3,2},{4,5},{5,4},{6,7},{7,6},{8,9},{9,8},{10,11... | collective-permute-start | bytes 1572872 | tf_op jit(solution)/shard_map/ppermute | solution.py:53
  115.6 50.0 %all-to-all-start.3 = ((bf16[32,16,1024]{2,1,0:T(8,128)(2,1)}), bf16[32,16,1024]{2,1,0:T(8,128)(2,1)S(1)}, u32[]{:S(2)}, u32[]{:S(2)}) async-start(bf16[32,16,1024]{2,1,0:T(8,128)(2,1)} %broadcast_in_dim.8), calls=%async_computation.3 | async-start | bytes 2097152 | tf_op jit(solution)/shard_map/all_to_all | solution.py:73
  128.8 30.5 %copy-start.3 = (bf16[256,512]{1,0:T(8,128)(2,1)S(1)}, bf16[256,512]{1,0:T(8,128)(2,1)}, u32[]{:S(2)}) copy-start(bf16[256,512]{1,0:T(8,128)(2,1)} %param.11) | copy-start | bytes 786436
  128.8 36.9 %collective-permute-start.4 = (bf16[512,1024]{1,0:T(8,128)(2,1)}, bf16[512,1024]{1,0:T(8,128)(2,1)}, u32[]{:S(2)}, u32[]{:S(2)}) collective-permute-start(bf16[512,1024]{1,0:T(8,128)(2,1)} %bitcast.12), channel_id=1, source_target_pairs={{0,1},{1,0},{2,3},{3,2},{4,5},{5,4},{6,7},{7,6},{8,9},{9,8},{10,11... | collective-permute-start | bytes 3145736 | tf_op jit(solution)/shard_map/ppermute | solution.py:53
  133.1 21.9 %collective-permute-start.7 = (bf16[256,512]{1,0:T(8,128)(2,1)S(1)}, bf16[256,512]{1,0:T(8,128)(2,1)S(1)}, u32[]{:S(2)}, u32[]{:S(2)}) collective-permute-start(bf16[256,512]{1,0:T(8,128)(2,1)S(1)} %slice.92), channel_id=1, source_target_pairs={{0,64},{64,0},{1,65},{65,1},{2,66},{66,2},{3,67},{67,3},{4,68},{68... | collective-permute-start | bytes 786440 | tf_op jit(solution)/shard_map/ppermute | solution.py:53
  136.6 24.6 %copy-start.9 = (bf16[256,512]{1,0:T(8,128)(2,1)S(1)}, bf16[256,512]{1,0:T(8,128)(2,1)}, u32[]{:S(2)}) copy-start(bf16[256,512]{1,0:T(8,128)(2,1)} %param.12) | copy-start | bytes 786436
  155.2 9.5 %collective-permute-start.8 = (bf16[512,512]{1,0:T(8,128)(2,1)S(1)}, bf16[512,512]{1,0:T(8,128)(2,1)S(1)}, u32[]{:S(2)}, u32[]{:S(2)}) collective-permute-start(bf16[512,512]{1,0:T(8,128)(2,1)S(1)} %maximum_select_fusion), channel_id=1, source_target_pairs={{0,1},{1,0},{2,3},{3,2},{4,5},{5,4},{6,7},{7,6},{8,9},{9,8},{10,11... | collective-permute-start | bytes 1572872 | tf_op jit(solution)/shard_map/ppermute | solution.py:53
  159.3 4.4 %collective-permute-start.5 = (bf16[256,512]{1,0:T(8,128)(2,1)S(1)}, bf16[256,512]{1,0:T(8,128)(2,1)S(1)}, u32[]{:S(2)}, u32[]{:S(2)}) collective-permute-start(bf16[256,512]{1,0:T(8,128)(2,1)S(1)} %copy-done.3), channel_id=1, source_target_pairs={{0,1},{1,0},{2,3},{3,2},{4,5},{5,4},{6,7},{7,6},{8,9},{9,8},{10,11... | collective-permute-start | bytes 786440 | tf_op jit(solution)/shard_map/ppermute | solution.py:53
  161.2 3.6 %collective-permute-start.6 = (bf16[256,512]{1,0:T(8,128)(2,1)S(1)}, bf16[256,512]{1,0:T(8,128)(2,1)S(1)}, u32[]{:S(2)}, u32[]{:S(2)}) collective-permute-start(bf16[256,512]{1,0:T(8,128)(2,1)S(1)} %copy-done.9), channel_id=1, source_target_pairs={{0,1},{1,0},{2,3},{3,2},{4,5},{5,4},{6,7},{7,6},{8,9},{9,8},{10,11... | collective-permute-start | bytes 786440 | tf_op jit(solution)/shard_map/ppermute | solution.py:53
  163.6 2.0 copy-start.7
  164.8 0.9 copy-start.4
  164.8 0.8 copy-start.1
  168.0 3.7 %copy-start.5 = (bf16[256,512]{1,0:T(8,128)(2,1)S(1)}, bf16[256,512]{1,0:T(8,128)(2,1)}, u32[]{:S(2)}) copy-start(bf16[256,512]{1,0:T(8,128)(2,1)} %copy-done.4) | copy-start | bytes 786436
  169.2 3.1 %copy-start.10 = (bf16[256,512]{1,0:T(8,128)(2,1)S(1)}, bf16[256,512]{1,0:T(8,128)(2,1)}, u32[]{:S(2)}) copy-start(bf16[256,512]{1,0:T(8,128)(2,1)} %param.12) | copy-start | bytes 786436
  169.2 14.5 %collective-permute-start.9 = (bf16[512,1536]{1,0:T(8,128)(2,1)}, bf16[512,1536]{1,0:T(8,128)(2,1)}, u32[]{:S(2)}, u32[]{:S(2)}) collective-permute-start(bf16[512,1536]{1,0:T(8,128)(2,1)} %pad_maximum_fusion), channel_id=1, source_target_pairs={{0,1},{1,0},{2,3},{3,2},{4,5},{5,4},{6,7},{7,6},{8,9},{9,8},{10,11... | collective-permute-start | bytes 4718600 | tf_op jit(solution)/shard_map/ppermute | solution.py:53
  172.3 1.0 copy-start.8
  174.3 9.3 %all-to-all-start.4 = ((bf16[8,64,256]{2,1,0:T(8,128)(2,1)}), bf16[8,64,256]{2,1,0:T(8,128)(2,1)S(1)}, u32[]{:S(2)}, u32[]{:S(2)}) async-start(bf16[8,64,256]{2,1,0:T(8,128)(2,1)} %bitcast.38), calls=%async_computation.4 | async-start | bytes 524288 | tf_op jit(solution)/shard_map/all_to_all | solution.py:79
  183.7 3.0 %copy-start.2 = (bf16[512,512]{1,0:T(8,128)(2,1)S(1)}, bf16[512,512]{1,0:T(8,128)(2,1)}, u32[]{:S(2)}) copy-start(bf16[512,512]{1,0:T(8,128)(2,1)} %copy-done.1) | copy-start | bytes 1572868
  188.1 19.4 %collective-permute-start.10 = (bf16[32,256]{1,0:T(8,128)(2,1)S(1)}, bf16[32,256]{1,0:T(8,128)(2,1)S(1)}, u32[]{:S(2)}, u32[]{:S(2)}) collective-permute-start(bf16[32,256]{1,0:T(8,128)(2,1)S(1)} %get-tuple-element.50), channel_id=1, source_target_pairs={{16,0},{48,1},{80,2},{112,3},{144,4},{176,5},{208,6},{240,7},{272,... | collective-permute-start | bytes 49160 | tf_op jit(solution)/shard_map/ppermute | solution.py:67
  200.2 14.3 %collective-permute-start.11 = (bf16[32,256]{1,0:T(8,128)(2,1)S(1)}, bf16[32,256]{1,0:T(8,128)(2,1)S(1)}, u32[]{:S(2)}, u32[]{:S(2)}) collective-permute-start(bf16[32,256]{1,0:T(8,128)(2,1)S(1)} %get-tuple-element.51), channel_id=1, source_target_pairs={{0,0},{32,1},{64,2},{96,3},{128,4},{160,5},{192,6},{224,7},{256,8}... | collective-permute-start | bytes 49160 | tf_op jit(solution)/shard_map/ppermute | solution.py:67
Sparse Core Ops, SparseCore 0:
  48.0 66.3 all-gather.1

commit v9 on v8

--- a/solution.py
+++ b/solution.py
@@ -6,7 +6,6 @@
 
 AXES = ("yh", "yl", "zh", "x", "zl", "core")
 ROW = ("yh", "yl", "zh")
-ORDER = ("yl", "yh", "zh")
 HALF = ("yh", "zh")
 COL = ("x", "zl", "core")
 PLANE = ("x", "zl")
@@ -27,7 +26,7 @@
 
 def turn_out(half_of):
     return [
-        ((2 * f + half_of(zh % 2)) * C + (yl * 2 + yh // 2) * 4 + yh % 2 * 2 + zh // 2, t * C + f)
+        ((2 * f + half_of(zh % 2)) * C + yh * 4 + yl * 2 + zh // 2, t * C + f)
         for t, yh, yl, zh in TILES
         for f in range(C)
     ]
@@ -100,24 +99,21 @@
     pre = gather_copies(jnp.concatenate([gate_pre, up_pre], axis=1), "zh", 4)
     tiles = to_features(jnp.stack([out_grad, activations]), upper, mine)
     (own, other), pre, down_y = lax.optimization_barrier((tiles, pre, swap(down_weight, "yl")))
-    pre = lax.all_gather(pre, ("yl", "yh"), axis=0, tiled=True)
+    pre = lax.all_gather(pre, ("yh", "yl"), axis=0, tiled=True)
     cols = gather_copies(jnp.concatenate([own[0], other[0], other[1], own[1]], axis=1), PLANE, 8)
     down = jnp.concatenate([down_weight, down_y], axis=1)
     down = jnp.concatenate([down, swap(down)], axis=0)
     partial = contract_cols(cols[:, :512], down).astype(jnp.bfloat16)
     hidden_grad = scatter_sum(partial, HALF, C)
-    hidden_grad, pre, cols = lax.optimization_barrier((hidden_grad, pre, cols))
+    cols_y = swap(cols[:, 256:768], "yl")
+    hidden_grad, pre, cols, cols_y = lax.optimization_barrier((hidden_grad, pre, cols, cols_y))
 
-    hidden_grad = gather_copies(hidden_grad, ORDER, R)
+    hidden_grad = gather_copies(hidden_grad, ROW, R)
     pre_mine, pre_theirs = choose(core == 1, *(pre.reshape(8, 2, 64, 1024)[:, at] for at in (1, 0)))
     pre_mine, pre_theirs = pre_mine.reshape(512, 1024), swap(pre_theirs.reshape(512, 1024))
-    cols_y = swap(cols[:, 256:768], "yl")
-    cols_own = jnp.concatenate([cols[:, :256], cols[:, 768:]], axis=1)
-    cols = jnp.where(
-        yl == 0,
-        jnp.concatenate([cols_own, cols_y], axis=0),
-        jnp.concatenate([cols_y, cols_own], axis=0),
-    )
+    cols = jnp.concatenate([cols[:, :256], cols[:, 768:]], axis=1).reshape(4, 64, 512)
+    cols_y = cols_y.reshape(4, 64, 512)
+    cols = jnp.stack(choose(yl == 0, cols, cols_y), axis=1).reshape(512, 512)
     hidden_grad, pre_mine, pre_theirs, gate_other, up_other, cols, cols_x = lax.optimization_barrier(
         (hidden_grad, pre_mine, pre_theirs, swap(gate_weight), swap(up_weight), cols, swap(cols))
     )

time: 223 us -> 199 us (0.89)
  the two profiles are of different devices: /device:TPU:7 before, /device:TPU:5 now
where the time goes in v9:
time: 199 us; the launch traced here: 198 us
  starting transfers between devices  91.3 us (46%)
  waiting for transfers between devices  68.1 us (34%)
  between operations  14.4 us (7%)
  matrix products  11.3 us (6%)
  other arithmetic  7.79 us (4%)
  local copies, waits for them, and re-layouts  4.79 us (2%)
    all_to_all x3, starting transfers between devices, gather_copies(): got = lax.all_to_all(copies, axes, 0, 0, tiled=True)  26.3 us
    all_to_all x2, waiting for transfers between devices, scatter_sum(): got = lax.all_to_all(pieces, axes, 0, 0, tiled=True)  26.1 us
    ppermute x8, starting transfers between devices, swap(): return lax.ppermute(value, axis, [(0, 1), (1, 0)])  23.8 us
    all_to_all x3, waiting for transfers between devices, gather_copies(): got = lax.all_to_all(copies, axes, 0, 0, tiled=True)  13.4 us
    ppermute x1, starting transfers between devices, to_features(): lax.ppermute(two, AXES, IN_TWO)  11.2 us
    ppermute x1, waiting for transfers between devices, to_features(): lax.ppermute(one, AXES, IN_ONE)  10.9 us
    ppermute x1, starting transfers between devices, to_tokens(): lax.ppermute(two, AXES, OUT_TWO)  9.63 us
    ppermute x8, waiting for transfers between devices, swap(): return lax.ppermute(value, axis, [(0, 1), (1, 0)])  9.21 us
  transfers between devices with their start and end apart: 18, of which 10 were waited for; matrix products, arithmetic and copies ran while one was open for 5% of the time, Pallas kernels for 0%

profile of v9, /device:TPU:5, one launch (start us, length us, event | category | flops | bytes accessed | tf_op | source)
XLA Modules:
  0.0 197.8 jit_solution(2663491096727087065)
XLA Ops:
  7.2 0.8 pad_maximum_fusion.3
  7.9 0.7 broadcast_in_dim.6
  8.7 10.1 %all-to-all-start = ((bf16[4,32,1024]{2,1,0:T(8,128)(2,1)}), bf16[4,32,1024]{2,1,0:T(8,128)(2,1)S(1)}, u32[]{:S(2)}, u32[]{:S(2)}) async-start(bf16[4,32,1024]{2,1,0:T(8,128)(2,1)} %broadcast_in_dim.6), calls=%async_computation | async-start | bytes 524288 | tf_op jit(solution)/shard_map/all_to_all | solution.py:72
  18.8 3.2 %collective-permute-start.2 = (bf16[512,256]{1,0:T(8,128)(2,1)}, bf16[512,256]{1,0:T(8,128)(2,1)S(1)}, u32[]{:S(2)}, u32[]{:S(2)}) collective-permute-start(bf16[512,256]{1,0:T(8,128)(2,1)} %param.13), channel_id=1, source_target_pairs={{0,64},{64,0},{1,65},{65,1},{2,66},{66,2},{3,67},{67,3},{4,68},{68... | collective-permute-start | bytes 786440 | tf_op jit(solution)/shard_map/ppermute | solution.py:52
  22.0 0.8 broadcast_select_fusion.4
  22.9 11.2 %collective-permute-start.1 = (bf16[2,32,256]{2,1,0:T(8,128)(2,1)S(1)}, bf16[2,32,256]{2,1,0:T(8,128)(2,1)S(1)}, u32[]{:S(2)}, u32[]{:S(2)}) collective-permute-start(bf16[2,32,256]{2,1,0:T(8,128)(2,1)S(1)} %get-tuple-element.50), channel_id=1, source_target_pairs={{0,16},{1,48},{2,0},{3,32},{4,144},{5,176},{6,128},{7,160},{8,272}... | collective-permute-start | bytes 98312 | tf_op jit(solution)/shard_map/ppermute | solution.py:61
  34.1 5.8 %collective-permute-start = (bf16[2,32,256]{2,1,0:T(8,128)(2,1)S(1)}, bf16[2,32,256]{2,1,0:T(8,128)(2,1)S(1)}, u32[]{:S(2)}, u32[]{:S(2)}) collective-permute-start(bf16[2,32,256]{2,1,0:T(8,128)(2,1)S(1)} %get-tuple-element.51), channel_id=1, source_target_pairs={{0,0},{1,32},{2,16},{3,48},{4,128},{5,160},{6,144},{7,176},{8,256}... | collective-permute-start | bytes 98312 | tf_op jit(solution)/shard_map/ppermute | solution.py:61
  39.9 10.9 %collective-permute-done = bf16[2,32,256]{2,1,0:T(8,128)(2,1)S(1)} collective-permute-done((bf16[2,32,256]{2,1,0:T(8,128)(2,1)S(1)}, bf16[2,32,256]{2,1,0:T(8,128)(2,1)S(1)}, u32[]{:S(2)}, u32[]{:S(2)}) %collective-permute-start) | collective-permute-done | bytes 32800 | tf_op jit(solution)/shard_map/ppermute | solution.py:61
  50.8 0.7 copy-done
  51.6 0.9 broadcast_in_dim.7
  52.4 5.1 %all-to-all-start.1 = ((bf16[8,32,1024]{2,1,0:T(8,128)(2,1)}), bf16[8,32,1024]{2,1,0:T(8,128)(2,1)S(1)}, u32[]{:S(2)}, u32[]{:S(2)}) async-start(bf16[8,32,1024]{2,1,0:T(8,128)(2,1)} %broadcast_in_dim.7), calls=%async_computation.1 | async-start | bytes 1048576 | tf_op jit(solution)/shard_map/all_to_all | solution.py:72
  57.6 1.9 collective-permute-start.3
  59.5 1.9 collective-permute-done.3
  61.4 1.3 all-to-all-done.1
  62.7 1.3 convolution_convert_fusion
  64.0 4.0 %all-to-all-start.2 = ((bf16[16,16,1024]{2,1,0:T(8,128)(2,1)}), bf16[16,16,1024]{2,1,0:T(8,128)(2,1)S(1)}, u32[]{:S(2)}, u32[]{:S(2)}) async-start(bf16[16,16,1024]{2,1,0:T(8,128)(2,1)} %bitcast.8), calls=%async_computation.2 | async-start | bytes 1048576 | tf_op jit(solution)/shard_map/all_to_all | solution.py:78
  68.0 3.0 %collective-permute-start.4 = (bf16[256,512]{1,0:T(8,128)(2,1)S(1)}, bf16[256,512]{1,0:T(8,128)(2,1)S(1)}, u32[]{:S(2)}, u32[]{:S(2)}) collective-permute-start(bf16[256,512]{1,0:T(8,128)(2,1)S(1)} %slice.111), channel_id=1, source_target_pairs={{0,64},{64,0},{1,65},{65,1},{2,66},{66,2},{3,67},{67,3},{4,68},{68... | collective-permute-start | bytes 786440 | tf_op jit(solution)/shard_map/ppermute | solution.py:52
  71.0 21.4 %all-to-all-done.2 = bf16[16,16,1024]{2,1,0:T(8,128)(2,1)S(1)} async-done(((bf16[16,16,1024]{2,1,0:T(8,128)(2,1)}), bf16[16,16,1024]{2,1,0:T(8,128)(2,1)S(1)}, u32[]{:S(2)}, u32[]{:S(2)}) %all-to-all-start.2) | async-done | bytes 524320 | tf_op jit(solution)/shard_map/all_to_all | solution.py:78
  92.5 5.8 %collective-permute-done.4 = bf16[256,512]{1,0:T(8,128)(2,1)S(1)} collective-permute-done((bf16[256,512]{1,0:T(8,128)(2,1)S(1)}, bf16[256,512]{1,0:T(8,128)(2,1)S(1)}, u32[]{:S(2)}, u32[]{:S(2)}) %collective-permute-start.4) | collective-permute-done | bytes 262176 | tf_op jit(solution)/shard_map/ppermute | solution.py:52
  98.3 2.0 %all-gather.2.cloned.1.call-done = bf16[1024,1024]{1,0:T(8,128)(2,1)} async-done(((bf16[128,1024]{1,0:T(8,128)(2,1)}), bf16[1024,1024]{1,0:T(8,128)(2,1)}) %all-gather.2.cloned.1.call-update) | async-done | bytes 2097168 | tf_op jit(solution)/shard_map/all_gather | solution.py:102
  100.3 1.1 broadcast_in_dim.8
  101.4 11.1 %all-to-all-start.3 = ((bf16[32,16,1024]{2,1,0:T(8,128)(2,1)}), bf16[32,16,1024]{2,1,0:T(8,128)(2,1)S(1)}, u32[]{:S(2)}, u32[]{:S(2)}) async-start(bf16[32,16,1024]{2,1,0:T(8,128)(2,1)} %broadcast_in_dim.8), calls=%async_computation.3 | async-start | bytes 2097152 | tf_op jit(solution)/shard_map/all_to_all | solution.py:72
  112.5 1.7 broadcast_select_fusion
  114.2 3.5 %collective-permute-start.5 = (bf16[512,1024]{1,0:T(8,128)(2,1)S(1)}, bf16[512,1024]{1,0:T(8,128)(2,1)}, u32[]{:S(2)}, u32[]{:S(2)}) collective-permute-start(bf16[512,1024]{1,0:T(8,128)(2,1)S(1)} %bitcast.44), channel_id=1, source_target_pairs={{0,1},{1,0},{2,3},{3,2},{4,5},{5,4},{6,7},{7,6},{8,9},{9,8},{10,11... | collective-permute-start | bytes 3145736 | tf_op jit(solution)/shard_map/ppermute | solution.py:52
  118.0 1.9 collective-permute-start.8
  119.9 2.4 %collective-permute-start.6 = (bf16[256,512]{1,0:T(8,128)(2,1)S(1)}, bf16[256,512]{1,0:T(8,128)(2,1)S(1)}, u32[]{:S(2)}, u32[]{:S(2)}) collective-permute-start(bf16[256,512]{1,0:T(8,128)(2,1)S(1)} %copy-done.3), channel_id=1, source_target_pairs={{0,1},{1,0},{2,3},{3,2},{4,5},{5,4},{6,7},{7,6},{8,9},{9,8},{10,11... | collective-permute-start | bytes 786440 | tf_op jit(solution)/shard_map/ppermute | solution.py:52
  122.3 1.9 collective-permute-start.7
  124.3 1.5 collective-permute-done.7
  125.8 0.8 copy-done.1
  126.6 12.2 %all-to-all-done.3 = bf16[32,16,1024]{2,1,0:T(8,128)(2,1)S(1)} async-done(((bf16[32,16,1024]{2,1,0:T(8,128)(2,1)}), bf16[32,16,1024]{2,1,0:T(8,128)(2,1)S(1)}, u32[]{:S(2)}, u32[]{:S(2)}) %all-to-all-start.3) | async-done | bytes 1048608 | tf_op jit(solution)/shard_map/all_to_all | solution.py:72
  138.7 2.3 %fusion.13 = (bf16[512,512]{1,0:T(8,128)(2,1)S(1)}, bf16[512,512]{1,0:T(8,128)(2,1)S(1)}, bf16[512,512]{1,0:T(8,128)(2,1)S(1)}, bf16[512,512]{1,0:T(8,128)(2,1)S(1)}) fusion(bf16[512,1024]{1,0:T(8,128)(2,1)} %collective-permute-done.5, bf16[512,1024]{1,0:T(8,128)(2,1)S(1)} %bitcast.33, bf16[512,1024]{1,0:T(8,128)(2,1)S(1)} %bitcast.29), kind=kLoop, calls=%fused_computation.32 | loop fusion | flops 8126464 | bytes 5242880 | tf_op jit(solution)/shard_map/convert_element_type | solution.py:90
  141.1 1.2 pad_maximum_fusion
  142.3 5.9 %collective-permute-start.9 = (bf16[512,1536]{1,0:T(8,128)(2,1)}, bf16[512,1536]{1,0:T(8,128)(2,1)}, u32[]{:S(2)}, u32[]{:S(2)}) collective-permute-start(bf16[512,1536]{1,0:T(8,128)(2,1)} %pad_maximum_fusion), channel_id=1, source_target_pairs={{0,1},{1,0},{2,3},{3,2},{4,5},{5,4},{6,7},{7,6},{8,9},{9,8},{10,11... | collective-permute-start | bytes 4718600 | tf_op jit(solution)/shard_map/ppermute | solution.py:52
  148.9 0.5 convolution_add_fusion.4
  149.4 0.4 copy-done.8
  149.9 1.0 fusion.1
  150.9 4.5 %all-to-all-start.4 = ((bf16[8,64,256]{2,1,0:T(8,128)(2,1)}), bf16[8,64,256]{2,1,0:T(8,128)(2,1)S(1)}, u32[]{:S(2)}, u32[]{:S(2)}) async-start(bf16[8,64,256]{2,1,0:T(8,128)(2,1)} %bitcast.48), calls=%async_computation.4 | async-start | bytes 524288 | tf_op jit(solution)/shard_map/all_to_all | solution.py:78
  155.4 4.7 %all-to-all-done.4 = bf16[8,64,256]{2,1,0:T(8,128)(2,1)S(1)} async-done(((bf16[8,64,256]{2,1,0:T(8,128)(2,1)}), bf16[8,64,256]{2,1,0:T(8,128)(2,1)S(1)}, u32[]{:S(2)}, u32[]{:S(2)}) %all-to-all-start.4) | async-done | bytes 262176 | tf_op jit(solution)/shard_map/all_to_all | solution.py:78
  160.2 1.5 fusion.31
  161.7 1.4 fusion.29
  163.1 1.4 fusion.27
  164.5 9.6 %collective-permute-start.10 = (bf16[32,256]{1,0:T(8,128)(2,1)S(1)}, bf16[32,256]{1,0:T(8,128)(2,1)S(1)}, u32[]{:S(2)}, u32[]{:S(2)}) collective-permute-start(bf16[32,256]{1,0:T(8,128)(2,1)S(1)} %get-tuple-element.54), channel_id=1, source_target_pairs={{16,0},{48,1},{80,2},{112,3},{144,4},{176,5},{208,6},{240,7},{272,... | collective-permute-start | bytes 49160 | tf_op jit(solution)/shard_map/ppermute | solution.py:66
  174.2 6.2 %collective-permute-start.11 = (bf16[32,256]{1,0:T(8,128)(2,1)S(1)}, bf16[32,256]{1,0:T(8,128)(2,1)S(1)}, u32[]{:S(2)}, u32[]{:S(2)}) collective-permute-start(bf16[32,256]{1,0:T(8,128)(2,1)S(1)} %get-tuple-element.55), channel_id=1, source_target_pairs={{0,0},{32,1},{64,2},{96,3},{128,4},{160,5},{192,6},{224,7},{256,8}... | collective-permute-start | bytes 49160 | tf_op jit(solution)/shard_map/ppermute | solution.py:66
  180.3 1.2 fusion.3
  181.6 1.3 fusion.4
  182.9 1.0 fusion.2
  183.9 6.4 %collective-permute-done.11 = bf16[32,256]{1,0:T(8,128)(2,1)S(1)} collective-permute-done((bf16[32,256]{1,0:T(8,128)(2,1)S(1)}, bf16[32,256]{1,0:T(8,128)(2,1)S(1)}, u32[]{:S(2)}, u32[]{:S(2)}) %collective-permute-start.11) | collective-permute-done | bytes 16416 | tf_op jit(solution)/shard_map/ppermute | solution.py:66
  190.3 0.6 pad_maximum_fusion.6
  (44 shorter events, 1.1 us)
Async XLA Ops:
  8.7 48.9 %copy-start.6 = (bf16[512,256]{1,0:T(8,128)(2,1)S(1)}, bf16[512,256]{1,0:T(8,128)(2,1)}, u32[]{:S(2)}) copy-start(bf16[512,256]{1,0:T(8,128)(2,1)} %param.13) | copy-start | bytes 786436
  8.7 42.1 %all-to-all-start = ((bf16[4,32,1024]{2,1,0:T(8,128)(2,1)}), bf16[4,32,1024]{2,1,0:T(8,128)(2,1)S(1)}, u32[]{:S(2)}, u32[]{:S(2)}) async-start(bf16[4,32,1024]{2,1,0:T(8,128)(2,1)} %broadcast_in_dim.6), calls=%async_computation | async-start | bytes 524288 | tf_op jit(solution)/shard_map/all_to_all | solution.py:72
  18.8 81.5 %all-gather.2.cloned.1.call-start = ((), (), s32[]{:S(2)}) async-start(), calls=%async_computation.5 | async-start | bytes 2359296 | tf_op jit(solution)/shard_map/all_gather | solution.py:102
  18.8 31.9 %collective-permute-start.2 = (bf16[512,256]{1,0:T(8,128)(2,1)}, bf16[512,256]{1,0:T(8,128)(2,1)S(1)}, u32[]{:S(2)}, u32[]{:S(2)}) collective-permute-start(bf16[512,256]{1,0:T(8,128)(2,1)} %param.13), channel_id=1, source_target_pairs={{0,64},{64,0},{1,65},{65,1},{2,66},{66,2},{3,67},{67,3},{4,68},{68... | collective-permute-start | bytes 786440 | tf_op jit(solution)/shard_map/ppermute | solution.py:52
  22.9 17.0 %collective-permute-start.1 = (bf16[2,32,256]{2,1,0:T(8,128)(2,1)S(1)}, bf16[2,32,256]{2,1,0:T(8,128)(2,1)S(1)}, u32[]{:S(2)}, u32[]{:S(2)}) collective-permute-start(bf16[2,32,256]{2,1,0:T(8,128)(2,1)S(1)} %get-tuple-element.50), channel_id=1, source_target_pairs={{0,16},{1,48},{2,0},{3,32},{4,144},{5,176},{6,128},{7,160},{8,272}... | collective-permute-start | bytes 98312 | tf_op jit(solution)/shard_map/ppermute | solution.py:61
  34.1 16.7 %collective-permute-start = (bf16[2,32,256]{2,1,0:T(8,128)(2,1)S(1)}, bf16[2,32,256]{2,1,0:T(8,128)(2,1)S(1)}, u32[]{:S(2)}, u32[]{:S(2)}) collective-permute-start(bf16[2,32,256]{2,1,0:T(8,128)(2,1)S(1)} %get-tuple-element.51), channel_id=1, source_target_pairs={{0,0},{1,32},{2,16},{3,48},{4,128},{5,160},{6,144},{7,176},{8,256}... | collective-permute-start | bytes 98312 | tf_op jit(solution)/shard_map/ppermute | solution.py:61
  50.8 0.7 copy-start
  52.4 10.3 %all-to-all-start.1 = ((bf16[8,32,1024]{2,1,0:T(8,128)(2,1)}), bf16[8,32,1024]{2,1,0:T(8,128)(2,1)S(1)}, u32[]{:S(2)}, u32[]{:S(2)}) async-start(bf16[8,32,1024]{2,1,0:T(8,128)(2,1)} %broadcast_in_dim.7), calls=%async_computation.1 | async-start | bytes 1048576 | tf_op jit(solution)/shard_map/all_to_all | solution.py:72
  57.6 3.8 %collective-permute-start.3 = (bf16[512,512]{1,0:T(8,128)(2,1)S(1)}, bf16[512,512]{1,0:T(8,128)(2,1)S(1)}, u32[]{:S(2)}, u32[]{:S(2)}) collective-permute-start(bf16[512,512]{1,0:T(8,128)(2,1)S(1)} %constant_dynamic-update-slice_fusion), channel_id=1, source_target_pairs={{0,1},{1,0},{2,3},{3,2},{4,5},{5,4},{6,7},{7,6},{8,9},{9,8},{10,11... | collective-permute-start | bytes 1572872 | tf_op jit(solution)/shard_map/ppermute | solution.py:52
  64.0 28.4 %all-to-all-start.2 = ((bf16[16,16,1024]{2,1,0:T(8,128)(2,1)}), bf16[16,16,1024]{2,1,0:T(8,128)(2,1)S(1)}, u32[]{:S(2)}, u32[]{:S(2)}) async-start(bf16[16,16,1024]{2,1,0:T(8,128)(2,1)} %bitcast.8), calls=%async_computation.2 | async-start | bytes 1048576 | tf_op jit(solution)/shard_map/all_to_all | solution.py:78
  68.0 30.3 %collective-permute-start.4 = (bf16[256,512]{1,0:T(8,128)(2,1)S(1)}, bf16[256,512]{1,0:T(8,128)(2,1)S(1)}, u32[]{:S(2)}, u32[]{:S(2)}) collective-permute-start(bf16[256,512]{1,0:T(8,128)(2,1)S(1)} %slice.111), channel_id=1, source_target_pairs={{0,64},{64,0},{1,65},{65,1},{2,66},{66,2},{3,67},{67,3},{4,68},{68... | collective-permute-start | bytes 786440 | tf_op jit(solution)/shard_map/ppermute | solution.py:52
  101.4 37.3 %all-to-all-start.3 = ((bf16[32,16,1024]{2,1,0:T(8,128)(2,1)}), bf16[32,16,1024]{2,1,0:T(8,128)(2,1)S(1)}, u32[]{:S(2)}, u32[]{:S(2)}) async-start(bf16[32,16,1024]{2,1,0:T(8,128)(2,1)} %broadcast_in_dim.8), calls=%async_computation.3 | async-start | bytes 2097152 | tf_op jit(solution)/shard_map/all_to_all | solution.py:72
  114.2 5.7 %copy-start.3 = (bf16[256,512]{1,0:T(8,128)(2,1)S(1)}, bf16[256,512]{1,0:T(8,128)(2,1)}, u32[]{:S(2)}) copy-start(bf16[256,512]{1,0:T(8,128)(2,1)} %param.11) | copy-start | bytes 786436
  114.2 8.1 %copy-start.9 = (bf16[256,512]{1,0:T(8,128)(2,1)S(1)}, bf16[256,512]{1,0:T(8,128)(2,1)}, u32[]{:S(2)}) copy-start(bf16[256,512]{1,0:T(8,128)(2,1)} %param.12) | copy-start | bytes 786436
  114.2 12.3 %collective-permute-start.5 = (bf16[512,1024]{1,0:T(8,128)(2,1)S(1)}, bf16[512,1024]{1,0:T(8,128)(2,1)}, u32[]{:S(2)}, u32[]{:S(2)}) collective-permute-start(bf16[512,1024]{1,0:T(8,128)(2,1)S(1)} %bitcast.44), channel_id=1, source_target_pairs={{0,1},{1,0},{2,3},{3,2},{4,5},{5,4},{6,7},{7,6},{8,9},{9,8},{10,11... | collective-permute-start | bytes 3145736 | tf_op jit(solution)/shard_map/ppermute | solution.py:52
  118.0 7.8 %collective-permute-start.8 = (bf16[512,512]{1,0:T(8,128)(2,1)S(1)}, bf16[512,512]{1,0:T(8,128)(2,1)S(1)}, u32[]{:S(2)}, u32[]{:S(2)}) collective-permute-start(bf16[512,512]{1,0:T(8,128)(2,1)S(1)} %bitcast.40), channel_id=1, source_target_pairs={{0,1},{1,0},{2,3},{3,2},{4,5},{5,4},{6,7},{7,6},{8,9},{9,8},{10,11... | collective-permute-start | bytes 1572872 | tf_op jit(solution)/shard_map/ppermute | solution.py:52
  119.9 4.4 %collective-permute-start.6 = (bf16[256,512]{1,0:T(8,128)(2,1)S(1)}, bf16[256,512]{1,0:T(8,128)(2,1)S(1)}, u32[]{:S(2)}, u32[]{:S(2)}) collective-permute-start(bf16[256,512]{1,0:T(8,128)(2,1)S(1)} %copy-done.3), channel_id=1, source_target_pairs={{0,1},{1,0},{2,3},{3,2},{4,5},{5,4},{6,7},{7,6},{8,9},{9,8},{10,11... | collective-permute-start | bytes 786440 | tf_op jit(solution)/shard_map/ppermute | solution.py:52
  122.3 3.4 %collective-permute-start.7 = (bf16[256,512]{1,0:T(8,128)(2,1)S(1)}, bf16[256,512]{1,0:T(8,128)(2,1)S(1)}, u32[]{:S(2)}, u32[]{:S(2)}) collective-permute-start(bf16[256,512]{1,0:T(8,128)(2,1)S(1)} %copy-done.9), channel_id=1, source_target_pairs={{0,1},{1,0},{2,3},{3,2},{4,5},{5,4},{6,7},{7,6},{8,9},{9,8},{10,11... | collective-permute-start | bytes 786440 | tf_op jit(solution)/shard_map/ppermute | solution.py:52
  124.3 14.5 %copy-start.7 = (bf16[256,512]{1,0:T(8,128)(2,1)}, bf16[256,512]{1,0:T(8,128)(2,1)S(1)}, u32[]{:S(2)}) copy-start(bf16[256,512]{1,0:T(8,128)(2,1)S(1)} %collective-permute-done.6) | copy-start | bytes 786436
  125.7 13.0 %copy-start.4 = (bf16[256,512]{1,0:T(8,128)(2,1)}, bf16[256,512]{1,0:T(8,128)(2,1)S(1)}, u32[]{:S(2)}) copy-start(bf16[256,512]{1,0:T(8,128)(2,1)S(1)} %collective-permute-done.7) | copy-start | bytes 786436
  125.8 0.8 copy-start.1
  141.1 7.2 %copy-start.5 = (bf16[256,512]{1,0:T(8,128)(2,1)S(1)}, bf16[256,512]{1,0:T(8,128)(2,1)}, u32[]{:S(2)}) copy-start(bf16[256,512]{1,0:T(8,128)(2,1)} %copy-done.4) | copy-start | bytes 786436
  142.3 6.6 %copy-start.10 = (bf16[256,512]{1,0:T(8,128)(2,1)S(1)}, bf16[256,512]{1,0:T(8,128)(2,1)}, u32[]{:S(2)}) copy-start(bf16[256,512]{1,0:T(8,128)(2,1)} %param.12) | copy-start | bytes 786436
  142.3 17.8 %collective-permute-start.9 = (bf16[512,1536]{1,0:T(8,128)(2,1)}, bf16[512,1536]{1,0:T(8,128)(2,1)}, u32[]{:S(2)}, u32[]{:S(2)}) collective-permute-start(bf16[512,1536]{1,0:T(8,128)(2,1)} %pad_maximum_fusion), channel_id=1, source_target_pairs={{0,1},{1,0},{2,3},{3,2},{4,5},{5,4},{6,7},{7,6},{8,9},{9,8},{10,11... | collective-permute-start | bytes 4718600 | tf_op jit(solution)/shard_map/ppermute | solution.py:52
  148.9 1.0 copy-start.8
  150.9 9.2 %all-to-all-start.4 = ((bf16[8,64,256]{2,1,0:T(8,128)(2,1)}), bf16[8,64,256]{2,1,0:T(8,128)(2,1)S(1)}, u32[]{:S(2)}, u32[]{:S(2)}) async-start(bf16[8,64,256]{2,1,0:T(8,128)(2,1)} %bitcast.48), calls=%async_computation.4 | async-start | bytes 524288 | tf_op jit(solution)/shard_map/all_to_all | solution.py:78
  160.1 3.0 %copy-start.2 = (bf16[512,512]{1,0:T(8,128)(2,1)S(1)}, bf16[512,512]{1,0:T(8,128)(2,1)}, u32[]{:S(2)}) copy-start(bf16[512,512]{1,0:T(8,128)(2,1)} %copy-done.1) | copy-start | bytes 1572868
  164.5 19.4 %collective-permute-start.10 = (bf16[32,256]{1,0:T(8,128)(2,1)S(1)}, bf16[32,256]{1,0:T(8,128)(2,1)S(1)}, u32[]{:S(2)}, u32[]{:S(2)}) collective-permute-start(bf16[32,256]{1,0:T(8,128)(2,1)S(1)} %get-tuple-element.54), channel_id=1, source_target_pairs={{16,0},{48,1},{80,2},{112,3},{144,4},{176,5},{208,6},{240,7},{272,... | collective-permute-start | bytes 49160 | tf_op jit(solution)/shard_map/ppermute | solution.py:66
  174.2 16.2 %collective-permute-start.11 = (bf16[32,256]{1,0:T(8,128)(2,1)S(1)}, bf16[32,256]{1,0:T(8,128)(2,1)S(1)}, u32[]{:S(2)}, u32[]{:S(2)}) collective-permute-start(bf16[32,256]{1,0:T(8,128)(2,1)S(1)} %get-tuple-element.55), channel_id=1, source_target_pairs={{0,0},{32,1},{64,2},{96,3},{128,4},{160,5},{192,6},{224,7},{256,8}... | collective-permute-start | bytes 49160 | tf_op jit(solution)/shard_map/ppermute | solution.py:66
Sparse Core Ops, SparseCore 0:
  51.6 48.6 all-gather.1

commit v10 on v7

--- a/solution.py
+++ b/solution.py
@@ -46,12 +46,13 @@
     return jnp.concatenate([first, second], axis=-2)
 
 
-def to_tokens(piece, odd):
+def to_tokens(piece, odd, beside):
     one, two = choose(odd, piece[32:], piece[:32])
     one = lax.ppermute(one, AXES, inverse(SAME))
     two = lax.ppermute(two, AXES, inverse(OTHER))
+    one, two, beside = lax.optimization_barrier((one, two, beside))
     high, low = choose(odd, one, two)
-    return jnp.concatenate([low, high], axis=1)
+    return (jnp.concatenate([low, high], axis=1),) + beside
 
 
 def gather_copies(block, axes, size):
@@ -86,37 +87,36 @@
     pre = gather_copies(jnp.concatenate([gate_pre, up_pre], axis=1), "zh", 4)
     tiles = to_features(jnp.stack([out_grad, activations]), odd)
     tiles, pre = lax.optimization_barrier((tiles, pre))
-    mine, theirs = choose(upper, pre[64:], pre[:64])
-    theirs = swap(theirs)
-    pre = jnp.concatenate([mine[:, :512], theirs[:, :512], mine[:, 512:], theirs[:, 512:]], axis=1)
     pre = lax.all_gather(pre, "y", axis=0, tiled=True)
     cols = gather_copies(jnp.concatenate([tiles[0], tiles[1]], axis=1), PLANE, 8)
-    grads, tokens = cols[:, :256], cols[:, 256:]
     down_both = jnp.concatenate([down_weight, swap(down_weight)], axis=0)
-    gate_both = jnp.concatenate([gate_weight, swap(gate_weight)], axis=1)
-    up_both = jnp.concatenate([up_weight, swap(up_weight)], axis=1)
+    hidden_grad = scatter_sum(contract_cols(cols[:, :256], down_both), ROW, R)
+    hidden_grad, pre, cols = lax.optimization_barrier((hidden_grad, pre, cols))
 
-    hidden_grad = scatter_sum(contract_cols(grads, down_both), ROW, R)
-    hidden_grad, pre = lax.optimization_barrier((hidden_grad, pre))
     hidden_grad = gather_copies(hidden_grad, ROW, R)
-    gate, up, hidden = swiglu_back(hidden_grad, pre[:, :1024], pre[:, 1024:])
-    partial = contract_cols(gate, gate_both) + contract_cols(up, up_both)
+    pre = pre.reshape(8, 2, 64, 1024)
+    pre_a, pre_b = choose(upper, pre[:, 1], pre[:, 0])
+    pre_a, pre_b = pre_a.reshape(512, 1024), pre_b.reshape(512, 1024)
+    hidden_grad, pre_a, pre_b, pre_y, gate_other, up_other, cols, cols_b = lax.optimization_barrier(
+        (hidden_grad, pre_a, pre_b, swap(pre_b), swap(gate_weight), swap(up_weight), cols, swap(cols))
+    )
+    gate_a, up_a, hidden_a = swiglu_back(hidden_grad[:, :512], pre_a[:, :512], pre_a[:, 512:])
+    gate_y, up_y, _ = swiglu_back(hidden_grad[:, 512:], pre_y[:, :512], pre_y[:, 512:])
+    partial = contract_cols(gate_a, gate_weight) + contract_cols(up_a, up_weight)
+    partial = partial + contract_cols(gate_y, gate_other) + contract_cols(up_y, up_other)
     summed = scatter_sum(partial, PLANE, 8)
-    cols_x = swap(cols)
-    grads_x, tokens_x = cols_x[:, :256], cols_x[:, 256:]
-    swapped = swap(jnp.concatenate([gate[:, 512:], up[:, 512:], hidden[:, 512:]], axis=1))
-    summed, swapped = lax.optimization_barrier((summed, swapped))
-    gate_x, up_x, hidden_x = swapped[:, :512], swapped[:, 512:1024], swapped[:, 1024:]
-    input_grad = to_tokens(summed, odd)
-    gate_weight_grad = contract_rows(tokens, gate[:, :512]) + contract_rows(tokens_x, gate_x)
-    up_weight_grad = contract_rows(tokens, up[:, :512]) + contract_rows(tokens_x, up_x)
-    down_weight_grad = contract_rows(hidden[:, :512], grads) + contract_rows(hidden_x, grads_x)
-    return (
-        input_grad,
-        gate_weight_grad.astype(jnp.bfloat16),
-        up_weight_grad.astype(jnp.bfloat16),
-        down_weight_grad.astype(jnp.bfloat16),
+    hidden_grad_b, pre_b = lax.optimization_barrier((swap(hidden_grad[:, 512:]), pre_b))
+    gate_b, up_b, hidden_b = swiglu_back(hidden_grad_b, pre_b[:, :512], pre_b[:, 512:])
+    grads_a, tokens_a = cols[:, :256], cols[:, 256:]
+    grads_b, tokens_b = cols_b[:, :256], cols_b[:, 256:]
+    products = contract_rows(tokens_a, gate_a), contract_rows(tokens_a, up_a), contract_rows(hidden_a, grads_a)
+    summed, products = lax.optimization_barrier((summed, products))
+    weight_grads = (
+        (products[0] + contract_rows(tokens_b, gate_b)).astype(jnp.bfloat16),
+        (products[1] + contract_rows(tokens_b, up_b)).astype(jnp.bfloat16),
+        (products[2] + contract_rows(hidden_b, grads_b)).astype(jnp.bfloat16),
     )
+    return to_tokens(summed, odd, weight_grads)
 
 
 def solution(mesh):

time: 204 us -> 196 us (0.961)
  blocking collectives: 77.6 us -> 44.3 us
  starting transfers between devices: 68.4 us -> 80 us
  waiting for transfers between devices: 23 us -> 30.4 us
  local copies, waits for them, and re-layouts: 1.9 us -> 5.76 us
  matrix products: 11.6 us -> 15 us
    all_to_all x1 -> x0, blocking collectives: 34.5 us -> none  [gather_copies(): got = lax.all_to_all(copies, axes, 0, 0, tiled=True)]
    all_to_all x2 -> x3, starting transfers between devices: 14.3 us -> 24 us  [gather_copies(): got = lax.all_to_all(copies, axes, 0, 0, tiled=True)]
    all_to_all x2 -> x3, waiting for transfers between devices: 3.7 us -> 12.9 us  [gather_copies(): got = lax.all_to_all(copies, axes, 0, 0, tiled=True)]
    dot_general x3 -> x5, matrix products: 2.12 us -> 5.25 us  [contract_cols(): lax.dot_general(left, right, (((1,), (1,)), ((), ())), preferred_element_...]
    unnamed x10 -> x32, local copies, waits for them, and re-layouts: 0.08 us -> 2.24 us
    ppermute x6, starting transfers between devices: 16.6 us -> 18.6 us  [swap(): return lax.ppermute(value, 'core', [(0, 1), (1, 0)])]
  transfers between devices with their start and end apart: 14 -> 15, of which waited for: 6 -> 6; matrix products, arithmetic and copies ran while one was open for 7% -> 7% of each run, Pallas kernels for 0% -> 0%
where the time goes in v10:
time: 196 us; the launch traced here: 195 us
  starting transfers between devices  80 us (41%)
  blocking collectives  44.3 us (23%)
  waiting for transfers between devices  30.4 us (16%)
  matrix products  15 us (8%)
  between operations  14.4 us (7%)
  local copies, waits for them, and re-layouts  5.76 us (3%)
  other arithmetic  4.83 us (2%)
    all_to_all x1, blocking collectives, scatter_sum(): got = lax.all_to_all(pieces, axes, 0, 0, tiled=True)  44.3 us
    all_to_all x3, starting transfers between devices, gather_copies(): got = lax.all_to_all(copies, axes, 0, 0, tiled=True)  24 us
    ppermute x6, starting transfers between devices, swap(): return lax.ppermute(value, 'core', [(0, 1), (1, 0)])  18.6 us
    all_to_all x3, waiting for transfers between devices, gather_copies(): got = lax.all_to_all(copies, axes, 0, 0, tiled=True)  12.9 us
    ppermute x1, starting transfers between devices, to_features(): two = lax.ppermute(two, AXES, OTHER)  11.8 us
    ppermute x1, waiting for transfers between devices, to_features(): one = lax.ppermute(one, AXES, SAME)  11.5 us
    dot_general x6, matrix products, contract_rows(): lax.dot_general(left, right, (((0,), (0,)), ((), ())), preferred_element_...  9.71 us
    ppermute x1, starting transfers between devices, to_tokens(): two = lax.ppermute(two, AXES, inverse(OTHER))  8.59 us
  transfers between devices with their start and end apart: 15, of which 6 were waited for; matrix products, arithmetic and copies ran while one was open for 7% of the time, Pallas kernels for 0%

profile of v10, /device:TPU:5, one launch (start us, length us, event | category | flops | bytes accessed | tf_op | source)
XLA Modules:
  0.0 194.7 jit_solution(15013718841884386250)
XLA Ops:
  7.2 0.8 pad_maximum_fusion.1
  8.0 0.7 broadcast_in_dim.6
  8.7 10.0 %all-to-all-start = ((bf16[4,32,1024]{2,1,0:T(8,128)(2,1)}), bf16[4,32,1024]{2,1,0:T(8,128)(2,1)S(1)}, u32[]{:S(2)}, u32[]{:S(2)}) async-start(bf16[4,32,1024]{2,1,0:T(8,128)(2,1)} %broadcast_in_dim.6), calls=%async_computation | async-start | bytes 524288 | tf_op jit(solution)/shard_map/all_to_all | solution.py:60
  18.7 0.8 broadcast_select_fusion.5
  19.6 11.8 %collective-permute-start = (bf16[2,32,256]{2,1,0:T(8,128)(2,1)S(1)}, bf16[2,32,256]{2,1,0:T(8,128)(2,1)S(1)}, u32[]{:S(2)}, u32[]{:S(2)}) collective-permute-start(bf16[2,32,256]{2,1,0:T(8,128)(2,1)S(1)} %get-tuple-element.60), channel_id=1, source_target_pairs={{0,16},{1,48},{2,80},{3,112},{4,144},{5,176},{6,208},{7,240},{8,27... | collective-permute-start | bytes 98312 | tf_op jit(solution)/shard_map/ppermute | solution.py:44
  31.4 5.2 %collective-permute-start.1 = (bf16[2,32,256]{2,1,0:T(8,128)(2,1)S(1)}, bf16[2,32,256]{2,1,0:T(8,128)(2,1)S(1)}, u32[]{:S(2)}, u32[]{:S(2)}) collective-permute-start(bf16[2,32,256]{2,1,0:T(8,128)(2,1)S(1)} %get-tuple-element.61), channel_id=1, source_target_pairs={{0,0},{1,32},{2,64},{3,96},{4,128},{5,160},{6,192},{7,224},{8,256}... | collective-permute-start | bytes 98312 | tf_op jit(solution)/shard_map/ppermute | solution.py:43
  36.6 11.5 %collective-permute-done.1 = bf16[2,32,256]{2,1,0:T(8,128)(2,1)S(1)} collective-permute-done((bf16[2,32,256]{2,1,0:T(8,128)(2,1)S(1)}, bf16[2,32,256]{2,1,0:T(8,128)(2,1)S(1)}, u32[]{:S(2)}, u32[]{:S(2)}) %collective-permute-start.1) | collective-permute-done | bytes 32800 | tf_op jit(solution)/shard_map/ppermute | solution.py:43
  48.1 0.7 copy-done.2
  48.8 0.0 all-gather.2.cloned.1.call-update
  48.9 0.9 broadcast_in_dim.7
  49.7 4.2 %all-to-all-start.1 = ((bf16[8,64,512]{2,1,0:T(8,128)(2,1)}), bf16[8,64,512]{2,1,0:T(8,128)(2,1)S(1)}, u32[]{:S(2)}, u32[]{:S(2)}) async-start(bf16[8,64,512]{2,1,0:T(8,128)(2,1)} %broadcast_in_dim.7), calls=%async_computation.1 | async-start | bytes 1048576 | tf_op jit(solution)/shard_map/all_to_all | solution.py:60
  54.0 1.9 collective-permute-start.2
  55.9 1.5 collective-permute-done.2
  57.4 1.7 all-to-all-done.1
  59.1 0.5 convolution_convert_fusion
  59.6 44.3 %all_to_all.25 = bf16[32,16,1024]{2,1,0:T(8,128)(2,1)S(1)} all-to-all(bf16[32,16,1024]{2,1,0:T(8,128)(2,1)S(1)} %bitcast.28), channel_id=1, replica_groups=mesh['y'=8,'zh'=4,'x'=4,'zl'=2,'core'=2] {'y','zh'}, dimensions={0} | all-to-all | bytes 2097152 | tf_op jit(solution)/shard_map/all_to_all | solution.py:66
  103.9 0.2 reduce_sum.24
  104.1 0.0 all-gather.2.cloned.1.call-done
  104.1 1.1 broadcast_in_dim.8
  105.2 9.8 %all-to-all-start.3 = ((bf16[32,16,1024]{2,1,0:T(8,128)(2,1)}), bf16[32,16,1024]{2,1,0:T(8,128)(2,1)S(1)}, u32[]{:S(2)}, u32[]{:S(2)}) async-start(bf16[32,16,1024]{2,1,0:T(8,128)(2,1)} %broadcast_in_dim.8), calls=%async_computation.3 | async-start | bytes 2097152 | tf_op jit(solution)/shard_map/all_to_all | solution.py:60
  115.0 0.0 copy-start.7
  115.0 1.7 broadcast_select_fusion
  116.7 3.9 %collective-permute-start.3 = (bf16[512,1024]{1,0:T(8,128)(2,1)S(1)}, bf16[512,1024]{1,0:T(8,128)(2,1)}, u32[]{:S(2)}, u32[]{:S(2)}) collective-permute-start(bf16[512,1024]{1,0:T(8,128)(2,1)S(1)} %bitcast.35), channel_id=1, source_target_pairs={{0,1},{1,0},{2,3},{3,2},{4,5},{5,4},{6,7},{7,6},{8,9},{9,8},{10,11... | collective-permute-start | bytes 3145736 | tf_op jit(solution)/shard_map/ppermute | solution.py:34
  120.6 1.9 collective-permute-start.6
  122.6 2.4 %collective-permute-start.4 = (bf16[256,512]{1,0:T(8,128)(2,1)S(1)}, bf16[256,512]{1,0:T(8,128)(2,1)S(1)}, u32[]{:S(2)}, u32[]{:S(2)}) collective-permute-start(bf16[256,512]{1,0:T(8,128)(2,1)S(1)} %copy-done.6), channel_id=1, source_target_pairs={{0,1},{1,0},{2,3},{3,2},{4,5},{5,4},{6,7},{7,6},{8,9},{9,8},{10,11... | collective-permute-start | bytes 786440 | tf_op jit(solution)/shard_map/ppermute | solution.py:34
  125.0 1.9 collective-permute-start.5
  126.9 1.5 collective-permute-done.5
  128.4 0.7 copy-done.13
  129.1 0.8 copy-done.9
  129.9 11.2 %all-to-all-done.3 = bf16[32,16,1024]{2,1,0:T(8,128)(2,1)S(1)} async-done(((bf16[32,16,1024]{2,1,0:T(8,128)(2,1)}), bf16[32,16,1024]{2,1,0:T(8,128)(2,1)S(1)}, u32[]{:S(2)}, u32[]{:S(2)}) %all-to-all-start.3) | async-done | bytes 1048608 | tf_op jit(solution)/shard_map/all_to_all | solution.py:60
  141.1 0.8 slice.74
  141.9 0.6 fusion.5
  142.5 0.3 fusion.69
  142.9 1.1 fusion.55
  144.0 0.3 convolution_add_fusion.4
  144.4 1.6 fusion.42
  146.0 2.6 %fusion.1 = bf16[512,256]{1,0:T(8,128)(2,1)} fusion(f32[512,256]{1,0:T(8,128)S(1)} %fusion.42, f32[512,256]{1,0:T(8,128)S(1)} %convolution_add_fusion.4, bf16[256,512]{1,0:T(8,128)(2,1)S(1)} %copy-done.12, bf16[512,1024]{1,0:T(8,128)(2,1)} %collective-permute-done.3, bf16[512,1024]{1,0:T(8,128)(2,1)S(1)} %bitcast.27), kind=kOutput, calls=%fused_computation.24 | convolution fusion | flops 138018816 | bytes 3145728 | tf_op jit(solution)/shard_map/dot_general | solution.py:28
  148.5 4.7 %all-to-all-start.4 = ((bf16[8,64,256]{2,1,0:T(8,128)(2,1)}), bf16[8,64,256]{2,1,0:T(8,128)(2,1)S(1)}, u32[]{:S(2)}, u32[]{:S(2)}) async-start(bf16[8,64,256]{2,1,0:T(8,128)(2,1)} %bitcast.40), calls=%async_computation.4 | async-start | bytes 524288 | tf_op jit(solution)/shard_map/all_to_all | solution.py:66
  153.2 6.6 %collective-permute-start.9 = (bf16[512,512]{1,0:T(8,128)(2,1)}, bf16[512,512]{1,0:T(8,128)(2,1)}, u32[]{:S(2)}, u32[]{:S(2)}) collective-permute-start(bf16[512,512]{1,0:T(8,128)(2,1)} %slice.74), channel_id=1, source_target_pairs={{0,1},{1,0},{2,3},{3,2},{4,5},{5,4},{6,7},{7,6},{8,9},{9,8},{10,11... | collective-permute-start | bytes 1572872 | tf_op jit(solution)/shard_map/ppermute | solution.py:34
  159.8 1.1 fusion.57
  160.9 1.3 fusion.34
  162.3 8.6 %collective-permute-start.8 = (bf16[32,256]{1,0:T(8,128)(2,1)S(1)}, bf16[32,256]{1,0:T(8,128)(2,1)S(1)}, u32[]{:S(2)}, u32[]{:S(2)}) collective-permute-start(bf16[32,256]{1,0:T(8,128)(2,1)S(1)} %get-tuple-element.64), channel_id=1, source_target_pairs={{16,0},{48,1},{80,2},{112,3},{144,4},{176,5},{208,6},{240,7},{272,... | collective-permute-start | bytes 49160 | tf_op jit(solution)/shard_map/ppermute | solution.py:52
  170.9 7.1 %collective-permute-start.7 = (bf16[32,256]{1,0:T(8,128)(2,1)S(1)}, bf16[32,256]{1,0:T(8,128)(2,1)S(1)}, u32[]{:S(2)}, u32[]{:S(2)}) collective-permute-start(bf16[32,256]{1,0:T(8,128)(2,1)S(1)} %get-tuple-element.65), channel_id=1, source_target_pairs={{0,0},{32,1},{64,2},{96,3},{128,4},{160,5},{192,6},{224,7},{256,8}... | collective-permute-start | bytes 49160 | tf_op jit(solution)/shard_map/ppermute | solution.py:51
  178.1 2.4 %fusion.3 = bf16[256,512]{1,0:T(8,128)(2,1)} fusion(f32[256,512]{1,0:T(8,128)S(1)} %copy-done.3, bf16[512,512]{1,0:T(8,128)(2,1)} %collective-permute-done.9, bf16[512,1024]{1,0:T(8,128)(2,1)S(1)} %bitcast.36, bf16[512,512]{1,0:T(8,128)(2,1)} %copy-done.9), kind=kOutput, calls=%fused_computation.26 | convolution fusion | flops 136577024 | bytes 2097152 | tf_op jit(solution)/shard_map/dot_general | solution.py:22
  180.5 2.5 %fusion.2 = bf16[256,512]{1,0:T(8,128)(2,1)} fusion(f32[256,512]{1,0:T(8,128)S(1)} %copy-done.4, bf16[512,512]{1,0:T(8,128)(2,1)} %collective-permute-done.9, bf16[512,1024]{1,0:T(8,128)(2,1)S(1)} %bitcast.37, bf16[512,512]{1,0:T(8,128)(2,1)S(1)} %copy-done.10), kind=kOutput, calls=%fused_computation.25 | convolution fusion | flops 137887744 | bytes 2621440 | tf_op jit(solution)/shard_map/dot_general | solution.py:22
  183.0 1.3 fusion.4
  184.2 3.0 %collective-permute-done.7 = bf16[32,256]{1,0:T(8,128)(2,1)S(1)} collective-permute-done((bf16[32,256]{1,0:T(8,128)(2,1)S(1)}, bf16[32,256]{1,0:T(8,128)(2,1)S(1)}, u32[]{:S(2)}, u32[]{:S(2)}) %collective-permute-start.7) | collective-permute-done | bytes 16416 | tf_op jit(solution)/shard_map/ppermute | solution.py:51
  187.2 0.6 pad_maximum_fusion.4
  (44 shorter events, 0.2 us)
Async XLA Ops:
  7.2 46.8 %copy-start.5 = (bf16[512,256]{1,0:T(8,128)(2,1)S(1)}, bf16[512,256]{1,0:T(8,128)(2,1)}, u32[]{:S(2)}) copy-start(bf16[512,256]{1,0:T(8,128)(2,1)} %param.13) | copy-start | bytes 786436
  8.7 39.4 %all-to-all-start = ((bf16[4,32,1024]{2,1,0:T(8,128)(2,1)}), bf16[4,32,1024]{2,1,0:T(8,128)(2,1)S(1)}, u32[]{:S(2)}, u32[]{:S(2)}) async-start(bf16[4,32,1024]{2,1,0:T(8,128)(2,1)} %broadcast_in_dim.6), calls=%async_computation | async-start | bytes 524288 | tf_op jit(solution)/shard_map/all_to_all | solution.py:60
  18.7 85.3 %all-gather.2.cloned.1.call-start = ((), (), s32[]{:S(2)}) async-start(), calls=%async_computation.5 | async-start | bytes 2359296 | tf_op jit(solution)/shard_map/all_gather | solution.py:90
  19.6 17.0 %collective-permute-start = (bf16[2,32,256]{2,1,0:T(8,128)(2,1)S(1)}, bf16[2,32,256]{2,1,0:T(8,128)(2,1)S(1)}, u32[]{:S(2)}, u32[]{:S(2)}) collective-permute-start(bf16[2,32,256]{2,1,0:T(8,128)(2,1)S(1)} %get-tuple-element.60), channel_id=1, source_target_pairs={{0,16},{1,48},{2,80},{3,112},{4,144},{5,176},{6,208},{7,240},{8,27... | collective-permute-start | bytes 98312 | tf_op jit(solution)/shard_map/ppermute | solution.py:44
  31.4 16.7 %collective-permute-start.1 = (bf16[2,32,256]{2,1,0:T(8,128)(2,1)S(1)}, bf16[2,32,256]{2,1,0:T(8,128)(2,1)S(1)}, u32[]{:S(2)}, u32[]{:S(2)}) collective-permute-start(bf16[2,32,256]{2,1,0:T(8,128)(2,1)S(1)} %get-tuple-element.61), channel_id=1, source_target_pairs={{0,0},{1,32},{2,64},{3,96},{4,128},{5,160},{6,192},{7,224},{8,256}... | collective-permute-start | bytes 98312 | tf_op jit(solution)/shard_map/ppermute | solution.py:43
  48.1 0.7 copy-start.2
  49.7 9.4 %all-to-all-start.1 = ((bf16[8,64,512]{2,1,0:T(8,128)(2,1)}), bf16[8,64,512]{2,1,0:T(8,128)(2,1)S(1)}, u32[]{:S(2)}, u32[]{:S(2)}) async-start(bf16[8,64,512]{2,1,0:T(8,128)(2,1)} %broadcast_in_dim.7), calls=%async_computation.1 | async-start | bytes 1048576 | tf_op jit(solution)/shard_map/all_to_all | solution.py:60
  54.0 3.4 %collective-permute-start.2 = (bf16[512,256]{1,0:T(8,128)(2,1)S(1)}, bf16[512,256]{1,0:T(8,128)(2,1)S(1)}, u32[]{:S(2)}, u32[]{:S(2)}) collective-permute-start(bf16[512,256]{1,0:T(8,128)(2,1)S(1)} %copy-done.5), channel_id=1, source_target_pairs={{0,1},{1,0},{2,3},{3,2},{4,5},{5,4},{6,7},{7,6},{8,9},{9,8},{10,11... | collective-permute-start | bytes 786440 | tf_op jit(solution)/shard_map/ppermute | solution.py:34
  105.2 35.9 %all-to-all-start.3 = ((bf16[32,16,1024]{2,1,0:T(8,128)(2,1)}), bf16[32,16,1024]{2,1,0:T(8,128)(2,1)S(1)}, u32[]{:S(2)}, u32[]{:S(2)}) async-start(bf16[32,16,1024]{2,1,0:T(8,128)(2,1)} %broadcast_in_dim.8), calls=%async_computation.3 | async-start | bytes 2097152 | tf_op jit(solution)/shard_map/all_to_all | solution.py:60
  115.0 7.6 %copy-start.6 = (bf16[256,512]{1,0:T(8,128)(2,1)S(1)}, bf16[256,512]{1,0:T(8,128)(2,1)}, u32[]{:S(2)}) copy-start(bf16[256,512]{1,0:T(8,128)(2,1)} %param.11) | copy-start | bytes 786436
  115.0 10.0 %copy-start.7 = (bf16[256,512]{1,0:T(8,128)(2,1)S(1)}, bf16[256,512]{1,0:T(8,128)(2,1)}, u32[]{:S(2)}) copy-start(bf16[256,512]{1,0:T(8,128)(2,1)} %param.12) | copy-start | bytes 786436
  116.7 11.7 %copy-start = (bf16[8,1,64,1024]{3,2,1,0:T(8,128)(2,1)}, bf16[8,1,64,1024]{3,2,1,0:T(8,128)(2,1)S(1)}, u32[]{:S(2)}) copy-start(bf16[8,1,64,1024]{3,2,1,0:T(8,128)(2,1)S(1)} %get-tuple-element.54) | copy-start | bytes 3145732
  116.7 13.2 %collective-permute-start.3 = (bf16[512,1024]{1,0:T(8,128)(2,1)S(1)}, bf16[512,1024]{1,0:T(8,128)(2,1)}, u32[]{:S(2)}, u32[]{:S(2)}) collective-permute-start(bf16[512,1024]{1,0:T(8,128)(2,1)S(1)} %bitcast.35), channel_id=1, source_target_pairs={{0,1},{1,0},{2,3},{3,2},{4,5},{5,4},{6,7},{7,6},{8,9},{9,8},{10,11... | collective-permute-start | bytes 3145736 | tf_op jit(solution)/shard_map/ppermute | solution.py:34
  120.6 7.8 %collective-permute-start.6 = (bf16[512,512]{1,0:T(8,128)(2,1)S(1)}, bf16[512,512]{1,0:T(8,128)(2,1)S(1)}, u32[]{:S(2)}, u32[]{:S(2)}) collective-permute-start(bf16[512,512]{1,0:T(8,128)(2,1)S(1)} %bitcast.30), channel_id=1, source_target_pairs={{0,1},{1,0},{2,3},{3,2},{4,5},{5,4},{6,7},{7,6},{8,9},{9,8},{10,11... | collective-permute-start | bytes 1572872 | tf_op jit(solution)/shard_map/ppermute | solution.py:34
  122.6 4.4 %collective-permute-start.4 = (bf16[256,512]{1,0:T(8,128)(2,1)S(1)}, bf16[256,512]{1,0:T(8,128)(2,1)S(1)}, u32[]{:S(2)}, u32[]{:S(2)}) collective-permute-start(bf16[256,512]{1,0:T(8,128)(2,1)S(1)} %copy-done.6), channel_id=1, source_target_pairs={{0,1},{1,0},{2,3},{3,2},{4,5},{5,4},{6,7},{7,6},{8,9},{9,8},{10,11... | collective-permute-start | bytes 786440 | tf_op jit(solution)/shard_map/ppermute | solution.py:34
  125.0 3.4 %collective-permute-start.5 = (bf16[256,512]{1,0:T(8,128)(2,1)S(1)}, bf16[256,512]{1,0:T(8,128)(2,1)S(1)}, u32[]{:S(2)}, u32[]{:S(2)}) collective-permute-start(bf16[256,512]{1,0:T(8,128)(2,1)S(1)} %copy-done.7), channel_id=1, source_target_pairs={{0,1},{1,0},{2,3},{3,2},{4,5},{5,4},{6,7},{7,6},{8,9},{9,8},{10,11... | collective-permute-start | bytes 786440 | tf_op jit(solution)/shard_map/ppermute | solution.py:34
  126.9 1.5 copy-start.11
  128.4 0.7 copy-start.13
  129.1 0.8 copy-start.9
  141.9 2.1 %copy-start.8 = (bf16[256,512]{1,0:T(8,128)(2,1)S(1)}, bf16[256,512]{1,0:T(8,128)(2,1)}, u32[]{:S(2)}) copy-start(bf16[256,512]{1,0:T(8,128)(2,1)} %param.12) | copy-start | bytes 786436
  142.5 1.8 copy-start.14
  144.4 1.6 copy-start.12
  148.5 13.7 %all-to-all-start.4 = ((bf16[8,64,256]{2,1,0:T(8,128)(2,1)}), bf16[8,64,256]{2,1,0:T(8,128)(2,1)S(1)}, u32[]{:S(2)}, u32[]{:S(2)}) async-start(bf16[8,64,256]{2,1,0:T(8,128)(2,1)} %bitcast.40), calls=%async_computation.4 | async-start | bytes 524288 | tf_op jit(solution)/shard_map/all_to_all | solution.py:66
  153.2 24.9 %collective-permute-start.9 = (bf16[512,512]{1,0:T(8,128)(2,1)}, bf16[512,512]{1,0:T(8,128)(2,1)}, u32[]{:S(2)}, u32[]{:S(2)}) collective-permute-start(bf16[512,512]{1,0:T(8,128)(2,1)} %slice.74), channel_id=1, source_target_pairs={{0,1},{1,0},{2,3},{3,2},{4,5},{5,4},{6,7},{7,6},{8,9},{9,8},{10,11... | collective-permute-start | bytes 1572872 | tf_op jit(solution)/shard_map/ppermute | solution.py:34
  160.9 17.2 %copy-start.1 = (bf16[8,1,64,1024]{3,2,1,0:T(8,128)(2,1)S(1)}, bf16[8,1,64,1024]{3,2,1,0:T(8,128)(2,1)}, u32[]{:S(2)}) copy-start(bf16[8,1,64,1024]{3,2,1,0:T(8,128)(2,1)} %copy-done) | copy-start | bytes 3145732
  160.9 17.2 %copy-start.3 = (f32[256,512]{1,0:T(8,128)S(1)}, f32[256,512]{1,0:T(8,128)}, u32[]{:S(2)}) copy-start(f32[256,512]{1,0:T(8,128)} %fusion.55) | copy-start | bytes 1572868
  162.3 22.0 %collective-permute-start.8 = (bf16[32,256]{1,0:T(8,128)(2,1)S(1)}, bf16[32,256]{1,0:T(8,128)(2,1)S(1)}, u32[]{:S(2)}, u32[]{:S(2)}) collective-permute-start(bf16[32,256]{1,0:T(8,128)(2,1)S(1)} %get-tuple-element.64), channel_id=1, source_target_pairs={{16,0},{48,1},{80,2},{112,3},{144,4},{176,5},{208,6},{240,7},{272,... | collective-permute-start | bytes 49160 | tf_op jit(solution)/shard_map/ppermute | solution.py:52
  170.9 9.6 %copy-start.4 = (f32[256,512]{1,0:T(8,128)S(1)}, f32[256,512]{1,0:T(8,128)}, u32[]{:S(2)}) copy-start(f32[256,512]{1,0:T(8,128)} %fusion.57) | copy-start | bytes 1572868
  170.9 9.6 %copy-start.10 = (bf16[512,512]{1,0:T(8,128)(2,1)S(1)}, bf16[512,512]{1,0:T(8,128)(2,1)}, u32[]{:S(2)}) copy-start(bf16[512,512]{1,0:T(8,128)(2,1)} %copy-done.9) | copy-start | bytes 1572868
  170.9 16.3 %collective-permute-start.7 = (bf16[32,256]{1,0:T(8,128)(2,1)S(1)}, bf16[32,256]{1,0:T(8,128)(2,1)S(1)}, u32[]{:S(2)}, u32[]{:S(2)}) collective-permute-start(bf16[32,256]{1,0:T(8,128)(2,1)S(1)} %get-tuple-element.65), channel_id=1, source_target_pairs={{0,0},{32,1},{64,2},{96,3},{128,4},{160,5},{192,6},{224,7},{256,8}... | collective-permute-start | bytes 49160 | tf_op jit(solution)/shard_map/ppermute | solution.py:51
  180.5 2.5 %copy-start.15 = (f32[512,256]{1,0:T(8,128)S(1)}, f32[512,256]{1,0:T(8,128)}, u32[]{:S(2)}) copy-start(f32[512,256]{1,0:T(8,128)} %fusion.34) | copy-start | bytes 1572868
Sparse Core Ops, SparseCore 0:
  49.0 53.8 all-gather.1

commit v11 on v9

--- a/solution.py
+++ b/solution.py
@@ -61,10 +61,12 @@
     return choose(mine, lax.ppermute(one, AXES, IN_ONE), lax.ppermute(two, AXES, IN_TWO))
 
 
-def to_tokens(piece, odd):
+def to_tokens(piece, odd, beside):
     one, two = choose(odd, piece[32:], piece[:32])
-    high, low = choose(odd, lax.ppermute(one, AXES, OUT_ONE), lax.ppermute(two, AXES, OUT_TWO))
-    return jnp.concatenate([low, high], axis=1)
+    one, two = lax.ppermute(one, AXES, OUT_ONE), lax.ppermute(two, AXES, OUT_TWO)
+    one, two, beside = lax.optimization_barrier((one, two, beside))
+    high, low = choose(odd, one, two)
+    return (jnp.concatenate([low, high], axis=1),) + beside
 
 
 def gather_copies(block, axes, size):
@@ -105,39 +107,38 @@
     down = jnp.concatenate([down, swap(down)], axis=0)
     partial = contract_cols(cols[:, :512], down).astype(jnp.bfloat16)
     hidden_grad = scatter_sum(partial, HALF, C)
-    cols_y = swap(cols[:, 256:768], "yl")
-    hidden_grad, pre, cols, cols_y = lax.optimization_barrier((hidden_grad, pre, cols, cols_y))
+    hidden_grad, pre, cols, gate_other, up_other = lax.optimization_barrier(
+        (hidden_grad, pre, cols, swap(gate_weight), swap(up_weight))
+    )
 
     hidden_grad = gather_copies(hidden_grad, ROW, R)
-    pre_mine, pre_theirs = choose(core == 1, *(pre.reshape(8, 2, 64, 1024)[:, at] for at in (1, 0)))
-    pre_mine, pre_theirs = pre_mine.reshape(512, 1024), swap(pre_theirs.reshape(512, 1024))
+    pre = pre.reshape(8, 2, 64, 1024)
+    pre_a, pre_b = choose(core == 1, pre[:, 1], pre[:, 0])
+    pre_a, pre_b = pre_a.reshape(512, 1024), pre_b.reshape(512, 1024)
+    cols_y = swap(cols[:, 256:768], "yl").reshape(4, 64, 512)
     cols = jnp.concatenate([cols[:, :256], cols[:, 768:]], axis=1).reshape(4, 64, 512)
-    cols_y = cols_y.reshape(4, 64, 512)
     cols = jnp.stack(choose(yl == 0, cols, cols_y), axis=1).reshape(512, 512)
-    hidden_grad, pre_mine, pre_theirs, gate_other, up_other, cols, cols_x = lax.optimization_barrier(
-        (hidden_grad, pre_mine, pre_theirs, swap(gate_weight), swap(up_weight), cols, swap(cols))
+    hidden_grad, pre_a, pre_b, pre_y, cols = lax.optimization_barrier(
+        (hidden_grad, pre_a, pre_b, swap(pre_b), cols)
     )
-    gate, up, hidden = swiglu_back(hidden_grad[:, :512], pre_mine[:, :512], pre_mine[:, 512:])
-    gate_y, up_y, hidden_y = swiglu_back(hidden_grad[:, 512:], pre_theirs[:, :512], pre_theirs[:, 512:])
-    partial = contract_cols(gate, gate_weight) + contract_cols(up, up_weight)
+    cols_b = swap(cols)
+    gate_a, up_a, hidden_a = swiglu_back(hidden_grad[:, :512], pre_a[:, :512], pre_a[:, 512:])
+    gate_y, up_y, _ = swiglu_back(hidden_grad[:, 512:], pre_y[:, :512], pre_y[:, 512:])
+    partial = contract_cols(gate_a, gate_weight) + contract_cols(up_a, up_weight)
     partial = partial + contract_cols(gate_y, gate_other) + contract_cols(up_y, up_other)
     summed = scatter_sum(partial, PLANE, 8)
-
-    grads, tokens = cols[:, :256], cols[:, 256:]
-    grads_x, tokens_x = cols_x[:, :256], cols_x[:, 256:]
-    swapped = swap(jnp.concatenate([gate_y, up_y, hidden_y], axis=1))
-    summed, swapped = lax.optimization_barrier((summed, swapped))
-    gate_x, up_x, hidden_x = swapped[:, :512], swapped[:, 512:1024], swapped[:, 1024:]
-    input_grad = to_tokens(summed, odd)
-    gate_weight_grad = contract_rows(tokens, gate) + contract_rows(tokens_x, gate_x)
-    up_weight_grad = contract_rows(tokens, up) + contract_rows(tokens_x, up_x)
-    down_weight_grad = contract_rows(hidden, grads) + contract_rows(hidden_x, grads_x)
-    return (
-        input_grad,
-        gate_weight_grad.astype(jnp.bfloat16),
-        up_weight_grad.astype(jnp.bfloat16),
-        down_weight_grad.astype(jnp.bfloat16),
+    hidden_grad_b, pre_b = lax.optimization_barrier((swap(hidden_grad[:, 512:]), pre_b))
+    gate_b, up_b, hidden_b = swiglu_back(hidden_grad_b, pre_b[:, :512], pre_b[:, 512:])
+    grads_a, tokens_a = cols[:, :256], cols[:, 256:]
+    grads_b, tokens_b = cols_b[:, :256], cols_b[:, 256:]
+    products = contract_rows(tokens_a, gate_a), contract_rows(tokens_a, up_a), contract_rows(hidden_a, grads_a)
+    summed, products = lax.optimization_barrier((summed, products))
+    weight_grads = (
+        (products[0] + contract_rows(tokens_b, gate_b)).astype(jnp.bfloat16),
+        (products[1] + contract_rows(tokens_b, up_b)).astype(jnp.bfloat16),
+        (products[2] + contract_rows(hidden_b, grads_b)).astype(jnp.bfloat16),
     )
+    return to_tokens(summed, odd, weight_grads)
 
 
 def solution(mesh):

time: 199 us -> 195 us (0.980)
  waiting for transfers between devices: 68.1 us -> 59.8 us
  matrix products: 11.3 us -> 16.7 us
    all_to_all x3, waiting for transfers between devices: 13.4 us -> 1.14 us  [gather_copies(): got = lax.all_to_all(copies, axes, 0, 0, tiled=True)]
    ppermute x8, waiting for transfers between devices: 9.21 us -> 20.2 us  [swap(): return lax.ppermute(value, axis, [(0, 1), (1, 0)])]
    ppermute x1, starting transfers between devices: 6.17 us -> 13.7 us  [to_tokens(): lax.ppermute(one, AXES, OUT_ONE)]
    ppermute x1, starting transfers between devices: 9.63 us -> 2.77 us  [to_tokens(): lax.ppermute(two, AXES, OUT_TWO)]
    ppermute x1, waiting for transfers between devices: 6.45 us -> 0.01 us  [to_tokens(): lax.ppermute(one, AXES, OUT_ONE)]
    all_to_all x2, waiting for transfers between devices: 26.1 us -> 19.9 us  [scatter_sum(): got = lax.all_to_all(pieces, axes, 0, 0, tiled=True)]
    ppermute x1, waiting for transfers between devices: 0.01 us -> 3.79 us  [to_tokens(): lax.ppermute(two, AXES, OUT_TWO)]
    dot_general x6, matrix products: 7.86 us -> 10.7 us  [contract_rows(): lax.dot_general(left, right, (((0,), (0,)), ((), ())), preferred_element_...]
  transfers between devices with their start and end apart: 18 -> 18, of which waited for: 10 -> 8; matrix products, arithmetic and copies ran while one was open for 5% -> 10% of each run, Pallas kernels for 0% -> 0%
where the time goes in v11:
time: 195 us; the launch traced here: 194 us
  starting transfers between devices  92.6 us (47%)
  waiting for transfers between devices  59.8 us (31%)
  matrix products  16.7 us (9%)
  between operations  14.5 us (7%)
  other arithmetic  5.82 us (3%)
  local copies, waits for them, and re-layouts  4.37 us (2%)
    all_to_all x3, starting transfers between devices, gather_copies(): got = lax.all_to_all(copies, axes, 0, 0, tiled=True)  25.6 us
    ppermute x8, starting transfers between devices, swap(): return lax.ppermute(value, axis, [(0, 1), (1, 0)])  25.1 us
    ppermute x8, waiting for transfers between devices, swap(): return lax.ppermute(value, axis, [(0, 1), (1, 0)])  20.2 us
    all_to_all x2, waiting for transfers between devices, scatter_sum(): got = lax.all_to_all(pieces, axes, 0, 0, tiled=True)  19.9 us
    ppermute x1, starting transfers between devices, to_tokens(): lax.ppermute(one, AXES, OUT_ONE)  13.7 us
    ppermute x1, starting transfers between devices, to_features(): lax.ppermute(two, AXES, IN_TWO)  11.2 us
    ppermute x1, waiting for transfers between devices, to_features(): lax.ppermute(one, AXES, IN_ONE)  10.9 us
    dot_general x6, matrix products, contract_rows(): lax.dot_general(left, right, (((0,), (0,)), ((), ())), preferred_element_...  10.7 us
  transfers between devices with their start and end apart: 18, of which 8 were waited for; matrix products, arithmetic and copies ran while one was open for 10% of the time, Pallas kernels for 0%

profile of v11, /device:TPU:5, one launch (start us, length us, event | category | flops | bytes accessed | tf_op | source)
XLA Modules:
  0.0 193.8 jit_solution(10429913227765465012)
XLA Ops:
  7.2 0.8 pad_maximum_fusion.2
  8.0 0.7 broadcast_in_dim.6
  8.7 10.0 %all-to-all-start = ((bf16[4,32,1024]{2,1,0:T(8,128)(2,1)}), bf16[4,32,1024]{2,1,0:T(8,128)(2,1)S(1)}, u32[]{:S(2)}, u32[]{:S(2)}) async-start(bf16[4,32,1024]{2,1,0:T(8,128)(2,1)} %broadcast_in_dim.6), calls=%async_computation | async-start | bytes 524288 | tf_op jit(solution)/shard_map/all_to_all | solution.py:74
  18.8 3.2 %collective-permute-start.2 = (bf16[512,256]{1,0:T(8,128)(2,1)}, bf16[512,256]{1,0:T(8,128)(2,1)S(1)}, u32[]{:S(2)}, u32[]{:S(2)}) collective-permute-start(bf16[512,256]{1,0:T(8,128)(2,1)} %param.13), channel_id=1, source_target_pairs={{0,64},{64,0},{1,65},{65,1},{2,66},{66,2},{3,67},{67,3},{4,68},{68... | collective-permute-start | bytes 786440 | tf_op jit(solution)/shard_map/ppermute | solution.py:52
  22.0 0.8 broadcast_select_fusion.4
  22.8 11.2 %collective-permute-start.1 = (bf16[2,32,256]{2,1,0:T(8,128)(2,1)S(1)}, bf16[2,32,256]{2,1,0:T(8,128)(2,1)S(1)}, u32[]{:S(2)}, u32[]{:S(2)}) collective-permute-start(bf16[2,32,256]{2,1,0:T(8,128)(2,1)S(1)} %get-tuple-element.64), channel_id=1, source_target_pairs={{0,16},{1,48},{2,0},{3,32},{4,144},{5,176},{6,128},{7,160},{8,272}... | collective-permute-start | bytes 98312 | tf_op jit(solution)/shard_map/ppermute | solution.py:61
  34.0 5.8 %collective-permute-start = (bf16[2,32,256]{2,1,0:T(8,128)(2,1)S(1)}, bf16[2,32,256]{2,1,0:T(8,128)(2,1)S(1)}, u32[]{:S(2)}, u32[]{:S(2)}) collective-permute-start(bf16[2,32,256]{2,1,0:T(8,128)(2,1)S(1)} %get-tuple-element.65), channel_id=1, source_target_pairs={{0,0},{1,32},{2,16},{3,48},{4,128},{5,160},{6,144},{7,176},{8,256}... | collective-permute-start | bytes 98312 | tf_op jit(solution)/shard_map/ppermute | solution.py:61
  39.8 10.9 %collective-permute-done = bf16[2,32,256]{2,1,0:T(8,128)(2,1)S(1)} collective-permute-done((bf16[2,32,256]{2,1,0:T(8,128)(2,1)S(1)}, bf16[2,32,256]{2,1,0:T(8,128)(2,1)S(1)}, u32[]{:S(2)}, u32[]{:S(2)}) %collective-permute-start) | collective-permute-done | bytes 32800 | tf_op jit(solution)/shard_map/ppermute | solution.py:61
  50.7 0.7 copy-done
  51.5 0.9 broadcast_in_dim.7
  52.3 5.1 %all-to-all-start.1 = ((bf16[8,32,1024]{2,1,0:T(8,128)(2,1)}), bf16[8,32,1024]{2,1,0:T(8,128)(2,1)S(1)}, u32[]{:S(2)}, u32[]{:S(2)}) async-start(bf16[8,32,1024]{2,1,0:T(8,128)(2,1)} %broadcast_in_dim.7), calls=%async_computation.1 | async-start | bytes 1048576 | tf_op jit(solution)/shard_map/all_to_all | solution.py:74
  57.6 2.1 %collective-permute-start.3 = (bf16[512,512]{1,0:T(8,128)(2,1)S(1)}, bf16[512,512]{1,0:T(8,128)(2,1)S(1)}, u32[]{:S(2)}, u32[]{:S(2)}) collective-permute-start(bf16[512,512]{1,0:T(8,128)(2,1)S(1)} %constant_dynamic-update-slice_fusion), channel_id=1, source_target_pairs={{0,1},{1,0},{2,3},{3,2},{4,5},{5,4},{6,7},{7,6},{8,9},{9,8},{10,11... | collective-permute-start | bytes 1572872 | tf_op jit(solution)/shard_map/ppermute | solution.py:52
  59.6 1.9 collective-permute-done.3
  61.5 1.1 all-to-all-done.1
  62.6 1.3 convolution_convert_fusion
  63.9 4.0 %all-to-all-start.2 = ((bf16[16,16,1024]{2,1,0:T(8,128)(2,1)}), bf16[16,16,1024]{2,1,0:T(8,128)(2,1)S(1)}, u32[]{:S(2)}, u32[]{:S(2)}) async-start(bf16[16,16,1024]{2,1,0:T(8,128)(2,1)} %bitcast.8), calls=%async_computation.2 | async-start | bytes 1048576 | tf_op jit(solution)/shard_map/all_to_all | solution.py:80
  67.9 3.2 %collective-permute-start.4 = (bf16[256,512]{1,0:T(8,128)(2,1)S(1)}, bf16[256,512]{1,0:T(8,128)(2,1)S(1)}, u32[]{:S(2)}, u32[]{:S(2)}) collective-permute-start(bf16[256,512]{1,0:T(8,128)(2,1)S(1)} %copy-done.3), channel_id=1, source_target_pairs={{0,1},{1,0},{2,3},{3,2},{4,5},{5,4},{6,7},{7,6},{8,9},{9,8},{10,11... | collective-permute-start | bytes 786440 | tf_op jit(solution)/shard_map/ppermute | solution.py:52
  71.1 1.9 collective-permute-start.5
  73.0 19.3 %all-to-all-done.2 = bf16[16,16,1024]{2,1,0:T(8,128)(2,1)S(1)} async-done(((bf16[16,16,1024]{2,1,0:T(8,128)(2,1)}), bf16[16,16,1024]{2,1,0:T(8,128)(2,1)S(1)}, u32[]{:S(2)}, u32[]{:S(2)}) %all-to-all-start.2) | async-done | bytes 524320 | tf_op jit(solution)/shard_map/all_to_all | solution.py:80
  92.3 0.1 reduce_sum.24
  92.4 3.9 %all-gather.2.cloned.1.call-done = bf16[1024,1024]{1,0:T(8,128)(2,1)} async-done(((bf16[128,1024]{1,0:T(8,128)(2,1)}), bf16[1024,1024]{1,0:T(8,128)(2,1)}) %all-gather.2.cloned.1.call-update) | async-done | bytes 2097168 | tf_op jit(solution)/shard_map/all_gather | solution.py:104
  96.3 1.1 broadcast_in_dim.8
  97.4 10.4 %all-to-all-start.3 = ((bf16[32,16,1024]{2,1,0:T(8,128)(2,1)}), bf16[32,16,1024]{2,1,0:T(8,128)(2,1)S(1)}, u32[]{:S(2)}, u32[]{:S(2)}) async-start(bf16[32,16,1024]{2,1,0:T(8,128)(2,1)} %broadcast_in_dim.8), calls=%async_computation.3 | async-start | bytes 2097152 | tf_op jit(solution)/shard_map/all_to_all | solution.py:74
  107.9 2.7 %broadcast_select_fusion = (bf16[8,1,64,1024]{3,2,1,0:T(8,128)(2,1)}, bf16[8,1,64,1024]{3,2,1,0:T(8,128)(2,1)S(1)}) fusion(pred[]{:T(512)S(6)} %eq.21, bf16[8,2,64,1024]{3,2,1,0:T(8,128)(2,1)} %bitcast.39), kind=kLoop, calls=%fused_computation.57 | loop fusion | flops 1048576 | bytes 4194305 | tf_op jit(solution)/shard_map/jit(_where)/select_n | solution.py:56
  110.6 4.4 %collective-permute-start.6 = (bf16[512,1024]{1,0:T(8,128)(2,1)}, bf16[512,1024]{1,0:T(8,128)(2,1)}, u32[]{:S(2)}, u32[]{:S(2)}) collective-permute-start(bf16[512,1024]{1,0:T(8,128)(2,1)} %bitcast.12), channel_id=1, source_target_pairs={{0,1},{1,0},{2,3},{3,2},{4,5},{5,4},{6,7},{7,6},{8,9},{9,8},{10,11... | collective-permute-start | bytes 3145736 | tf_op jit(solution)/shard_map/ppermute | solution.py:52
  115.0 3.4 %collective-permute-start.7 = (bf16[256,512]{1,0:T(8,128)(2,1)S(1)}, bf16[256,512]{1,0:T(8,128)(2,1)S(1)}, u32[]{:S(2)}, u32[]{:S(2)}) collective-permute-start(bf16[256,512]{1,0:T(8,128)(2,1)S(1)} %slice.90), channel_id=1, source_target_pairs={{0,64},{64,0},{1,65},{65,1},{2,66},{66,2},{3,67},{67,3},{4,68},{68... | collective-permute-start | bytes 786440 | tf_op jit(solution)/shard_map/ppermute | solution.py:52
  118.5 18.3 %collective-permute-done.7 = bf16[256,512]{1,0:T(8,128)(2,1)S(1)} collective-permute-done((bf16[256,512]{1,0:T(8,128)(2,1)S(1)}, bf16[256,512]{1,0:T(8,128)(2,1)S(1)}, u32[]{:S(2)}, u32[]{:S(2)}) %collective-permute-start.7) | collective-permute-done | bytes 262176 | tf_op jit(solution)/shard_map/ppermute | solution.py:52
  136.8 0.1 broadcast_select_fusion.3
  137.0 0.8 slice.94
  137.8 0.6 fusion.5
  138.4 0.3 fusion.70
  138.7 1.1 fusion.57
  139.9 4.4 %collective-permute-start.10 = (bf16[512,512]{1,0:T(8,128)(2,1)S(1)}, bf16[512,512]{1,0:T(8,128)(2,1)}, u32[]{:S(2)}, u32[]{:S(2)}) collective-permute-start(bf16[512,512]{1,0:T(8,128)(2,1)S(1)} %bitcast.36), channel_id=1, source_target_pairs={{0,1},{1,0},{2,3},{3,2},{4,5},{5,4},{6,7},{7,6},{8,9},{9,8},{10,11... | collective-permute-start | bytes 1572872 | tf_op jit(solution)/shard_map/ppermute | solution.py:52
  144.3 1.5 fusion.42
  145.9 0.3 convolution_add_fusion.4
  146.2 2.6 %fusion.1 = bf16[512,256]{1,0:T(8,128)(2,1)} fusion(f32[512,256]{1,0:T(8,128)S(1)} %fusion.42, f32[512,256]{1,0:T(8,128)S(1)} %convolution_add_fusion.4, bf16[256,512]{1,0:T(8,128)(2,1)S(1)} %copy-done.8, bf16[512,1024]{1,0:T(8,128)(2,1)} %collective-permute-done.6, bf16[512,1024]{1,0:T(8,128)(2,1)S(1)} %bitcast.34), kind=kOutput, calls=%fused_computation.24 | convolution fusion | flops 138018816 | bytes 3145728 | tf_op jit(solution)/shard_map/dot_general | solution.py:46
  148.8 4.5 %all-to-all-start.4 = ((bf16[8,64,256]{2,1,0:T(8,128)(2,1)}), bf16[8,64,256]{2,1,0:T(8,128)(2,1)S(1)}, u32[]{:S(2)}, u32[]{:S(2)}) async-start(bf16[8,64,256]{2,1,0:T(8,128)(2,1)} %bitcast.16), calls=%async_computation.4 | async-start | bytes 524288 | tf_op jit(solution)/shard_map/all_to_all | solution.py:80
  153.3 2.5 %collective-permute-start.11 = (bf16[512,512]{1,0:T(8,128)(2,1)}, bf16[512,512]{1,0:T(8,128)(2,1)}, u32[]{:S(2)}, u32[]{:S(2)}) collective-permute-start(bf16[512,512]{1,0:T(8,128)(2,1)} %slice.94), channel_id=1, source_target_pairs={{0,1},{1,0},{2,3},{3,2},{4,5},{5,4},{6,7},{7,6},{8,9},{9,8},{10,11... | collective-permute-start | bytes 1572872 | tf_op jit(solution)/shard_map/ppermute | solution.py:52
  155.8 1.1 fusion.55
  156.9 0.5 fusion.37
  157.4 0.6 all-to-all-done.4
  158.1 13.7 %collective-permute-start.8 = (bf16[32,256]{1,0:T(8,128)(2,1)S(1)}, bf16[32,256]{1,0:T(8,128)(2,1)S(1)}, u32[]{:S(2)}, u32[]{:S(2)}) collective-permute-start(bf16[32,256]{1,0:T(8,128)(2,1)S(1)} %get-tuple-element.69), channel_id=1, source_target_pairs={{0,0},{32,1},{64,2},{96,3},{128,4},{160,5},{192,6},{224,7},{256,8}... | collective-permute-start | bytes 49160 | tf_op jit(solution)/shard_map/ppermute | solution.py:66
  171.8 2.8 %collective-permute-start.9 = (bf16[32,256]{1,0:T(8,128)(2,1)S(1)}, bf16[32,256]{1,0:T(8,128)(2,1)S(1)}, u32[]{:S(2)}, u32[]{:S(2)}) collective-permute-start(bf16[32,256]{1,0:T(8,128)(2,1)S(1)} %get-tuple-element.68), channel_id=1, source_target_pairs={{16,0},{48,1},{80,2},{112,3},{144,4},{176,5},{208,6},{240,7},{272,... | collective-permute-start | bytes 49160 | tf_op jit(solution)/shard_map/ppermute | solution.py:66
  174.6 2.8 %fusion.2 = bf16[256,512]{1,0:T(8,128)(2,1)} fusion(f32[256,512]{1,0:T(8,128)S(1)} %copy-done.1, bf16[512,512]{1,0:T(8,128)(2,1)} %collective-permute-done.11, bf16[512,1024]{1,0:T(8,128)(2,1)} %bitcast.12, bf16[512,512]{1,0:T(8,128)(2,1)} %collective-permute-done.10), kind=kOutput, calls=%fused_computation.25 | convolution fusion | flops 137887744 | bytes 2621440 | tf_op jit(solution)/shard_map/dot_general | solution.py:40
  177.5 2.5 %fusion.3 = bf16[256,512]{1,0:T(8,128)(2,1)} fusion(f32[256,512]{1,0:T(8,128)S(1)} %copy-done.2, bf16[512,512]{1,0:T(8,128)(2,1)} %collective-permute-done.11, bf16[512,1024]{1,0:T(8,128)(2,1)} %bitcast.12, bf16[512,512]{1,0:T(8,128)(2,1)} %collective-permute-done.10), kind=kOutput, calls=%fused_computation.26 | convolution fusion | flops 136577024 | bytes 2097152 | tf_op jit(solution)/shard_map/dot_general | solution.py:40
  180.0 2.5 %fusion.4 = bf16[512,256]{1,0:T(8,128)(2,1)} fusion(f32[512,256]{1,0:T(8,128)S(1)} %fusion.37, bf16[512,1024]{1,0:T(8,128)(2,1)} %bitcast.12, bf16[512,512]{1,0:T(8,128)(2,1)} %collective-permute-done.10), kind=kOutput, calls=%fused_computation.27 | convolution fusion | flops 136577024 | bytes 2097152 | tf_op jit(solution)/shard_map/dot_general | solution.py:40
  182.5 3.8 %collective-permute-done.9 = bf16[32,256]{1,0:T(8,128)(2,1)S(1)} collective-permute-done((bf16[32,256]{1,0:T(8,128)(2,1)S(1)}, bf16[32,256]{1,0:T(8,128)(2,1)S(1)}, u32[]{:S(2)}, u32[]{:S(2)}) %collective-permute-start.9) | collective-permute-done | bytes 16416 | tf_op jit(solution)/shard_map/ppermute | solution.py:66
  186.3 0.6 pad_maximum_fusion.5
  (44 shorter events, 0.3 us)
Async XLA Ops:
  7.2 50.3 %copy-start.6 = (bf16[512,256]{1,0:T(8,128)(2,1)S(1)}, bf16[512,256]{1,0:T(8,128)(2,1)}, u32[]{:S(2)}) copy-start(bf16[512,256]{1,0:T(8,128)(2,1)} %param.13) | copy-start | bytes 786436
  8.7 42.0 %all-to-all-start = ((bf16[4,32,1024]{2,1,0:T(8,128)(2,1)}), bf16[4,32,1024]{2,1,0:T(8,128)(2,1)S(1)}, u32[]{:S(2)}, u32[]{:S(2)}) async-start(bf16[4,32,1024]{2,1,0:T(8,128)(2,1)} %broadcast_in_dim.6), calls=%async_computation | async-start | bytes 524288 | tf_op jit(solution)/shard_map/all_to_all | solution.py:74
  18.7 77.6 %all-gather.2.cloned.1.call-start = ((), (), s32[]{:S(2)}) async-start(), calls=%async_computation.5 | async-start | bytes 2359296 | tf_op jit(solution)/shard_map/all_gather | solution.py:104
  18.8 31.9 %collective-permute-start.2 = (bf16[512,256]{1,0:T(8,128)(2,1)}, bf16[512,256]{1,0:T(8,128)(2,1)S(1)}, u32[]{:S(2)}, u32[]{:S(2)}) collective-permute-start(bf16[512,256]{1,0:T(8,128)(2,1)} %param.13), channel_id=1, source_target_pairs={{0,64},{64,0},{1,65},{65,1},{2,66},{66,2},{3,67},{67,3},{4,68},{68... | collective-permute-start | bytes 786440 | tf_op jit(solution)/shard_map/ppermute | solution.py:52
  22.8 17.0 %collective-permute-start.1 = (bf16[2,32,256]{2,1,0:T(8,128)(2,1)S(1)}, bf16[2,32,256]{2,1,0:T(8,128)(2,1)S(1)}, u32[]{:S(2)}, u32[]{:S(2)}) collective-permute-start(bf16[2,32,256]{2,1,0:T(8,128)(2,1)S(1)} %get-tuple-element.64), channel_id=1, source_target_pairs={{0,16},{1,48},{2,0},{3,32},{4,144},{5,176},{6,128},{7,160},{8,272}... | collective-permute-start | bytes 98312 | tf_op jit(solution)/shard_map/ppermute | solution.py:61
  34.0 16.7 %collective-permute-start = (bf16[2,32,256]{2,1,0:T(8,128)(2,1)S(1)}, bf16[2,32,256]{2,1,0:T(8,128)(2,1)S(1)}, u32[]{:S(2)}, u32[]{:S(2)}) collective-permute-start(bf16[2,32,256]{2,1,0:T(8,128)(2,1)S(1)} %get-tuple-element.65), channel_id=1, source_target_pairs={{0,0},{1,32},{2,16},{3,48},{4,128},{5,160},{6,144},{7,176},{8,256}... | collective-permute-start | bytes 98312 | tf_op jit(solution)/shard_map/ppermute | solution.py:61
  50.7 0.7 copy-start
  52.3 10.3 %all-to-all-start.1 = ((bf16[8,32,1024]{2,1,0:T(8,128)(2,1)}), bf16[8,32,1024]{2,1,0:T(8,128)(2,1)S(1)}, u32[]{:S(2)}, u32[]{:S(2)}) async-start(bf16[8,32,1024]{2,1,0:T(8,128)(2,1)} %broadcast_in_dim.7), calls=%async_computation.1 | async-start | bytes 1048576 | tf_op jit(solution)/shard_map/all_to_all | solution.py:74
  57.5 10.4 %copy-start.3 = (bf16[256,512]{1,0:T(8,128)(2,1)S(1)}, bf16[256,512]{1,0:T(8,128)(2,1)}, u32[]{:S(2)}) copy-start(bf16[256,512]{1,0:T(8,128)(2,1)} %param.11) | copy-start | bytes 786436
  57.5 13.6 %copy-start.4 = (bf16[256,512]{1,0:T(8,128)(2,1)S(1)}, bf16[256,512]{1,0:T(8,128)(2,1)}, u32[]{:S(2)}) copy-start(bf16[256,512]{1,0:T(8,128)(2,1)} %param.12) | copy-start | bytes 786436
  57.6 3.9 %collective-permute-start.3 = (bf16[512,512]{1,0:T(8,128)(2,1)S(1)}, bf16[512,512]{1,0:T(8,128)(2,1)S(1)}, u32[]{:S(2)}, u32[]{:S(2)}) collective-permute-start(bf16[512,512]{1,0:T(8,128)(2,1)S(1)} %constant_dynamic-update-slice_fusion), channel_id=1, source_target_pairs={{0,1},{1,0},{2,3},{3,2},{4,5},{5,4},{6,7},{7,6},{8,9},{9,8},{10,11... | collective-permute-start | bytes 1572872 | tf_op jit(solution)/shard_map/ppermute | solution.py:52
  63.9 28.4 %all-to-all-start.2 = ((bf16[16,16,1024]{2,1,0:T(8,128)(2,1)}), bf16[16,16,1024]{2,1,0:T(8,128)(2,1)S(1)}, u32[]{:S(2)}, u32[]{:S(2)}) async-start(bf16[16,16,1024]{2,1,0:T(8,128)(2,1)} %bitcast.8), calls=%async_computation.2 | async-start | bytes 1048576 | tf_op jit(solution)/shard_map/all_to_all | solution.py:80
  67.9 24.5 %collective-permute-start.4 = (bf16[256,512]{1,0:T(8,128)(2,1)S(1)}, bf16[256,512]{1,0:T(8,128)(2,1)S(1)}, u32[]{:S(2)}, u32[]{:S(2)}) collective-permute-start(bf16[256,512]{1,0:T(8,128)(2,1)S(1)} %copy-done.3), channel_id=1, source_target_pairs={{0,1},{1,0},{2,3},{3,2},{4,5},{5,4},{6,7},{7,6},{8,9},{9,8},{10,11... | collective-permute-start | bytes 786440 | tf_op jit(solution)/shard_map/ppermute | solution.py:52
  71.1 21.3 %collective-permute-start.5 = (bf16[256,512]{1,0:T(8,128)(2,1)S(1)}, bf16[256,512]{1,0:T(8,128)(2,1)S(1)}, u32[]{:S(2)}, u32[]{:S(2)}) collective-permute-start(bf16[256,512]{1,0:T(8,128)(2,1)S(1)} %copy-done.4), channel_id=1, source_target_pairs={{0,1},{1,0},{2,3},{3,2},{4,5},{5,4},{6,7},{7,6},{8,9},{9,8},{10,11... | collective-permute-start | bytes 786440 | tf_op jit(solution)/shard_map/ppermute | solution.py:52
  92.4 15.5 %copy-start.7 = (bf16[256,512]{1,0:T(8,128)(2,1)}, bf16[256,512]{1,0:T(8,128)(2,1)S(1)}, u32[]{:S(2)}) copy-start(bf16[256,512]{1,0:T(8,128)(2,1)S(1)} %collective-permute-done.4) | copy-start | bytes 786436
  92.4 15.5 %copy-start.9 = (bf16[256,512]{1,0:T(8,128)(2,1)}, bf16[256,512]{1,0:T(8,128)(2,1)S(1)}, u32[]{:S(2)}) copy-start(bf16[256,512]{1,0:T(8,128)(2,1)S(1)} %collective-permute-done.5) | copy-start | bytes 786436
  97.4 39.6 %all-to-all-start.3 = ((bf16[32,16,1024]{2,1,0:T(8,128)(2,1)}), bf16[32,16,1024]{2,1,0:T(8,128)(2,1)S(1)}, u32[]{:S(2)}, u32[]{:S(2)}) async-start(bf16[32,16,1024]{2,1,0:T(8,128)(2,1)} %broadcast_in_dim.8), calls=%async_computation.3 | async-start | bytes 2097152 | tf_op jit(solution)/shard_map/all_to_all | solution.py:74
  110.6 26.4 %collective-permute-start.6 = (bf16[512,1024]{1,0:T(8,128)(2,1)}, bf16[512,1024]{1,0:T(8,128)(2,1)}, u32[]{:S(2)}, u32[]{:S(2)}) collective-permute-start(bf16[512,1024]{1,0:T(8,128)(2,1)} %bitcast.12), channel_id=1, source_target_pairs={{0,1},{1,0},{2,3},{3,2},{4,5},{5,4},{6,7},{7,6},{8,9},{9,8},{10,11... | collective-permute-start | bytes 3145736 | tf_op jit(solution)/shard_map/ppermute | solution.py:52
  115.0 21.8 %collective-permute-start.7 = (bf16[256,512]{1,0:T(8,128)(2,1)S(1)}, bf16[256,512]{1,0:T(8,128)(2,1)S(1)}, u32[]{:S(2)}, u32[]{:S(2)}) collective-permute-start(bf16[256,512]{1,0:T(8,128)(2,1)S(1)} %slice.90), channel_id=1, source_target_pairs={{0,64},{64,0},{1,65},{65,1},{2,66},{66,2},{3,67},{67,3},{4,68},{68... | collective-permute-start | bytes 786440 | tf_op jit(solution)/shard_map/ppermute | solution.py:52
  137.8 6.5 %copy-start.10 = (bf16[256,512]{1,0:T(8,128)(2,1)S(1)}, bf16[256,512]{1,0:T(8,128)(2,1)}, u32[]{:S(2)}) copy-start(bf16[256,512]{1,0:T(8,128)(2,1)} %copy-done.9) | copy-start | bytes 786436
  139.9 6.0 %copy-start.5 = (bf16[256,512]{1,0:T(8,128)(2,1)S(1)}, bf16[256,512]{1,0:T(8,128)(2,1)}, u32[]{:S(2)}) copy-start(bf16[256,512]{1,0:T(8,128)(2,1)} %param.12) | copy-start | bytes 786436
  139.9 6.4 %copy-start.8 = (bf16[256,512]{1,0:T(8,128)(2,1)S(1)}, bf16[256,512]{1,0:T(8,128)(2,1)}, u32[]{:S(2)}) copy-start(bf16[256,512]{1,0:T(8,128)(2,1)} %copy-done.7) | copy-start | bytes 786436
  139.9 34.7 %collective-permute-start.10 = (bf16[512,512]{1,0:T(8,128)(2,1)S(1)}, bf16[512,512]{1,0:T(8,128)(2,1)}, u32[]{:S(2)}, u32[]{:S(2)}) collective-permute-start(bf16[512,512]{1,0:T(8,128)(2,1)S(1)} %bitcast.36), channel_id=1, source_target_pairs={{0,1},{1,0},{2,3},{3,2},{4,5},{5,4},{6,7},{7,6},{8,9},{9,8},{10,11... | collective-permute-start | bytes 1572872 | tf_op jit(solution)/shard_map/ppermute | solution.py:52
  148.8 9.2 %all-to-all-start.4 = ((bf16[8,64,256]{2,1,0:T(8,128)(2,1)}), bf16[8,64,256]{2,1,0:T(8,128)(2,1)S(1)}, u32[]{:S(2)}, u32[]{:S(2)}) async-start(bf16[8,64,256]{2,1,0:T(8,128)(2,1)} %bitcast.16), calls=%async_computation.4 | async-start | bytes 524288 | tf_op jit(solution)/shard_map/all_to_all | solution.py:80
  153.3 21.3 %collective-permute-start.11 = (bf16[512,512]{1,0:T(8,128)(2,1)}, bf16[512,512]{1,0:T(8,128)(2,1)}, u32[]{:S(2)}, u32[]{:S(2)}) collective-permute-start(bf16[512,512]{1,0:T(8,128)(2,1)} %slice.94), channel_id=1, source_target_pairs={{0,1},{1,0},{2,3},{3,2},{4,5},{5,4},{6,7},{7,6},{8,9},{9,8},{10,11... | collective-permute-start | bytes 1572872 | tf_op jit(solution)/shard_map/ppermute | solution.py:52
  156.9 17.7 %copy-start.1 = (f32[256,512]{1,0:T(8,128)S(1)}, f32[256,512]{1,0:T(8,128)}, u32[]{:S(2)}) copy-start(f32[256,512]{1,0:T(8,128)} %fusion.57) | copy-start | bytes 1572868
  158.1 24.5 %collective-permute-start.8 = (bf16[32,256]{1,0:T(8,128)(2,1)S(1)}, bf16[32,256]{1,0:T(8,128)(2,1)S(1)}, u32[]{:S(2)}, u32[]{:S(2)}) collective-permute-start(bf16[32,256]{1,0:T(8,128)(2,1)S(1)} %get-tuple-element.69), channel_id=1, source_target_pairs={{0,0},{32,1},{64,2},{96,3},{128,4},{160,5},{192,6},{224,7},{256,8}... | collective-permute-start | bytes 49160 | tf_op jit(solution)/shard_map/ppermute | solution.py:66
  171.8 5.7 %copy-start.2 = (f32[256,512]{1,0:T(8,128)S(1)}, f32[256,512]{1,0:T(8,128)}, u32[]{:S(2)}) copy-start(f32[256,512]{1,0:T(8,128)} %fusion.55) | copy-start | bytes 1572868
  171.8 14.5 %collective-permute-start.9 = (bf16[32,256]{1,0:T(8,128)(2,1)S(1)}, bf16[32,256]{1,0:T(8,128)(2,1)S(1)}, u32[]{:S(2)}, u32[]{:S(2)}) collective-permute-start(bf16[32,256]{1,0:T(8,128)(2,1)S(1)} %get-tuple-element.68), channel_id=1, source_target_pairs={{16,0},{48,1},{80,2},{112,3},{144,4},{176,5},{208,6},{240,7},{272,... | collective-permute-start | bytes 49160 | tf_op jit(solution)/shard_map/ppermute | solution.py:66
Sparse Core Ops, SparseCore 0:
  51.6 44.7 all-gather.1

commit v12 on v11

--- a/solution.py
+++ b/solution.py
@@ -107,8 +107,8 @@
     down = jnp.concatenate([down, swap(down)], axis=0)
     partial = contract_cols(cols[:, :512], down).astype(jnp.bfloat16)
     hidden_grad = scatter_sum(partial, HALF, C)
-    hidden_grad, pre, cols, gate_other, up_other = lax.optimization_barrier(
-        (hidden_grad, pre, cols, swap(gate_weight), swap(up_weight))
+    hidden_grad, cols, gate_other, up_other = lax.optimization_barrier(
+        (hidden_grad, cols, swap(gate_weight), swap(up_weight))
     )
 
     hidden_grad = gather_copies(hidden_grad, ROW, R)
@@ -121,18 +121,23 @@
     hidden_grad, pre_a, pre_b, pre_y, cols = lax.optimization_barrier(
         (hidden_grad, pre_a, pre_b, swap(pre_b), cols)
     )
-    cols_b = swap(cols)
-    gate_a, up_a, hidden_a = swiglu_back(hidden_grad[:, :512], pre_a[:, :512], pre_a[:, 512:])
-    gate_y, up_y, _ = swiglu_back(hidden_grad[:, 512:], pre_y[:, :512], pre_y[:, 512:])
+    made_a = swiglu_back(hidden_grad[:, :512], pre_a[:, :512], pre_a[:, 512:])
+    made_y = swiglu_back(hidden_grad[:, 512:], pre_y[:, :512], pre_y[:, 512:])[:2]
+    (gate_a, up_a, hidden_a), (gate_y, up_y) = lax.optimization_barrier((made_a, made_y))
     partial = contract_cols(gate_a, gate_weight) + contract_cols(up_a, up_weight)
     partial = partial + contract_cols(gate_y, gate_other) + contract_cols(up_y, up_other)
+    partial, cols, crossing = lax.optimization_barrier(
+        (partial.astype(jnp.bfloat16), cols, hidden_grad[:, 512:])
+    )
     summed = scatter_sum(partial, PLANE, 8)
-    hidden_grad_b, pre_b = lax.optimization_barrier((swap(hidden_grad[:, 512:]), pre_b))
-    gate_b, up_b, hidden_b = swiglu_back(hidden_grad_b, pre_b[:, :512], pre_b[:, 512:])
+    cols_b, crossed = swap(cols), swap(crossing)
+    made_b = swiglu_back(crossed, pre_b[:, :512], pre_b[:, 512:])
+
     grads_a, tokens_a = cols[:, :256], cols[:, 256:]
     grads_b, tokens_b = cols_b[:, :256], cols_b[:, 256:]
     products = contract_rows(tokens_a, gate_a), contract_rows(tokens_a, up_a), contract_rows(hidden_a, grads_a)
     summed, products = lax.optimization_barrier((summed, products))
+    gate_b, up_b, hidden_b = lax.optimization_barrier(made_b)
     weight_grads = (
         (products[0] + contract_rows(tokens_b, gate_b)).astype(jnp.bfloat16),
         (products[1] + contract_rows(tokens_b, up_b)).astype(jnp.bfloat16),

time: 195 us -> 187 us (0.959)
  starting transfers between devices: 92.6 us -> 83.4 us
  matrix products: 16.7 us -> 11.3 us
  other arithmetic: 5.82 us -> 10.5 us
    ppermute x1, waiting for transfers between devices: 0.01 us -> 12 us  [to_features(): lax.ppermute(two, AXES, IN_TWO)]
    ppermute x1, waiting for transfers between devices: 10.9 us -> 0.59 us  [to_features(): lax.ppermute(one, AXES, IN_ONE)]
    ppermute x1, starting transfers between devices: 11.2 us -> 2.81 us  [to_features(): lax.ppermute(two, AXES, IN_TWO)]
    ppermute x1, starting transfers between devices: 5.77 us -> 13 us  [to_features(): lax.ppermute(one, AXES, IN_ONE)]
    all_to_all x3, starting transfers between devices: 25.6 us -> 18.8 us  [gather_copies(): got = lax.all_to_all(copies, axes, 0, 0, tiled=True)]
    convert_element_type x1 -> x2, other arithmetic: 0.58 us -> 5.25 us  [swiglu_back(): up_grad = (grad_float * activated).astype(jnp.bfloat16)]
    all_gather x1, waiting for transfers between devices: 3.89 us -> 0.02 us  [local(): pre = lax.all_gather(pre, ('yh', 'yl'), axis=0, tiled=True)]
    ppermute x8, starting transfers between devices: 25.1 us -> 22.3 us  [swap(): return lax.ppermute(value, axis, [(0, 1), (1, 0)])]
  transfers between devices with their start and end apart: 18 -> 18, of which waited for: 8 -> 8; matrix products, arithmetic and copies ran while one was open for 10% -> 9% of each run, Pallas kernels for 0% -> 0%
where the time goes in v12:
time: 187 us; the launch traced here: 186 us
  starting transfers between devices  83.4 us (45%)
  waiting for transfers between devices  61.4 us (33%)
  between operations  14.5 us (8%)
  matrix products  11.3 us (6%)
  other arithmetic  10.5 us (6%)
  local copies, waits for them, and re-layouts  4.65 us (2%)
    ppermute x8, starting transfers between devices, swap(): return lax.ppermute(value, axis, [(0, 1), (1, 0)])  22.3 us
    all_to_all x2, waiting for transfers between devices, scatter_sum(): got = lax.all_to_all(pieces, axes, 0, 0, tiled=True)  22 us
    ppermute x8, waiting for transfers between devices, swap(): return lax.ppermute(value, axis, [(0, 1), (1, 0)])  21.5 us
    all_to_all x3, starting transfers between devices, gather_copies(): got = lax.all_to_all(copies, axes, 0, 0, tiled=True)  18.8 us
    ppermute x1, starting transfers between devices, to_tokens(): lax.ppermute(one, AXES, OUT_ONE)  14.1 us
    ppermute x1, starting transfers between devices, to_features(): lax.ppermute(one, AXES, IN_ONE)  13 us
    ppermute x1, waiting for transfers between devices, to_features(): lax.ppermute(two, AXES, IN_TWO)  12 us
    all_to_all x2, starting transfers between devices, scatter_sum(): got = lax.all_to_all(pieces, axes, 0, 0, tiled=True)  9.83 us
  transfers between devices with their start and end apart: 18, of which 8 were waited for; matrix products, arithmetic and copies ran while one was open for 9% of the time, Pallas kernels for 0%

profile of v12, /device:TPU:5, one launch (start us, length us, event | category | flops | bytes accessed | tf_op | source)
XLA Modules:
  0.0 185.7 jit_solution(4765828815670006991)
XLA Ops:
  7.2 0.8 pad_maximum_fusion.2
  8.0 0.7 broadcast_in_dim.6
  8.7 10.0 %all-to-all-start = ((bf16[4,32,1024]{2,1,0:T(8,128)(2,1)}), bf16[4,32,1024]{2,1,0:T(8,128)(2,1)S(1)}, u32[]{:S(2)}, u32[]{:S(2)}) async-start(bf16[4,32,1024]{2,1,0:T(8,128)(2,1)} %broadcast_in_dim.6), calls=%async_computation | async-start | bytes 524288 | tf_op jit(solution)/shard_map/all_to_all | solution.py:74
  18.8 3.2 %collective-permute-start.2 = (bf16[512,256]{1,0:T(8,128)(2,1)}, bf16[512,256]{1,0:T(8,128)(2,1)S(1)}, u32[]{:S(2)}, u32[]{:S(2)}) collective-permute-start(bf16[512,256]{1,0:T(8,128)(2,1)} %param.13), channel_id=1, source_target_pairs={{0,64},{64,0},{1,65},{65,1},{2,66},{66,2},{3,67},{67,3},{4,68},{68... | collective-permute-start | bytes 786440 | tf_op jit(solution)/shard_map/ppermute | solution.py:52
  22.0 0.8 broadcast_select_fusion.4
  22.8 13.0 %collective-permute-start = (bf16[2,32,256]{2,1,0:T(8,128)(2,1)S(1)}, bf16[2,32,256]{2,1,0:T(8,128)(2,1)S(1)}, u32[]{:S(2)}, u32[]{:S(2)}) collective-permute-start(bf16[2,32,256]{2,1,0:T(8,128)(2,1)S(1)} %get-tuple-element.89), channel_id=1, source_target_pairs={{0,0},{1,32},{2,16},{3,48},{4,128},{5,160},{6,144},{7,176},{8,256}... | collective-permute-start | bytes 98312 | tf_op jit(solution)/shard_map/ppermute | solution.py:61
  35.8 2.8 %collective-permute-start.1 = (bf16[2,32,256]{2,1,0:T(8,128)(2,1)S(1)}, bf16[2,32,256]{2,1,0:T(8,128)(2,1)S(1)}, u32[]{:S(2)}, u32[]{:S(2)}) collective-permute-start(bf16[2,32,256]{2,1,0:T(8,128)(2,1)S(1)} %get-tuple-element.88), channel_id=1, source_target_pairs={{0,16},{1,48},{2,0},{3,32},{4,144},{5,176},{6,128},{7,160},{8,272}... | collective-permute-start | bytes 98312 | tf_op jit(solution)/shard_map/ppermute | solution.py:61
  38.6 0.6 collective-permute-done
  39.2 12.0 %collective-permute-done.1 = bf16[2,32,256]{2,1,0:T(8,128)(2,1)S(1)} collective-permute-done((bf16[2,32,256]{2,1,0:T(8,128)(2,1)S(1)}, bf16[2,32,256]{2,1,0:T(8,128)(2,1)S(1)}, u32[]{:S(2)}, u32[]{:S(2)}) %collective-permute-start.1) | collective-permute-done | bytes 32800 | tf_op jit(solution)/shard_map/ppermute | solution.py:61
  51.3 0.7 copy-done
  52.0 0.9 broadcast_in_dim.7
  52.9 4.2 %all-to-all-start.1 = ((bf16[8,32,1024]{2,1,0:T(8,128)(2,1)}), bf16[8,32,1024]{2,1,0:T(8,128)(2,1)S(1)}, u32[]{:S(2)}, u32[]{:S(2)}) async-start(bf16[8,32,1024]{2,1,0:T(8,128)(2,1)} %broadcast_in_dim.7), calls=%async_computation.1 | async-start | bytes 1048576 | tf_op jit(solution)/shard_map/all_to_all | solution.py:74
  57.2 2.1 %collective-permute-start.3 = (bf16[512,512]{1,0:T(8,128)(2,1)S(1)}, bf16[512,512]{1,0:T(8,128)(2,1)S(1)}, u32[]{:S(2)}, u32[]{:S(2)}) collective-permute-start(bf16[512,512]{1,0:T(8,128)(2,1)S(1)} %constant_dynamic-update-slice_fusion), channel_id=1, source_target_pairs={{0,1},{1,0},{2,3},{3,2},{4,5},{5,4},{6,7},{7,6},{8,9},{9,8},{10,11... | collective-permute-start | bytes 1572872 | tf_op jit(solution)/shard_map/ppermute | solution.py:52
  59.3 1.9 %collective-permute-done.3 = bf16[512,512]{1,0:T(8,128)(2,1)S(1)} collective-permute-done((bf16[512,512]{1,0:T(8,128)(2,1)S(1)}, bf16[512,512]{1,0:T(8,128)(2,1)S(1)}, u32[]{:S(2)}, u32[]{:S(2)}) %collective-permute-start.3) | collective-permute-done | bytes 524320 | tf_op jit(solution)/shard_map/ppermute | solution.py:52
  61.2 1.2 all-to-all-done.1
  62.3 1.3 convolution_convert_fusion
  63.6 4.0 %all-to-all-start.2 = ((bf16[16,16,1024]{2,1,0:T(8,128)(2,1)}), bf16[16,16,1024]{2,1,0:T(8,128)(2,1)S(1)}, u32[]{:S(2)}, u32[]{:S(2)}) async-start(bf16[16,16,1024]{2,1,0:T(8,128)(2,1)} %bitcast.8), calls=%async_computation.2 | async-start | bytes 1048576 | tf_op jit(solution)/shard_map/all_to_all | solution.py:80
  67.6 2.2 %collective-permute-start.4 = (bf16[256,512]{1,0:T(8,128)(2,1)S(1)}, bf16[256,512]{1,0:T(8,128)(2,1)S(1)}, u32[]{:S(2)}, u32[]{:S(2)}) collective-permute-start(bf16[256,512]{1,0:T(8,128)(2,1)S(1)} %copy-done.1), channel_id=1, source_target_pairs={{0,1},{1,0},{2,3},{3,2},{4,5},{5,4},{6,7},{7,6},{8,9},{9,8},{10,11... | collective-permute-start | bytes 786440 | tf_op jit(solution)/shard_map/ppermute | solution.py:52
  69.8 2.1 %collective-permute-start.5 = (bf16[256,512]{1,0:T(8,128)(2,1)S(1)}, bf16[256,512]{1,0:T(8,128)(2,1)S(1)}, u32[]{:S(2)}, u32[]{:S(2)}) collective-permute-start(bf16[256,512]{1,0:T(8,128)(2,1)S(1)} %copy-done.2), channel_id=1, source_target_pairs={{0,1},{1,0},{2,3},{3,2},{4,5},{5,4},{6,7},{7,6},{8,9},{9,8},{10,11... | collective-permute-start | bytes 786440 | tf_op jit(solution)/shard_map/ppermute | solution.py:52
  72.0 21.2 %all-to-all-done.2 = bf16[16,16,1024]{2,1,0:T(8,128)(2,1)S(1)} async-done(((bf16[16,16,1024]{2,1,0:T(8,128)(2,1)}), bf16[16,16,1024]{2,1,0:T(8,128)(2,1)S(1)}, u32[]{:S(2)}, u32[]{:S(2)}) %all-to-all-start.2) | async-done | bytes 524320 | tf_op jit(solution)/shard_map/all_to_all | solution.py:80
  93.3 1.1 broadcast_in_dim.8
  94.4 4.5 %all-to-all-start.3 = ((bf16[32,16,1024]{2,1,0:T(8,128)(2,1)}), bf16[32,16,1024]{2,1,0:T(8,128)(2,1)S(1)}, u32[]{:S(2)}, u32[]{:S(2)}) async-start(bf16[32,16,1024]{2,1,0:T(8,128)(2,1)} %broadcast_in_dim.8), calls=%async_computation.3 | async-start | bytes 2097152 | tf_op jit(solution)/shard_map/all_to_all | solution.py:74
  99.0 2.7 %broadcast_select_fusion = (bf16[8,1,64,1024]{3,2,1,0:T(8,128)(2,1)S(1)}, bf16[8,1,64,1024]{3,2,1,0:T(8,128)(2,1)}) fusion(pred[]{:T(512)S(6)} %eq.21, bf16[8,2,64,1024]{3,2,1,0:T(8,128)(2,1)} %bitcast.44), kind=kLoop, calls=%fused_computation.57 | loop fusion | flops 1048576 | bytes 4194305 | tf_op jit(solution)/shard_map/jit(_where)/select_n | solution.py:56
  101.6 3.4 %collective-permute-start.6 = (bf16[512,1024]{1,0:T(8,128)(2,1)S(1)}, bf16[512,1024]{1,0:T(8,128)(2,1)}, u32[]{:S(2)}, u32[]{:S(2)}) collective-permute-start(bf16[512,1024]{1,0:T(8,128)(2,1)S(1)} %bitcast.37), channel_id=1, source_target_pairs={{0,1},{1,0},{2,3},{3,2},{4,5},{5,4},{6,7},{7,6},{8,9},{9,8},{10,11... | collective-permute-start | bytes 3145736 | tf_op jit(solution)/shard_map/ppermute | solution.py:52
  105.1 3.4 %collective-permute-start.7 = (bf16[256,512]{1,0:T(8,128)(2,1)S(1)}, bf16[256,512]{1,0:T(8,128)(2,1)S(1)}, u32[]{:S(2)}, u32[]{:S(2)}) collective-permute-start(bf16[256,512]{1,0:T(8,128)(2,1)S(1)} %slice.90), channel_id=1, source_target_pairs={{0,64},{64,0},{1,65},{65,1},{2,66},{66,2},{3,67},{67,3},{4,68},{68... | collective-permute-start | bytes 786440 | tf_op jit(solution)/shard_map/ppermute | solution.py:52
  108.5 19.6 %collective-permute-done.7 = bf16[256,512]{1,0:T(8,128)(2,1)S(1)} collective-permute-done((bf16[256,512]{1,0:T(8,128)(2,1)S(1)}, bf16[256,512]{1,0:T(8,128)(2,1)S(1)}, u32[]{:S(2)}, u32[]{:S(2)}) %collective-permute-start.7) | collective-permute-done | bytes 262176 | tf_op jit(solution)/shard_map/ppermute | solution.py:52
  128.3 0.8 slice.94
  129.2 3.6 %fusion.13 = (bf16[512,512]{1,0:T(8,128)(2,1)S(1)}, bf16[512,512]{1,0:T(8,128)(2,1)S(1)}, bf16[512,512]{1,0:T(8,128)(2,1)S(1)}, bf16[512,512]{1,0:T(8,128)(2,1)S(1)}, bf16[512,512]{1,0:T(8,128)(2,1)}) fusion(bf16[512,1024]{1,0:T(8,128)(2,1)} %collective-permute-done.6, bf16[512,1024]{1,0:T(8,128)(2,1)S(1)} %bitcast.36, bf16[512,1024]{1,0:T(8,128)(2,1)} %bitcast.39), kind=kLoop, calls=%fused_computation.36 | loop fusion | flops 8912896 | bytes 5767168 | tf_op jit(solution)/shard_map/convert_element_type | solution.py:93
  132.8 0.3 fusion.47
  133.1 0.3 convolution_add_fusion.4
  133.4 0.3 copy-done.5
  133.7 0.3 fusion.48
  134.0 1.0 fusion.1
  135.1 3.7 %collective-permute-start.11 = (bf16[512,512]{1,0:T(8,128)(2,1)}, bf16[512,512]{1,0:T(8,128)(2,1)}, u32[]{:S(2)}, u32[]{:S(2)}) collective-permute-start(bf16[512,512]{1,0:T(8,128)(2,1)} %slice.94), channel_id=1, source_target_pairs={{0,1},{1,0},{2,3},{3,2},{4,5},{5,4},{6,7},{7,6},{8,9},{9,8},{10,11... | collective-permute-start | bytes 1572872 | tf_op jit(solution)/shard_map/ppermute | solution.py:52
  138.8 0.3 fusion.40
  139.1 5.9 %all-to-all-start.4 = ((bf16[8,64,256]{2,1,0:T(8,128)(2,1)}), bf16[8,64,256]{2,1,0:T(8,128)(2,1)S(1)}, u32[]{:S(2)}, u32[]{:S(2)}) async-start(bf16[8,64,256]{2,1,0:T(8,128)(2,1)} %bitcast.51), calls=%async_computation.4 | async-start | bytes 524288 | tf_op jit(solution)/shard_map/all_to_all | solution.py:80
  145.0 0.3 fusion.42
  145.3 2.2 %collective-permute-start.10 = (bf16[512,512]{1,0:T(8,128)(2,1)S(1)}, bf16[512,512]{1,0:T(8,128)(2,1)}, u32[]{:S(2)}, u32[]{:S(2)}) collective-permute-start(bf16[512,512]{1,0:T(8,128)(2,1)S(1)} %bitcast.42), channel_id=1, source_target_pairs={{0,1},{1,0},{2,3},{3,2},{4,5},{5,4},{6,7},{7,6},{8,9},{9,8},{10,11... | collective-permute-start | bytes 1572872 | tf_op jit(solution)/shard_map/ppermute | solution.py:52
  147.5 1.4 fusion.36
  148.9 0.8 all-to-all-done.4
  149.8 14.1 %collective-permute-start.8 = (bf16[32,256]{1,0:T(8,128)(2,1)S(1)}, bf16[32,256]{1,0:T(8,128)(2,1)S(1)}, u32[]{:S(2)}, u32[]{:S(2)}) collective-permute-start(bf16[32,256]{1,0:T(8,128)(2,1)S(1)} %get-tuple-element.93), channel_id=1, source_target_pairs={{0,0},{32,1},{64,2},{96,3},{128,4},{160,5},{192,6},{224,7},{256,8}... | collective-permute-start | bytes 49160 | tf_op jit(solution)/shard_map/ppermute | solution.py:66
  163.8 2.6 %collective-permute-start.9 = (bf16[32,256]{1,0:T(8,128)(2,1)S(1)}, bf16[32,256]{1,0:T(8,128)(2,1)S(1)}, u32[]{:S(2)}, u32[]{:S(2)}) collective-permute-start(bf16[32,256]{1,0:T(8,128)(2,1)S(1)} %get-tuple-element.92), channel_id=1, source_target_pairs={{16,0},{48,1},{80,2},{112,3},{144,4},{176,5},{208,6},{240,7},{272,... | collective-permute-start | bytes 49160 | tf_op jit(solution)/shard_map/ppermute | solution.py:66
  166.5 1.7 fusion.14
  168.2 2.0 %fusion.4 = bf16[512,256]{1,0:T(8,128)(2,1)} fusion(f32[512,256]{1,0:T(8,128)S(1)} %fusion.36, bf16[512,512]{1,0:T(8,128)(2,1)S(1)} %get-tuple-element.64, bf16[512,512]{1,0:T(8,128)(2,1)} %collective-permute-done.10), kind=kOutput, calls=%fused_computation.27 | convolution fusion | flops 134479872 | bytes 1572864 | tf_op jit(solution)/shard_map/dot_general | solution.py:40
  170.2 2.0 %fusion.3 = bf16[256,512]{1,0:T(8,128)(2,1)} fusion(f32[256,512]{1,0:T(8,128)S(1)} %fusion.40, bf16[512,512]{1,0:T(8,128)(2,1)S(1)} %get-tuple-element.62, bf16[512,512]{1,0:T(8,128)(2,1)} %collective-permute-done.10), kind=kOutput, calls=%fused_computation.26 | convolution fusion | flops 134479872 | bytes 1572864 | tf_op jit(solution)/shard_map/dot_general | solution.py:40
  172.2 2.0 %fusion.2 = bf16[256,512]{1,0:T(8,128)(2,1)} fusion(f32[256,512]{1,0:T(8,128)S(1)} %fusion.42, bf16[512,512]{1,0:T(8,128)(2,1)S(1)} %get-tuple-element.60, bf16[512,512]{1,0:T(8,128)(2,1)} %collective-permute-done.10), kind=kOutput, calls=%fused_computation.25 | convolution fusion | flops 134479872 | bytes 1572864 | tf_op jit(solution)/shard_map/dot_general | solution.py:40
  174.1 4.1 %collective-permute-done.9 = bf16[32,256]{1,0:T(8,128)(2,1)S(1)} collective-permute-done((bf16[32,256]{1,0:T(8,128)(2,1)S(1)}, bf16[32,256]{1,0:T(8,128)(2,1)S(1)}, u32[]{:S(2)}, u32[]{:S(2)}) %collective-permute-start.9) | collective-permute-done | bytes 16416 | tf_op jit(solution)/shard_map/ppermute | solution.py:66
  178.2 0.6 pad_maximum_fusion.5
  (41 shorter events, 0.5 us)
Async XLA Ops:
  7.2 50.0 %copy-start.6 = (bf16[512,256]{1,0:T(8,128)(2,1)S(1)}, bf16[512,256]{1,0:T(8,128)(2,1)}, u32[]{:S(2)}) copy-start(bf16[512,256]{1,0:T(8,128)(2,1)} %param.13) | copy-start | bytes 786436
  8.7 42.5 %all-to-all-start = ((bf16[4,32,1024]{2,1,0:T(8,128)(2,1)}), bf16[4,32,1024]{2,1,0:T(8,128)(2,1)S(1)}, u32[]{:S(2)}, u32[]{:S(2)}) async-start(bf16[4,32,1024]{2,1,0:T(8,128)(2,1)} %broadcast_in_dim.6), calls=%async_computation | async-start | bytes 524288 | tf_op jit(solution)/shard_map/all_to_all | solution.py:74
  18.7 80.2 %all-gather.2.cloned.1.call-start = ((), (), s32[]{:S(2)}) async-start(), calls=%async_computation.5 | async-start | bytes 2359296 | tf_op jit(solution)/shard_map/all_gather | solution.py:104
  18.8 32.5 %collective-permute-start.2 = (bf16[512,256]{1,0:T(8,128)(2,1)}, bf16[512,256]{1,0:T(8,128)(2,1)S(1)}, u32[]{:S(2)}, u32[]{:S(2)}) collective-permute-start(bf16[512,256]{1,0:T(8,128)(2,1)} %param.13), channel_id=1, source_target_pairs={{0,64},{64,0},{1,65},{65,1},{2,66},{66,2},{3,67},{67,3},{4,68},{68... | collective-permute-start | bytes 786440 | tf_op jit(solution)/shard_map/ppermute | solution.py:52
  22.8 16.4 %collective-permute-start = (bf16[2,32,256]{2,1,0:T(8,128)(2,1)S(1)}, bf16[2,32,256]{2,1,0:T(8,128)(2,1)S(1)}, u32[]{:S(2)}, u32[]{:S(2)}) collective-permute-start(bf16[2,32,256]{2,1,0:T(8,128)(2,1)S(1)} %get-tuple-element.89), channel_id=1, source_target_pairs={{0,0},{1,32},{2,16},{3,48},{4,128},{5,160},{6,144},{7,176},{8,256}... | collective-permute-start | bytes 98312 | tf_op jit(solution)/shard_map/ppermute | solution.py:61
  35.8 15.5 %collective-permute-start.1 = (bf16[2,32,256]{2,1,0:T(8,128)(2,1)S(1)}, bf16[2,32,256]{2,1,0:T(8,128)(2,1)S(1)}, u32[]{:S(2)}, u32[]{:S(2)}) collective-permute-start(bf16[2,32,256]{2,1,0:T(8,128)(2,1)S(1)} %get-tuple-element.88), channel_id=1, source_target_pairs={{0,16},{1,48},{2,0},{3,32},{4,144},{5,176},{6,128},{7,160},{8,272}... | collective-permute-start | bytes 98312 | tf_op jit(solution)/shard_map/ppermute | solution.py:61
  51.3 0.7 copy-start
  52.9 9.4 %all-to-all-start.1 = ((bf16[8,32,1024]{2,1,0:T(8,128)(2,1)}), bf16[8,32,1024]{2,1,0:T(8,128)(2,1)S(1)}, u32[]{:S(2)}, u32[]{:S(2)}) async-start(bf16[8,32,1024]{2,1,0:T(8,128)(2,1)} %broadcast_in_dim.7), calls=%async_computation.1 | async-start | bytes 1048576 | tf_op jit(solution)/shard_map/all_to_all | solution.py:74
  57.2 10.4 %copy-start.1 = (bf16[256,512]{1,0:T(8,128)(2,1)S(1)}, bf16[256,512]{1,0:T(8,128)(2,1)}, u32[]{:S(2)}) copy-start(bf16[256,512]{1,0:T(8,128)(2,1)} %param.11) | copy-start | bytes 786436
  57.2 12.7 %copy-start.2 = (bf16[256,512]{1,0:T(8,128)(2,1)S(1)}, bf16[256,512]{1,0:T(8,128)(2,1)}, u32[]{:S(2)}) copy-start(bf16[256,512]{1,0:T(8,128)(2,1)} %param.12) | copy-start | bytes 786436
  57.2 3.9 %collective-permute-start.3 = (bf16[512,512]{1,0:T(8,128)(2,1)S(1)}, bf16[512,512]{1,0:T(8,128)(2,1)S(1)}, u32[]{:S(2)}, u32[]{:S(2)}) collective-permute-start(bf16[512,512]{1,0:T(8,128)(2,1)S(1)} %constant_dynamic-update-slice_fusion), channel_id=1, source_target_pairs={{0,1},{1,0},{2,3},{3,2},{4,5},{5,4},{6,7},{7,6},{8,9},{9,8},{10,11... | collective-permute-start | bytes 1572872 | tf_op jit(solution)/shard_map/ppermute | solution.py:52
  63.6 29.5 %all-to-all-start.2 = ((bf16[16,16,1024]{2,1,0:T(8,128)(2,1)}), bf16[16,16,1024]{2,1,0:T(8,128)(2,1)S(1)}, u32[]{:S(2)}, u32[]{:S(2)}) async-start(bf16[16,16,1024]{2,1,0:T(8,128)(2,1)} %bitcast.8), calls=%async_computation.2 | async-start | bytes 1048576 | tf_op jit(solution)/shard_map/all_to_all | solution.py:80
  67.6 25.6 %collective-permute-start.4 = (bf16[256,512]{1,0:T(8,128)(2,1)S(1)}, bf16[256,512]{1,0:T(8,128)(2,1)S(1)}, u32[]{:S(2)}, u32[]{:S(2)}) collective-permute-start(bf16[256,512]{1,0:T(8,128)(2,1)S(1)} %copy-done.1), channel_id=1, source_target_pairs={{0,1},{1,0},{2,3},{3,2},{4,5},{5,4},{6,7},{7,6},{8,9},{9,8},{10,11... | collective-permute-start | bytes 786440 | tf_op jit(solution)/shard_map/ppermute | solution.py:52
  69.8 23.4 %collective-permute-start.5 = (bf16[256,512]{1,0:T(8,128)(2,1)S(1)}, bf16[256,512]{1,0:T(8,128)(2,1)S(1)}, u32[]{:S(2)}, u32[]{:S(2)}) collective-permute-start(bf16[256,512]{1,0:T(8,128)(2,1)S(1)} %copy-done.2), channel_id=1, source_target_pairs={{0,1},{1,0},{2,3},{3,2},{4,5},{5,4},{6,7},{7,6},{8,9},{9,8},{10,11... | collective-permute-start | bytes 786440 | tf_op jit(solution)/shard_map/ppermute | solution.py:52
  93.2 1.2 copy-start.7
  93.2 5.7 %copy-start.4 = (bf16[256,512]{1,0:T(8,128)(2,1)}, bf16[256,512]{1,0:T(8,128)(2,1)S(1)}, u32[]{:S(2)}) copy-start(bf16[256,512]{1,0:T(8,128)(2,1)S(1)} %collective-permute-done.5) | copy-start | bytes 786436
  94.4 34.0 %all-to-all-start.3 = ((bf16[32,16,1024]{2,1,0:T(8,128)(2,1)}), bf16[32,16,1024]{2,1,0:T(8,128)(2,1)S(1)}, u32[]{:S(2)}, u32[]{:S(2)}) async-start(bf16[32,16,1024]{2,1,0:T(8,128)(2,1)} %broadcast_in_dim.8), calls=%async_computation.3 | async-start | bytes 2097152 | tf_op jit(solution)/shard_map/all_to_all | solution.py:74
  101.6 26.7 %collective-permute-start.6 = (bf16[512,1024]{1,0:T(8,128)(2,1)S(1)}, bf16[512,1024]{1,0:T(8,128)(2,1)}, u32[]{:S(2)}, u32[]{:S(2)}) collective-permute-start(bf16[512,1024]{1,0:T(8,128)(2,1)S(1)} %bitcast.37), channel_id=1, source_target_pairs={{0,1},{1,0},{2,3},{3,2},{4,5},{5,4},{6,7},{7,6},{8,9},{9,8},{10,11... | collective-permute-start | bytes 3145736 | tf_op jit(solution)/shard_map/ppermute | solution.py:52
  105.1 23.1 %collective-permute-start.7 = (bf16[256,512]{1,0:T(8,128)(2,1)S(1)}, bf16[256,512]{1,0:T(8,128)(2,1)S(1)}, u32[]{:S(2)}, u32[]{:S(2)}) collective-permute-start(bf16[256,512]{1,0:T(8,128)(2,1)S(1)} %slice.90), channel_id=1, source_target_pairs={{0,64},{64,0},{1,65},{65,1},{2,66},{66,2},{3,67},{67,3},{4,68},{68... | collective-permute-start | bytes 786440 | tf_op jit(solution)/shard_map/ppermute | solution.py:52
  129.2 3.9 %copy-start.3 = (bf16[256,512]{1,0:T(8,128)(2,1)S(1)}, bf16[256,512]{1,0:T(8,128)(2,1)}, u32[]{:S(2)}) copy-start(bf16[256,512]{1,0:T(8,128)(2,1)} %param.12) | copy-start | bytes 786436
  132.7 0.9 copy-start.5
  132.8 1.3 copy-start.8
  135.1 31.4 %collective-permute-start.11 = (bf16[512,512]{1,0:T(8,128)(2,1)}, bf16[512,512]{1,0:T(8,128)(2,1)}, u32[]{:S(2)}, u32[]{:S(2)}) collective-permute-start(bf16[512,512]{1,0:T(8,128)(2,1)} %slice.94), channel_id=1, source_target_pairs={{0,1},{1,0},{2,3},{3,2},{4,5},{5,4},{6,7},{7,6},{8,9},{9,8},{10,11... | collective-permute-start | bytes 1572872 | tf_op jit(solution)/shard_map/ppermute | solution.py:52
  139.1 10.6 %all-to-all-start.4 = ((bf16[8,64,256]{2,1,0:T(8,128)(2,1)}), bf16[8,64,256]{2,1,0:T(8,128)(2,1)S(1)}, u32[]{:S(2)}, u32[]{:S(2)}) async-start(bf16[8,64,256]{2,1,0:T(8,128)(2,1)} %bitcast.51), calls=%async_computation.4 | async-start | bytes 524288 | tf_op jit(solution)/shard_map/all_to_all | solution.py:80
  145.3 22.9 %collective-permute-start.10 = (bf16[512,512]{1,0:T(8,128)(2,1)S(1)}, bf16[512,512]{1,0:T(8,128)(2,1)}, u32[]{:S(2)}, u32[]{:S(2)}) collective-permute-start(bf16[512,512]{1,0:T(8,128)(2,1)S(1)} %bitcast.42), channel_id=1, source_target_pairs={{0,1},{1,0},{2,3},{3,2},{4,5},{5,4},{6,7},{7,6},{8,9},{9,8},{10,11... | collective-permute-start | bytes 1572872 | tf_op jit(solution)/shard_map/ppermute | solution.py:52
  149.8 24.4 %collective-permute-start.8 = (bf16[32,256]{1,0:T(8,128)(2,1)S(1)}, bf16[32,256]{1,0:T(8,128)(2,1)S(1)}, u32[]{:S(2)}, u32[]{:S(2)}) collective-permute-start(bf16[32,256]{1,0:T(8,128)(2,1)S(1)} %get-tuple-element.93), channel_id=1, source_target_pairs={{0,0},{32,1},{64,2},{96,3},{128,4},{160,5},{192,6},{224,7},{256,8}... | collective-permute-start | bytes 49160 | tf_op jit(solution)/shard_map/ppermute | solution.py:66
  163.8 14.4 %collective-permute-start.9 = (bf16[32,256]{1,0:T(8,128)(2,1)S(1)}, bf16[32,256]{1,0:T(8,128)(2,1)S(1)}, u32[]{:S(2)}, u32[]{:S(2)}) collective-permute-start(bf16[32,256]{1,0:T(8,128)(2,1)S(1)} %get-tuple-element.92), channel_id=1, source_target_pairs={{16,0},{48,1},{80,2},{112,3},{144,4},{176,5},{208,6},{240,7},{272,... | collective-permute-start | bytes 49160 | tf_op jit(solution)/shard_map/ppermute | solution.py:66
Sparse Core Ops, SparseCore 0:
  52.1 43.3 all-gather.1

commit v13 on v12

--- a/solution.py
+++ b/solution.py
@@ -81,18 +81,18 @@
     return jnp.sum(got.astype(jnp.float32), axis=0).astype(jnp.bfloat16)
 
 
-def swiglu_back(hidden_grad, gate_pre, up_pre):
-    grad_float = hidden_grad.astype(jnp.float32)
+def slopes(gate_pre, up_pre):
     gate_float = gate_pre.astype(jnp.float32)
     up_float = up_pre.astype(jnp.float32)
     sigmoid_gate = jax.nn.sigmoid(gate_float)
     activated = gate_float * sigmoid_gate
-    gate_grad = (
-        grad_float * up_float * sigmoid_gate * (1.0 + gate_float * (1.0 - sigmoid_gate))
-    ).astype(jnp.bfloat16)
-    up_grad = (grad_float * activated).astype(jnp.bfloat16)
-    hidden = (activated * up_float).astype(jnp.bfloat16)
-    return gate_grad, up_grad, hidden
+    slope = up_float * sigmoid_gate * (1.0 + gate_float * (1.0 - sigmoid_gate))
+    return slope, activated, (activated * up_float).astype(jnp.bfloat16)
+
+
+def scaled(hidden_grad, slope, activated):
+    grad_float = hidden_grad.astype(jnp.float32)
+    return (grad_float * slope).astype(jnp.bfloat16), (grad_float * activated).astype(jnp.bfloat16)
 
 
 def local(activations, out_grad, gate_pre, up_pre, gate_weight, up_weight, down_weight):
@@ -115,29 +115,33 @@
     pre = pre.reshape(8, 2, 64, 1024)
     pre_a, pre_b = choose(core == 1, pre[:, 1], pre[:, 0])
     pre_a, pre_b = pre_a.reshape(512, 1024), pre_b.reshape(512, 1024)
-    cols_y = swap(cols[:, 256:768], "yl").reshape(4, 64, 512)
+    cols_y = swap(cols[:, 256:768], "yl")
+    pre_y = swap(pre_b)
+    slope_a, active_a, hidden_a = slopes(pre_a[:, :512], pre_a[:, 512:])
+    slope_b, active_b, hidden_b = slopes(pre_b[:, :512], pre_b[:, 512:])
+    slope_y, active_y, _ = slopes(pre_y[:, :512], pre_y[:, 512:])
+    by_a, by_b, by_y, hidden_a, hidden_b, cols_y = lax.optimization_barrier(
+        ((slope_a, active_a), (slope_b, active_b), (slope_y, active_y), hidden_a, hidden_b, cols_y)
+    )
     cols = jnp.concatenate([cols[:, :256], cols[:, 768:]], axis=1).reshape(4, 64, 512)
-    cols = jnp.stack(choose(yl == 0, cols, cols_y), axis=1).reshape(512, 512)
-    hidden_grad, pre_a, pre_b, pre_y, cols = lax.optimization_barrier(
-        (hidden_grad, pre_a, pre_b, swap(pre_b), cols)
-    )
-    made_a = swiglu_back(hidden_grad[:, :512], pre_a[:, :512], pre_a[:, 512:])
-    made_y = swiglu_back(hidden_grad[:, 512:], pre_y[:, :512], pre_y[:, 512:])[:2]
-    (gate_a, up_a, hidden_a), (gate_y, up_y) = lax.optimization_barrier((made_a, made_y))
+    cols = jnp.stack(choose(yl == 0, cols, cols_y.reshape(4, 64, 512)), axis=1).reshape(512, 512)
+    hidden_grad, cols, by_a, by_y = lax.optimization_barrier((hidden_grad, cols, by_a, by_y))
+    made = scaled(hidden_grad[:, :512], *by_a), scaled(hidden_grad[:, 512:], *by_y)
+    (gate_a, up_a), (gate_y, up_y) = lax.optimization_barrier(made)
     partial = contract_cols(gate_a, gate_weight) + contract_cols(up_a, up_weight)
     partial = partial + contract_cols(gate_y, gate_other) + contract_cols(up_y, up_other)
     partial, cols, crossing = lax.optimization_barrier(
         (partial.astype(jnp.bfloat16), cols, hidden_grad[:, 512:])
     )
     summed = scatter_sum(partial, PLANE, 8)
-    cols_b, crossed = swap(cols), swap(crossing)
-    made_b = swiglu_back(crossed, pre_b[:, :512], pre_b[:, 512:])
+    cols_b = swap(cols)
+    made_b = scaled(swap(crossing), *by_b)
 
     grads_a, tokens_a = cols[:, :256], cols[:, 256:]
     grads_b, tokens_b = cols_b[:, :256], cols_b[:, 256:]
     products = contract_rows(tokens_a, gate_a), contract_rows(tokens_a, up_a), contract_rows(hidden_a, grads_a)
     summed, products = lax.optimization_barrier((summed, products))
-    gate_b, up_b, hidden_b = lax.optimization_barrier(made_b)
+    gate_b, up_b = lax.optimization_barrier(made_b)
     weight_grads = (
         (products[0] + contract_rows(tokens_b, gate_b)).astype(jnp.bfloat16),
         (products[1] + contract_rows(tokens_b, up_b)).astype(jnp.bfloat16),

time: 187 us -> 185 us (0.989)
  waiting for transfers between devices: 61.4 us -> 50.9 us
  other arithmetic: 10.5 us -> 16.2 us
  matrix products: 11.3 us -> 13.7 us
    ppermute x8, waiting for transfers between devices: 21.5 us -> 14.8 us  [swap(): return lax.ppermute(value, axis, [(0, 1), (1, 0)])]
    ppermute x1, starting transfers between devices: 2.63 us -> 5.97 us  [to_tokens(): lax.ppermute(two, AXES, OUT_TWO)]
    ppermute x1, starting transfers between devices: 14.1 us -> 11 us  [to_tokens(): lax.ppermute(one, AXES, OUT_ONE)]
    mul x0 -> x1, other arithmetic: none -> 3.03 us  [slopes(): activated = gate_float * sigmoid_gate]
    ppermute x1, waiting for transfers between devices: 4.07 us -> 1.11 us  [to_tokens(): lax.ppermute(two, AXES, OUT_TWO)]
    convert_element_type x2 -> x3, other arithmetic: 5.25 us -> 7.91 us  [the longest x2 4.21 us: scaled(): (grad_float * activated).astype(jnp.bfloat16)]
    dot_general x6, matrix products: 7.96 us -> 10.4 us  [contract_rows(): lax.dot_general(left, right, (((0,), (0,)), ((), ())), preferred_element_...]
  transfers between devices with their start and end apart: 18 -> 18, of which waited for: 8 -> 7; matrix products, arithmetic and copies ran while one was open for 9% -> 13% of each run, Pallas kernels for 0% -> 0%
where the time goes in v13:
time: 185 us; the launch traced here: 184 us
  starting transfers between devices  83.7 us (45%)
  waiting for transfers between devices  50.9 us (28%)
  other arithmetic  16.2 us (9%)
  between operations  14.5 us (8%)
  matrix products  13.7 us (7%)
  local copies, waits for them, and re-layouts  4.66 us (3%)
    ppermute x8, starting transfers between devices, swap(): return lax.ppermute(value, axis, [(0, 1), (1, 0)])  22.3 us
    all_to_all x2, waiting for transfers between devices, scatter_sum(): got = lax.all_to_all(pieces, axes, 0, 0, tiled=True)  21.2 us
    all_to_all x3, starting transfers between devices, gather_copies(): got = lax.all_to_all(copies, axes, 0, 0, tiled=True)  18.8 us
    ppermute x8, waiting for transfers between devices, swap(): return lax.ppermute(value, axis, [(0, 1), (1, 0)])  14.8 us
    ppermute x1, starting transfers between devices, to_features(): lax.ppermute(one, AXES, IN_ONE)  13 us
    ppermute x1, waiting for transfers between devices, to_features(): lax.ppermute(two, AXES, IN_TWO)  12 us
    ppermute x1, starting transfers between devices, to_tokens(): lax.ppermute(one, AXES, OUT_ONE)  11 us
    dot_general x6, matrix products, contract_rows(): lax.dot_general(left, right, (((0,), (0,)), ((), ())), preferred_element_...  10.4 us
  transfers between devices with their start and end apart: 18, of which 7 were waited for; matrix products, arithmetic and copies ran while one was open for 13% of the time, Pallas kernels for 0%

profile of v13, /device:TPU:5, one launch (start us, length us, event | category | flops | bytes accessed | tf_op | source)
XLA Modules:
  0.0 183.7 jit_solution(2394439682183232634)
XLA Ops:
  7.2 0.8 pad_maximum_fusion.2
  8.0 0.7 broadcast_in_dim.6
  8.7 10.0 %all-to-all-start = ((bf16[4,32,1024]{2,1,0:T(8,128)(2,1)}), bf16[4,32,1024]{2,1,0:T(8,128)(2,1)S(1)}, u32[]{:S(2)}, u32[]{:S(2)}) async-start(bf16[4,32,1024]{2,1,0:T(8,128)(2,1)} %broadcast_in_dim.6), calls=%async_computation | async-start | bytes 524288 | tf_op jit(solution)/shard_map/all_to_all | solution.py:74
  18.8 3.2 %collective-permute-start.2 = (bf16[512,256]{1,0:T(8,128)(2,1)}, bf16[512,256]{1,0:T(8,128)(2,1)S(1)}, u32[]{:S(2)}, u32[]{:S(2)}) collective-permute-start(bf16[512,256]{1,0:T(8,128)(2,1)} %param.13), channel_id=1, source_target_pairs={{0,64},{64,0},{1,65},{65,1},{2,66},{66,2},{3,67},{67,3},{4,68},{68... | collective-permute-start | bytes 786440 | tf_op jit(solution)/shard_map/ppermute | solution.py:52
  22.0 0.8 broadcast_select_fusion.4
  22.8 13.0 %collective-permute-start = (bf16[2,32,256]{2,1,0:T(8,128)(2,1)S(1)}, bf16[2,32,256]{2,1,0:T(8,128)(2,1)S(1)}, u32[]{:S(2)}, u32[]{:S(2)}) collective-permute-start(bf16[2,32,256]{2,1,0:T(8,128)(2,1)S(1)} %get-tuple-element.109), channel_id=1, source_target_pairs={{0,0},{1,32},{2,16},{3,48},{4,128},{5,160},{6,144},{7,176},{8,256}... | collective-permute-start | bytes 98312 | tf_op jit(solution)/shard_map/ppermute | solution.py:61
  35.8 2.8 %collective-permute-start.1 = (bf16[2,32,256]{2,1,0:T(8,128)(2,1)S(1)}, bf16[2,32,256]{2,1,0:T(8,128)(2,1)S(1)}, u32[]{:S(2)}, u32[]{:S(2)}) collective-permute-start(bf16[2,32,256]{2,1,0:T(8,128)(2,1)S(1)} %get-tuple-element.108), channel_id=1, source_target_pairs={{0,16},{1,48},{2,0},{3,32},{4,144},{5,176},{6,128},{7,160},{8,272}... | collective-permute-start | bytes 98312 | tf_op jit(solution)/shard_map/ppermute | solution.py:61
  38.6 0.6 collective-permute-done
  39.2 12.0 %collective-permute-done.1 = bf16[2,32,256]{2,1,0:T(8,128)(2,1)S(1)} collective-permute-done((bf16[2,32,256]{2,1,0:T(8,128)(2,1)S(1)}, bf16[2,32,256]{2,1,0:T(8,128)(2,1)S(1)}, u32[]{:S(2)}, u32[]{:S(2)}) %collective-permute-start.1) | collective-permute-done | bytes 32800 | tf_op jit(solution)/shard_map/ppermute | solution.py:61
  51.3 0.7 copy-done.5
  52.0 0.9 broadcast_in_dim.7
  52.9 4.2 %all-to-all-start.1 = ((bf16[8,32,1024]{2,1,0:T(8,128)(2,1)}), bf16[8,32,1024]{2,1,0:T(8,128)(2,1)S(1)}, u32[]{:S(2)}, u32[]{:S(2)}) async-start(bf16[8,32,1024]{2,1,0:T(8,128)(2,1)} %broadcast_in_dim.7), calls=%async_computation.1 | async-start | bytes 1048576 | tf_op jit(solution)/shard_map/all_to_all | solution.py:74
  57.2 2.1 %collective-permute-start.3 = (bf16[512,512]{1,0:T(8,128)(2,1)S(1)}, bf16[512,512]{1,0:T(8,128)(2,1)S(1)}, u32[]{:S(2)}, u32[]{:S(2)}) collective-permute-start(bf16[512,512]{1,0:T(8,128)(2,1)S(1)} %constant_dynamic-update-slice_fusion), channel_id=1, source_target_pairs={{0,1},{1,0},{2,3},{3,2},{4,5},{5,4},{6,7},{7,6},{8,9},{9,8},{10,11... | collective-permute-start | bytes 1572872 | tf_op jit(solution)/shard_map/ppermute | solution.py:52
  59.3 1.9 %collective-permute-done.3 = bf16[512,512]{1,0:T(8,128)(2,1)S(1)} collective-permute-done((bf16[512,512]{1,0:T(8,128)(2,1)S(1)}, bf16[512,512]{1,0:T(8,128)(2,1)S(1)}, u32[]{:S(2)}, u32[]{:S(2)}) %collective-permute-start.3) | collective-permute-done | bytes 524320 | tf_op jit(solution)/shard_map/ppermute | solution.py:52
  61.1 1.2 all-to-all-done.1
  62.3 1.3 convolution_convert_fusion
  63.6 4.0 %all-to-all-start.2 = ((bf16[16,16,1024]{2,1,0:T(8,128)(2,1)}), bf16[16,16,1024]{2,1,0:T(8,128)(2,1)S(1)}, u32[]{:S(2)}, u32[]{:S(2)}) async-start(bf16[16,16,1024]{2,1,0:T(8,128)(2,1)} %bitcast.8), calls=%async_computation.2 | async-start | bytes 1048576 | tf_op jit(solution)/shard_map/all_to_all | solution.py:80
  67.6 2.2 %collective-permute-start.4 = (bf16[256,512]{1,0:T(8,128)(2,1)S(1)}, bf16[256,512]{1,0:T(8,128)(2,1)S(1)}, u32[]{:S(2)}, u32[]{:S(2)}) collective-permute-start(bf16[256,512]{1,0:T(8,128)(2,1)S(1)} %copy-done.6), channel_id=1, source_target_pairs={{0,1},{1,0},{2,3},{3,2},{4,5},{5,4},{6,7},{7,6},{8,9},{9,8},{10,11... | collective-permute-start | bytes 786440 | tf_op jit(solution)/shard_map/ppermute | solution.py:52
  69.8 2.1 %collective-permute-start.5 = (bf16[256,512]{1,0:T(8,128)(2,1)S(1)}, bf16[256,512]{1,0:T(8,128)(2,1)S(1)}, u32[]{:S(2)}, u32[]{:S(2)}) collective-permute-start(bf16[256,512]{1,0:T(8,128)(2,1)S(1)} %copy-done.7), channel_id=1, source_target_pairs={{0,1},{1,0},{2,3},{3,2},{4,5},{5,4},{6,7},{7,6},{8,9},{9,8},{10,11... | collective-permute-start | bytes 786440 | tf_op jit(solution)/shard_map/ppermute | solution.py:52
  72.0 21.2 %all-to-all-done.2 = bf16[16,16,1024]{2,1,0:T(8,128)(2,1)S(1)} async-done(((bf16[16,16,1024]{2,1,0:T(8,128)(2,1)}), bf16[16,16,1024]{2,1,0:T(8,128)(2,1)S(1)}, u32[]{:S(2)}, u32[]{:S(2)}) %all-to-all-start.2) | async-done | bytes 524320 | tf_op jit(solution)/shard_map/all_to_all | solution.py:80
  93.2 1.1 broadcast_in_dim.8
  94.4 4.6 %all-to-all-start.3 = ((bf16[32,16,1024]{2,1,0:T(8,128)(2,1)}), bf16[32,16,1024]{2,1,0:T(8,128)(2,1)S(1)}, u32[]{:S(2)}, u32[]{:S(2)}) async-start(bf16[32,16,1024]{2,1,0:T(8,128)(2,1)} %broadcast_in_dim.8), calls=%async_computation.3 | async-start | bytes 2097152 | tf_op jit(solution)/shard_map/all_to_all | solution.py:74
  99.0 2.7 %broadcast_select_fusion = (bf16[8,1,64,1024]{3,2,1,0:T(8,128)(2,1)}, bf16[8,1,64,1024]{3,2,1,0:T(8,128)(2,1)S(1)}) fusion(pred[]{:T(512)S(6)} %eq.22, bf16[8,2,64,1024]{3,2,1,0:T(8,128)(2,1)} %bitcast.42), kind=kLoop, calls=%fused_computation.56 | loop fusion | flops 1048576 | bytes 4194305 | tf_op jit(solution)/shard_map/jit(_where)/select_n | solution.py:56
  101.6 3.4 %collective-permute-start.6 = (bf16[512,1024]{1,0:T(8,128)(2,1)}, bf16[512,1024]{1,0:T(8,128)(2,1)}, u32[]{:S(2)}, u32[]{:S(2)}) collective-permute-start(bf16[512,1024]{1,0:T(8,128)(2,1)} %bitcast.12), channel_id=1, source_target_pairs={{0,1},{1,0},{2,3},{3,2},{4,5},{5,4},{6,7},{7,6},{8,9},{9,8},{10,11... | collective-permute-start | bytes 3145736 | tf_op jit(solution)/shard_map/ppermute | solution.py:52
  105.1 3.4 %collective-permute-start.7 = (bf16[256,512]{1,0:T(8,128)(2,1)S(1)}, bf16[256,512]{1,0:T(8,128)(2,1)S(1)}, u32[]{:S(2)}, u32[]{:S(2)}) collective-permute-start(bf16[256,512]{1,0:T(8,128)(2,1)S(1)} %slice.96), channel_id=1, source_target_pairs={{0,64},{64,0},{1,65},{65,1},{2,66},{66,2},{3,67},{67,3},{4,68},{68... | collective-permute-start | bytes 786440 | tf_op jit(solution)/shard_map/ppermute | solution.py:52
  108.5 3.7 %fusion.6 = (bf16[512,512]{1,0:T(8,128)(2,1)}, f32[512,512]{1,0:T(8,128)}, f32[512,512]{1,0:T(8,128)}, f32[512,512]{1,0:T(8,128)S(1)}, f32[512,512]{1,0:T(8,128)}, /*index=5*/bf16[512,512]{1,0:T(8,128)(2,1)}) fusion(bf16[512,1024]{1,0:T(8,128)(2,1)S(1)} %bitcast.37, bf16[512,1024]{1,0:T(8,128)(2,1)} %bitcast.12), kind=kLoop, calls=%fused_computation.31 | loop fusion | flops 6815744 | bytes 7340032 | tf_op jit(solution)/shard_map/convert_element_type | solution.py:90
  112.2 3.0 %convert_multiply_fusion = (f32[512,512]{1,0:T(8,128)}, f32[512,512]{1,0:T(8,128)}) fusion(bf16[512,1024]{1,0:T(8,128)(2,1)} %collective-permute-done.6), kind=kLoop, calls=%fused_computation | loop fusion | flops 2883584 | bytes 3145728 | tf_op jit(solution)/shard_map/mul | solution.py:88
  115.3 12.9 %collective-permute-done.7 = bf16[256,512]{1,0:T(8,128)(2,1)S(1)} collective-permute-done((bf16[256,512]{1,0:T(8,128)(2,1)S(1)}, bf16[256,512]{1,0:T(8,128)(2,1)S(1)}, u32[]{:S(2)}, u32[]{:S(2)}) %collective-permute-start.7) | collective-permute-done | bytes 262176 | tf_op jit(solution)/shard_map/ppermute | solution.py:52
  128.3 0.8 slice.98
  129.2 2.9 %fusion.12 = (bf16[512,512]{1,0:T(8,128)(2,1)S(1)}, bf16[512,512]{1,0:T(8,128)(2,1)S(1)}, bf16[512,512]{1,0:T(8,128)(2,1)S(1)}, bf16[512,512]{1,0:T(8,128)(2,1)S(1)}) fusion(f32[512,512]{1,0:T(8,128)} %get-tuple-element.60, bf16[512,1024]{1,0:T(8,128)(2,1)S(1)} %bitcast.36, f32[512,512]{1,0:T(8,128)} %get-tuple-element.59, f32[512,512]{1,0:T(8,128)} %get-tuple-element.58, ...), kind=kLoop, calls=%fused_computation.37 | loop fusion | flops 2621440 | bytes 7340032 | tf_op jit(solution)/shard_map/convert_element_type | solution.py:95
  132.1 0.3 fusion.44
  132.4 0.3 convolution_add_fusion.4
  133.0 0.3 fusion.45
  133.3 1.0 fusion.1
  134.4 1.1 fusion.37
  135.5 5.9 %all-to-all-start.4 = ((bf16[8,64,256]{2,1,0:T(8,128)(2,1)}), bf16[8,64,256]{2,1,0:T(8,128)(2,1)S(1)}, u32[]{:S(2)}, u32[]{:S(2)}) async-start(bf16[8,64,256]{2,1,0:T(8,128)(2,1)} %bitcast.49), calls=%async_computation.4 | async-start | bytes 524288 | tf_op jit(solution)/shard_map/all_to_all | solution.py:80
  141.4 4.0 %collective-permute-start.11 = (bf16[512,512]{1,0:T(8,128)(2,1)}, bf16[512,512]{1,0:T(8,128)(2,1)}, u32[]{:S(2)}, u32[]{:S(2)}) collective-permute-start(bf16[512,512]{1,0:T(8,128)(2,1)} %slice.98), channel_id=1, source_target_pairs={{0,1},{1,0},{2,3},{3,2},{4,5},{5,4},{6,7},{7,6},{8,9},{9,8},{10,11... | collective-permute-start | bytes 1572872 | tf_op jit(solution)/shard_map/ppermute | solution.py:52
  145.4 1.1 fusion.39
  146.5 1.9 %collective-permute-start.10 = (bf16[512,512]{1,0:T(8,128)(2,1)S(1)}, bf16[512,512]{1,0:T(8,128)(2,1)}, u32[]{:S(2)}, u32[]{:S(2)}) collective-permute-start(bf16[512,512]{1,0:T(8,128)(2,1)S(1)} %bitcast.40), channel_id=1, source_target_pairs={{0,1},{1,0},{2,3},{3,2},{4,5},{5,4},{6,7},{7,6},{8,9},{9,8},{10,11... | collective-permute-start | bytes 1572872 | tf_op jit(solution)/shard_map/ppermute | solution.py:52
  148.4 2.2 %fusion.33 = f32[512,256]{1,0:T(8,128)} fusion(bf16[512,512]{1,0:T(8,128)(2,1)} %get-tuple-element.70, bf16[512,512]{1,0:T(8,128)(2,1)S(1)} %bitcast.41), kind=kOutput, calls=%fused_computation.62 | convolution fusion | flops 134217728 | bytes 1310720 | tf_op jit(solution)/shard_map/dot_general | solution.py:40
  150.7 11.0 %collective-permute-start.8 = (bf16[32,256]{1,0:T(8,128)(2,1)S(1)}, bf16[32,256]{1,0:T(8,128)(2,1)S(1)}, u32[]{:S(2)}, u32[]{:S(2)}) collective-permute-start(bf16[32,256]{1,0:T(8,128)(2,1)S(1)} %get-tuple-element.113), channel_id=1, source_target_pairs={{0,0},{32,1},{64,2},{96,3},{128,4},{160,5},{192,6},{224,7},{256,8}... | collective-permute-start | bytes 49160 | tf_op jit(solution)/shard_map/ppermute | solution.py:66
  161.7 6.0 %collective-permute-start.9 = (bf16[32,256]{1,0:T(8,128)(2,1)S(1)}, bf16[32,256]{1,0:T(8,128)(2,1)S(1)}, u32[]{:S(2)}, u32[]{:S(2)}) collective-permute-start(bf16[32,256]{1,0:T(8,128)(2,1)S(1)} %get-tuple-element.112), channel_id=1, source_target_pairs={{16,0},{48,1},{80,2},{112,3},{144,4},{176,5},{208,6},{240,7},{272,... | collective-permute-start | bytes 49160 | tf_op jit(solution)/shard_map/ppermute | solution.py:66
  167.7 1.3 fusion.14
  169.1 2.1 %fusion.4 = bf16[512,256]{1,0:T(8,128)(2,1)} fusion(f32[512,256]{1,0:T(8,128)S(1)} %copy-done.4, bf16[512,512]{1,0:T(8,128)(2,1)S(1)} %copy-done.1, bf16[512,512]{1,0:T(8,128)(2,1)} %collective-permute-done.10), kind=kOutput, calls=%fused_computation.29 | convolution fusion | flops 134479872 | bytes 1572864 | tf_op jit(solution)/shard_map/dot_general | solution.py:40
  171.1 2.0 %fusion.3 = bf16[256,512]{1,0:T(8,128)(2,1)} fusion(f32[256,512]{1,0:T(8,128)S(1)} %copy-done.2, bf16[512,512]{1,0:T(8,128)(2,1)S(1)} %get-tuple-element.78, bf16[512,512]{1,0:T(8,128)(2,1)} %collective-permute-done.10), kind=kOutput, calls=%fused_computation.28 | convolution fusion | flops 134479872 | bytes 1572864 | tf_op jit(solution)/shard_map/dot_general | solution.py:40
  173.1 2.0 %fusion.2 = bf16[256,512]{1,0:T(8,128)(2,1)} fusion(f32[256,512]{1,0:T(8,128)S(1)} %copy-done.3, bf16[512,512]{1,0:T(8,128)(2,1)S(1)} %get-tuple-element.76, bf16[512,512]{1,0:T(8,128)(2,1)} %collective-permute-done.10), kind=kOutput, calls=%fused_computation.27 | convolution fusion | flops 134479872 | bytes 1572864 | tf_op jit(solution)/shard_map/dot_general | solution.py:40
  175.1 1.1 collective-permute-done.9
  176.2 0.6 pad_maximum_fusion.5
  (53 shorter events, 0.8 us)
Async XLA Ops:
  7.2 50.0 %copy-start.11 = (bf16[512,256]{1,0:T(8,128)(2,1)S(1)}, bf16[512,256]{1,0:T(8,128)(2,1)}, u32[]{:S(2)}) copy-start(bf16[512,256]{1,0:T(8,128)(2,1)} %param.13) | copy-start | bytes 786436
  8.7 42.5 %all-to-all-start = ((bf16[4,32,1024]{2,1,0:T(8,128)(2,1)}), bf16[4,32,1024]{2,1,0:T(8,128)(2,1)S(1)}, u32[]{:S(2)}, u32[]{:S(2)}) async-start(bf16[4,32,1024]{2,1,0:T(8,128)(2,1)} %broadcast_in_dim.6), calls=%async_computation | async-start | bytes 524288 | tf_op jit(solution)/shard_map/all_to_all | solution.py:74
  18.7 80.2 %all-gather.2.cloned.1.call-start = ((), (), s32[]{:S(2)}) async-start(), calls=%async_computation.5 | async-start | bytes 2359296 | tf_op jit(solution)/shard_map/all_gather | solution.py:104
  18.8 32.5 %collective-permute-start.2 = (bf16[512,256]{1,0:T(8,128)(2,1)}, bf16[512,256]{1,0:T(8,128)(2,1)S(1)}, u32[]{:S(2)}, u32[]{:S(2)}) collective-permute-start(bf16[512,256]{1,0:T(8,128)(2,1)} %param.13), channel_id=1, source_target_pairs={{0,64},{64,0},{1,65},{65,1},{2,66},{66,2},{3,67},{67,3},{4,68},{68... | collective-permute-start | bytes 786440 | tf_op jit(solution)/shard_map/ppermute | solution.py:52
  22.8 16.4 %collective-permute-start = (bf16[2,32,256]{2,1,0:T(8,128)(2,1)S(1)}, bf16[2,32,256]{2,1,0:T(8,128)(2,1)S(1)}, u32[]{:S(2)}, u32[]{:S(2)}) collective-permute-start(bf16[2,32,256]{2,1,0:T(8,128)(2,1)S(1)} %get-tuple-element.109), channel_id=1, source_target_pairs={{0,0},{1,32},{2,16},{3,48},{4,128},{5,160},{6,144},{7,176},{8,256}... | collective-permute-start | bytes 98312 | tf_op jit(solution)/shard_map/ppermute | solution.py:61
  35.8 15.5 %collective-permute-start.1 = (bf16[2,32,256]{2,1,0:T(8,128)(2,1)S(1)}, bf16[2,32,256]{2,1,0:T(8,128)(2,1)S(1)}, u32[]{:S(2)}, u32[]{:S(2)}) collective-permute-start(bf16[2,32,256]{2,1,0:T(8,128)(2,1)S(1)} %get-tuple-element.108), channel_id=1, source_target_pairs={{0,16},{1,48},{2,0},{3,32},{4,144},{5,176},{6,128},{7,160},{8,272}... | collective-permute-start | bytes 98312 | tf_op jit(solution)/shard_map/ppermute | solution.py:61
  51.3 0.7 copy-start.5
  52.9 9.4 %all-to-all-start.1 = ((bf16[8,32,1024]{2,1,0:T(8,128)(2,1)}), bf16[8,32,1024]{2,1,0:T(8,128)(2,1)S(1)}, u32[]{:S(2)}, u32[]{:S(2)}) async-start(bf16[8,32,1024]{2,1,0:T(8,128)(2,1)} %broadcast_in_dim.7), calls=%async_computation.1 | async-start | bytes 1048576 | tf_op jit(solution)/shard_map/all_to_all | solution.py:74
  57.2 10.4 %copy-start.6 = (bf16[256,512]{1,0:T(8,128)(2,1)S(1)}, bf16[256,512]{1,0:T(8,128)(2,1)}, u32[]{:S(2)}) copy-start(bf16[256,512]{1,0:T(8,128)(2,1)} %param.11) | copy-start | bytes 786436
  57.2 12.7 %copy-start.7 = (bf16[256,512]{1,0:T(8,128)(2,1)S(1)}, bf16[256,512]{1,0:T(8,128)(2,1)}, u32[]{:S(2)}) copy-start(bf16[256,512]{1,0:T(8,128)(2,1)} %param.12) | copy-start | bytes 786436
  57.2 3.9 %collective-permute-start.3 = (bf16[512,512]{1,0:T(8,128)(2,1)S(1)}, bf16[512,512]{1,0:T(8,128)(2,1)S(1)}, u32[]{:S(2)}, u32[]{:S(2)}) collective-permute-start(bf16[512,512]{1,0:T(8,128)(2,1)S(1)} %constant_dynamic-update-slice_fusion), channel_id=1, source_target_pairs={{0,1},{1,0},{2,3},{3,2},{4,5},{5,4},{6,7},{7,6},{8,9},{9,8},{10,11... | collective-permute-start | bytes 1572872 | tf_op jit(solution)/shard_map/ppermute | solution.py:52
  63.6 29.5 %all-to-all-start.2 = ((bf16[16,16,1024]{2,1,0:T(8,128)(2,1)}), bf16[16,16,1024]{2,1,0:T(8,128)(2,1)S(1)}, u32[]{:S(2)}, u32[]{:S(2)}) async-start(bf16[16,16,1024]{2,1,0:T(8,128)(2,1)} %bitcast.8), calls=%async_computation.2 | async-start | bytes 1048576 | tf_op jit(solution)/shard_map/all_to_all | solution.py:80
  67.6 25.6 %collective-permute-start.4 = (bf16[256,512]{1,0:T(8,128)(2,1)S(1)}, bf16[256,512]{1,0:T(8,128)(2,1)S(1)}, u32[]{:S(2)}, u32[]{:S(2)}) collective-permute-start(bf16[256,512]{1,0:T(8,128)(2,1)S(1)} %copy-done.6), channel_id=1, source_target_pairs={{0,1},{1,0},{2,3},{3,2},{4,5},{5,4},{6,7},{7,6},{8,9},{9,8},{10,11... | collective-permute-start | bytes 786440 | tf_op jit(solution)/shard_map/ppermute | solution.py:52
  69.8 23.4 %collective-permute-start.5 = (bf16[256,512]{1,0:T(8,128)(2,1)S(1)}, bf16[256,512]{1,0:T(8,128)(2,1)S(1)}, u32[]{:S(2)}, u32[]{:S(2)}) collective-permute-start(bf16[256,512]{1,0:T(8,128)(2,1)S(1)} %copy-done.7), channel_id=1, source_target_pairs={{0,1},{1,0},{2,3},{3,2},{4,5},{5,4},{6,7},{7,6},{8,9},{9,8},{10,11... | collective-permute-start | bytes 786440 | tf_op jit(solution)/shard_map/ppermute | solution.py:52
  93.2 1.2 copy-start.12
  93.2 1.1 copy-start.9
  94.4 34.0 %all-to-all-start.3 = ((bf16[32,16,1024]{2,1,0:T(8,128)(2,1)}), bf16[32,16,1024]{2,1,0:T(8,128)(2,1)S(1)}, u32[]{:S(2)}, u32[]{:S(2)}) async-start(bf16[32,16,1024]{2,1,0:T(8,128)(2,1)} %broadcast_in_dim.8), calls=%async_computation.3 | async-start | bytes 2097152 | tf_op jit(solution)/shard_map/all_to_all | solution.py:74
  101.6 10.6 %collective-permute-start.6 = (bf16[512,1024]{1,0:T(8,128)(2,1)}, bf16[512,1024]{1,0:T(8,128)(2,1)}, u32[]{:S(2)}, u32[]{:S(2)}) collective-permute-start(bf16[512,1024]{1,0:T(8,128)(2,1)} %bitcast.12), channel_id=1, source_target_pairs={{0,1},{1,0},{2,3},{3,2},{4,5},{5,4},{6,7},{7,6},{8,9},{9,8},{10,11... | collective-permute-start | bytes 3145736 | tf_op jit(solution)/shard_map/ppermute | solution.py:52
  105.1 23.1 %collective-permute-start.7 = (bf16[256,512]{1,0:T(8,128)(2,1)S(1)}, bf16[256,512]{1,0:T(8,128)(2,1)S(1)}, u32[]{:S(2)}, u32[]{:S(2)}) collective-permute-start(bf16[256,512]{1,0:T(8,128)(2,1)S(1)} %slice.96), channel_id=1, source_target_pairs={{0,64},{64,0},{1,65},{65,1},{2,66},{66,2},{3,67},{67,3},{4,68},{68... | collective-permute-start | bytes 786440 | tf_op jit(solution)/shard_map/ppermute | solution.py:52
  129.2 3.2 %copy-start.8 = (bf16[256,512]{1,0:T(8,128)(2,1)S(1)}, bf16[256,512]{1,0:T(8,128)(2,1)}, u32[]{:S(2)}) copy-start(bf16[256,512]{1,0:T(8,128)(2,1)} %param.12) | copy-start | bytes 786436
  132.0 1.0 copy-start.10
  132.0 1.3 copy-start.13
  134.4 33.3 %copy-start = (f32[512,512]{1,0:T(8,128)S(1)}, f32[512,512]{1,0:T(8,128)}, u32[]{:S(2)}) copy-start(f32[512,512]{1,0:T(8,128)} %get-tuple-element.75) | copy-start | bytes 3145732
  135.5 15.1 %all-to-all-start.4 = ((bf16[8,64,256]{2,1,0:T(8,128)(2,1)}), bf16[8,64,256]{2,1,0:T(8,128)(2,1)S(1)}, u32[]{:S(2)}, u32[]{:S(2)}) async-start(bf16[8,64,256]{2,1,0:T(8,128)(2,1)} %bitcast.49), calls=%async_computation.4 | async-start | bytes 524288 | tf_op jit(solution)/shard_map/all_to_all | solution.py:80
  141.4 26.3 %collective-permute-start.11 = (bf16[512,512]{1,0:T(8,128)(2,1)}, bf16[512,512]{1,0:T(8,128)(2,1)}, u32[]{:S(2)}, u32[]{:S(2)}) collective-permute-start(bf16[512,512]{1,0:T(8,128)(2,1)} %slice.98), channel_id=1, source_target_pairs={{0,1},{1,0},{2,3},{3,2},{4,5},{5,4},{6,7},{7,6},{8,9},{9,8},{10,11... | collective-permute-start | bytes 1572872 | tf_op jit(solution)/shard_map/ppermute | solution.py:52
  146.5 22.5 %collective-permute-start.10 = (bf16[512,512]{1,0:T(8,128)(2,1)S(1)}, bf16[512,512]{1,0:T(8,128)(2,1)}, u32[]{:S(2)}, u32[]{:S(2)}) collective-permute-start(bf16[512,512]{1,0:T(8,128)(2,1)S(1)} %bitcast.40), channel_id=1, source_target_pairs={{0,1},{1,0},{2,3},{3,2},{4,5},{5,4},{6,7},{7,6},{8,9},{9,8},{10,11... | collective-permute-start | bytes 1572872 | tf_op jit(solution)/shard_map/ppermute | solution.py:52
  150.6 18.5 %copy-start.1 = (bf16[512,512]{1,0:T(8,128)(2,1)S(1)}, bf16[512,512]{1,0:T(8,128)(2,1)}, u32[]{:S(2)}) copy-start(bf16[512,512]{1,0:T(8,128)(2,1)} %get-tuple-element.80) | copy-start | bytes 1572868
  150.6 18.4 %copy-start.4 = (f32[512,256]{1,0:T(8,128)S(1)}, f32[512,256]{1,0:T(8,128)}, u32[]{:S(2)}) copy-start(f32[512,256]{1,0:T(8,128)} %fusion.33) | copy-start | bytes 1572868
  150.7 24.4 %collective-permute-start.8 = (bf16[32,256]{1,0:T(8,128)(2,1)S(1)}, bf16[32,256]{1,0:T(8,128)(2,1)S(1)}, u32[]{:S(2)}, u32[]{:S(2)}) collective-permute-start(bf16[32,256]{1,0:T(8,128)(2,1)S(1)} %get-tuple-element.113), channel_id=1, source_target_pairs={{0,0},{32,1},{64,2},{96,3},{128,4},{160,5},{192,6},{224,7},{256,8}... | collective-permute-start | bytes 49160 | tf_op jit(solution)/shard_map/ppermute | solution.py:66
  161.7 9.5 %copy-start.2 = (f32[256,512]{1,0:T(8,128)S(1)}, f32[256,512]{1,0:T(8,128)}, u32[]{:S(2)}) copy-start(f32[256,512]{1,0:T(8,128)} %fusion.37) | copy-start | bytes 1572868
  161.7 14.5 %collective-permute-start.9 = (bf16[32,256]{1,0:T(8,128)(2,1)S(1)}, bf16[32,256]{1,0:T(8,128)(2,1)S(1)}, u32[]{:S(2)}, u32[]{:S(2)}) collective-permute-start(bf16[32,256]{1,0:T(8,128)(2,1)S(1)} %get-tuple-element.112), channel_id=1, source_target_pairs={{16,0},{48,1},{80,2},{112,3},{144,4},{176,5},{208,6},{240,7},{272,... | collective-permute-start | bytes 49160 | tf_op jit(solution)/shard_map/ppermute | solution.py:66
  169.0 4.1 %copy-start.3 = (f32[256,512]{1,0:T(8,128)S(1)}, f32[256,512]{1,0:T(8,128)}, u32[]{:S(2)}) copy-start(f32[256,512]{1,0:T(8,128)} %fusion.39) | copy-start | bytes 1572868
Sparse Core Ops, SparseCore 0:
  52.1 43.3 all-gather.1

commit v14 on v13

--- a/solution.py
+++ b/solution.py
@@ -98,10 +98,9 @@
 def local(activations, out_grad, gate_pre, up_pre, gate_weight, up_weight, down_weight):
     yl, zh, core = lax.axis_index("yl"), lax.axis_index("zh"), lax.axis_index("core")
     upper, mine, odd = lax.axis_index("zl") == 1, zh % 2 == yl, zh % 2 == 1
-    pre = gather_copies(jnp.concatenate([gate_pre, up_pre], axis=1), "zh", 4)
+    pre = lax.all_gather(jnp.concatenate([gate_pre, up_pre], axis=1), ROW, axis=0, tiled=True)
     tiles = to_features(jnp.stack([out_grad, activations]), upper, mine)
-    (own, other), pre, down_y = lax.optimization_barrier((tiles, pre, swap(down_weight, "yl")))
-    pre = lax.all_gather(pre, ("yh", "yl"), axis=0, tiled=True)
+    (own, other), down_y = lax.optimization_barrier((tiles, swap(down_weight, "yl")))
     cols = gather_copies(jnp.concatenate([own[0], other[0], other[1], own[1]], axis=1), PLANE, 8)
     down = jnp.concatenate([down_weight, down_y], axis=1)
     down = jnp.concatenate([down, swap(down)], axis=0)
@@ -142,11 +141,10 @@
     products = contract_rows(tokens_a, gate_a), contract_rows(tokens_a, up_a), contract_rows(hidden_a, grads_a)
     summed, products = lax.optimization_barrier((summed, products))
     gate_b, up_b = lax.optimization_barrier(made_b)
-    weight_grads = (
-        (products[0] + contract_rows(tokens_b, gate_b)).astype(jnp.bfloat16),
-        (products[1] + contract_rows(tokens_b, up_b)).astype(jnp.bfloat16),
-        (products[2] + contract_rows(hidden_b, grads_b)).astype(jnp.bfloat16),
+    rest = lax.optimization_barrier(
+        (contract_rows(tokens_b, gate_b), contract_rows(tokens_b, up_b), contract_rows(hidden_b, grads_b))
     )
+    weight_grads = tuple((one + two).astype(jnp.bfloat16) for one, two in zip(products, rest))
     return to_tokens(summed, odd, weight_grads)
 
 

time: 185 us -> 201 us (1.086)
  waiting for transfers between devices: 50.9 us -> 70.5 us
  other arithmetic: 16.2 us -> 19.1 us
  starting transfers between devices: 83.7 us -> 81.1 us
    all_gather x1, waiting for transfers between devices: 0.02 us -> 33.8 us  [local(): lax.all_gather(jnp.concatenate([gate_pre, up_pre], axis=1), ROW, axis=0,...]
    ppermute x8, waiting for transfers between devices: 14.8 us -> 2.75 us  [swap(): return lax.ppermute(value, axis, [(0, 1), (1, 0)])]
    all_to_all x2, waiting for transfers between devices: 21.2 us -> 15.8 us  [scatter_sum(): got = lax.all_to_all(pieces, axes, 0, 0, tiled=True)]
    all_to_all x3 -> x2, starting transfers between devices: 18.8 us -> 13.7 us  [gather_copies(): got = lax.all_to_all(copies, axes, 0, 0, tiled=True)]
    ppermute x1, starting transfers between devices: 11 us -> 14.7 us  [to_tokens(): lax.ppermute(one, AXES, OUT_ONE)]
    ppermute x1, starting transfers between devices: 5.97 us -> 3.16 us  [to_tokens(): lax.ppermute(two, AXES, OUT_TWO)]
    ppermute x1, starting transfers between devices: 13 us -> 15.8 us  [to_features(): lax.ppermute(one, AXES, IN_ONE)]
    ppermute x1, waiting for transfers between devices: 1.11 us -> 3.46 us  [to_tokens(): lax.ppermute(two, AXES, OUT_TWO)]
  transfers between devices with their start and end apart: 18 -> 17, of which waited for: 7 -> 9; matrix products, arithmetic and copies ran while one was open for 13% -> 13% of each run, Pallas kernels for 0% -> 0%
where the time goes in v14:
time: 201 us; the launch traced here: 200 us
  starting transfers between devices  81.1 us (40%)
  waiting for transfers between devices  70.5 us (35%)
  other arithmetic  19.1 us (10%)
  between operations  14.5 us (7%)
  matrix products  11.7 us (6%)
  local copies, waits for them, and re-layouts  3.23 us (2%)
    all_gather x1, waiting for transfers between devices, local(): lax.all_gather(jnp.concatenate([gate_pre, up_pre], axis=1), ROW, axis=0,...  33.8 us
    ppermute x8, starting transfers between devices, swap(): return lax.ppermute(value, axis, [(0, 1), (1, 0)])  21.4 us
    ppermute x1, starting transfers between devices, to_features(): lax.ppermute(one, AXES, IN_ONE)  15.8 us
    all_to_all x2, waiting for transfers between devices, scatter_sum(): got = lax.all_to_all(pieces, axes, 0, 0, tiled=True)  15.8 us
    ppermute x1, starting transfers between devices, to_tokens(): lax.ppermute(one, AXES, OUT_ONE)  14.7 us
    all_to_all x2, starting transfers between devices, gather_copies(): got = lax.all_to_all(copies, axes, 0, 0, tiled=True)  13.7 us
    ppermute x1, waiting for transfers between devices, to_features(): lax.ppermute(two, AXES, IN_TWO)  11.6 us
    all_to_all x2, starting transfers between devices, scatter_sum(): got = lax.all_to_all(pieces, axes, 0, 0, tiled=True)  10.4 us
  transfers between devices with their start and end apart: 17, of which 9 were waited for; matrix products, arithmetic and copies ran while one was open for 13% of the time, Pallas kernels for 0%

profile of v14, /device:TPU:5, one launch (start us, length us, event | category | flops | bytes accessed | tf_op | source)
XLA Modules:
  0.0 200.2 jit_solution(216442193777300909)
XLA Ops:
  7.2 1.4 pad_maximum_fusion.3
  8.7 3.2 %collective-permute-start.2 = (bf16[512,256]{1,0:T(8,128)(2,1)}, bf16[512,256]{1,0:T(8,128)(2,1)S(1)}, u32[]{:S(2)}, u32[]{:S(2)}) collective-permute-start(bf16[512,256]{1,0:T(8,128)(2,1)} %param.13), channel_id=1, source_target_pairs={{0,64},{64,0},{1,65},{65,1},{2,66},{66,2},{3,67},{67,3},{4,68},{68... | collective-permute-start | bytes 786440 | tf_op jit(solution)/shard_map/ppermute | solution.py:52
  11.9 0.8 broadcast_select_fusion.4
  12.7 15.8 %collective-permute-start = (bf16[2,32,256]{2,1,0:T(8,128)(2,1)S(1)}, bf16[2,32,256]{2,1,0:T(8,128)(2,1)S(1)}, u32[]{:S(2)}, u32[]{:S(2)}) collective-permute-start(bf16[2,32,256]{2,1,0:T(8,128)(2,1)S(1)} %get-tuple-element.113), channel_id=1, source_target_pairs={{0,0},{1,32},{2,16},{3,48},{4,128},{5,160},{6,144},{7,176},{8,256}... | collective-permute-start | bytes 98312 | tf_op jit(solution)/shard_map/ppermute | solution.py:61
  28.5 1.9 collective-permute-start.1
  30.5 2.0 collective-permute-done
  32.5 11.6 %collective-permute-done.1 = bf16[2,32,256]{2,1,0:T(8,128)(2,1)S(1)} collective-permute-done((bf16[2,32,256]{2,1,0:T(8,128)(2,1)S(1)}, bf16[2,32,256]{2,1,0:T(8,128)(2,1)S(1)}, u32[]{:S(2)}, u32[]{:S(2)}) %collective-permute-start.1) | collective-permute-done | bytes 32800 | tf_op jit(solution)/shard_map/ppermute | solution.py:61
  44.2 0.9 broadcast_in_dim.4
  45.0 4.2 %all-to-all-start = ((bf16[8,32,1024]{2,1,0:T(8,128)(2,1)}), bf16[8,32,1024]{2,1,0:T(8,128)(2,1)S(1)}, u32[]{:S(2)}, u32[]{:S(2)}) async-start(bf16[8,32,1024]{2,1,0:T(8,128)(2,1)} %broadcast_in_dim.4), calls=%async_computation | async-start | bytes 1048576 | tf_op jit(solution)/shard_map/all_to_all | solution.py:74
  49.3 2.1 %collective-permute-start.3 = (bf16[512,512]{1,0:T(8,128)(2,1)S(1)}, bf16[512,512]{1,0:T(8,128)(2,1)S(1)}, u32[]{:S(2)}, u32[]{:S(2)}) collective-permute-start(bf16[512,512]{1,0:T(8,128)(2,1)S(1)} %constant_dynamic-update-slice_fusion), channel_id=1, source_target_pairs={{0,1},{1,0},{2,3},{3,2},{4,5},{5,4},{6,7},{7,6},{8,9},{9,8},{10,11... | collective-permute-start | bytes 1572872 | tf_op jit(solution)/shard_map/ppermute | solution.py:52
  51.4 1.9 collective-permute-done.3
  53.3 1.1 all-to-all-done
  54.4 1.3 convolution_convert_fusion
  55.7 5.4 %all-to-all-start.1 = ((bf16[16,16,1024]{2,1,0:T(8,128)(2,1)}), bf16[16,16,1024]{2,1,0:T(8,128)(2,1)S(1)}, u32[]{:S(2)}, u32[]{:S(2)}) async-start(bf16[16,16,1024]{2,1,0:T(8,128)(2,1)} %bitcast.7), calls=%async_computation.1 | async-start | bytes 1048576 | tf_op jit(solution)/shard_map/all_to_all | solution.py:80
  61.1 1.9 collective-permute-start.4
  63.0 2.4 %collective-permute-start.5 = (bf16[256,512]{1,0:T(8,128)(2,1)S(1)}, bf16[256,512]{1,0:T(8,128)(2,1)S(1)}, u32[]{:S(2)}, u32[]{:S(2)}) collective-permute-start(bf16[256,512]{1,0:T(8,128)(2,1)S(1)} %copy-done.6), channel_id=1, source_target_pairs={{0,1},{1,0},{2,3},{3,2},{4,5},{5,4},{6,7},{7,6},{8,9},{9,8},{10,11... | collective-permute-start | bytes 786440 | tf_op jit(solution)/shard_map/ppermute | solution.py:52
  65.4 14.6 %all-to-all-done.1 = bf16[16,16,1024]{2,1,0:T(8,128)(2,1)S(1)} async-done(((bf16[16,16,1024]{2,1,0:T(8,128)(2,1)}), bf16[16,16,1024]{2,1,0:T(8,128)(2,1)S(1)}, u32[]{:S(2)}, u32[]{:S(2)}) %all-to-all-start.1) | async-done | bytes 524320 | tf_op jit(solution)/shard_map/all_to_all | solution.py:80
  80.1 1.1 broadcast_in_dim.5
  81.3 9.5 %all-to-all-start.2 = ((bf16[32,16,1024]{2,1,0:T(8,128)(2,1)}), bf16[32,16,1024]{2,1,0:T(8,128)(2,1)S(1)}, u32[]{:S(2)}, u32[]{:S(2)}) async-start(bf16[32,16,1024]{2,1,0:T(8,128)(2,1)} %broadcast_in_dim.5), calls=%async_computation.2 | async-start | bytes 2097152 | tf_op jit(solution)/shard_map/all_to_all | solution.py:74
  90.8 33.8 %all-gather.2.cloned.1.call-done = bf16[1024,1024]{1,0:T(8,128)(2,1)} async-done(((bf16[32,1024]{1,0:T(8,128)(2,1)}), bf16[1024,1024]{1,0:T(8,128)(2,1)}) %all-gather.2.cloned.1.call-update) | async-done | bytes 2097168 | tf_op jit(solution)/shard_map/all_gather | solution.py:101
  124.5 2.7 %broadcast_select_fusion = (bf16[8,1,64,1024]{3,2,1,0:T(8,128)(2,1)}, bf16[8,1,64,1024]{3,2,1,0:T(8,128)(2,1)S(1)}) fusion(pred[]{:T(512)S(6)} %eq.22, bf16[8,2,64,1024]{3,2,1,0:T(8,128)(2,1)} %bitcast.41), kind=kLoop, calls=%fused_computation.50 | loop fusion | flops 1048576 | bytes 4194305 | tf_op jit(solution)/shard_map/jit(_where)/select_n | solution.py:56
  127.2 4.9 %collective-permute-start.6 = (bf16[512,1024]{1,0:T(8,128)(2,1)}, bf16[512,1024]{1,0:T(8,128)(2,1)}, u32[]{:S(2)}, u32[]{:S(2)}) collective-permute-start(bf16[512,1024]{1,0:T(8,128)(2,1)} %bitcast.11), channel_id=1, source_target_pairs={{0,1},{1,0},{2,3},{3,2},{4,5},{5,4},{6,7},{7,6},{8,9},{9,8},{10,11... | collective-permute-start | bytes 3145736 | tf_op jit(solution)/shard_map/ppermute | solution.py:52
  132.2 2.2 %collective-permute-start.7 = (bf16[256,512]{1,0:T(8,128)(2,1)S(1)}, bf16[256,512]{1,0:T(8,128)(2,1)S(1)}, u32[]{:S(2)}, u32[]{:S(2)}) collective-permute-start(bf16[256,512]{1,0:T(8,128)(2,1)S(1)} %slice.96), channel_id=1, source_target_pairs={{0,64},{64,0},{1,65},{65,1},{2,66},{66,2},{3,67},{67,3},{4,68},{68... | collective-permute-start | bytes 786440 | tf_op jit(solution)/shard_map/ppermute | solution.py:52
  134.4 3.7 %fusion.3 = (bf16[512,512]{1,0:T(8,128)(2,1)}, f32[512,512]{1,0:T(8,128)}, f32[512,512]{1,0:T(8,128)}, f32[512,512]{1,0:T(8,128)S(1)}, f32[512,512]{1,0:T(8,128)}, /*index=5*/bf16[512,512]{1,0:T(8,128)(2,1)}) fusion(bf16[512,1024]{1,0:T(8,128)(2,1)S(1)} %bitcast.36, bf16[512,1024]{1,0:T(8,128)(2,1)} %bitcast.11), kind=kLoop, calls=%fused_computation.25 | loop fusion | flops 6815744 | bytes 7340032 | tf_op jit(solution)/shard_map/convert_element_type | solution.py:90
  138.1 3.0 %convert_multiply_fusion = (f32[512,512]{1,0:T(8,128)}, f32[512,512]{1,0:T(8,128)}) fusion(bf16[512,1024]{1,0:T(8,128)(2,1)} %collective-permute-done.6), kind=kLoop, calls=%fused_computation | loop fusion | flops 2883584 | bytes 3145728 | tf_op jit(solution)/shard_map/mul | solution.py:88
  141.1 0.9 collective-permute-done.7
  142.2 0.8 slice.98
  143.0 2.9 %fusion.9 = (bf16[512,512]{1,0:T(8,128)(2,1)S(1)}, bf16[512,512]{1,0:T(8,128)(2,1)S(1)}, bf16[512,512]{1,0:T(8,128)(2,1)S(1)}, bf16[512,512]{1,0:T(8,128)(2,1)S(1)}) fusion(f32[512,512]{1,0:T(8,128)} %get-tuple-element.61, bf16[512,1024]{1,0:T(8,128)(2,1)S(1)} %bitcast.35, f32[512,512]{1,0:T(8,128)} %get-tuple-element.60, f32[512,512]{1,0:T(8,128)} %get-tuple-element.59, ...), kind=kLoop, calls=%fused_computation.31 | loop fusion | flops 2621440 | bytes 7340032 | tf_op jit(solution)/shard_map/convert_element_type | solution.py:95
  145.9 0.3 fusion.44
  147.2 1.0 fusion.1
  148.2 2.8 %collective-permute-start.10 = (bf16[512,512]{1,0:T(8,128)(2,1)S(1)}, bf16[512,512]{1,0:T(8,128)(2,1)}, u32[]{:S(2)}, u32[]{:S(2)}) collective-permute-start(bf16[512,512]{1,0:T(8,128)(2,1)S(1)} %bitcast.37), channel_id=1, source_target_pairs={{0,1},{1,0},{2,3},{3,2},{4,5},{5,4},{6,7},{7,6},{8,9},{9,8},{10,11... | collective-permute-start | bytes 1572872 | tf_op jit(solution)/shard_map/ppermute | solution.py:52
  151.0 1.1 fusion.37
  152.2 1.9 collective-permute-start.11
  154.1 5.0 %all-to-all-start.3 = ((bf16[8,64,256]{2,1,0:T(8,128)(2,1)}), bf16[8,64,256]{2,1,0:T(8,128)(2,1)S(1)}, u32[]{:S(2)}, u32[]{:S(2)}) async-start(bf16[8,64,256]{2,1,0:T(8,128)(2,1)} %bitcast.47), calls=%async_computation.3 | async-start | bytes 524288 | tf_op jit(solution)/shard_map/all_to_all | solution.py:80
  159.1 1.1 fusion.39
  160.3 2.2 %fusion.31 = f32[512,256]{1,0:T(8,128)} fusion(bf16[512,512]{1,0:T(8,128)(2,1)} %get-tuple-element.71, bf16[512,512]{1,0:T(8,128)(2,1)S(1)} %bitcast.40), kind=kOutput, calls=%fused_computation.60 | convolution fusion | flops 134217728 | bytes 1310720 | tf_op jit(solution)/shard_map/dot_general | solution.py:40
  162.4 1.2 all-to-all-done.3
  163.7 14.7 %collective-permute-start.8 = (bf16[32,256]{1,0:T(8,128)(2,1)S(1)}, bf16[32,256]{1,0:T(8,128)(2,1)S(1)}, u32[]{:S(2)}, u32[]{:S(2)}) collective-permute-start(bf16[32,256]{1,0:T(8,128)(2,1)S(1)} %get-tuple-element.117), channel_id=1, source_target_pairs={{0,0},{32,1},{64,2},{96,3},{128,4},{160,5},{192,6},{224,7},{256,8}... | collective-permute-start | bytes 49160 | tf_op jit(solution)/shard_map/ppermute | solution.py:66
  178.4 3.2 %collective-permute-start.9 = (bf16[32,256]{1,0:T(8,128)(2,1)S(1)}, bf16[32,256]{1,0:T(8,128)(2,1)S(1)}, u32[]{:S(2)}, u32[]{:S(2)}) collective-permute-start(bf16[32,256]{1,0:T(8,128)(2,1)S(1)} %get-tuple-element.116), channel_id=1, source_target_pairs={{16,0},{48,1},{80,2},{112,3},{144,4},{176,5},{208,6},{240,7},{272,... | collective-permute-start | bytes 49160 | tf_op jit(solution)/shard_map/ppermute | solution.py:66
  181.6 1.3 fusion.11
  182.9 1.3 fusion.28
  184.3 1.3 fusion.33
  185.6 1.3 fusion.35
  187.0 0.8 add_convert_fusion
  187.7 0.8 add_convert_fusion.1
  188.5 0.8 add_convert_fusion.2
  189.3 3.5 %collective-permute-done.9 = bf16[32,256]{1,0:T(8,128)(2,1)S(1)} collective-permute-done((bf16[32,256]{1,0:T(8,128)(2,1)S(1)}, bf16[32,256]{1,0:T(8,128)(2,1)S(1)}, u32[]{:S(2)}, u32[]{:S(2)}) %collective-permute-start.9) | collective-permute-done | bytes 16416 | tf_op jit(solution)/shard_map/ppermute | solution.py:66
  192.7 0.6 pad_maximum_fusion.5
  (51 shorter events, 1.4 us)
Async XLA Ops:
  7.2 42.1 %copy-start.10 = (bf16[512,256]{1,0:T(8,128)(2,1)S(1)}, bf16[512,256]{1,0:T(8,128)(2,1)}, u32[]{:S(2)}) copy-start(bf16[512,256]{1,0:T(8,128)(2,1)} %param.13) | copy-start | bytes 786436
  7.2 117.4 %all-gather.2.cloned.1.call-start = ((), (), s32[]{:S(2)}) async-start(), calls=%async_computation.4 | async-start | bytes 2162688 | tf_op jit(solution)/shard_map/all_gather | solution.py:101
  8.7 35.4 %collective-permute-start.2 = (bf16[512,256]{1,0:T(8,128)(2,1)}, bf16[512,256]{1,0:T(8,128)(2,1)S(1)}, u32[]{:S(2)}, u32[]{:S(2)}) collective-permute-start(bf16[512,256]{1,0:T(8,128)(2,1)} %param.13), channel_id=1, source_target_pairs={{0,64},{64,0},{1,65},{65,1},{2,66},{66,2},{3,67},{67,3},{4,68},{68... | collective-permute-start | bytes 786440 | tf_op jit(solution)/shard_map/ppermute | solution.py:52
  12.7 19.7 %collective-permute-start = (bf16[2,32,256]{2,1,0:T(8,128)(2,1)S(1)}, bf16[2,32,256]{2,1,0:T(8,128)(2,1)S(1)}, u32[]{:S(2)}, u32[]{:S(2)}) collective-permute-start(bf16[2,32,256]{2,1,0:T(8,128)(2,1)S(1)} %get-tuple-element.113), channel_id=1, source_target_pairs={{0,0},{1,32},{2,16},{3,48},{4,128},{5,160},{6,144},{7,176},{8,256}... | collective-permute-start | bytes 98312 | tf_op jit(solution)/shard_map/ppermute | solution.py:61
  28.5 15.6 %collective-permute-start.1 = (bf16[2,32,256]{2,1,0:T(8,128)(2,1)S(1)}, bf16[2,32,256]{2,1,0:T(8,128)(2,1)S(1)}, u32[]{:S(2)}, u32[]{:S(2)}) collective-permute-start(bf16[2,32,256]{2,1,0:T(8,128)(2,1)S(1)} %get-tuple-element.112), channel_id=1, source_target_pairs={{0,16},{1,48},{2,0},{3,32},{4,144},{5,176},{6,128},{7,160},{8,272}... | collective-permute-start | bytes 98312 | tf_op jit(solution)/shard_map/ppermute | solution.py:61
  45.0 9.4 %all-to-all-start = ((bf16[8,32,1024]{2,1,0:T(8,128)(2,1)}), bf16[8,32,1024]{2,1,0:T(8,128)(2,1)S(1)}, u32[]{:S(2)}, u32[]{:S(2)}) async-start(bf16[8,32,1024]{2,1,0:T(8,128)(2,1)} %broadcast_in_dim.4), calls=%async_computation | async-start | bytes 1048576 | tf_op jit(solution)/shard_map/all_to_all | solution.py:74
  49.3 11.8 %copy-start.5 = (bf16[256,512]{1,0:T(8,128)(2,1)S(1)}, bf16[256,512]{1,0:T(8,128)(2,1)}, u32[]{:S(2)}) copy-start(bf16[256,512]{1,0:T(8,128)(2,1)} %param.11) | copy-start | bytes 786436
  49.3 13.7 %copy-start.6 = (bf16[256,512]{1,0:T(8,128)(2,1)S(1)}, bf16[256,512]{1,0:T(8,128)(2,1)}, u32[]{:S(2)}) copy-start(bf16[256,512]{1,0:T(8,128)(2,1)} %param.12) | copy-start | bytes 786436
  49.3 3.9 %collective-permute-start.3 = (bf16[512,512]{1,0:T(8,128)(2,1)S(1)}, bf16[512,512]{1,0:T(8,128)(2,1)S(1)}, u32[]{:S(2)}, u32[]{:S(2)}) collective-permute-start(bf16[512,512]{1,0:T(8,128)(2,1)S(1)} %constant_dynamic-update-slice_fusion), channel_id=1, source_target_pairs={{0,1},{1,0},{2,3},{3,2},{4,5},{5,4},{6,7},{7,6},{8,9},{9,8},{10,11... | collective-permute-start | bytes 1572872 | tf_op jit(solution)/shard_map/ppermute | solution.py:52
  55.7 24.3 %all-to-all-start.1 = ((bf16[16,16,1024]{2,1,0:T(8,128)(2,1)}), bf16[16,16,1024]{2,1,0:T(8,128)(2,1)S(1)}, u32[]{:S(2)}, u32[]{:S(2)}) async-start(bf16[16,16,1024]{2,1,0:T(8,128)(2,1)} %bitcast.7), calls=%async_computation.1 | async-start | bytes 1048576 | tf_op jit(solution)/shard_map/all_to_all | solution.py:80
  61.1 19.0 %collective-permute-start.4 = (bf16[256,512]{1,0:T(8,128)(2,1)S(1)}, bf16[256,512]{1,0:T(8,128)(2,1)S(1)}, u32[]{:S(2)}, u32[]{:S(2)}) collective-permute-start(bf16[256,512]{1,0:T(8,128)(2,1)S(1)} %copy-done.5), channel_id=1, source_target_pairs={{0,1},{1,0},{2,3},{3,2},{4,5},{5,4},{6,7},{7,6},{8,9},{9,8},{10,11... | collective-permute-start | bytes 786440 | tf_op jit(solution)/shard_map/ppermute | solution.py:52
  63.0 17.1 %collective-permute-start.5 = (bf16[256,512]{1,0:T(8,128)(2,1)S(1)}, bf16[256,512]{1,0:T(8,128)(2,1)S(1)}, u32[]{:S(2)}, u32[]{:S(2)}) collective-permute-start(bf16[256,512]{1,0:T(8,128)(2,1)S(1)} %copy-done.6), channel_id=1, source_target_pairs={{0,1},{1,0},{2,3},{3,2},{4,5},{5,4},{6,7},{7,6},{8,9},{9,8},{10,11... | collective-permute-start | bytes 786440 | tf_op jit(solution)/shard_map/ppermute | solution.py:52
  80.1 1.2 copy-start.11
  80.1 1.2 copy-start.8
  81.3 60.9 %all-to-all-start.2 = ((bf16[32,16,1024]{2,1,0:T(8,128)(2,1)}), bf16[32,16,1024]{2,1,0:T(8,128)(2,1)S(1)}, u32[]{:S(2)}, u32[]{:S(2)}) async-start(bf16[32,16,1024]{2,1,0:T(8,128)(2,1)} %broadcast_in_dim.5), calls=%async_computation.2 | async-start | bytes 2097152 | tf_op jit(solution)/shard_map/all_to_all | solution.py:74
  127.2 10.9 %collective-permute-start.6 = (bf16[512,1024]{1,0:T(8,128)(2,1)}, bf16[512,1024]{1,0:T(8,128)(2,1)}, u32[]{:S(2)}, u32[]{:S(2)}) collective-permute-start(bf16[512,1024]{1,0:T(8,128)(2,1)} %bitcast.11), channel_id=1, source_target_pairs={{0,1},{1,0},{2,3},{3,2},{4,5},{5,4},{6,7},{7,6},{8,9},{9,8},{10,11... | collective-permute-start | bytes 3145736 | tf_op jit(solution)/shard_map/ppermute | solution.py:52
  132.2 9.8 %collective-permute-start.7 = (bf16[256,512]{1,0:T(8,128)(2,1)S(1)}, bf16[256,512]{1,0:T(8,128)(2,1)S(1)}, u32[]{:S(2)}, u32[]{:S(2)}) collective-permute-start(bf16[256,512]{1,0:T(8,128)(2,1)S(1)} %slice.96), channel_id=1, source_target_pairs={{0,64},{64,0},{1,65},{65,1},{2,66},{66,2},{3,67},{67,3},{4,68},{68... | collective-permute-start | bytes 786440 | tf_op jit(solution)/shard_map/ppermute | solution.py:52
  143.0 3.2 %copy-start.7 = (bf16[256,512]{1,0:T(8,128)(2,1)S(1)}, bf16[256,512]{1,0:T(8,128)(2,1)}, u32[]{:S(2)}) copy-start(bf16[256,512]{1,0:T(8,128)(2,1)} %param.12) | copy-start | bytes 786436
  145.9 1.0 copy-start.9
  145.9 1.3 copy-start.12
  148.2 33.3 %copy-start = (f32[512,512]{1,0:T(8,128)S(1)}, f32[512,512]{1,0:T(8,128)}, u32[]{:S(2)}) copy-start(f32[512,512]{1,0:T(8,128)} %get-tuple-element.76) | copy-start | bytes 3145732
  148.2 34.7 %collective-permute-start.10 = (bf16[512,512]{1,0:T(8,128)(2,1)S(1)}, bf16[512,512]{1,0:T(8,128)(2,1)}, u32[]{:S(2)}, u32[]{:S(2)}) collective-permute-start(bf16[512,512]{1,0:T(8,128)(2,1)S(1)} %bitcast.37), channel_id=1, source_target_pairs={{0,1},{1,0},{2,3},{3,2},{4,5},{5,4},{6,7},{7,6},{8,9},{9,8},{10,11... | collective-permute-start | bytes 1572872 | tf_op jit(solution)/shard_map/ppermute | solution.py:52
  152.2 29.4 %collective-permute-start.11 = (bf16[512,512]{1,0:T(8,128)(2,1)}, bf16[512,512]{1,0:T(8,128)(2,1)}, u32[]{:S(2)}, u32[]{:S(2)}) collective-permute-start(bf16[512,512]{1,0:T(8,128)(2,1)} %slice.98), channel_id=1, source_target_pairs={{0,1},{1,0},{2,3},{3,2},{4,5},{5,4},{6,7},{7,6},{8,9},{9,8},{10,11... | collective-permute-start | bytes 1572872 | tf_op jit(solution)/shard_map/ppermute | solution.py:52
  154.1 9.5 %all-to-all-start.3 = ((bf16[8,64,256]{2,1,0:T(8,128)(2,1)}), bf16[8,64,256]{2,1,0:T(8,128)(2,1)S(1)}, u32[]{:S(2)}, u32[]{:S(2)}) async-start(bf16[8,64,256]{2,1,0:T(8,128)(2,1)} %bitcast.47), calls=%async_computation.3 | async-start | bytes 524288 | tf_op jit(solution)/shard_map/all_to_all | solution.py:80
  162.4 20.5 %copy-start.1 = (bf16[512,512]{1,0:T(8,128)(2,1)S(1)}, bf16[512,512]{1,0:T(8,128)(2,1)}, u32[]{:S(2)}) copy-start(bf16[512,512]{1,0:T(8,128)(2,1)} %get-tuple-element.79) | copy-start | bytes 1572868
  163.7 25.6 %collective-permute-start.8 = (bf16[32,256]{1,0:T(8,128)(2,1)S(1)}, bf16[32,256]{1,0:T(8,128)(2,1)S(1)}, u32[]{:S(2)}, u32[]{:S(2)}) collective-permute-start(bf16[32,256]{1,0:T(8,128)(2,1)S(1)} %get-tuple-element.117), channel_id=1, source_target_pairs={{0,0},{32,1},{64,2},{96,3},{128,4},{160,5},{192,6},{224,7},{256,8}... | collective-permute-start | bytes 49160 | tf_op jit(solution)/shard_map/ppermute | solution.py:66
  178.4 14.4 %collective-permute-start.9 = (bf16[32,256]{1,0:T(8,128)(2,1)S(1)}, bf16[32,256]{1,0:T(8,128)(2,1)S(1)}, u32[]{:S(2)}, u32[]{:S(2)}) collective-permute-start(bf16[32,256]{1,0:T(8,128)(2,1)S(1)} %get-tuple-element.116), channel_id=1, source_target_pairs={{16,0},{48,1},{80,2},{112,3},{144,4},{176,5},{208,6},{240,7},{272,... | collective-permute-start | bytes 49160 | tf_op jit(solution)/shard_map/ppermute | solution.py:66
  182.9 4.1 %copy-start.4 = (f32[512,256]{1,0:T(8,128)S(1)}, f32[512,256]{1,0:T(8,128)}, u32[]{:S(2)}) copy-start(f32[512,256]{1,0:T(8,128)} %fusion.31) | copy-start | bytes 1572868
  184.3 3.4 %copy-start.2 = (f32[256,512]{1,0:T(8,128)S(1)}, f32[256,512]{1,0:T(8,128)}, u32[]{:S(2)}) copy-start(f32[256,512]{1,0:T(8,128)} %fusion.37) | copy-start | bytes 1572868
  185.6 2.9 %copy-start.3 = (f32[256,512]{1,0:T(8,128)S(1)}, f32[256,512]{1,0:T(8,128)}, u32[]{:S(2)}) copy-start(f32[256,512]{1,0:T(8,128)} %fusion.39) | copy-start | bytes 1572868
Sparse Core Ops, SparseCore 0:
  11.8 112.7 all-gather.1

commit v15 on v13

--- a/solution.py
+++ b/solution.py
@@ -98,10 +98,13 @@
 def local(activations, out_grad, gate_pre, up_pre, gate_weight, up_weight, down_weight):
     yl, zh, core = lax.axis_index("yl"), lax.axis_index("zh"), lax.axis_index("core")
     upper, mine, odd = lax.axis_index("zl") == 1, zh % 2 == yl, zh % 2 == 1
-    pre = gather_copies(jnp.concatenate([gate_pre, up_pre], axis=1), "zh", 4)
+    pre = jnp.concatenate([gate_pre, up_pre], axis=1)
     tiles = to_features(jnp.stack([out_grad, activations]), upper, mine)
-    (own, other), pre, down_y = lax.optimization_barrier((tiles, pre, swap(down_weight, "yl")))
-    pre = lax.all_gather(pre, ("yh", "yl"), axis=0, tiled=True)
+    (own, other), pre_x, down_y = lax.optimization_barrier(
+        (tiles, swap(pre, "yl"), swap(down_weight, "yl"))
+    )
+    pre = jnp.concatenate(choose(yl == 0, pre, pre_x), axis=0)
+    pre = lax.all_gather(pre, HALF, axis=0, tiled=True)
     cols = gather_copies(jnp.concatenate([own[0], other[0], other[1], own[1]], axis=1), PLANE, 8)
     down = jnp.concatenate([down_weight, down_y], axis=1)
     down = jnp.concatenate([down, swap(down)], axis=0)
@@ -112,9 +115,9 @@
     )
 
     hidden_grad = gather_copies(hidden_grad, ROW, R)
-    pre = pre.reshape(8, 2, 64, 1024)
-    pre_a, pre_b = choose(core == 1, pre[:, 1], pre[:, 0])
-    pre_a, pre_b = pre_a.reshape(512, 1024), pre_b.reshape(512, 1024)
+    pre = pre.reshape(4, 2, 2, 2, 32, 1024)
+    pre = tuple(pre[:, at].transpose(0, 2, 1, 3, 4).reshape(512, 1024) for at in (1, 0))
+    pre_a, pre_b = choose(core == 1, *pre)
     cols_y = swap(cols[:, 256:768], "yl")
     pre_y = swap(pre_b)
     slope_a, active_a, hidden_a = slopes(pre_a[:, :512], pre_a[:, 512:])

time: 185 us -> 209 us (1.13)
  waiting for transfers between devices: 50.9 us -> 64.5 us
  starting transfers between devices: 83.7 us -> 94.2 us
  other arithmetic: 16.2 us -> 13.9 us
  local copies, waits for them, and re-layouts: 4.66 us -> 6.83 us
    all_gather x1, waiting for transfers between devices: 0.02 us -> 43.1 us  [local(): pre = lax.all_gather(pre, HALF, axis=0, tiled=True)]
    ppermute x8 -> x9, waiting for transfers between devices: 14.8 us -> 1.9 us  [swap(): return lax.ppermute(value, axis, [(0, 1), (1, 0)])]
    all_to_all x2, waiting for transfers between devices: 21.2 us -> 11.3 us  [scatter_sum(): got = lax.all_to_all(pieces, axes, 0, 0, tiled=True)]
    all_to_all x2, starting transfers between devices: 9.84 us -> 16.9 us  [scatter_sum(): got = lax.all_to_all(pieces, axes, 0, 0, tiled=True)]
    all_to_all x3 -> x2, starting transfers between devices: 18.8 us -> 13 us  [gather_copies(): got = lax.all_to_all(copies, axes, 0, 0, tiled=True)]
    ppermute x1, waiting for transfers between devices: 12 us -> 7.06 us  [to_features(): lax.ppermute(two, AXES, IN_TWO)]
    ppermute x1, starting transfers between devices: 13 us -> 16.4 us  [to_features(): lax.ppermute(one, AXES, IN_ONE)]
    ppermute x8 -> x9, starting transfers between devices: 22.3 us -> 25.6 us  [swap(): return lax.ppermute(value, axis, [(0, 1), (1, 0)])]
  transfers between devices with their start and end apart: 18 -> 18, of which waited for: 7 -> 5; matrix products, arithmetic and copies ran while one was open for 13% -> 12% of each run, Pallas kernels for 0% -> 0%
where the time goes in v15:
time: 209 us; the launch traced here: 208 us
  starting transfers between devices  94.2 us (45%)
  waiting for transfers between devices  64.5 us (31%)
  between operations  14.5 us (7%)
  other arithmetic  13.9 us (7%)
  matrix products  13.8 us (7%)
  local copies, waits for them, and re-layouts  6.83 us (3%)
    all_gather x1, waiting for transfers between devices, local(): pre = lax.all_gather(pre, HALF, axis=0, tiled=True)  43.1 us
    ppermute x9, starting transfers between devices, swap(): return lax.ppermute(value, axis, [(0, 1), (1, 0)])  25.6 us
    all_to_all x2, starting transfers between devices, scatter_sum(): got = lax.all_to_all(pieces, axes, 0, 0, tiled=True)  16.9 us
    ppermute x1, starting transfers between devices, to_features(): lax.ppermute(one, AXES, IN_ONE)  16.4 us
    all_to_all x2, starting transfers between devices, gather_copies(): got = lax.all_to_all(copies, axes, 0, 0, tiled=True)  13 us
    ppermute x1, starting transfers between devices, to_tokens(): lax.ppermute(one, AXES, OUT_ONE)  12.8 us
    all_to_all x2, waiting for transfers between devices, scatter_sum(): got = lax.all_to_all(pieces, axes, 0, 0, tiled=True)  11.3 us
    dot_general x6, matrix products, contract_rows(): lax.dot_general(left, right, (((0,), (0,)), ((), ())), preferred_element_...  10.5 us
  transfers between devices with their start and end apart: 18, of which 5 were waited for; matrix products, arithmetic and copies ran while one was open for 12% of the time, Pallas kernels for 0%

profile of v15, /device:TPU:5, one launch (start us, length us, event | category | flops | bytes accessed | tf_op | source)
XLA Modules:
  0.0 207.7 jit_solution(11897306897892146422)
XLA Ops:
  7.2 0.9 broadcast_select_fusion.4
  8.1 16.4 %collective-permute-start = (bf16[2,32,256]{2,1,0:T(8,128)(2,1)S(1)}, bf16[2,32,256]{2,1,0:T(8,128)(2,1)S(1)}, u32[]{:S(2)}, u32[]{:S(2)}) collective-permute-start(bf16[2,32,256]{2,1,0:T(8,128)(2,1)S(1)} %get-tuple-element.111), channel_id=1, source_target_pairs={{0,0},{1,32},{2,16},{3,48},{4,128},{5,160},{6,144},{7,176},{8,256}... | collective-permute-start | bytes 98312 | tf_op jit(solution)/shard_map/ppermute | solution.py:61
  24.5 1.9 collective-permute-start.1
  26.4 2.3 %collective-permute-start.3 = (bf16[512,256]{1,0:T(8,128)(2,1)}, bf16[512,256]{1,0:T(8,128)(2,1)S(1)}, u32[]{:S(2)}, u32[]{:S(2)}) collective-permute-start(bf16[512,256]{1,0:T(8,128)(2,1)} %param.13), channel_id=1, source_target_pairs={{0,64},{64,0},{1,65},{65,1},{2,66},{66,2},{3,67},{67,3},{4,68},{68... | collective-permute-start | bytes 786440 | tf_op jit(solution)/shard_map/ppermute | solution.py:52
  28.8 0.8 constant_dynamic-update-slice_fusion.1
  29.5 0.8 constant_dynamic-update-slice_fusion
  30.3 3.0 %collective-permute-start.2 = (bf16[32,1024]{1,0:T(8,128)(2,1)S(1)}, bf16[32,1024]{1,0:T(8,128)(2,1)S(1)}, u32[]{:S(2)}, u32[]{:S(2)}) collective-permute-start(bf16[32,1024]{1,0:T(8,128)(2,1)S(1)} %constant_dynamic-update-slice_fusion), channel_id=1, source_target_pairs={{0,64},{64,0},{1,65},{65,1},{2,66},{66,2},{3,67},{67,3},{4,68},{68... | collective-permute-start | bytes 196616 | tf_op jit(solution)/shard_map/ppermute | solution.py:52
  33.3 7.1 %collective-permute-done.1 = bf16[2,32,256]{2,1,0:T(8,128)(2,1)S(1)} collective-permute-done((bf16[2,32,256]{2,1,0:T(8,128)(2,1)S(1)}, bf16[2,32,256]{2,1,0:T(8,128)(2,1)S(1)}, u32[]{:S(2)}, u32[]{:S(2)}) %collective-permute-start.1) | collective-permute-done | bytes 32800 | tf_op jit(solution)/shard_map/ppermute | solution.py:61
  40.4 0.7 pad_maximum_fusion.2
  41.1 0.9 broadcast_in_dim.4
  42.0 4.2 %all-to-all-start = ((bf16[8,32,1024]{2,1,0:T(8,128)(2,1)}), bf16[8,32,1024]{2,1,0:T(8,128)(2,1)S(1)}, u32[]{:S(2)}, u32[]{:S(2)}) async-start(bf16[8,32,1024]{2,1,0:T(8,128)(2,1)} %broadcast_in_dim.4), calls=%async_computation | async-start | bytes 1048576 | tf_op jit(solution)/shard_map/all_to_all | solution.py:74
  46.3 2.1 collective-permute-start.4
  48.4 1.9 collective-permute-done.4
  50.2 1.1 all-to-all-done
  51.4 1.3 convolution_convert_fusion
  52.7 8.9 %all-to-all-start.1 = ((bf16[16,16,1024]{2,1,0:T(8,128)(2,1)}), bf16[16,16,1024]{2,1,0:T(8,128)(2,1)S(1)}, u32[]{:S(2)}, u32[]{:S(2)}) async-start(bf16[16,16,1024]{2,1,0:T(8,128)(2,1)} %bitcast.7), calls=%async_computation.1 | async-start | bytes 1048576 | tf_op jit(solution)/shard_map/all_to_all | solution.py:80
  61.6 4.6 %collective-permute-start.5 = (bf16[256,512]{1,0:T(8,128)(2,1)S(1)}, bf16[256,512]{1,0:T(8,128)(2,1)S(1)}, u32[]{:S(2)}, u32[]{:S(2)}) collective-permute-start(bf16[256,512]{1,0:T(8,128)(2,1)S(1)} %copy-done.6), channel_id=1, source_target_pairs={{0,1},{1,0},{2,3},{3,2},{4,5},{5,4},{6,7},{7,6},{8,9},{9,8},{10,11... | collective-permute-start | bytes 786440 | tf_op jit(solution)/shard_map/ppermute | solution.py:52
  66.2 1.9 collective-permute-start.6
  68.1 11.3 %all-to-all-done.1 = bf16[16,16,1024]{2,1,0:T(8,128)(2,1)S(1)} async-done(((bf16[16,16,1024]{2,1,0:T(8,128)(2,1)}), bf16[16,16,1024]{2,1,0:T(8,128)(2,1)S(1)}, u32[]{:S(2)}, u32[]{:S(2)}) %all-to-all-start.1) | async-done | bytes 524320 | tf_op jit(solution)/shard_map/all_to_all | solution.py:80
  79.5 1.1 broadcast_in_dim.5
  80.7 8.8 %all-to-all-start.2 = ((bf16[32,16,1024]{2,1,0:T(8,128)(2,1)}), bf16[32,16,1024]{2,1,0:T(8,128)(2,1)S(1)}, u32[]{:S(2)}, u32[]{:S(2)}) async-start(bf16[32,16,1024]{2,1,0:T(8,128)(2,1)} %broadcast_in_dim.5), calls=%async_computation.2 | async-start | bytes 2097152 | tf_op jit(solution)/shard_map/all_to_all | solution.py:74
  89.4 43.1 %all-gather.2.cloned.1.call-done = bf16[1024,1024]{1,0:T(8,128)(2,1)} async-done(((bf16[64,1024]{1,0:T(8,128)(2,1)}), bf16[1024,1024]{1,0:T(8,128)(2,1)}) %all-gather.2.cloned.1.call-update) | async-done | bytes 2097168 | tf_op jit(solution)/shard_map/all_gather | solution.py:107
  132.5 1.7 select_bitcast_fusion
  134.2 2.5 %collective-permute-start.7 = (bf16[512,1024]{1,0:T(8,128)(2,1)S(1)}, bf16[512,1024]{1,0:T(8,128)(2,1)}, u32[]{:S(2)}, u32[]{:S(2)}) collective-permute-start(bf16[512,1024]{1,0:T(8,128)(2,1)S(1)} %bitcast.44), channel_id=1, source_target_pairs={{0,1},{1,0},{2,3},{3,2},{4,5},{5,4},{6,7},{7,6},{8,9},{9,8},{10,11... | collective-permute-start | bytes 3145736 | tf_op jit(solution)/shard_map/ppermute | solution.py:52
  136.7 1.0 slice.96
  137.7 4.2 %collective-permute-start.8 = (bf16[256,512]{1,0:T(8,128)(2,1)S(1)}, bf16[256,512]{1,0:T(8,128)(2,1)S(1)}, u32[]{:S(2)}, u32[]{:S(2)}) collective-permute-start(bf16[256,512]{1,0:T(8,128)(2,1)S(1)} %slice.96), channel_id=1, source_target_pairs={{0,64},{64,0},{1,65},{65,1},{2,66},{66,2},{3,67},{67,3},{4,68},{68... | collective-permute-start | bytes 786440 | tf_op jit(solution)/shard_map/ppermute | solution.py:52
  141.9 1.0 fusion.43
  143.0 2.5 %fusion.6 = (bf16[512,512]{1,0:T(8,128)(2,1)}, f32[512,512]{1,0:T(8,128)}, f32[512,512]{1,0:T(8,128)}, f32[512,512]{1,0:T(8,128)S(1)}, f32[512,512]{1,0:T(8,128)}, /*index=5*/bf16[512,512]{1,0:T(8,128)(2,1)}) fusion(bf16[512,1024]{1,0:T(8,128)(2,1)S(1)} %bitcast.46, bf16[512,1024]{1,0:T(8,128)(2,1)S(1)} %bitcast.45), kind=kLoop, calls=%fused_computation.31 | loop fusion | flops 6815744 | bytes 7340032 | tf_op jit(solution)/shard_map/convert_element_type | solution.py:90
  145.5 3.0 %convert_multiply_fusion = (f32[512,512]{1,0:T(8,128)}, f32[512,512]{1,0:T(8,128)}) fusion(bf16[512,1024]{1,0:T(8,128)(2,1)} %collective-permute-done.7), kind=kLoop, calls=%fused_computation | loop fusion | flops 2883584 | bytes 3145728 | tf_op jit(solution)/shard_map/mul | solution.py:88
  148.7 0.8 slice.98
  149.5 2.9 %fusion.12 = (bf16[512,512]{1,0:T(8,128)(2,1)S(1)}, bf16[512,512]{1,0:T(8,128)(2,1)S(1)}, bf16[512,512]{1,0:T(8,128)(2,1)S(1)}, bf16[512,512]{1,0:T(8,128)(2,1)S(1)}) fusion(f32[512,512]{1,0:T(8,128)} %get-tuple-element.60, bf16[512,1024]{1,0:T(8,128)(2,1)S(1)} %bitcast.43, f32[512,512]{1,0:T(8,128)} %get-tuple-element.59, f32[512,512]{1,0:T(8,128)} %get-tuple-element.58, ...), kind=kLoop, calls=%fused_computation.37 | loop fusion | flops 2621440 | bytes 7340032 | tf_op jit(solution)/shard_map/convert_element_type | solution.py:95
  152.4 0.3 fusion.44
  152.8 0.3 convolution_add_fusion.4
  153.3 0.3 fusion.45
  153.7 1.0 fusion.1
  154.7 1.1 fusion.37
  155.9 8.0 %all-to-all-start.3 = ((bf16[8,64,256]{2,1,0:T(8,128)(2,1)}), bf16[8,64,256]{2,1,0:T(8,128)(2,1)S(1)}, u32[]{:S(2)}, u32[]{:S(2)}) async-start(bf16[8,64,256]{2,1,0:T(8,128)(2,1)} %bitcast.57), calls=%async_computation.3 | async-start | bytes 524288 | tf_op jit(solution)/shard_map/all_to_all | solution.py:80
  163.9 3.3 %collective-permute-start.12 = (bf16[512,512]{1,0:T(8,128)(2,1)}, bf16[512,512]{1,0:T(8,128)(2,1)}, u32[]{:S(2)}, u32[]{:S(2)}) collective-permute-start(bf16[512,512]{1,0:T(8,128)(2,1)} %slice.98), channel_id=1, source_target_pairs={{0,1},{1,0},{2,3},{3,2},{4,5},{5,4},{6,7},{7,6},{8,9},{9,8},{10,11... | collective-permute-start | bytes 1572872 | tf_op jit(solution)/shard_map/ppermute | solution.py:52
  167.2 1.1 fusion.39
  168.3 1.9 collective-permute-start.11
  170.2 2.2 %fusion.33 = f32[512,256]{1,0:T(8,128)} fusion(bf16[512,512]{1,0:T(8,128)(2,1)} %get-tuple-element.70, bf16[512,512]{1,0:T(8,128)(2,1)S(1)} %bitcast.50), kind=kOutput, calls=%fused_computation.62 | convolution fusion | flops 134217728 | bytes 1310720 | tf_op jit(solution)/shard_map/dot_general | solution.py:40
  172.5 7.5 %collective-permute-start.10 = (bf16[32,256]{1,0:T(8,128)(2,1)S(1)}, bf16[32,256]{1,0:T(8,128)(2,1)S(1)}, u32[]{:S(2)}, u32[]{:S(2)}) collective-permute-start(bf16[32,256]{1,0:T(8,128)(2,1)S(1)} %get-tuple-element.114), channel_id=1, source_target_pairs={{16,0},{48,1},{80,2},{112,3},{144,4},{176,5},{208,6},{240,7},{272,... | collective-permute-start | bytes 49160 | tf_op jit(solution)/shard_map/ppermute | solution.py:66
  180.0 12.8 %collective-permute-start.9 = (bf16[32,256]{1,0:T(8,128)(2,1)S(1)}, bf16[32,256]{1,0:T(8,128)(2,1)S(1)}, u32[]{:S(2)}, u32[]{:S(2)}) collective-permute-start(bf16[32,256]{1,0:T(8,128)(2,1)S(1)} %get-tuple-element.115), channel_id=1, source_target_pairs={{0,0},{32,1},{64,2},{96,3},{128,4},{160,5},{192,6},{224,7},{256,8}... | collective-permute-start | bytes 49160 | tf_op jit(solution)/shard_map/ppermute | solution.py:66
  192.8 1.3 fusion.14
  194.2 2.1 fusion.4
  196.3 2.0 fusion.3
  198.3 2.0 fusion.2
  200.2 0.6 pad_maximum_fusion.5
  (57 shorter events, 0.9 us)
Async XLA Ops:
  7.2 39.1 %copy-start.11 = (bf16[512,256]{1,0:T(8,128)(2,1)S(1)}, bf16[512,256]{1,0:T(8,128)(2,1)}, u32[]{:S(2)}) copy-start(bf16[512,256]{1,0:T(8,128)(2,1)} %param.13) | copy-start | bytes 786436
  7.2 125.3 %all-gather.2.cloned.1.call-start = ((), (), s32[]{:S(2)}) async-start(), calls=%async_computation.4 | async-start | bytes 2228224 | tf_op jit(solution)/shard_map/all_gather | solution.py:107
  8.1 25.2 %collective-permute-start = (bf16[2,32,256]{2,1,0:T(8,128)(2,1)S(1)}, bf16[2,32,256]{2,1,0:T(8,128)(2,1)S(1)}, u32[]{:S(2)}, u32[]{:S(2)}) collective-permute-start(bf16[2,32,256]{2,1,0:T(8,128)(2,1)S(1)} %get-tuple-element.111), channel_id=1, source_target_pairs={{0,0},{1,32},{2,16},{3,48},{4,128},{5,160},{6,144},{7,176},{8,256}... | collective-permute-start | bytes 98312 | tf_op jit(solution)/shard_map/ppermute | solution.py:61
  24.5 15.9 %collective-permute-start.1 = (bf16[2,32,256]{2,1,0:T(8,128)(2,1)S(1)}, bf16[2,32,256]{2,1,0:T(8,128)(2,1)S(1)}, u32[]{:S(2)}, u32[]{:S(2)}) collective-permute-start(bf16[2,32,256]{2,1,0:T(8,128)(2,1)S(1)} %get-tuple-element.110), channel_id=1, source_target_pairs={{0,16},{1,48},{2,0},{3,32},{4,144},{5,176},{6,128},{7,160},{8,272}... | collective-permute-start | bytes 98312 | tf_op jit(solution)/shard_map/ppermute | solution.py:61
  26.4 13.9 %collective-permute-start.3 = (bf16[512,256]{1,0:T(8,128)(2,1)}, bf16[512,256]{1,0:T(8,128)(2,1)S(1)}, u32[]{:S(2)}, u32[]{:S(2)}) collective-permute-start(bf16[512,256]{1,0:T(8,128)(2,1)} %param.13), channel_id=1, source_target_pairs={{0,64},{64,0},{1,65},{65,1},{2,66},{66,2},{3,67},{67,3},{4,68},{68... | collective-permute-start | bytes 786440 | tf_op jit(solution)/shard_map/ppermute | solution.py:52
  30.3 10.1 %collective-permute-start.2 = (bf16[32,1024]{1,0:T(8,128)(2,1)S(1)}, bf16[32,1024]{1,0:T(8,128)(2,1)S(1)}, u32[]{:S(2)}, u32[]{:S(2)}) collective-permute-start(bf16[32,1024]{1,0:T(8,128)(2,1)S(1)} %constant_dynamic-update-slice_fusion), channel_id=1, source_target_pairs={{0,64},{64,0},{1,65},{65,1},{2,66},{66,2},{3,67},{67,3},{4,68},{68... | collective-permute-start | bytes 196616 | tf_op jit(solution)/shard_map/ppermute | solution.py:52
  42.0 9.4 %all-to-all-start = ((bf16[8,32,1024]{2,1,0:T(8,128)(2,1)}), bf16[8,32,1024]{2,1,0:T(8,128)(2,1)S(1)}, u32[]{:S(2)}, u32[]{:S(2)}) async-start(bf16[8,32,1024]{2,1,0:T(8,128)(2,1)} %broadcast_in_dim.4), calls=%async_computation | async-start | bytes 1048576 | tf_op jit(solution)/shard_map/all_to_all | solution.py:74
  46.3 15.3 %copy-start.6 = (bf16[256,512]{1,0:T(8,128)(2,1)S(1)}, bf16[256,512]{1,0:T(8,128)(2,1)}, u32[]{:S(2)}) copy-start(bf16[256,512]{1,0:T(8,128)(2,1)} %param.11) | copy-start | bytes 786436
  46.3 19.9 %copy-start.7 = (bf16[256,512]{1,0:T(8,128)(2,1)S(1)}, bf16[256,512]{1,0:T(8,128)(2,1)}, u32[]{:S(2)}) copy-start(bf16[256,512]{1,0:T(8,128)(2,1)} %param.12) | copy-start | bytes 786436
  46.3 3.9 %collective-permute-start.4 = (bf16[512,512]{1,0:T(8,128)(2,1)S(1)}, bf16[512,512]{1,0:T(8,128)(2,1)S(1)}, u32[]{:S(2)}, u32[]{:S(2)}) collective-permute-start(bf16[512,512]{1,0:T(8,128)(2,1)S(1)} %constant_dynamic-update-slice_fusion.2), channel_id=1, source_target_pairs={{0,1},{1,0},{2,3},{3,2},{4,5},{5,4},{6,7},{7,6},{8,9},{9,8},{10,11... | collective-permute-start | bytes 1572872 | tf_op jit(solution)/shard_map/ppermute | solution.py:52
  51.4 1.3 copy-start.5
  52.7 26.8 %all-to-all-start.1 = ((bf16[16,16,1024]{2,1,0:T(8,128)(2,1)}), bf16[16,16,1024]{2,1,0:T(8,128)(2,1)S(1)}, u32[]{:S(2)}, u32[]{:S(2)}) async-start(bf16[16,16,1024]{2,1,0:T(8,128)(2,1)} %bitcast.7), calls=%async_computation.1 | async-start | bytes 1048576 | tf_op jit(solution)/shard_map/all_to_all | solution.py:80
  61.6 17.9 %collective-permute-start.5 = (bf16[256,512]{1,0:T(8,128)(2,1)S(1)}, bf16[256,512]{1,0:T(8,128)(2,1)S(1)}, u32[]{:S(2)}, u32[]{:S(2)}) collective-permute-start(bf16[256,512]{1,0:T(8,128)(2,1)S(1)} %copy-done.6), channel_id=1, source_target_pairs={{0,1},{1,0},{2,3},{3,2},{4,5},{5,4},{6,7},{7,6},{8,9},{9,8},{10,11... | collective-permute-start | bytes 786440 | tf_op jit(solution)/shard_map/ppermute | solution.py:52
  66.2 13.4 %collective-permute-start.6 = (bf16[256,512]{1,0:T(8,128)(2,1)S(1)}, bf16[256,512]{1,0:T(8,128)(2,1)S(1)}, u32[]{:S(2)}, u32[]{:S(2)}) collective-permute-start(bf16[256,512]{1,0:T(8,128)(2,1)S(1)} %copy-done.7), channel_id=1, source_target_pairs={{0,1},{1,0},{2,3},{3,2},{4,5},{5,4},{6,7},{7,6},{8,9},{9,8},{10,11... | collective-permute-start | bytes 786440 | tf_op jit(solution)/shard_map/ppermute | solution.py:52
  79.5 1.2 copy-start.12
  79.5 53.0 %copy-start.9 = (bf16[256,512]{1,0:T(8,128)(2,1)}, bf16[256,512]{1,0:T(8,128)(2,1)S(1)}, u32[]{:S(2)}) copy-start(bf16[256,512]{1,0:T(8,128)(2,1)S(1)} %collective-permute-done.6) | copy-start | bytes 786436
  80.7 68.0 %all-to-all-start.2 = ((bf16[32,16,1024]{2,1,0:T(8,128)(2,1)}), bf16[32,16,1024]{2,1,0:T(8,128)(2,1)S(1)}, u32[]{:S(2)}, u32[]{:S(2)}) async-start(bf16[32,16,1024]{2,1,0:T(8,128)(2,1)} %broadcast_in_dim.5), calls=%async_computation.2 | async-start | bytes 2097152 | tf_op jit(solution)/shard_map/all_to_all | solution.py:74
  134.2 11.2 %collective-permute-start.7 = (bf16[512,1024]{1,0:T(8,128)(2,1)S(1)}, bf16[512,1024]{1,0:T(8,128)(2,1)}, u32[]{:S(2)}, u32[]{:S(2)}) collective-permute-start(bf16[512,1024]{1,0:T(8,128)(2,1)S(1)} %bitcast.44), channel_id=1, source_target_pairs={{0,1},{1,0},{2,3},{3,2},{4,5},{5,4},{6,7},{7,6},{8,9},{9,8},{10,11... | collective-permute-start | bytes 3145736 | tf_op jit(solution)/shard_map/ppermute | solution.py:52
  137.7 10.8 %collective-permute-start.8 = (bf16[256,512]{1,0:T(8,128)(2,1)S(1)}, bf16[256,512]{1,0:T(8,128)(2,1)S(1)}, u32[]{:S(2)}, u32[]{:S(2)}) collective-permute-start(bf16[256,512]{1,0:T(8,128)(2,1)S(1)} %slice.96), channel_id=1, source_target_pairs={{0,64},{64,0},{1,65},{65,1},{2,66},{66,2},{3,67},{67,3},{4,68},{68... | collective-permute-start | bytes 786440 | tf_op jit(solution)/shard_map/ppermute | solution.py:52
  149.5 3.2 %copy-start.8 = (bf16[256,512]{1,0:T(8,128)(2,1)S(1)}, bf16[256,512]{1,0:T(8,128)(2,1)}, u32[]{:S(2)}) copy-start(bf16[256,512]{1,0:T(8,128)(2,1)} %param.12) | copy-start | bytes 786436
  152.4 1.0 copy-start.10
  152.4 1.3 copy-start.13
  154.7 38.1 %copy-start = (f32[512,512]{1,0:T(8,128)S(1)}, f32[512,512]{1,0:T(8,128)}, u32[]{:S(2)}) copy-start(f32[512,512]{1,0:T(8,128)} %get-tuple-element.75) | copy-start | bytes 3145732
  155.9 16.5 %all-to-all-start.3 = ((bf16[8,64,256]{2,1,0:T(8,128)(2,1)}), bf16[8,64,256]{2,1,0:T(8,128)(2,1)S(1)}, u32[]{:S(2)}, u32[]{:S(2)}) async-start(bf16[8,64,256]{2,1,0:T(8,128)(2,1)} %bitcast.57), calls=%async_computation.3 | async-start | bytes 524288 | tf_op jit(solution)/shard_map/all_to_all | solution.py:80
  163.9 28.9 %collective-permute-start.12 = (bf16[512,512]{1,0:T(8,128)(2,1)}, bf16[512,512]{1,0:T(8,128)(2,1)}, u32[]{:S(2)}, u32[]{:S(2)}) collective-permute-start(bf16[512,512]{1,0:T(8,128)(2,1)} %slice.98), channel_id=1, source_target_pairs={{0,1},{1,0},{2,3},{3,2},{4,5},{5,4},{6,7},{7,6},{8,9},{9,8},{10,11... | collective-permute-start | bytes 1572872 | tf_op jit(solution)/shard_map/ppermute | solution.py:52
  168.3 25.9 %collective-permute-start.11 = (bf16[512,512]{1,0:T(8,128)(2,1)S(1)}, bf16[512,512]{1,0:T(8,128)(2,1)}, u32[]{:S(2)}, u32[]{:S(2)}) collective-permute-start(bf16[512,512]{1,0:T(8,128)(2,1)S(1)} %bitcast.49), channel_id=1, source_target_pairs={{0,1},{1,0},{2,3},{3,2},{4,5},{5,4},{6,7},{7,6},{8,9},{9,8},{10,11... | collective-permute-start | bytes 1572872 | tf_op jit(solution)/shard_map/ppermute | solution.py:52
  172.4 21.8 %copy-start.1 = (bf16[512,512]{1,0:T(8,128)(2,1)S(1)}, bf16[512,512]{1,0:T(8,128)(2,1)}, u32[]{:S(2)}) copy-start(bf16[512,512]{1,0:T(8,128)(2,1)} %get-tuple-element.80) | copy-start | bytes 1572868
  172.4 21.8 %copy-start.4 = (f32[512,256]{1,0:T(8,128)S(1)}, f32[512,256]{1,0:T(8,128)}, u32[]{:S(2)}) copy-start(f32[512,256]{1,0:T(8,128)} %fusion.33) | copy-start | bytes 1572868
  172.5 27.8 %collective-permute-start.10 = (bf16[32,256]{1,0:T(8,128)(2,1)S(1)}, bf16[32,256]{1,0:T(8,128)(2,1)S(1)}, u32[]{:S(2)}, u32[]{:S(2)}) collective-permute-start(bf16[32,256]{1,0:T(8,128)(2,1)S(1)} %get-tuple-element.114), channel_id=1, source_target_pairs={{16,0},{48,1},{80,2},{112,3},{144,4},{176,5},{208,6},{240,7},{272,... | collective-permute-start | bytes 49160 | tf_op jit(solution)/shard_map/ppermute | solution.py:66
  180.0 16.3 %copy-start.2 = (f32[256,512]{1,0:T(8,128)S(1)}, f32[256,512]{1,0:T(8,128)}, u32[]{:S(2)}) copy-start(f32[256,512]{1,0:T(8,128)} %fusion.37) | copy-start | bytes 1572868
  180.0 20.2 %collective-permute-start.9 = (bf16[32,256]{1,0:T(8,128)(2,1)S(1)}, bf16[32,256]{1,0:T(8,128)(2,1)S(1)}, u32[]{:S(2)}, u32[]{:S(2)}) collective-permute-start(bf16[32,256]{1,0:T(8,128)(2,1)S(1)} %get-tuple-element.115), channel_id=1, source_target_pairs={{0,0},{32,1},{64,2},{96,3},{128,4},{160,5},{192,6},{224,7},{256,8}... | collective-permute-start | bytes 49160 | tf_op jit(solution)/shard_map/ppermute | solution.py:66
  194.2 4.1 %copy-start.3 = (f32[256,512]{1,0:T(8,128)S(1)}, f32[256,512]{1,0:T(8,128)}, u32[]{:S(2)}) copy-start(f32[256,512]{1,0:T(8,128)} %fusion.39) | copy-start | bytes 1572868
Sparse Core Ops, SparseCore 0:
  41.2 91.2 all-gather.1

commit v16 on v13

--- a/solution.py
+++ b/solution.py
@@ -98,9 +98,17 @@
 def local(activations, out_grad, gate_pre, up_pre, gate_weight, up_weight, down_weight):
     yl, zh, core = lax.axis_index("yl"), lax.axis_index("zh"), lax.axis_index("core")
     upper, mine, odd = lax.axis_index("zl") == 1, zh % 2 == yl, zh % 2 == 1
-    pre = gather_copies(jnp.concatenate([gate_pre, up_pre], axis=1), "zh", 4)
+    pre = jnp.concatenate([gate_pre, up_pre], axis=1)
+    others = tuple(
+        lax.ppermute(pre, "zh", [(at, (at - step) % 4) for at in range(4)]) for step in (1, 2, 3)
+    )
     tiles = to_features(jnp.stack([out_grad, activations]), upper, mine)
-    (own, other), pre, down_y = lax.optimization_barrier((tiles, pre, swap(down_weight, "yl")))
+    (own, other), others, down_y = lax.optimization_barrier(
+        (tiles, others, swap(down_weight, "yl"))
+    )
+    pre = jnp.stack((pre,) + others)
+    pre = jnp.where(odd, jnp.concatenate([pre[3:], pre[:3]]), pre)
+    pre = jnp.where(zh >= 2, jnp.concatenate([pre[2:], pre[:2]]), pre).reshape(128, 1024)
     pre = lax.all_gather(pre, ("yh", "yl"), axis=0, tiled=True)
     cols = gather_copies(jnp.concatenate([own[0], other[0], other[1], own[1]], axis=1), PLANE, 8)
     down = jnp.concatenate([down_weight, down_y], axis=1)

time: 185 us -> 190 us (1.027)
  starting transfers between devices: 83.7 us -> 103 us
  waiting for transfers between devices: 50.9 us -> 37.1 us
    ppermute x0 -> x3, starting transfers between devices: none -> 13.2 us  [local(): lax.ppermute(pre, 'zh', [(at, (at - step) % 4) for at in range(4)])]
    ppermute x1, waiting for transfers between devices: 12 us -> 0.01 us  [to_features(): lax.ppermute(two, AXES, IN_TWO)]
    all_to_all x3 -> x2, starting transfers between devices: 18.8 us -> 9.6 us  [gather_copies(): got = lax.all_to_all(copies, axes, 0, 0, tiled=True)]
    ppermute x8, starting transfers between devices: 22.3 us -> 30.5 us  [swap(): return lax.ppermute(value, axis, [(0, 1), (1, 0)])]
    ppermute x0 -> x3, waiting for transfers between devices: none -> 5.15 us  [local(): lax.ppermute(pre, 'zh', [(at, (at - step) % 4) for at in range(4)])]
    all_to_all x2, starting transfers between devices: 9.84 us -> 14.5 us  [scatter_sum(): got = lax.all_to_all(pieces, axes, 0, 0, tiled=True)]
    ppermute x1, starting transfers between devices: 13 us -> 16.4 us  [to_features(): lax.ppermute(one, AXES, IN_ONE)]
    all_to_all x2, waiting for transfers between devices: 21.2 us -> 18 us  [scatter_sum(): got = lax.all_to_all(pieces, axes, 0, 0, tiled=True)]
  transfers between devices with their start and end apart: 18 -> 20, of which waited for: 7 -> 6; matrix products, arithmetic and copies ran while one was open for 13% -> 13% of each run, Pallas kernels for 0% -> 0%
where the time goes in v16:
time: 190 us; the launch traced here: 189 us
  starting transfers between devices  103 us (54%)
  waiting for transfers between devices  37.1 us (20%)
  other arithmetic  16.2 us (9%)
  between operations  14.5 us (8%)
  matrix products  13.8 us (7%)
  local copies, waits for them, and re-layouts  4.75 us (2%)
    ppermute x8, starting transfers between devices, swap(): return lax.ppermute(value, axis, [(0, 1), (1, 0)])  30.5 us
    all_to_all x2, waiting for transfers between devices, scatter_sum(): got = lax.all_to_all(pieces, axes, 0, 0, tiled=True)  18 us
    ppermute x1, starting transfers between devices, to_features(): lax.ppermute(one, AXES, IN_ONE)  16.4 us
    all_to_all x2, starting transfers between devices, scatter_sum(): got = lax.all_to_all(pieces, axes, 0, 0, tiled=True)  14.5 us
    ppermute x3, starting transfers between devices, local(): lax.ppermute(pre, 'zh', [(at, (at - step) % 4) for at in range(4)])  13.2 us
    ppermute x8, waiting for transfers between devices, swap(): return lax.ppermute(value, axis, [(0, 1), (1, 0)])  12.9 us
    dot_general x6, matrix products, contract_rows(): lax.dot_general(left, right, (((0,), (0,)), ((), ())), preferred_element_...  10.5 us
    ppermute x1, starting transfers between devices, to_tokens(): lax.ppermute(one, AXES, OUT_ONE)  10.4 us
  transfers between devices with their start and end apart: 20, of which 6 were waited for; matrix products, arithmetic and copies ran while one was open for 13% of the time, Pallas kernels for 0%

profile of v16, /device:TPU:5, one launch (start us, length us, event | category | flops | bytes accessed | tf_op | source)
XLA Modules:
  0.0 189.1 jit_solution(15306461145675134812)
XLA Ops:
  7.2 0.8 broadcast_select_fusion.4
  8.0 16.4 %collective-permute-start = (bf16[2,32,256]{2,1,0:T(8,128)(2,1)S(1)}, bf16[2,32,256]{2,1,0:T(8,128)(2,1)S(1)}, u32[]{:S(2)}, u32[]{:S(2)}) collective-permute-start(bf16[2,32,256]{2,1,0:T(8,128)(2,1)S(1)} %get-tuple-element.115), channel_id=1, source_target_pairs={{0,0},{1,32},{2,16},{3,48},{4,128},{5,160},{6,144},{7,176},{8,256}... | collective-permute-start | bytes 98312 | tf_op jit(solution)/shard_map/ppermute | solution.py:61
  24.4 1.9 %collective-permute-start.1 = (bf16[2,32,256]{2,1,0:T(8,128)(2,1)S(1)}, bf16[2,32,256]{2,1,0:T(8,128)(2,1)S(1)}, u32[]{:S(2)}, u32[]{:S(2)}) collective-permute-start(bf16[2,32,256]{2,1,0:T(8,128)(2,1)S(1)} %get-tuple-element.114), channel_id=1, source_target_pairs={{0,16},{1,48},{2,0},{3,32},{4,144},{5,176},{6,128},{7,160},{8,272}... | collective-permute-start | bytes 98312 | tf_op jit(solution)/shard_map/ppermute | solution.py:61
  26.4 2.3 %collective-permute-start.5 = (bf16[512,256]{1,0:T(8,128)(2,1)}, bf16[512,256]{1,0:T(8,128)(2,1)S(1)}, u32[]{:S(2)}, u32[]{:S(2)}) collective-permute-start(bf16[512,256]{1,0:T(8,128)(2,1)} %param.13), channel_id=1, source_target_pairs={{0,64},{64,0},{1,65},{65,1},{2,66},{66,2},{3,67},{67,3},{4,68},{68... | collective-permute-start | bytes 786440 | tf_op jit(solution)/shard_map/ppermute | solution.py:52
  28.7 0.8 constant_dynamic-update-slice_fusion.1
  29.5 0.8 constant_dynamic-update-slice_fusion
  30.2 5.7 %collective-permute-start.2 = (bf16[32,1024]{1,0:T(8,128)(2,1)S(1)}, bf16[32,1024]{1,0:T(8,128)(2,1)S(1)}, u32[]{:S(2)}, u32[]{:S(2)}) collective-permute-start(bf16[32,1024]{1,0:T(8,128)(2,1)S(1)} %constant_dynamic-update-slice_fusion), channel_id=1, source_target_pairs={{0,48},{16,0},{32,16},{48,32},{1,49},{17,1},{33,17},{49,33},{2,50}... | collective-permute-start | bytes 196616 | tf_op jit(solution)/shard_map/ppermute | solution.py:103
  36.0 5.4 %collective-permute-start.3 = (bf16[32,1024]{1,0:T(8,128)(2,1)S(1)}, bf16[32,1024]{1,0:T(8,128)(2,1)S(1)}, u32[]{:S(2)}, u32[]{:S(2)}) collective-permute-start(bf16[32,1024]{1,0:T(8,128)(2,1)S(1)} %constant_dynamic-update-slice_fusion), channel_id=1, source_target_pairs={{0,32},{16,48},{32,0},{48,16},{1,33},{17,49},{33,1},{49,17},{2,34}... | collective-permute-start | bytes 196616 | tf_op jit(solution)/shard_map/ppermute | solution.py:103
  41.4 2.1 %collective-permute-start.4 = (bf16[32,1024]{1,0:T(8,128)(2,1)S(1)}, bf16[32,1024]{1,0:T(8,128)(2,1)S(1)}, u32[]{:S(2)}, u32[]{:S(2)}) collective-permute-start(bf16[32,1024]{1,0:T(8,128)(2,1)S(1)} %constant_dynamic-update-slice_fusion), channel_id=1, source_target_pairs={{0,16},{16,32},{32,48},{48,0},{1,17},{17,33},{33,49},{49,1},{2,18}... | collective-permute-start | bytes 196616 | tf_op jit(solution)/shard_map/ppermute | solution.py:103
  43.5 1.4 collective-permute-done.3
  45.0 3.7 %collective-permute-done.4 = bf16[32,1024]{1,0:T(8,128)(2,1)S(1)} collective-permute-done((bf16[32,1024]{1,0:T(8,128)(2,1)S(1)}, bf16[32,1024]{1,0:T(8,128)(2,1)S(1)}, u32[]{:S(2)}, u32[]{:S(2)}) %collective-permute-start.4) | collective-permute-done | bytes 65568 | tf_op jit(solution)/shard_map/ppermute | solution.py:103
  48.8 0.8 maximum_select_fusion.1
  49.6 0.9 broadcast_in_dim.4
  50.5 4.2 %all-to-all-start = ((bf16[8,32,1024]{2,1,0:T(8,128)(2,1)}), bf16[8,32,1024]{2,1,0:T(8,128)(2,1)S(1)}, u32[]{:S(2)}, u32[]{:S(2)}) async-start(bf16[8,32,1024]{2,1,0:T(8,128)(2,1)} %broadcast_in_dim.4), calls=%async_computation | async-start | bytes 1048576 | tf_op jit(solution)/shard_map/all_to_all | solution.py:74
  54.8 6.9 %collective-permute-start.6 = (bf16[512,512]{1,0:T(8,128)(2,1)S(1)}, bf16[512,512]{1,0:T(8,128)(2,1)S(1)}, u32[]{:S(2)}, u32[]{:S(2)}) collective-permute-start(bf16[512,512]{1,0:T(8,128)(2,1)S(1)} %constant_dynamic-update-slice_fusion.2), channel_id=1, source_target_pairs={{0,1},{1,0},{2,3},{3,2},{4,5},{5,4},{6,7},{7,6},{8,9},{9,8},{10,11... | collective-permute-start | bytes 1572872 | tf_op jit(solution)/shard_map/ppermute | solution.py:52
  61.7 1.5 collective-permute-done.6
  63.2 1.3 convolution_convert_fusion
  64.5 9.2 %all-to-all-start.1 = ((bf16[16,16,1024]{2,1,0:T(8,128)(2,1)}), bf16[16,16,1024]{2,1,0:T(8,128)(2,1)S(1)}, u32[]{:S(2)}, u32[]{:S(2)}) async-start(bf16[16,16,1024]{2,1,0:T(8,128)(2,1)} %bitcast.7), calls=%async_computation.1 | async-start | bytes 1048576 | tf_op jit(solution)/shard_map/all_to_all | solution.py:80
  73.8 4.6 %collective-permute-start.7 = (bf16[256,512]{1,0:T(8,128)(2,1)S(1)}, bf16[256,512]{1,0:T(8,128)(2,1)S(1)}, u32[]{:S(2)}, u32[]{:S(2)}) collective-permute-start(bf16[256,512]{1,0:T(8,128)(2,1)S(1)} %copy-done.5), channel_id=1, source_target_pairs={{0,1},{1,0},{2,3},{3,2},{4,5},{5,4},{6,7},{7,6},{8,9},{9,8},{10,11... | collective-permute-start | bytes 786440 | tf_op jit(solution)/shard_map/ppermute | solution.py:52
  78.3 1.9 %collective-permute-start.8 = (bf16[256,512]{1,0:T(8,128)(2,1)S(1)}, bf16[256,512]{1,0:T(8,128)(2,1)S(1)}, u32[]{:S(2)}, u32[]{:S(2)}) collective-permute-start(bf16[256,512]{1,0:T(8,128)(2,1)S(1)} %copy-done.6), channel_id=1, source_target_pairs={{0,1},{1,0},{2,3},{3,2},{4,5},{5,4},{6,7},{7,6},{8,9},{9,8},{10,11... | collective-permute-start | bytes 786440 | tf_op jit(solution)/shard_map/ppermute | solution.py:52
  80.3 18.0 %all-to-all-done.1 = bf16[16,16,1024]{2,1,0:T(8,128)(2,1)S(1)} async-done(((bf16[16,16,1024]{2,1,0:T(8,128)(2,1)}), bf16[16,16,1024]{2,1,0:T(8,128)(2,1)S(1)}, u32[]{:S(2)}, u32[]{:S(2)}) %all-to-all-start.1) | async-done | bytes 524320 | tf_op jit(solution)/shard_map/all_to_all | solution.py:80
  98.4 1.1 broadcast_in_dim.5
  99.5 5.4 %all-to-all-start.2 = ((bf16[32,16,1024]{2,1,0:T(8,128)(2,1)}), bf16[32,16,1024]{2,1,0:T(8,128)(2,1)S(1)}, u32[]{:S(2)}, u32[]{:S(2)}) async-start(bf16[32,16,1024]{2,1,0:T(8,128)(2,1)} %broadcast_in_dim.5), calls=%async_computation.2 | async-start | bytes 2097152 | tf_op jit(solution)/shard_map/all_to_all | solution.py:74
  104.9 2.7 %broadcast_select_fusion = (bf16[8,1,64,1024]{3,2,1,0:T(8,128)(2,1)}, bf16[8,1,64,1024]{3,2,1,0:T(8,128)(2,1)S(1)}) fusion(pred[]{:T(512)S(6)} %eq.22, bf16[8,2,64,1024]{3,2,1,0:T(8,128)(2,1)} %bitcast.46), kind=kLoop, calls=%fused_computation.56 | loop fusion | flops 1048576 | bytes 4194305 | tf_op jit(solution)/shard_map/jit(_where)/select_n | solution.py:56
  107.6 4.5 %collective-permute-start.9 = (bf16[512,1024]{1,0:T(8,128)(2,1)}, bf16[512,1024]{1,0:T(8,128)(2,1)}, u32[]{:S(2)}, u32[]{:S(2)}) collective-permute-start(bf16[512,1024]{1,0:T(8,128)(2,1)} %bitcast.16), channel_id=1, source_target_pairs={{0,1},{1,0},{2,3},{3,2},{4,5},{5,4},{6,7},{7,6},{8,9},{9,8},{10,11... | collective-permute-start | bytes 3145736 | tf_op jit(solution)/shard_map/ppermute | solution.py:52
  112.1 3.4 %collective-permute-start.10 = (bf16[256,512]{1,0:T(8,128)(2,1)S(1)}, bf16[256,512]{1,0:T(8,128)(2,1)S(1)}, u32[]{:S(2)}, u32[]{:S(2)}) collective-permute-start(bf16[256,512]{1,0:T(8,128)(2,1)S(1)} %slice.106), channel_id=1, source_target_pairs={{0,64},{64,0},{1,65},{65,1},{2,66},{66,2},{3,67},{67,3},{4,68},{68... | collective-permute-start | bytes 786440 | tf_op jit(solution)/shard_map/ppermute | solution.py:52
  115.6 3.7 %fusion.6 = (bf16[512,512]{1,0:T(8,128)(2,1)}, f32[512,512]{1,0:T(8,128)}, f32[512,512]{1,0:T(8,128)}, f32[512,512]{1,0:T(8,128)S(1)}, f32[512,512]{1,0:T(8,128)}, /*index=5*/bf16[512,512]{1,0:T(8,128)(2,1)}) fusion(bf16[512,1024]{1,0:T(8,128)(2,1)S(1)} %bitcast.41, bf16[512,1024]{1,0:T(8,128)(2,1)} %bitcast.16), kind=kLoop, calls=%fused_computation.31 | loop fusion | flops 6815744 | bytes 7340032 | tf_op jit(solution)/shard_map/convert_element_type | solution.py:90
  119.3 3.0 %convert_multiply_fusion = (f32[512,512]{1,0:T(8,128)}, f32[512,512]{1,0:T(8,128)}) fusion(bf16[512,1024]{1,0:T(8,128)(2,1)} %collective-permute-done.9), kind=kLoop, calls=%fused_computation | loop fusion | flops 2883584 | bytes 3145728 | tf_op jit(solution)/shard_map/mul | solution.py:88
  122.3 11.4 %collective-permute-done.10 = bf16[256,512]{1,0:T(8,128)(2,1)S(1)} collective-permute-done((bf16[256,512]{1,0:T(8,128)(2,1)S(1)}, bf16[256,512]{1,0:T(8,128)(2,1)S(1)}, u32[]{:S(2)}, u32[]{:S(2)}) %collective-permute-start.10) | collective-permute-done | bytes 262176 | tf_op jit(solution)/shard_map/ppermute | solution.py:52
  133.9 0.8 slice.108
  134.7 2.9 %fusion.12 = (bf16[512,512]{1,0:T(8,128)(2,1)S(1)}, bf16[512,512]{1,0:T(8,128)(2,1)S(1)}, bf16[512,512]{1,0:T(8,128)(2,1)S(1)}, bf16[512,512]{1,0:T(8,128)(2,1)S(1)}) fusion(f32[512,512]{1,0:T(8,128)} %get-tuple-element.64, bf16[512,1024]{1,0:T(8,128)(2,1)S(1)} %bitcast.40, f32[512,512]{1,0:T(8,128)} %get-tuple-element.63, f32[512,512]{1,0:T(8,128)} %get-tuple-element.62, ...), kind=kLoop, calls=%fused_computation.37 | loop fusion | flops 2621440 | bytes 7340032 | tf_op jit(solution)/shard_map/convert_element_type | solution.py:95
  137.6 0.3 fusion.45
  138.5 0.3 fusion.46
  138.9 1.0 fusion.1
  139.9 1.1 fusion.37
  141.1 5.3 %all-to-all-start.3 = ((bf16[8,64,256]{2,1,0:T(8,128)(2,1)}), bf16[8,64,256]{2,1,0:T(8,128)(2,1)S(1)}, u32[]{:S(2)}, u32[]{:S(2)}) async-start(bf16[8,64,256]{2,1,0:T(8,128)(2,1)} %bitcast.53), calls=%async_computation.3 | async-start | bytes 524288 | tf_op jit(solution)/shard_map/all_to_all | solution.py:80
  146.3 5.0 %collective-permute-start.14 = (bf16[512,512]{1,0:T(8,128)(2,1)}, bf16[512,512]{1,0:T(8,128)(2,1)}, u32[]{:S(2)}, u32[]{:S(2)}) collective-permute-start(bf16[512,512]{1,0:T(8,128)(2,1)} %slice.108), channel_id=1, source_target_pairs={{0,1},{1,0},{2,3},{3,2},{4,5},{5,4},{6,7},{7,6},{8,9},{9,8},{10,11... | collective-permute-start | bytes 1572872 | tf_op jit(solution)/shard_map/ppermute | solution.py:52
  151.3 1.1 fusion.39
  152.4 1.9 %collective-permute-start.13 = (bf16[512,512]{1,0:T(8,128)(2,1)S(1)}, bf16[512,512]{1,0:T(8,128)(2,1)}, u32[]{:S(2)}, u32[]{:S(2)}) collective-permute-start(bf16[512,512]{1,0:T(8,128)(2,1)S(1)} %bitcast.44), channel_id=1, source_target_pairs={{0,1},{1,0},{2,3},{3,2},{4,5},{5,4},{6,7},{7,6},{8,9},{9,8},{10,11... | collective-permute-start | bytes 1572872 | tf_op jit(solution)/shard_map/ppermute | solution.py:52
  154.4 2.2 %fusion.33 = f32[512,256]{1,0:T(8,128)} fusion(bf16[512,512]{1,0:T(8,128)(2,1)} %get-tuple-element.74, bf16[512,512]{1,0:T(8,128)(2,1)S(1)} %bitcast.45), kind=kOutput, calls=%fused_computation.64 | convolution fusion | flops 134217728 | bytes 1310720 | tf_op jit(solution)/shard_map/dot_general | solution.py:40
  156.6 10.4 %collective-permute-start.11 = (bf16[32,256]{1,0:T(8,128)(2,1)S(1)}, bf16[32,256]{1,0:T(8,128)(2,1)S(1)}, u32[]{:S(2)}, u32[]{:S(2)}) collective-permute-start(bf16[32,256]{1,0:T(8,128)(2,1)S(1)} %get-tuple-element.119), channel_id=1, source_target_pairs={{0,0},{32,1},{64,2},{96,3},{128,4},{160,5},{192,6},{224,7},{256,8}... | collective-permute-start | bytes 49160 | tf_op jit(solution)/shard_map/ppermute | solution.py:66
  167.1 6.1 %collective-permute-start.12 = (bf16[32,256]{1,0:T(8,128)(2,1)S(1)}, bf16[32,256]{1,0:T(8,128)(2,1)S(1)}, u32[]{:S(2)}, u32[]{:S(2)}) collective-permute-start(bf16[32,256]{1,0:T(8,128)(2,1)S(1)} %get-tuple-element.118), channel_id=1, source_target_pairs={{16,0},{48,1},{80,2},{112,3},{144,4},{176,5},{208,6},{240,7},{272,... | collective-permute-start | bytes 49160 | tf_op jit(solution)/shard_map/ppermute | solution.py:66
  173.2 1.3 fusion.14
  174.6 2.1 %fusion.4 = bf16[512,256]{1,0:T(8,128)(2,1)} fusion(f32[512,256]{1,0:T(8,128)S(1)} %copy-done.4, bf16[512,512]{1,0:T(8,128)(2,1)S(1)} %copy-done.1, bf16[512,512]{1,0:T(8,128)(2,1)} %collective-permute-done.13), kind=kOutput, calls=%fused_computation.29 | convolution fusion | flops 134479872 | bytes 1572864 | tf_op jit(solution)/shard_map/dot_general | solution.py:40
  176.6 2.0 %fusion.3 = bf16[256,512]{1,0:T(8,128)(2,1)} fusion(f32[256,512]{1,0:T(8,128)S(1)} %copy-done.2, bf16[512,512]{1,0:T(8,128)(2,1)S(1)} %get-tuple-element.82, bf16[512,512]{1,0:T(8,128)(2,1)} %collective-permute-done.13), kind=kOutput, calls=%fused_computation.28 | convolution fusion | flops 134479872 | bytes 1572864 | tf_op jit(solution)/shard_map/dot_general | solution.py:40
  178.6 2.0 %fusion.2 = bf16[256,512]{1,0:T(8,128)(2,1)} fusion(f32[256,512]{1,0:T(8,128)S(1)} %copy-done.3, bf16[512,512]{1,0:T(8,128)(2,1)S(1)} %get-tuple-element.80, bf16[512,512]{1,0:T(8,128)(2,1)} %collective-permute-done.13), kind=kOutput, calls=%fused_computation.27 | convolution fusion | flops 134479872 | bytes 1572864 | tf_op jit(solution)/shard_map/dot_general | solution.py:40
  180.6 1.0 collective-permute-done.12
  181.6 0.6 pad_maximum_fusion.4
  (58 shorter events, 1.2 us)
Async XLA Ops:
  7.2 97.7 %all-gather.2.cloned.1.call-start = ((), (), s32[]{:S(2)}) async-start(), calls=%async_computation.4 | async-start | bytes 2359296 | tf_op jit(solution)/shard_map/all_gather | solution.py:112
  8.0 33.4 %collective-permute-start = (bf16[2,32,256]{2,1,0:T(8,128)(2,1)S(1)}, bf16[2,32,256]{2,1,0:T(8,128)(2,1)S(1)}, u32[]{:S(2)}, u32[]{:S(2)}) collective-permute-start(bf16[2,32,256]{2,1,0:T(8,128)(2,1)S(1)} %get-tuple-element.115), channel_id=1, source_target_pairs={{0,0},{1,32},{2,16},{3,48},{4,128},{5,160},{6,144},{7,176},{8,256}... | collective-permute-start | bytes 98312 | tf_op jit(solution)/shard_map/ppermute | solution.py:61
  24.4 19.1 %collective-permute-start.1 = (bf16[2,32,256]{2,1,0:T(8,128)(2,1)S(1)}, bf16[2,32,256]{2,1,0:T(8,128)(2,1)S(1)}, u32[]{:S(2)}, u32[]{:S(2)}) collective-permute-start(bf16[2,32,256]{2,1,0:T(8,128)(2,1)S(1)} %get-tuple-element.114), channel_id=1, source_target_pairs={{0,16},{1,48},{2,0},{3,32},{4,144},{5,176},{6,128},{7,160},{8,272}... | collective-permute-start | bytes 98312 | tf_op jit(solution)/shard_map/ppermute | solution.py:61
  26.4 22.3 %collective-permute-start.5 = (bf16[512,256]{1,0:T(8,128)(2,1)}, bf16[512,256]{1,0:T(8,128)(2,1)S(1)}, u32[]{:S(2)}, u32[]{:S(2)}) collective-permute-start(bf16[512,256]{1,0:T(8,128)(2,1)} %param.13), channel_id=1, source_target_pairs={{0,64},{64,0},{1,65},{65,1},{2,66},{66,2},{3,67},{67,3},{4,68},{68... | collective-permute-start | bytes 786440 | tf_op jit(solution)/shard_map/ppermute | solution.py:52
  30.2 13.3 %collective-permute-start.2 = (bf16[32,1024]{1,0:T(8,128)(2,1)S(1)}, bf16[32,1024]{1,0:T(8,128)(2,1)S(1)}, u32[]{:S(2)}, u32[]{:S(2)}) collective-permute-start(bf16[32,1024]{1,0:T(8,128)(2,1)S(1)} %constant_dynamic-update-slice_fusion), channel_id=1, source_target_pairs={{0,48},{16,0},{32,16},{48,32},{1,49},{17,1},{33,17},{49,33},{2,50}... | collective-permute-start | bytes 196616 | tf_op jit(solution)/shard_map/ppermute | solution.py:103
  36.0 9.0 %collective-permute-start.3 = (bf16[32,1024]{1,0:T(8,128)(2,1)S(1)}, bf16[32,1024]{1,0:T(8,128)(2,1)S(1)}, u32[]{:S(2)}, u32[]{:S(2)}) collective-permute-start(bf16[32,1024]{1,0:T(8,128)(2,1)S(1)} %constant_dynamic-update-slice_fusion), channel_id=1, source_target_pairs={{0,32},{16,48},{32,0},{48,16},{1,33},{17,49},{33,1},{49,17},{2,34}... | collective-permute-start | bytes 196616 | tf_op jit(solution)/shard_map/ppermute | solution.py:103
  41.4 13.3 %copy-start.10 = (bf16[512,256]{1,0:T(8,128)(2,1)S(1)}, bf16[512,256]{1,0:T(8,128)(2,1)}, u32[]{:S(2)}) copy-start(bf16[512,256]{1,0:T(8,128)(2,1)} %param.13) | copy-start | bytes 786436
  41.4 7.3 %collective-permute-start.4 = (bf16[32,1024]{1,0:T(8,128)(2,1)S(1)}, bf16[32,1024]{1,0:T(8,128)(2,1)S(1)}, u32[]{:S(2)}, u32[]{:S(2)}) collective-permute-start(bf16[32,1024]{1,0:T(8,128)(2,1)S(1)} %constant_dynamic-update-slice_fusion), channel_id=1, source_target_pairs={{0,16},{16,32},{32,48},{48,0},{1,17},{17,33},{33,49},{49,1},{2,18}... | collective-permute-start | bytes 196616 | tf_op jit(solution)/shard_map/ppermute | solution.py:103
  50.5 12.8 %all-to-all-start = ((bf16[8,32,1024]{2,1,0:T(8,128)(2,1)}), bf16[8,32,1024]{2,1,0:T(8,128)(2,1)S(1)}, u32[]{:S(2)}, u32[]{:S(2)}) async-start(bf16[8,32,1024]{2,1,0:T(8,128)(2,1)} %broadcast_in_dim.4), calls=%async_computation | async-start | bytes 1048576 | tf_op jit(solution)/shard_map/all_to_all | solution.py:74
  54.7 19.0 %copy-start.5 = (bf16[256,512]{1,0:T(8,128)(2,1)S(1)}, bf16[256,512]{1,0:T(8,128)(2,1)}, u32[]{:S(2)}) copy-start(bf16[256,512]{1,0:T(8,128)(2,1)} %param.11) | copy-start | bytes 786436
  54.8 23.6 %copy-start.6 = (bf16[256,512]{1,0:T(8,128)(2,1)S(1)}, bf16[256,512]{1,0:T(8,128)(2,1)}, u32[]{:S(2)}) copy-start(bf16[256,512]{1,0:T(8,128)(2,1)} %param.12) | copy-start | bytes 786436
  54.8 8.4 %collective-permute-start.6 = (bf16[512,512]{1,0:T(8,128)(2,1)S(1)}, bf16[512,512]{1,0:T(8,128)(2,1)S(1)}, u32[]{:S(2)}, u32[]{:S(2)}) collective-permute-start(bf16[512,512]{1,0:T(8,128)(2,1)S(1)} %constant_dynamic-update-slice_fusion.2), channel_id=1, source_target_pairs={{0,1},{1,0},{2,3},{3,2},{4,5},{5,4},{6,7},{7,6},{8,9},{9,8},{10,11... | collective-permute-start | bytes 1572872 | tf_op jit(solution)/shard_map/ppermute | solution.py:52
  64.5 33.7 %all-to-all-start.1 = ((bf16[16,16,1024]{2,1,0:T(8,128)(2,1)}), bf16[16,16,1024]{2,1,0:T(8,128)(2,1)S(1)}, u32[]{:S(2)}, u32[]{:S(2)}) async-start(bf16[16,16,1024]{2,1,0:T(8,128)(2,1)} %bitcast.7), calls=%async_computation.1 | async-start | bytes 1048576 | tf_op jit(solution)/shard_map/all_to_all | solution.py:80
  73.8 24.6 %collective-permute-start.7 = (bf16[256,512]{1,0:T(8,128)(2,1)S(1)}, bf16[256,512]{1,0:T(8,128)(2,1)S(1)}, u32[]{:S(2)}, u32[]{:S(2)}) collective-permute-start(bf16[256,512]{1,0:T(8,128)(2,1)S(1)} %copy-done.5), channel_id=1, source_target_pairs={{0,1},{1,0},{2,3},{3,2},{4,5},{5,4},{6,7},{7,6},{8,9},{9,8},{10,11... | collective-permute-start | bytes 786440 | tf_op jit(solution)/shard_map/ppermute | solution.py:52
  78.3 20.0 %collective-permute-start.8 = (bf16[256,512]{1,0:T(8,128)(2,1)S(1)}, bf16[256,512]{1,0:T(8,128)(2,1)S(1)}, u32[]{:S(2)}, u32[]{:S(2)}) collective-permute-start(bf16[256,512]{1,0:T(8,128)(2,1)S(1)} %copy-done.6), channel_id=1, source_target_pairs={{0,1},{1,0},{2,3},{3,2},{4,5},{5,4},{6,7},{7,6},{8,9},{9,8},{10,11... | collective-permute-start | bytes 786440 | tf_op jit(solution)/shard_map/ppermute | solution.py:52
  98.3 1.1 copy-start.11
  98.4 1.1 copy-start.8
  99.5 34.4 %all-to-all-start.2 = ((bf16[32,16,1024]{2,1,0:T(8,128)(2,1)}), bf16[32,16,1024]{2,1,0:T(8,128)(2,1)S(1)}, u32[]{:S(2)}, u32[]{:S(2)}) async-start(bf16[32,16,1024]{2,1,0:T(8,128)(2,1)} %broadcast_in_dim.5), calls=%async_computation.2 | async-start | bytes 2097152 | tf_op jit(solution)/shard_map/all_to_all | solution.py:74
  107.6 11.7 %collective-permute-start.9 = (bf16[512,1024]{1,0:T(8,128)(2,1)}, bf16[512,1024]{1,0:T(8,128)(2,1)}, u32[]{:S(2)}, u32[]{:S(2)}) collective-permute-start(bf16[512,1024]{1,0:T(8,128)(2,1)} %bitcast.16), channel_id=1, source_target_pairs={{0,1},{1,0},{2,3},{3,2},{4,5},{5,4},{6,7},{7,6},{8,9},{9,8},{10,11... | collective-permute-start | bytes 3145736 | tf_op jit(solution)/shard_map/ppermute | solution.py:52
  112.1 21.6 %collective-permute-start.10 = (bf16[256,512]{1,0:T(8,128)(2,1)S(1)}, bf16[256,512]{1,0:T(8,128)(2,1)S(1)}, u32[]{:S(2)}, u32[]{:S(2)}) collective-permute-start(bf16[256,512]{1,0:T(8,128)(2,1)S(1)} %slice.106), channel_id=1, source_target_pairs={{0,64},{64,0},{1,65},{65,1},{2,66},{66,2},{3,67},{67,3},{4,68},{68... | collective-permute-start | bytes 786440 | tf_op jit(solution)/shard_map/ppermute | solution.py:52
  134.7 3.2 %copy-start.7 = (bf16[256,512]{1,0:T(8,128)(2,1)S(1)}, bf16[256,512]{1,0:T(8,128)(2,1)}, u32[]{:S(2)}) copy-start(bf16[256,512]{1,0:T(8,128)(2,1)} %param.12) | copy-start | bytes 786436
  137.6 1.0 copy-start.9
  137.6 1.3 copy-start.12
  139.9 33.2 %copy-start = (f32[512,512]{1,0:T(8,128)S(1)}, f32[512,512]{1,0:T(8,128)}, u32[]{:S(2)}) copy-start(f32[512,512]{1,0:T(8,128)} %get-tuple-element.79) | copy-start | bytes 3145732
  141.1 15.5 %all-to-all-start.3 = ((bf16[8,64,256]{2,1,0:T(8,128)(2,1)}), bf16[8,64,256]{2,1,0:T(8,128)(2,1)S(1)}, u32[]{:S(2)}, u32[]{:S(2)}) async-start(bf16[8,64,256]{2,1,0:T(8,128)(2,1)} %bitcast.53), calls=%async_computation.3 | async-start | bytes 524288 | tf_op jit(solution)/shard_map/all_to_all | solution.py:80
  146.3 26.8 %collective-permute-start.14 = (bf16[512,512]{1,0:T(8,128)(2,1)}, bf16[512,512]{1,0:T(8,128)(2,1)}, u32[]{:S(2)}, u32[]{:S(2)}) collective-permute-start(bf16[512,512]{1,0:T(8,128)(2,1)} %slice.108), channel_id=1, source_target_pairs={{0,1},{1,0},{2,3},{3,2},{4,5},{5,4},{6,7},{7,6},{8,9},{9,8},{10,11... | collective-permute-start | bytes 1572872 | tf_op jit(solution)/shard_map/ppermute | solution.py:52
  152.4 22.1 %collective-permute-start.13 = (bf16[512,512]{1,0:T(8,128)(2,1)S(1)}, bf16[512,512]{1,0:T(8,128)(2,1)}, u32[]{:S(2)}, u32[]{:S(2)}) collective-permute-start(bf16[512,512]{1,0:T(8,128)(2,1)S(1)} %bitcast.44), channel_id=1, source_target_pairs={{0,1},{1,0},{2,3},{3,2},{4,5},{5,4},{6,7},{7,6},{8,9},{9,8},{10,11... | collective-permute-start | bytes 1572872 | tf_op jit(solution)/shard_map/ppermute | solution.py:52
  156.6 18.0 %copy-start.1 = (bf16[512,512]{1,0:T(8,128)(2,1)S(1)}, bf16[512,512]{1,0:T(8,128)(2,1)}, u32[]{:S(2)}) copy-start(bf16[512,512]{1,0:T(8,128)(2,1)} %get-tuple-element.84) | copy-start | bytes 1572868
  156.6 17.9 %copy-start.4 = (f32[512,256]{1,0:T(8,128)S(1)}, f32[512,256]{1,0:T(8,128)}, u32[]{:S(2)}) copy-start(f32[512,256]{1,0:T(8,128)} %fusion.33) | copy-start | bytes 1572868
  156.6 23.9 %collective-permute-start.11 = (bf16[32,256]{1,0:T(8,128)(2,1)S(1)}, bf16[32,256]{1,0:T(8,128)(2,1)S(1)}, u32[]{:S(2)}, u32[]{:S(2)}) collective-permute-start(bf16[32,256]{1,0:T(8,128)(2,1)S(1)} %get-tuple-element.119), channel_id=1, source_target_pairs={{0,0},{32,1},{64,2},{96,3},{128,4},{160,5},{192,6},{224,7},{256,8}... | collective-permute-start | bytes 49160 | tf_op jit(solution)/shard_map/ppermute | solution.py:66
  167.1 9.5 %copy-start.2 = (f32[256,512]{1,0:T(8,128)S(1)}, f32[256,512]{1,0:T(8,128)}, u32[]{:S(2)}) copy-start(f32[256,512]{1,0:T(8,128)} %fusion.37) | copy-start | bytes 1572868
  167.1 14.5 %collective-permute-start.12 = (bf16[32,256]{1,0:T(8,128)(2,1)S(1)}, bf16[32,256]{1,0:T(8,128)(2,1)S(1)}, u32[]{:S(2)}, u32[]{:S(2)}) collective-permute-start(bf16[32,256]{1,0:T(8,128)(2,1)S(1)} %get-tuple-element.118), channel_id=1, source_target_pairs={{16,0},{48,1},{80,2},{112,3},{144,4},{176,5},{208,6},{240,7},{272,... | collective-permute-start | bytes 49160 | tf_op jit(solution)/shard_map/ppermute | solution.py:66
  174.5 4.1 %copy-start.3 = (f32[256,512]{1,0:T(8,128)S(1)}, f32[256,512]{1,0:T(8,128)}, u32[]{:S(2)}) copy-start(f32[256,512]{1,0:T(8,128)} %fusion.39) | copy-start | bytes 1572868
Sparse Core Ops, SparseCore 0:
  49.7 50.8 all-gather.1
